TPU v7x, 512 devices: a whole 4x8x8 slice. The times are simulated.
512 devices in a mesh: segment: 16 (over y, z_lo), tensor: 32 (over z_hi, x, core).
Axes of the slice: x: 4, y: 8, z: 8 (z_hi: 4, z_lo: 2; z = z_hi * 2 + z_lo), core: 2. Of those that a mesh axis runs over, the one named last changes fastest.
Arguments:
- entering: bfloat16 [16, 128, 6144], P('segment', None, 'tensor'), may hold values from -6 to 6
- fresh_rows: bfloat16 [1, 128, 6144], P(None, None, 'tensor'), may hold values from -6 to 6
- norm_gain: float32 [16, 6144], P('segment'), may hold values from 0.1 to 1.9
- segment_weight: bfloat16 [16, 6144, 6144], P('segment', 'tensor'), may hold values from -0.078125 to 0.078125
- projection: bfloat16 [6144, 9216], P('segment', 'tensor'), may hold values from -0.078125 to 0.078125
- teacher_rows: bfloat16 [16, 2, 128, 9216], P('segment', None, None, 'tensor'), may hold values from -6 to 6
Outputs:
- leaving: bfloat16 [16, 128, 6144], P('segment', None, 'tensor')
- projection_grad: float32 [6144, 9216], P('segment', 'tensor')
All inputs are finite; a program needn't handle non-finite values.
Results may differ from a plain program's by a relative error of at most 0.018.
Values may be sent and summed in bfloat16 or wider, within the bound.
No kernel may reach another device: no remote copies, remote signals or barrier semaphores. Data moves between devices by JAX's collectives and lax.ppermute only.
A program may use at most 64 MiB of HBM per device.

v0:
```python
import jax
import jax.numpy as jnp
from jax import lax
from jax.sharding import PartitionSpec as P

TICKS = 2


EPSILON = 1e-05


def shifted(shard, axis, by):
    length = lax.axis_size(axis)
    pairs = [(i, i + by) for i in range(length) if 0 <= i + by < length]
    return lax.ppermute(shard, axis, pairs)


def gathered_rows(local_rows):
    return lax.all_gather(local_rows, "tensor", axis=1, tiled=True)


def on_device(entering, fresh_rows, norm_gain, segment_weight, projection, teacher_rows):
    segment_index = lax.axis_index("segment")
    columns = lax.all_gather(projection, "segment", axis=0, tiled=True)
    norm_scales = norm_gain[0]
    weights = segment_weight[0]
    kept_rows = []
    kept_diffs = []
    local_rows = entering[0]
    outgoing = local_rows
    outgoing_full = None
    for tick_index in range(TICKS):
        if tick_index > 0:
            received = shifted(outgoing, "segment", 1)
            local_rows = jnp.where(segment_index == 0, fresh_rows[tick_index - 1], received)
            full_rows = gathered_rows(local_rows)
        else:
            local_rows = entering[0]
            full_rows = gathered_rows(local_rows)
        full_float = full_rows.astype(jnp.float32)
        mean_square = jnp.mean(full_float * full_float, axis=-1, keepdims=True)
        normed = (full_float * lax.rsqrt(mean_square + EPSILON) * norm_scales[None, :]).astype(
            jnp.bfloat16
        )
        hidden_sum = lax.dot_general(
            normed, weights, (((1,), (1,)), ((), ())), preferred_element_type=jnp.float32
        )
        outgoing = (local_rows.astype(jnp.float32) + jax.nn.silu(hidden_sum)).astype(jnp.bfloat16)
        outgoing_full = gathered_rows(outgoing)
        predicted = jnp.dot(outgoing_full, columns, preferred_element_type=jnp.float32)
        difference = (predicted - teacher_rows[0, tick_index].astype(jnp.float32)).astype(
            jnp.bfloat16
        )
        kept_rows.append(outgoing_full)
        kept_diffs.append(difference)
    stacked_rows = jnp.concatenate(kept_rows, axis=0)
    stacked_diffs = jnp.concatenate(kept_diffs, axis=0)
    row_count = stacked_rows.shape[0]
    scale_factor = 1.0 / row_count
    segment_term = lax.dot_general(
        stacked_rows, stacked_diffs, (((0,), (0,)), ((), ())), preferred_element_type=jnp.float32
    )
    rounded = lax.optimization_barrier((segment_term * scale_factor).astype(jnp.bfloat16)).astype(
        jnp.float32
    )
    gradient = lax.psum_scatter(
        rounded.astype(jnp.bfloat16), "segment", scatter_dimension=0, tiled=True
    ).astype(jnp.float32)
    return (outgoing[None], gradient)


def solution(mesh):
    return jax.shard_map(
        on_device,
        mesh=mesh,
        in_specs=(
            P("segment", None, "tensor"),
            P(None, None, "tensor"),
            P("segment", None),
            P("segment", "tensor", None),
            P("segment", "tensor"),
            P("segment", None, None, "tensor"),
        ),
        out_specs=(P("segment", None, "tensor"), P("segment", "tensor")),
        check_vma=False,
    )
```

profile of v0, /device:TPU:1, one launch (start us, length us, event | category | flops | bytes accessed | tf_op | source)
XLA Modules:
  0.0 487.7 jit_solution(12139011849657465198)
XLA Ops:
  7.2 0.0 copy-start
  7.2 0.0 all-gather.15.cloned.1.call-start
  7.2 0.7 all-gather.15.cloned.1.call-update
  7.9 0.0 all-gather.7.cloned.1.call-start
  8.0 68.3 %all-gather.15.cloned.1.call-done = bf16[1,128,6144]{1,2,0:T(8,128)(2,1)} async-done(((bf16[1,128,192]{1,2,0:T(8,128)(2,1)}), bf16[1,128,6144]{1,2,0:T(8,128)(2,1)}) %all-gather.15.cloned.1.call-update) | async-done | bytes 1572880 | tf_op jit(solution)/shard_map/all_gather | solution.py:19
  76.3 2.2 fusion.4
  78.6 2.7 fusion.26
  81.3 1.8 collective-permute-start
  83.1 1.2 collective-permute-done
  84.3 0.6 bitcast_select_fusion
  84.9 0.0 all-gather.7.cloned.1.call-update
  84.9 0.0 all-gather.9.cloned.1.call-start
  85.0 0.7 all-gather.9.cloned.1.call-update
  85.7 0.0 all-gather.13.cloned.1.call-start
  85.7 0.5 all-gather.13.cloned.1.call-update
  86.2 0.0 all-gather.11.cloned.1.call-start
  86.3 60.3 %all-gather.7.cloned.1.call-done = bf16[128,6144]{0,1:T(8,128)(2,1)} async-done(((bf16[128,192]{0,1:T(8,128)(2,1)}), bf16[128,6144]{0,1:T(8,128)(2,1)}) %all-gather.7.cloned.1.call-update) | async-done | bytes 1572880 | tf_op jit(solution)/shard_map/all_gather | solution.py:19
  146.6 2.2 fusion.1
  148.8 3.3 add_convert_fusion
  152.2 0.0 all-gather.11.cloned.1.call-update
  152.2 0.0 reduce-scatter.4.cloned.1.call-start
  152.2 54.5 %all-gather.9.cloned.1.call-done = bf16[128,6144]{0,1:T(8,128)(2,1)} async-done(((bf16[128,192]{0,1:T(8,128)(2,1)}), bf16[128,6144]{0,1:T(8,128)(2,1)}) %all-gather.9.cloned.1.call-update) | async-done | bytes 1572880 | tf_op jit(solution)/shard_map/all_gather | solution.py:19
  206.7 85.9 %all-gather.13.cloned.1.call-done = bf16[6144,288]{0,1:T(8,128)(2,1)} async-done(((bf16[384,288]{0,1:T(8,128)(2,1)}), bf16[6144,288]{0,1:T(8,128)(2,1)}) %all-gather.13.cloned.1.call-update) | async-done | bytes 3538960 | tf_op jit(solution)/shard_map/all_gather | solution.py:24
  292.7 3.5 fusion.21
  296.2 62.3 %all-gather.11.cloned.1.call-done = bf16[128,6144]{0,1:T(8,128)(2,1)} async-done(((bf16[128,192]{0,1:T(8,128)(2,1)}), bf16[128,6144]{0,1:T(8,128)(2,1)}) %all-gather.11.cloned.1.call-update) | async-done | bytes 1572880 | tf_op jit(solution)/shard_map/all_gather | solution.py:19
  358.5 3.7 fusion.22
  362.2 2.9 fusion
  365.1 6.3 %copy.8 = bf16[6144,288]{1,0:T(8,128)(2,1)} copy(bf16[6144,288]{0,1:T(8,128)(2,1)} %fusion) | data formatting | bytes 7077888
  371.4 0.0 reduce-scatter.4.cloned.1.call-update
  371.4 107.5 %reduce-scatter.4.cloned.1.call-done = bf16[384,288]{1,0:T(8,128)(2,1)} async-done(((bf16[6144,288]{1,0:T(8,128)(2,1)}), bf16[384,288]{1,0:T(8,128)(2,1)}) %reduce-scatter.4.cloned.1.call-update) | async-done | bytes 221200
  478.9 1.1 copy.9
  480.1 0.8 convert_element_type.65
  (15 shorter events, 0.0 us)
Async XLA Ops:
  7.2 71.4 %copy-start = (bf16[1,192,6144]{2,1,0:T(8,128)(2,1)S(1)}, bf16[1,192,6144]{2,1,0:T(8,128)(2,1)}, u32[]{:S(2)}) copy-start(bf16[1,192,6144]{2,1,0:T(8,128)(2,1)} %param.9) | copy-start | bytes 7077892
  7.2 69.1 %all-gather.15.cloned.1.call-start = ((), (), s32[]{:S(2)}) async-start(), calls=%async_computation.5 | async-start | bytes 1622016 | tf_op jit(solution)/shard_map/all_gather | solution.py:19
  7.9 138.7 %all-gather.7.cloned.1.call-start = ((), (), s32[]{:S(2)}) async-start(), calls=%async_computation.1 | async-start | bytes 1622016 | tf_op jit(solution)/shard_map/all_gather | solution.py:19
  78.5 5.7 %copy-start.5 = (bf16[1,128,192]{1,2,0:T(8,128)(2,1)S(1)}, bf16[1,128,192]{1,2,0:T(8,128)(2,1)}, u32[]{:S(2)}) copy-start(bf16[1,128,192]{1,2,0:T(8,128)(2,1)} %param.7) | copy-start | bytes 147460
  78.5 70.3 %copy-start.6 = (f32[1,6144]{1,0:T(1,128)S(1)}, f32[1,6144]{1,0:T(1,128)}, u32[]{:S(2)}) copy-start(f32[1,6144]{1,0:T(1,128)} %param.8) | copy-start | bytes 73732
  81.2 3.7 copy-start.4
  81.3 3.0 collective-permute-start
  84.9 121.8 %all-gather.9.cloned.1.call-start = ((), (), s32[]{:S(2)}) async-start(), calls=%async_computation.2 | async-start | bytes 1622016 | tf_op jit(solution)/shard_map/all_gather | solution.py:19
  85.7 207.0 %all-gather.13.cloned.1.call-start = ((), (), s32[]{:S(2)}) async-start(), calls=%async_computation.4 | async-start | bytes 3760128 | tf_op jit(solution)/shard_map/all_gather | solution.py:24
  86.2 272.3 %all-gather.11.cloned.1.call-start = ((), (), s32[]{:S(2)}) async-start(), calls=%async_computation.3 | async-start | bytes 1622016 | tf_op jit(solution)/shard_map/all_gather | solution.py:19
  148.8 143.9 %copy-start.3 = (bf16[1,2,128,288]{2,3,1,0:T(8,128)(2,1)S(1)}, bf16[1,2,128,288]{2,3,1,0:T(8,128)(2,1)}, u32[]{:S(2)}) copy-start(bf16[1,2,128,288]{2,3,1,0:T(8,128)(2,1)} %param.11) | copy-start | bytes 442372
  152.2 326.7 %reduce-scatter.4.cloned.1.call-start = ((), (), s32[]{:S(2)}) async-start(), calls=%async_computation.6 | async-start | bytes 5013504
  358.5 3.7 copy-start.1
  358.5 3.7 copy-start.2
Sparse Core Ops, SparseCore 0:
  11.1 65.1 all-gather.14
  85.0 61.4 all-gather.6
  150.3 56.4 all-gather.8
  208.7 83.9 all-gather.12
  296.2 62.2 all-gather.10
  371.5 107.3 reduce-scatter.3
where the time goes:
time: 489 us; the launch traced here: 488 us
  waiting for transfers between devices  442 us (90%)
  matrix products  16.2 us (3%)
  between operations  14.2 us (3%)
  local copies, waits for them, and re-layouts  7.44 us (2%)
  other arithmetic  5.9 us (1%)
    all_gather x4, waiting for transfers between devices, gathered_rows(): return lax.all_gather(local_rows, 'tensor', axis=1, tiled=True)  245 us
    unnamed x7, waiting for transfers between devices  109 us
    all_gather x1, waiting for transfers between devices, on_device(): columns = lax.all_gather(projection, 'segment', axis=0, tiled=True)  85.9 us
  transfers between devices with their start and end apart: 7, of which 7 were waited for; matrix products, arithmetic and copies ran while one was open for 2% of the time, Pallas kernels for 0%

commit v1 on v0

v1 whole, which is shorter than its diff:
```python
import functools

import jax
import jax.numpy as jnp
from jax import lax
from jax.experimental import pallas as pl
from jax.experimental.pallas import tpu as pltpu
from jax.sharding import PartitionSpec as P

EPSILON = 1e-05
TICKS = 2
NZ, NX, NC, NY = 4, 4, 2, 8
ROWS = 128
PIECE = 192
WIDTH = 6144
COLS = 288
BLOCK = 384
ORDER = (0, 8, 4, 12, 1, 9, 5, 13, 2, 10, 6, 14, 3, 11, 7, 15)
VMEM_LIMIT = 48 * 1024 * 1024
SMEM_SPEC = pl.BlockSpec(memory_space=pltpu.SMEM)
VMEM_SPEC = pl.BlockSpec(memory_space=pltpu.VMEM)


def t_index(z, x, c):
    return (z % NZ) * 8 + (x % NX) * 2 + c % NC


Z_GROUPS = [[t_index(z, x, c) for z in range(NZ)] for x in range(NX) for c in range(NC)]
X_GROUPS = [[t_index(z, x, c) for x in range(NX)] for z in range(NZ) for c in range(NC)]
Y_GROUPS = [[(2 * i + par) * 2 + zl for i in range(4)] for par in range(2) for zl in range(2)]


def all_t():
    return [(z, x, c) for z in range(NZ) for x in range(NX) for c in range(NC)]


def over_tensor(value, move):
    return lax.ppermute(value, "tensor", [(t_index(*p), t_index(*move(*p))) for p in all_t()])


def over_segment(value, mask):
    return lax.ppermute(value, "segment", [(i, i ^ mask) for i in range(16)])


def z_gather(value):
    return lax.all_gather(value, "tensor", axis=0, tiled=True, axis_index_groups=Z_GROUPS)


def x_gather(value):
    return lax.all_gather(value, "tensor", axis=0, tiled=True, axis_index_groups=X_GROUPS)


def core_swap(value):
    return over_tensor(value, lambda z, x, c: (z, x, c + 1))


def x_relative(value):
    got = [over_tensor(value, lambda z, x, c, k=k: (z, x - k, c)) for k in (1, 2, 3)]
    return jnp.concatenate([value] + got, axis=0)


def transposition():
    pairs = []
    for yy in range(NY):
        for zl in range(2):
            for z, x, c in all_t():
                y = z * 2 + (x >> 1)
                there = t_index(yy >> 1, (yy & 1) * 2 + (x & 1), c)
                pairs.append(((yy * 2 + zl) * 32 + t_index(z, x, c), (y * 2 + zl) * 32 + there))
    return pairs


def scaled_weights(weights, gain):
    return (weights.astype(jnp.float32) * gain).astype(jnp.bfloat16)


def tick_kernel(where_ref, own_ref, other_ref, weight_ref, mine_ref, out_ref, full):
    core = where_ref[0]
    square = jnp.zeros((8, ROWS), jnp.float32)
    for x in range(NX):
        for z in range(NZ):
            base = t_index(z, x, 0) * PIECE
            source = pl.ds((x * NZ + z) * PIECE, PIECE)
            for ref, c in ((own_ref, core), (other_ref, 1 - core)):
                piece = ref[source, :]
                full[pl.ds(pl.multiple_of(base + c * PIECE, PIECE), PIECE), :] = piece
                wide = piece.astype(jnp.float32)
                square += jnp.sum((wide * wide).reshape(PIECE // 8, 8, ROWS), axis=0)
    mean_square = jnp.sum(square, axis=0, keepdims=True) * (1.0 / WIDTH)
    scale = lax.rsqrt(mean_square + EPSILON)
    hidden = jnp.dot(weight_ref[...], full[...], preferred_element_type=jnp.float32) * scale
    silu = hidden / (1.0 + jnp.exp(-hidden))
    out_ref[...] = (mine_ref[...].astype(jnp.float32) + silu).astype(jnp.bfloat16)


def tick(where, own, other, weights, mine):
    return pl.pallas_call(
        tick_kernel,
        out_shape=jax.ShapeDtypeStruct((PIECE, ROWS), jnp.bfloat16),
        in_specs=[SMEM_SPEC] + [VMEM_SPEC] * 4,
        out_specs=VMEM_SPEC,
        scratch_shapes=[pltpu.VMEM((WIDTH, ROWS), jnp.bfloat16)],
        compiler_params=pltpu.CompilerParams(vmem_limit_bytes=VMEM_LIMIT),
        name="tick",
    )(where, own, other, weights, mine)


def predict_kernel(where_ref, own_ref, other_ref, block_ref, teacher_ref, out_ref, full):
    core, segment, x_mine = where_ref[0], where_ref[1], where_ref[2]
    for k in range(NX):
        x = (x_mine + k) % NX
        for z in range(NZ):
            for tau in range(TICKS):
                source = pl.ds(((k * NZ + z) * TICKS + tau) * PIECE, PIECE)
                for ref, c in ((own_ref, core), (other_ref, 1 - core)):
                    at = pl.multiple_of((z * 8 + x * 2 + c) * PIECE, PIECE)
                    full[pl.ds(at, PIECE), tau * ROWS : (tau + 1) * ROWS] = ref[source, :]
    total = jnp.zeros((COLS, TICKS * ROWS), jnp.float32)
    for j, mask in enumerate(ORDER):
        at = pl.multiple_of((segment ^ mask) * BLOCK, BLOCK)
        total += jnp.dot(
            block_ref[j * COLS : (j + 1) * COLS, :],
            full[pl.ds(at, BLOCK), :],
            preferred_element_type=jnp.float32,
        )
    for tau in range(TICKS):
        taught = teacher_ref[tau].astype(jnp.float32)
        difference = total[:, tau * ROWS : (tau + 1) * ROWS] - taught
        out_ref[tau * COLS : (tau + 1) * COLS, :] = difference.astype(jnp.bfloat16)


def predict(where, own, other, blocks, teacher):
    return pl.pallas_call(
        predict_kernel,
        out_shape=jax.ShapeDtypeStruct((TICKS * COLS, ROWS), jnp.bfloat16),
        in_specs=[SMEM_SPEC] + [VMEM_SPEC] * 4,
        out_specs=VMEM_SPEC,
        scratch_shapes=[pltpu.VMEM((WIDTH, TICKS * ROWS), jnp.bfloat16)],
        compiler_params=pltpu.CompilerParams(vmem_limit_bytes=VMEM_LIMIT),
        name="predict",
    )(where, own, other, blocks, teacher)


def gradient_kernel(where_ref, near_ref, far_ref, own_ref, other_ref, keep_ref, send_ref, rows, diffs):
    core, segment, x_mine = where_ref[0], where_ref[1], where_ref[2]
    parity, half = (segment >> 1) & 1, segment & 1
    for i in range(4):
        for ref, p in ((near_ref, parity), (far_ref, 1 - parity)):
            for tau in range(TICKS):
                source = pl.ds((i * TICKS + tau) * COLS, COLS)
                diffs[2 * i + p, :, tau * ROWS : (tau + 1) * ROWS] = ref[source, :]
    for k in range(NX):
        x = (x_mine + k) % NX
        for z in range(NZ):
            y = z * 2 + (x >> 1)
            for ref, c in ((own_ref, core), (other_ref, 1 - core)):
                at = pl.multiple_of(((x & 1) * 2 + c) * PIECE, PIECE)
                for tau in range(TICKS):
                    source = pl.ds(((k * NZ + z) * TICKS + tau) * PIECE, PIECE)
                    rows[y, pl.ds(at, PIECE), tau * ROWS : (tau + 1) * ROWS] = ref[source, :]
    for part, ref in ((half, keep_ref), (1 - half, send_ref)):
        total = jnp.zeros((COLS, BLOCK), jnp.float32)
        for y in range(NY):
            total += lax.dot_general(
                diffs[y],
                rows[y, pl.ds(pl.multiple_of(part * BLOCK, BLOCK), BLOCK), :],
                (((1,), (1,)), ((), ())),
                preferred_element_type=jnp.float32,
            )
        ref[...] = (total * (1.0 / (TICKS * ROWS))).astype(ref.dtype)


def gradient(where, near, far, own, other):
    return pl.pallas_call(
        gradient_kernel,
        out_shape=(
            jax.ShapeDtypeStruct((COLS, BLOCK), jnp.float32),
            jax.ShapeDtypeStruct((COLS, BLOCK), jnp.bfloat16),
        ),
        in_specs=[SMEM_SPEC] + [VMEM_SPEC] * 4,
        out_specs=(VMEM_SPEC, VMEM_SPEC),
        scratch_shapes=[
            pltpu.VMEM((NY, 2 * BLOCK, TICKS * ROWS), jnp.bfloat16),
            pltpu.VMEM((NY, COLS, TICKS * ROWS), jnp.bfloat16),
        ],
        compiler_params=pltpu.CompilerParams(vmem_limit_bytes=VMEM_LIMIT),
        name="gradient",
    )(where, near, far, own, other)


def on_device(entering, fresh_rows, norm_gain, segment_weight, projection, teacher_rows):
    t, segment = lax.axis_index("tensor"), lax.axis_index("segment")
    where = jnp.stack([t & 1, segment, (t >> 1) & 3]).astype(jnp.int32)
    weights = scaled_weights(segment_weight[0], norm_gain)
    teacher = teacher_rows[0].swapaxes(1, 2)

    blocks = projection.T
    for mask in (8, 4, 1, 2):
        blocks = jnp.concatenate([blocks, over_segment(blocks, mask)], axis=0)

    entering_t, fresh_t = entering[0].T, fresh_rows[0].T
    first = z_gather(jnp.concatenate([entering_t, fresh_t], axis=0)).reshape(NZ, 2, PIECE, ROWS)
    own = x_gather(first[:, 0].reshape(NZ * PIECE, ROWS))
    out0 = tick(where, own, core_swap(own), weights, entering_t)

    shifted = lax.ppermute(out0, "segment", [(i, i + 1) for i in range(15)])
    mine = jnp.where(segment == 0, fresh_t, shifted)
    column = z_gather(mine)
    own = x_gather(column)
    out1 = tick(where, own, core_swap(own), weights, mine)

    both = jnp.concatenate([out0, out1], axis=0)
    turned = lax.ppermute(both, ("segment", "tensor"), transposition())
    own = x_relative(z_gather(both))
    difference = predict(where, own, core_swap(own), blocks, teacher)

    own_rows = x_relative(z_gather(turned))
    other_rows = core_swap(own_rows)
    near = lax.all_gather(difference, "segment", axis=0, tiled=True, axis_index_groups=Y_GROUPS)
    far = over_segment(near, 2)
    keep, send = gradient(where, near, far, own_rows, other_rows)
    got = over_segment(send, 1)
    total = keep + got.astype(jnp.float32)
    return (out1.T[None], total.T)


def solution(mesh):
    return jax.shard_map(
        on_device,
        mesh=mesh,
        in_specs=(
            P("segment", None, "tensor"),
            P(None, None, "tensor"),
            P("segment", None),
            P("segment", "tensor", None),
            P("segment", "tensor"),
            P("segment", None, None, "tensor"),
        ),
        out_specs=(P("segment", None, "tensor"), P("segment", "tensor")),
        check_vma=False,
    )
```

time: 489 us -> 276 us (0.56)
  waiting for transfers between devices: 442 us -> 24.8 us
  blocking collectives: 0 us -> 145 us
  starting transfers between devices: 2.07 us -> 77.3 us
  matrix products: 16.2 us -> 0 us
  between operations: 14.2 us -> 1.1 us
  Pallas kernels: 0 us -> 11.3 us
    all_gather x5 -> x0, waiting for transfers between devices: 331 us -> none  [the longest x4 245 us: gathered_rows(): return lax.all_gather(local_rows, 'tensor', axis=1, tiled=True)]
    all_gather x0 -> x7, blocking collectives: none -> 145 us  [the longest x4 108 us: z_gather(): lax.all_gather(value, 'tensor', axis=0, tiled=True, axis_index_groups=Z_G...]
    unnamed x7 -> x0, waiting for transfers between devices: 109 us -> none
    ppermute x1 -> x18, starting transfers between devices: 1.83 us -> 77.3 us  [the longest x10 46 us: over_tensor(): lax.ppermute(value, 'tensor', [(t_index(*p), t_index(*move(*p))) for p in...]
    ppermute x1 -> x18, waiting for transfers between devices: 1.15 us -> 24.8 us  [the longest x6 13.1 us: over_segment(): return lax.ppermute(value, 'segment', [(i, i ^ mask) for i in range(16)])]
    dot_general x5 -> x0, matrix products: 16.2 us -> none  [the longest x2 7.25 us: on_device(): jnp.dot(outgoing_full, columns, preferred_element_type=jnp.float32)]
    pallas_call x0 -> x4, Pallas kernels: none -> 11.3 us  [the longest x2 4.77 us: tick(): pl.pallas_call(tick_kernel, out_shape=jax.ShapeDtypeStruct((PIECE, ROWS),...]
  transfers between devices with their start and end apart: 7 -> 18, of which waited for: 7 -> 3; matrix products, arithmetic and copies ran while one was open for 2% -> 3% of each run, Pallas kernels for 0% -> 3%
where the time goes in v1:
time: 276 us; the launch traced here: 272 us
  blocking collectives  145 us (53%)
  starting transfers between devices  77.3 us (28%)
  waiting for transfers between devices  24.8 us (9%)
  Pallas kernels  11.3 us (4%)
  other arithmetic  7.83 us (3%)
  local copies, waits for them, and re-layouts  5.1 us (2%)
    all_gather x4, blocking collectives, z_gather(): lax.all_gather(value, 'tensor', axis=0, tiled=True, axis_index_groups=Z_G...  108 us
    ppermute x10, starting transfers between devices, over_tensor(): lax.ppermute(value, 'tensor', [(t_index(*p), t_index(*move(*p))) for p in...  46 us
    ppermute x6, starting transfers between devices, over_segment(): return lax.ppermute(value, 'segment', [(i, i ^ mask) for i in range(16)])  27.7 us
    all_gather x2, blocking collectives, x_gather(): lax.all_gather(value, 'tensor', axis=0, tiled=True, axis_index_groups=X_G...  21.9 us
    all_gather x1, blocking collectives, on_device(): lax.all_gather(difference, 'segment', axis=0, tiled=True, axis_index_grou...  15.2 us
    ppermute x6, waiting for transfers between devices, over_segment(): return lax.ppermute(value, 'segment', [(i, i ^ mask) for i in range(16)])  13.1 us
    ppermute x10, waiting for transfers between devices, over_tensor(): lax.ppermute(value, 'tensor', [(t_index(*p), t_index(*move(*p))) for p in...  11.6 us
  transfers between devices with their start and end apart: 18, of which 3 were waited for; matrix products, arithmetic and copies ran while one was open for 3% of the time, Pallas kernels for 3%

profile of v1, /device:TPU:1, one launch (start us, length us, event | category | flops | bytes accessed | tf_op | source)
XLA Modules:
  0.0 272.1 jit_solution(14658094161510834351)
XLA Ops:
  1.5 19.9 %all_gather.21 = bf16[1536,128]{1,0:T(8,128)(2,1)S(1)} all-gather(bf16[384,128]{1,0:T(8,128)(2,1)S(1)} %pad_maximum_fusion.3), channel_id=1, replica_groups={{0,8,16,24},{1,9,17,25},{2,10,18,26},{3,11,19,27},{4,12,20,28},{5,13,21..., dimensions={0}, use_global_device_ids=true | all-gather | bytes 491520 | tf_op jit(solution)/shard_map/all_gather | solution.py:46
  21.4 11.2 %all_gather.22.own_ref = bf16[3072,128]{1,0:T(8,128)(2,1)S(1)} all-gather(bf16[768,128]{1,0:T(8,128)(2,1)S(1)} %bitcast.34), channel_id=1, replica_groups={{0,2,4,6},{1,3,5,7},{8,10,12,14},{9,11,13,15},{16,18,20,22},{17,19,21,2..., dimensions={0}, use_global_device_ids=true | all-gather | bytes 983040 | tf_op jit(solution)/shard_map/all_gather | solution.py:50
  32.6 8.0 %collective-permute-start = (bf16[3072,128]{1,0:T(8,128)(2,1)S(1)}, bf16[3072,128]{1,0:T(8,128)(2,1)}, u32[]{:S(2)}, u32[]{:S(2)}) collective-permute-start(bf16[3072,128]{1,0:T(8,128)(2,1)S(1)} %all_gather.22.own_ref), channel_id=1, source_target_pairs={{0,1},{1,0},{2,3},{3,2},{4,5},{5,4},{6,7},{7,6},{8,9},{9,8},{10,11... | collective-permute-start | bytes 2359304 | tf_op jit(solution)/shard_map/ppermute | solution.py:38
  40.6 7.5 %collective-permute-start.7 = (bf16[288,384]{1,0:T(8,128)(2,1)S(1)}, bf16[288,384]{1,0:T(8,128)(2,1)}, u32[]{:S(2)}, u32[]{:S(2)}) collective-permute-start(bf16[288,384]{1,0:T(8,128)(2,1)S(1)} %bitcast.29), channel_id=1, source_target_pairs={{0,256},{32,288},{64,320},{96,352},{128,384},{160,416},{192,448},{... | collective-permute-start | bytes 663560 | tf_op jit(solution)/shard_map/ppermute | solution.py:42
  48.1 2.1 fusion.weight_ref
  50.3 2.4 tick.2
  52.7 2.9 %collective-permute-start.1 = (bf16[192,128]{1,0:T(8,128)(2,1)S(1)}, bf16[192,128]{1,0:T(8,128)(2,1)S(1)}, u32[]{:S(2)}, u32[]{:S(2)}) collective-permute-start(bf16[192,128]{1,0:T(8,128)(2,1)S(1)} %tick.2), channel_id=1, source_target_pairs={{0,32},{32,64},{64,96},{96,128},{128,160},{160,192},{192,224},{224... | collective-permute-start | bytes 147464 | tf_op jit(solution)/shard_map/ppermute | solution.py:206
  56.6 7.2 %collective-permute-start.8 = (bf16[576,384]{1,0:T(8,128)(2,1)S(1)}, bf16[576,384]{1,0:T(8,128)(2,1)S(1)}, u32[]{:S(2)}, u32[]{:S(2)}) collective-permute-start(bf16[576,384]{1,0:T(8,128)(2,1)S(1)} %pad_maximum_fusion.2), channel_id=1, source_target_pairs={{0,128},{32,160},{64,192},{96,224},{128,0},{160,32},{192,64},{224,... | collective-permute-start | bytes 1327112 | tf_op jit(solution)/shard_map/ppermute | solution.py:42
  63.9 11.5 %all_gather.23 = bf16[768,128]{1,0:T(8,128)(2,1)S(1)} all-gather(bf16[192,128]{1,0:T(8,128)(2,1)S(1)} %broadcast_select_fusion.mine_ref), channel_id=1, replica_groups={{0,8,16,24},{1,9,17,25},{2,10,18,26},{3,11,19,27},{4,12,20,28},{5,13,21..., dimensions={0}, use_global_device_ids=true | all-gather | bytes 245760 | tf_op jit(solution)/shard_map/all_gather | solution.py:46
  75.3 10.7 %all_gather.24.own_ref = bf16[3072,128]{1,0:T(8,128)(2,1)S(1)} all-gather(bf16[768,128]{1,0:T(8,128)(2,1)S(1)} %all_gather.23), channel_id=1, replica_groups={{0,2,4,6},{1,3,5,7},{8,10,12,14},{9,11,13,15},{16,18,20,22},{17,19,21,2..., dimensions={0}, use_global_device_ids=true | all-gather | bytes 983040 | tf_op jit(solution)/shard_map/all_gather | solution.py:50
  86.0 8.5 %collective-permute-start.2 = (bf16[3072,128]{1,0:T(8,128)(2,1)S(1)}, bf16[3072,128]{1,0:T(8,128)(2,1)S(1)}, u32[]{:S(2)}, u32[]{:S(2)}) collective-permute-start(bf16[3072,128]{1,0:T(8,128)(2,1)S(1)} %all_gather.24.own_ref), channel_id=1, source_target_pairs={{0,1},{1,0},{2,3},{3,2},{4,5},{5,4},{6,7},{7,6},{8,9},{9,8},{10,11... | collective-permute-start | bytes 2359304 | tf_op jit(solution)/shard_map/ppermute | solution.py:38
  95.6 3.5 %collective-permute-start.9 = (bf16[1152,384]{1,0:T(8,128)(2,1)S(1)}, bf16[1152,384]{1,0:T(8,128)(2,1)S(1)}, u32[]{:S(2)}, u32[]{:S(2)}) collective-permute-start(bf16[1152,384]{1,0:T(8,128)(2,1)S(1)} %pad_maximum_fusion.1), channel_id=1, source_target_pairs={{0,32},{32,0},{64,96},{96,64},{128,160},{160,128},{192,224},{224,1... | collective-permute-start | bytes 2654216 | tf_op jit(solution)/shard_map/ppermute | solution.py:42
  101.4 2.4 tick.3
  104.6 25.4 %all_gather.25 = bf16[1536,128]{1,0:T(8,128)(2,1)S(1)} all-gather(bf16[384,128]{1,0:T(8,128)(2,1)S(1)} %pad_maximum_fusion.4), channel_id=1, replica_groups={{0,8,16,24},{1,9,17,25},{2,10,18,26},{3,11,19,27},{4,12,20,28},{5,13,21..., dimensions={0}, use_global_device_ids=true | all-gather | bytes 491520 | tf_op jit(solution)/shard_map/all_gather | solution.py:46
  130.0 4.9 %collective-permute-start.3 = (bf16[1536,128]{1,0:T(8,128)(2,1)S(1)}, bf16[1536,128]{1,0:T(8,128)(2,1)S(1)}, u32[]{:S(2)}, u32[]{:S(2)}) collective-permute-start(bf16[1536,128]{1,0:T(8,128)(2,1)S(1)} %all_gather.25), channel_id=1, source_target_pairs={{0,6},{1,7},{2,0},{3,1},{4,2},{5,3},{6,4},{7,5},{8,14},{9,15},{10,... | collective-permute-start | bytes 1179656 | tf_op jit(solution)/shard_map/ppermute | solution.py:38
  136.1 1.9 collective-permute-start.10
  138.0 2.5 collective-permute-start.4
  141.2 1.9 collective-permute-start.5
  143.1 50.9 %all_gather.27 = bf16[1536,128]{1,0:T(8,128)(2,1)S(1)} all-gather(bf16[384,128]{1,0:T(8,128)(2,1)S(1)} %collective-permute-done.12), channel_id=1, replica_groups={{0,8,16,24},{1,9,17,25},{2,10,18,26},{3,11,19,27},{4,12,20,28},{5,13,21..., dimensions={0}, use_global_device_ids=true | all-gather | bytes 491520 | tf_op jit(solution)/shard_map/all_gather | solution.py:46
  194.0 3.5 %collective-permute-start.13 = (bf16[1536,128]{1,0:T(8,128)(2,1)S(1)}, bf16[1536,128]{1,0:T(8,128)(2,1)S(1)}, u32[]{:S(2)}, u32[]{:S(2)}) collective-permute-start(bf16[1536,128]{1,0:T(8,128)(2,1)S(1)} %all_gather.27), channel_id=1, source_target_pairs={{0,6},{1,7},{2,0},{3,1},{4,2},{5,3},{6,4},{7,5},{8,14},{9,15},{10,... | collective-permute-start | bytes 1179656 | tf_op jit(solution)/shard_map/ppermute | solution.py:38
  197.5 3.2 %collective-permute-start.14 = (bf16[1536,128]{1,0:T(8,128)(2,1)S(1)}, bf16[1536,128]{1,0:T(8,128)(2,1)S(1)}, u32[]{:S(2)}, u32[]{:S(2)}) collective-permute-start(bf16[1536,128]{1,0:T(8,128)(2,1)S(1)} %all_gather.27), channel_id=1, source_target_pairs={{0,4},{1,5},{2,6},{3,7},{4,0},{5,1},{6,2},{7,3},{8,12},{9,13},{10,... | collective-permute-start | bytes 1179656 | tf_op jit(solution)/shard_map/ppermute | solution.py:38
  200.9 8.4 %collective-permute-start.6 = (bf16[6144,128]{1,0:T(8,128)(2,1)S(1)}, bf16[6144,128]{1,0:T(8,128)(2,1)S(1)}, u32[]{:S(2)}, u32[]{:S(2)}) collective-permute-start(bf16[6144,128]{1,0:T(8,128)(2,1)S(1)} %constant_dynamic-update-slice_fusion.own_ref), channel_id=1, source_target_pairs={{0,1},{1,0},{2,3},{3,2},{4,5},{5,4},{6,7},{7,6},{8,9},{9,8},{10,11... | collective-permute-start | bytes 4718600 | tf_op jit(solution)/shard_map/ppermute | solution.py:38
  209.3 2.8 %collective-permute-start.15 = (bf16[1536,128]{1,0:T(8,128)(2,1)S(1)}, bf16[1536,128]{1,0:T(8,128)(2,1)S(1)}, u32[]{:S(2)}, u32[]{:S(2)}) collective-permute-start(bf16[1536,128]{1,0:T(8,128)(2,1)S(1)} %all_gather.27), channel_id=1, source_target_pairs={{0,2},{1,3},{2,4},{3,5},{4,6},{5,7},{6,0},{7,1},{8,10},{9,11},{10,... | collective-permute-start | bytes 1179656 | tf_op jit(solution)/shard_map/ppermute | solution.py:38
  212.2 11.6 %collective-permute-done.15 = bf16[1536,128]{1,0:T(8,128)(2,1)S(1)} collective-permute-done((bf16[1536,128]{1,0:T(8,128)(2,1)S(1)}, bf16[1536,128]{1,0:T(8,128)(2,1)S(1)}, u32[]{:S(2)}, u32[]{:S(2)}) %collective-permute-start.15) | collective-permute-done | bytes 393248 | tf_op jit(solution)/shard_map/ppermute | solution.py:38
  223.9 2.5 collective-permute-start.16
  228.8 3.9 %predict.1 = bf16[576,128]{1,0:T(8,128)(2,1)S(1)} custom-call(s32[3]{0:T(128)S(1)} %pad_add_fusion.where_ref, bf16[6144,128]{1,0:T(8,128)(2,1)S(1)} %constant_dynamic-update-slice_fusion.own_ref, bf16[6144,128]{1,0:T(8,128)(2,1)S(1)} %collective-permute-done.6.other_ref, bf16[4608,384]{1,0:T(8,128)(2,1)} %copy-done.3, bf16[2,288,128]{2,1,0:T(8,128)(2,1)S(1)} %bitcast.28), custom_call_target="tpu_custom_call" | custom-call | tf_op jit(solution)/shard_map/predict/pallas_call | solution.py:133
  232.8 15.2 %all_gather.26.near_ref = bf16[2304,128]{1,0:T(8,128)(2,1)S(1)} all-gather(bf16[576,128]{1,0:T(8,128)(2,1)S(1)} %predict.1), channel_id=1, replica_groups={{0,128,256,384},{32,160,288,416},{64,192,320,448},{96,224,352,480},{1,1..., dimensions={0}, use_global_device_ids=true | all-gather | bytes 737280 | tf_op jit(solution)/shard_map/all_gather | solution.py:219
  248.0 3.1 %collective-permute-start.11 = (bf16[2304,128]{1,0:T(8,128)(2,1)S(1)}, bf16[2304,128]{1,0:T(8,128)(2,1)S(1)}, u32[]{:S(2)}, u32[]{:S(2)}) collective-permute-start(bf16[2304,128]{1,0:T(8,128)(2,1)S(1)} %all_gather.26.near_ref), channel_id=1, source_target_pairs={{0,64},{32,96},{64,0},{96,32},{128,192},{160,224},{192,128},{224,1... | collective-permute-start | bytes 1769480 | tf_op jit(solution)/shard_map/ppermute | solution.py:42
  251.2 9.8 %collective-permute-done.11.far_ref = bf16[2304,128]{1,0:T(8,128)(2,1)S(1)} collective-permute-done((bf16[2304,128]{1,0:T(8,128)(2,1)S(1)}, bf16[2304,128]{1,0:T(8,128)(2,1)S(1)}, u32[]{:S(2)}, u32[]{:S(2)}) %collective-permute-start.11) | collective-permute-done | bytes 589856 | tf_op jit(solution)/shard_map/ppermute | solution.py:42
  260.9 2.5 gradient.1
  263.5 4.5 %collective-permute-start.17 = (bf16[288,384]{1,0:T(8,128)(2,1)S(1)}, bf16[288,384]{1,0:T(8,128)(2,1)S(1)}, u32[]{:S(2)}, u32[]{:S(2)}) collective-permute-start(bf16[288,384]{1,0:T(8,128)(2,1)S(1)} %get-tuple-element.5), channel_id=1, source_target_pairs={{0,32},{32,0},{64,96},{96,64},{128,160},{160,128},{192,224},{224,1... | collective-permute-start | bytes 663560 | tf_op jit(solution)/shard_map/ppermute | solution.py:42
  268.0 3.3 %collective-permute-done.17 = bf16[288,384]{1,0:T(8,128)(2,1)S(1)} collective-permute-done((bf16[288,384]{1,0:T(8,128)(2,1)S(1)}, bf16[288,384]{1,0:T(8,128)(2,1)S(1)}, u32[]{:S(2)}, u32[]{:S(2)}) %collective-permute-start.17) | collective-permute-done | bytes 221216 | tf_op jit(solution)/shard_map/ppermute | solution.py:42
  (52 shorter events, 11.5 us)
Async XLA Ops:
  0.6 40.0 %copy-start.4 = (bf16[384,288]{0,1:T(8,128)(2,1)S(1)}, bf16[384,288]{0,1:T(8,128)(2,1)}, u32[]{:S(2)}) copy-start(bf16[384,288]{0,1:T(8,128)(2,1)} %param.10) | copy-start | bytes 663556
  0.6 47.4 %copy-start.6 = (f32[1,6144]{1,0:T(1,128)S(1)}, f32[1,6144]{1,0:T(1,128)}, u32[]{:S(2)}) copy-start(f32[1,6144]{1,0:T(1,128)} %param.8) | copy-start | bytes 73732
  32.6 17.7 %collective-permute-start = (bf16[3072,128]{1,0:T(8,128)(2,1)S(1)}, bf16[3072,128]{1,0:T(8,128)(2,1)}, u32[]{:S(2)}, u32[]{:S(2)}) collective-permute-start(bf16[3072,128]{1,0:T(8,128)(2,1)S(1)} %all_gather.22.own_ref), channel_id=1, source_target_pairs={{0,1},{1,0},{2,3},{3,2},{4,5},{5,4},{6,7},{7,6},{8,9},{9,8},{10,11... | collective-permute-start | bytes 2359304 | tf_op jit(solution)/shard_map/ppermute | solution.py:38
  40.6 15.0 %collective-permute-start.7 = (bf16[288,384]{1,0:T(8,128)(2,1)S(1)}, bf16[288,384]{1,0:T(8,128)(2,1)}, u32[]{:S(2)}, u32[]{:S(2)}) collective-permute-start(bf16[288,384]{1,0:T(8,128)(2,1)S(1)} %bitcast.29), channel_id=1, source_target_pairs={{0,256},{32,288},{64,320},{96,352},{128,384},{160,416},{192,448},{... | collective-permute-start | bytes 663560 | tf_op jit(solution)/shard_map/ppermute | solution.py:42
  48.1 2.2 copy-start
  50.3 13.5 %copy-start.5 = (bf16[1,128,192]{1,2,0:T(8,128)(2,1)S(1)}, bf16[1,128,192]{1,2,0:T(8,128)(2,1)}, u32[]{:S(2)}) copy-start(bf16[1,128,192]{1,2,0:T(8,128)(2,1)} %param.7) | copy-start | bytes 147460
  52.7 11.1 %collective-permute-start.1 = (bf16[192,128]{1,0:T(8,128)(2,1)S(1)}, bf16[192,128]{1,0:T(8,128)(2,1)S(1)}, u32[]{:S(2)}, u32[]{:S(2)}) collective-permute-start(bf16[192,128]{1,0:T(8,128)(2,1)S(1)} %tick.2), channel_id=1, source_target_pairs={{0,32},{32,64},{64,96},{96,128},{128,160},{160,192},{192,224},{224... | collective-permute-start | bytes 147464 | tf_op jit(solution)/shard_map/ppermute | solution.py:206
  56.6 37.9 %collective-permute-start.8 = (bf16[576,384]{1,0:T(8,128)(2,1)S(1)}, bf16[576,384]{1,0:T(8,128)(2,1)S(1)}, u32[]{:S(2)}, u32[]{:S(2)}) collective-permute-start(bf16[576,384]{1,0:T(8,128)(2,1)S(1)} %pad_maximum_fusion.2), channel_id=1, source_target_pairs={{0,128},{32,160},{64,192},{96,224},{128,0},{160,32},{192,64},{224,... | collective-permute-start | bytes 1327112 | tf_op jit(solution)/shard_map/ppermute | solution.py:42
  86.0 15.4 %collective-permute-start.2 = (bf16[3072,128]{1,0:T(8,128)(2,1)S(1)}, bf16[3072,128]{1,0:T(8,128)(2,1)S(1)}, u32[]{:S(2)}, u32[]{:S(2)}) collective-permute-start(bf16[3072,128]{1,0:T(8,128)(2,1)S(1)} %all_gather.24.own_ref), channel_id=1, source_target_pairs={{0,1},{1,0},{2,3},{3,2},{4,5},{5,4},{6,7},{7,6},{8,9},{9,8},{10,11... | collective-permute-start | bytes 2359304 | tf_op jit(solution)/shard_map/ppermute | solution.py:38
  95.6 39.4 %collective-permute-start.9 = (bf16[1152,384]{1,0:T(8,128)(2,1)S(1)}, bf16[1152,384]{1,0:T(8,128)(2,1)S(1)}, u32[]{:S(2)}, u32[]{:S(2)}) collective-permute-start(bf16[1152,384]{1,0:T(8,128)(2,1)S(1)} %pad_maximum_fusion.1), channel_id=1, source_target_pairs={{0,32},{32,0},{64,96},{96,64},{128,160},{160,128},{192,224},{224,1... | collective-permute-start | bytes 2654216 | tf_op jit(solution)/shard_map/ppermute | solution.py:42
  130.0 67.5 %collective-permute-start.3 = (bf16[1536,128]{1,0:T(8,128)(2,1)S(1)}, bf16[1536,128]{1,0:T(8,128)(2,1)S(1)}, u32[]{:S(2)}, u32[]{:S(2)}) collective-permute-start(bf16[1536,128]{1,0:T(8,128)(2,1)S(1)} %all_gather.25), channel_id=1, source_target_pairs={{0,6},{1,7},{2,0},{3,1},{4,2},{5,3},{6,4},{7,5},{8,14},{9,15},{10,... | collective-permute-start | bytes 1179656 | tf_op jit(solution)/shard_map/ppermute | solution.py:38
  136.1 90.6 %collective-permute-start.10 = (bf16[2304,384]{1,0:T(8,128)(2,1)S(1)}, bf16[2304,384]{1,0:T(8,128)(2,1)S(1)}, u32[]{:S(2)}, u32[]{:S(2)}) collective-permute-start(bf16[2304,384]{1,0:T(8,128)(2,1)S(1)} %pad_maximum_fusion), channel_id=1, source_target_pairs={{0,64},{32,96},{64,0},{96,32},{128,192},{160,224},{192,128},{224,1... | collective-permute-start | bytes 5308424 | tf_op jit(solution)/shard_map/ppermute | solution.py:42
  138.0 62.8 %collective-permute-start.4 = (bf16[1536,128]{1,0:T(8,128)(2,1)S(1)}, bf16[1536,128]{1,0:T(8,128)(2,1)S(1)}, u32[]{:S(2)}, u32[]{:S(2)}) collective-permute-start(bf16[1536,128]{1,0:T(8,128)(2,1)S(1)} %all_gather.25), channel_id=1, source_target_pairs={{0,4},{1,5},{2,6},{3,7},{4,0},{5,1},{6,2},{7,3},{8,12},{9,13},{10,... | collective-permute-start | bytes 1179656 | tf_op jit(solution)/shard_map/ppermute | solution.py:38
  140.5 2.6 collective-permute-start.12
  141.2 59.6 %collective-permute-start.5 = (bf16[1536,128]{1,0:T(8,128)(2,1)S(1)}, bf16[1536,128]{1,0:T(8,128)(2,1)S(1)}, u32[]{:S(2)}, u32[]{:S(2)}) collective-permute-start(bf16[1536,128]{1,0:T(8,128)(2,1)S(1)} %all_gather.25), channel_id=1, source_target_pairs={{0,2},{1,3},{2,4},{3,5},{4,6},{5,7},{6,0},{7,1},{8,10},{9,11},{10,... | collective-permute-start | bytes 1179656 | tf_op jit(solution)/shard_map/ppermute | solution.py:38
  194.0 18.0 %collective-permute-start.13 = (bf16[1536,128]{1,0:T(8,128)(2,1)S(1)}, bf16[1536,128]{1,0:T(8,128)(2,1)S(1)}, u32[]{:S(2)}, u32[]{:S(2)}) collective-permute-start(bf16[1536,128]{1,0:T(8,128)(2,1)S(1)} %all_gather.27), channel_id=1, source_target_pairs={{0,6},{1,7},{2,0},{3,1},{4,2},{5,3},{6,4},{7,5},{8,14},{9,15},{10,... | collective-permute-start | bytes 1179656 | tf_op jit(solution)/shard_map/ppermute | solution.py:38
  197.5 14.6 %collective-permute-start.14 = (bf16[1536,128]{1,0:T(8,128)(2,1)S(1)}, bf16[1536,128]{1,0:T(8,128)(2,1)S(1)}, u32[]{:S(2)}, u32[]{:S(2)}) collective-permute-start(bf16[1536,128]{1,0:T(8,128)(2,1)S(1)} %all_gather.27), channel_id=1, source_target_pairs={{0,4},{1,5},{2,6},{3,7},{4,0},{5,1},{6,2},{7,3},{8,12},{9,13},{10,... | collective-permute-start | bytes 1179656 | tf_op jit(solution)/shard_map/ppermute | solution.py:38
  200.8 25.6 %copy-start.2 = (bf16[4608,384]{1,0:T(8,128)(2,1)S(1)}, bf16[4608,384]{1,0:T(8,128)(2,1)}, u32[]{:S(2)}) copy-start(bf16[4608,384]{1,0:T(8,128)(2,1)} %constant_dynamic-update-slice_fusion.7) | copy-start | bytes 10616836
  200.9 26.2 %collective-permute-start.6 = (bf16[6144,128]{1,0:T(8,128)(2,1)S(1)}, bf16[6144,128]{1,0:T(8,128)(2,1)S(1)}, u32[]{:S(2)}, u32[]{:S(2)}) collective-permute-start(bf16[6144,128]{1,0:T(8,128)(2,1)S(1)} %constant_dynamic-update-slice_fusion.own_ref), channel_id=1, source_target_pairs={{0,1},{1,0},{2,3},{3,2},{4,5},{5,4},{6,7},{7,6},{8,9},{9,8},{10,11... | collective-permute-start | bytes 4718600 | tf_op jit(solution)/shard_map/ppermute | solution.py:38
  209.3 14.5 %collective-permute-start.15 = (bf16[1536,128]{1,0:T(8,128)(2,1)S(1)}, bf16[1536,128]{1,0:T(8,128)(2,1)S(1)}, u32[]{:S(2)}, u32[]{:S(2)}) collective-permute-start(bf16[1536,128]{1,0:T(8,128)(2,1)S(1)} %all_gather.27), channel_id=1, source_target_pairs={{0,2},{1,3},{2,4},{3,5},{4,6},{5,7},{6,0},{7,1},{8,10},{9,11},{10,... | collective-permute-start | bytes 1179656 | tf_op jit(solution)/shard_map/ppermute | solution.py:38
  223.9 27.2 %collective-permute-start.16 = (bf16[6144,128]{1,0:T(8,128)(2,1)S(1)}, bf16[6144,128]{1,0:T(8,128)(2,1)S(1)}, u32[]{:S(2)}, u32[]{:S(2)}) collective-permute-start(bf16[6144,128]{1,0:T(8,128)(2,1)S(1)} %constant_dynamic-update-slice_fusion.9.own_ref), channel_id=1, source_target_pairs={{0,1},{1,0},{2,3},{3,2},{4,5},{5,4},{6,7},{7,6},{8,9},{9,8},{10,11... | collective-permute-start | bytes 4718600 | tf_op jit(solution)/shard_map/ppermute | solution.py:38
  226.7 2.1 copy-start.1
  227.1 1.8 copy-start.3
  248.0 12.9 %collective-permute-start.11 = (bf16[2304,128]{1,0:T(8,128)(2,1)S(1)}, bf16[2304,128]{1,0:T(8,128)(2,1)S(1)}, u32[]{:S(2)}, u32[]{:S(2)}) collective-permute-start(bf16[2304,128]{1,0:T(8,128)(2,1)S(1)} %all_gather.26.near_ref), channel_id=1, source_target_pairs={{0,64},{32,96},{64,0},{96,32},{128,192},{160,224},{192,128},{224,1... | collective-permute-start | bytes 1769480 | tf_op jit(solution)/shard_map/ppermute | solution.py:42
  263.5 7.8 %collective-permute-start.17 = (bf16[288,384]{1,0:T(8,128)(2,1)S(1)}, bf16[288,384]{1,0:T(8,128)(2,1)S(1)}, u32[]{:S(2)}, u32[]{:S(2)}) collective-permute-start(bf16[288,384]{1,0:T(8,128)(2,1)S(1)} %get-tuple-element.5), channel_id=1, source_target_pairs={{0,32},{32,0},{64,96},{96,64},{128,160},{160,128},{192,224},{224,1... | collective-permute-start | bytes 663560 | tf_op jit(solution)/shard_map/ppermute | solution.py:42

commit v2 on v1

v2 whole, which is shorter than its diff:
```python
import jax
import jax.numpy as jnp
from jax import lax
from jax.experimental import pallas as pl
from jax.experimental.pallas import tpu as pltpu
from jax.sharding import PartitionSpec as P

EPSILON = 1e-05
TICKS = 2
NZ, NX, NC, NY = 4, 4, 2, 8
ROWS = 128
PIECE = 192
WIDTH = 6144
COLS = 288
BLOCK = 384
MASKS = (0, 1, 3, 2)
VMEM_LIMIT = 48 * 1024 * 1024
SMEM_SPEC = pl.BlockSpec(memory_space=pltpu.SMEM)
VMEM_SPEC = pl.BlockSpec(memory_space=pltpu.VMEM)


def t_index(z, x, c):
    return (z % NZ) * 8 + (x % NX) * 2 + c % NC


def all_t():
    return [(z, x, c) for z in range(NZ) for x in range(NX) for c in range(NC)]


def over_tensor(value, move):
    return lax.ppermute(value, "tensor", [(t_index(*p), t_index(*move(*p))) for p in all_t()])


def over_y(value, move):
    return lax.ppermute(
        value, "segment", [(y * 2 + zl, (move(y) % NY) * 2 + zl) for y in range(NY) for zl in range(2)]
    )


def z_swap(value, mask):
    return over_tensor(value, lambda z, x, c: (z ^ mask, x, c))


def x_swap(value, mask):
    return over_tensor(value, lambda z, x, c: (z, x ^ mask, c))


def core_swap(value):
    return over_tensor(value, lambda z, x, c: (z, x, c ^ 1))


def zl_swap(value):
    return lax.ppermute(value, "segment", [(i, i ^ 1) for i in range(16)])


def to_next_segment(value, mask):
    pairs = []
    for s in range(16):
        for z, x, c in all_t():
            pairs.append((s * 32 + t_index(z, x, c), ((s + 1) % 16) * 32 + t_index(z ^ mask, x, c)))
    return lax.ppermute(value, ("segment", "tensor"), pairs)


def transposition(value):
    pairs = []
    for yy in range(NY):
        for zl in range(2):
            for z, x, c in all_t():
                y = z * 2 + (x >> 1)
                there = t_index(yy >> 1, (yy & 1) * 2 + (x & 1), c)
                pairs.append(((yy * 2 + zl) * 32 + t_index(z, x, c), (y * 2 + zl) * 32 + there))
    return lax.ppermute(value, ("segment", "tensor"), pairs)


def stack(*values):
    return jnp.concatenate(values, axis=0)


def z_direct(value):
    return stack(value, *[z_swap(value, mask) for mask in MASKS[1:]])


def z_pairs(value):
    two = stack(value, z_swap(value, 1))
    return stack(two, z_swap(two, 3))


def x_and_core(value):
    near = stack(value, x_swap(value, 1))
    far = x_swap(near, 3)
    return near, far, core_swap(near), core_swap(far)


def other_neighbour(y):
    return y - 1 if y % 2 == 0 else y + 1


def y_gather(value):
    pair = stack(value, over_y(value, lambda y: y ^ 1))
    second = over_y(pair, other_neighbour)
    third = over_y(second, lambda y: y ^ 1)
    fourth = over_y(second, lambda y: y + 2 if y % 2 == 0 else y - 2)
    return pair, second, third, fourth


def y_labels(y):
    def other(v):
        return lax.rem(v + jnp.where(lax.rem(v, 2) == 0, NY - 1, 1), NY)

    away = lax.rem(y + jnp.where(lax.rem(y, 2) == 0, NY - 2, 2), NY)
    return y, other(y), other(y ^ 1), other(away)


def scaled_weights(weights, gain):
    return (weights.astype(jnp.float32) * gain).astype(jnp.bfloat16)


def pieces(where_ref, parts):
    core, z_mine, x_mine = where_ref[0], where_ref[2], where_ref[3]
    for ref, far, c in zip(parts, (0, 1, 0, 1), (core, core, core ^ 1, core ^ 1), strict=True):
        for i in range(2):
            for j in range(NZ):
                yield ref, i * NZ + j, z_mine ^ MASKS[j], x_mine ^ MASKS[2 * far + i], c


def feature_start(z, x, c):
    return pl.multiple_of((z * 8 + x * 2 + c) * PIECE, PIECE)


def tick_kernel(where_ref, *refs):
    parts, (weight_ref, mine_ref, out_ref, full, square) = refs[:-5], refs[-5:]

    def fill(four):
        square[...] = jnp.zeros((8, ROWS), jnp.float32)
        for ref, k, z, x, c in pieces(where_ref, four):
            piece = ref[k * PIECE : (k + 1) * PIECE, :]
            full[pl.ds(feature_start(z, x, c), PIECE), :] = piece
            wide = piece.astype(jnp.float32)
            square[...] += jnp.sum((wide * wide).reshape(PIECE // 8, 8, ROWS), axis=0)

    if len(parts) == 4:
        fill(parts)
    else:
        first = where_ref[1] == 0

        @pl.when(first)
        def _():
            fill(parts[4:])

        @pl.when(jnp.logical_not(first))
        def _():
            fill(parts[:4])

    mean_square = jnp.sum(square[...], axis=0, keepdims=True) * (1.0 / WIDTH)
    scale = lax.rsqrt(mean_square + EPSILON)
    hidden = jnp.dot(weight_ref[...], full[...], preferred_element_type=jnp.float32) * scale
    silu = hidden / (1.0 + jnp.exp(-hidden))
    out_ref[...] = (mine_ref[...].astype(jnp.float32) + silu).astype(jnp.bfloat16)


def tick(where, parts, weights, mine):
    return pl.pallas_call(
        tick_kernel,
        out_shape=jax.ShapeDtypeStruct((PIECE, ROWS), jnp.bfloat16),
        in_specs=[SMEM_SPEC] + [VMEM_SPEC] * (len(parts) + 2),
        out_specs=VMEM_SPEC,
        scratch_shapes=[pltpu.VMEM((WIDTH, ROWS), jnp.bfloat16), pltpu.VMEM((8, ROWS), jnp.float32)],
        compiler_params=pltpu.CompilerParams(vmem_limit_bytes=VMEM_LIMIT),
        name="tick",
    )(where, *parts, weights, mine)


def predict_kernel(where_ref, *refs):
    rows, blocks, taught, (out_ref, full) = refs[:8], refs[8:12], refs[12:14], refs[14:]
    segment = where_ref[1]
    for tau in range(TICKS):
        for ref, k, z, x, c in pieces(where_ref, rows[4 * tau : 4 * tau + 4]):
            at = pl.ds(feature_start(z, x, c), PIECE)
            full[at, tau * ROWS : (tau + 1) * ROWS] = ref[k * PIECE : (k + 1) * PIECE, :]
    total = jnp.zeros((COLS, TICKS * ROWS), jnp.float32)
    for ref, y in zip(blocks, y_labels(segment >> 1), strict=True):
        for i in range(2):
            for j in range(2):
                owner = (y ^ i) * 2 + ((segment & 1) ^ j)
                total += jnp.dot(
                    ref[(i * 2 + j) * COLS : (i * 2 + j + 1) * COLS, :],
                    full[pl.ds(pl.multiple_of(owner * BLOCK, BLOCK), BLOCK), :],
                    preferred_element_type=jnp.float32,
                )
    for tau in range(TICKS):
        difference = total[:, tau * ROWS : (tau + 1) * ROWS] - taught[tau][...].astype(jnp.float32)
        out_ref[tau * COLS : (tau + 1) * COLS, :] = difference.astype(jnp.bfloat16)


def predict(where, rows, blocks, taught):
    return pl.pallas_call(
        predict_kernel,
        out_shape=jax.ShapeDtypeStruct((TICKS * COLS, ROWS), jnp.bfloat16),
        in_specs=[SMEM_SPEC] + [VMEM_SPEC] * 14,
        out_specs=VMEM_SPEC,
        scratch_shapes=[pltpu.VMEM((WIDTH, TICKS * ROWS), jnp.bfloat16)],
        compiler_params=pltpu.CompilerParams(vmem_limit_bytes=VMEM_LIMIT),
        name="predict",
    )(where, *rows, *blocks, *taught)


def gradient_kernel(where_ref, *refs):
    diffs, parts, (keep_ref, send_ref, rows) = refs[:4], refs[4:8], refs[8:]
    segment = where_ref[1]
    for ref, k, z, x, c in pieces(where_ref, parts):
        y = z * 2 + (x >> 1)
        at = pl.ds(pl.multiple_of(((x & 1) * 2 + c) * PIECE, PIECE), PIECE)
        for tau in range(TICKS):
            source = pl.ds((k * TICKS + tau) * PIECE, PIECE)
            rows[y, at, tau * ROWS : (tau + 1) * ROWS] = ref[source, :]
    half = segment & 1
    for part, out_ref in ((half ^ 1, send_ref), (half, keep_ref)):
        total = jnp.zeros((COLS, BLOCK), jnp.float32)
        for ref, y in zip(diffs, y_labels(segment >> 1), strict=True):
            for i in range(2):
                both = [ref[(i * TICKS + tau) * COLS : (i * TICKS + tau + 1) * COLS, :] for tau in range(TICKS)]
                total += lax.dot_general(
                    jnp.concatenate(both, axis=1),
                    rows[y ^ i, pl.ds(pl.multiple_of(part * BLOCK, BLOCK), BLOCK), :],
                    (((1,), (1,)), ((), ())),
                    preferred_element_type=jnp.float32,
                )
        out_ref[...] = (total * (1.0 / (TICKS * ROWS))).astype(out_ref.dtype)


def gradient(where, diffs, parts):
    return pl.pallas_call(
        gradient_kernel,
        out_shape=(
            jax.ShapeDtypeStruct((COLS, BLOCK), jnp.float32),
            jax.ShapeDtypeStruct((COLS, BLOCK), jnp.bfloat16),
        ),
        in_specs=[SMEM_SPEC] + [VMEM_SPEC] * 8,
        out_specs=(VMEM_SPEC, VMEM_SPEC),
        scratch_shapes=[pltpu.VMEM((NY, 2 * BLOCK, TICKS * ROWS), jnp.bfloat16)],
        compiler_params=pltpu.CompilerParams(vmem_limit_bytes=VMEM_LIMIT),
        name="gradient",
    )(where, *diffs, *parts)


def on_device(entering, fresh_rows, norm_gain, segment_weight, projection, teacher_rows):
    t, segment = lax.axis_index("tensor"), lax.axis_index("segment")
    where = jnp.stack([t & 1, segment, t >> 3, (t >> 1) & 3]).astype(jnp.int32)
    weights = scaled_weights(segment_weight[0], norm_gain)
    teacher = teacher_rows[0].swapaxes(1, 2)
    entering_t, fresh_t = entering[0].T, fresh_rows[0].T

    mine_block = projection.T
    blocks = y_gather(stack(mine_block, zl_swap(mine_block)))
    taught = (to_next_segment(teacher[0], 0), teacher[1])

    out0 = tick(where, x_and_core(z_direct(entering_t)), weights, entering_t)

    moved = [to_next_segment(out0, mask) for mask in MASKS]
    earlier = x_and_core(stack(*moved))
    fresh = x_and_core(z_pairs(fresh_t))
    mine = jnp.where(segment == 0, fresh_t, moved[0])
    out1 = tick(where, earlier + fresh, weights, mine)

    turned = transposition(stack(moved[0], out1))
    later = x_and_core(z_direct(out1))
    difference = predict(where, earlier + later, blocks, taught)

    rows = x_and_core(z_pairs(turned))
    keep, send = gradient(where, y_gather(difference), rows)
    total = keep + zl_swap(send).astype(jnp.float32)
    return (out1.T[None], total.T)


def solution(mesh):
    return jax.shard_map(
        on_device,
        mesh=mesh,
        in_specs=(
            P("segment", None, "tensor"),
            P(None, None, "tensor"),
            P("segment", None),
            P("segment", "tensor", None),
            P("segment", "tensor"),
            P("segment", None, None, "tensor"),
        ),
        out_specs=(P("segment", None, "tensor"), P("segment", "tensor")),
        check_vma=False,
    )
```

time: 276 us -> 272 us (0.986)
  blocking collectives: 145 us -> 0 us
  starting transfers between devices: 77.3 us -> 190 us
  waiting for transfers between devices: 24.8 us -> 53.1 us
  local copies, waits for them, and re-layouts: 5.1 us -> 2.14 us
    all_gather x7 -> x0, blocking collectives: 145 us -> none  [the longest x4 108 us: z_gather(): lax.all_gather(value, 'tensor', axis=0, tiled=True, axis_index_groups=Z_G...]
    ppermute x10 -> x30, starting transfers between devices: 46 us -> 141 us  [over_tensor(): lax.ppermute(value, 'tensor', [(t_index(*p), t_index(*move(*p))) for p in...]
    ppermute x8 -> x16, waiting for transfers between devices: 13.1 us -> 31 us  [the longest x8 18.4 us: over_y(): lax.ppermute(value, 'segment', [(y * 2 + zl, move(y) % NY * 2 + zl) for y...]
    ppermute x8 -> x16, starting transfers between devices: 31.3 us -> 48.7 us  [the longest x8 23.9 us: over_y(): lax.ppermute(value, 'segment', [(y * 2 + zl, move(y) % NY * 2 + zl) for y...]
    ppermute x10 -> x30, waiting for transfers between devices: 11.6 us -> 22.1 us  [over_tensor(): lax.ppermute(value, 'tensor', [(t_index(*p), t_index(*move(*p))) for p in...]
    concatenate x5 -> x12, other arithmetic: 4.8 us -> 8.69 us  [stack(): return jnp.concatenate(values, axis=0)]
  transfers between devices with their start and end apart: 18 -> 46, of which waited for: 3 -> 15; matrix products, arithmetic and copies ran while one was open for 3% -> 4% of each run, Pallas kernels for 3% -> 3%
where the time goes in v2:
time: 272 us; the launch traced here: 267 us
  starting transfers between devices  190 us (70%)
  waiting for transfers between devices  53.1 us (20%)
  Pallas kernels  10.5 us (4%)
  other arithmetic  10.1 us (4%)
    ppermute x30, starting transfers between devices, over_tensor(): lax.ppermute(value, 'tensor', [(t_index(*p), t_index(*move(*p))) for p in...  141 us
    ppermute x8, starting transfers between devices, over_y(): lax.ppermute(value, 'segment', [(y * 2 + zl, move(y) % NY * 2 + zl) for y...  23.9 us
    ppermute x30, waiting for transfers between devices, over_tensor(): lax.ppermute(value, 'tensor', [(t_index(*p), t_index(*move(*p))) for p in...  22.1 us
    ppermute x8, waiting for transfers between devices, over_y(): lax.ppermute(value, 'segment', [(y * 2 + zl, move(y) % NY * 2 + zl) for y...  18.4 us
    ppermute x5, starting transfers between devices, to_next_segment(): return lax.ppermute(value, ('segment', 'tensor'), pairs)  17.5 us
    ppermute x5, waiting for transfers between devices, to_next_segment(): return lax.ppermute(value, ('segment', 'tensor'), pairs)  9.26 us
    concatenate x12, other arithmetic, stack(): return jnp.concatenate(values, axis=0)  8.69 us
    ppermute x2, starting transfers between devices, zl_swap(): return lax.ppermute(value, 'segment', [(i, i ^ 1) for i in range(16)])  6.58 us
  transfers between devices with their start and end apart: 46, of which 15 were waited for; matrix products, arithmetic and copies ran while one was open for 4% of the time, Pallas kernels for 3%

profile of v2, /device:TPU:1, one launch (start us, length us, event | category | flops | bytes accessed | tf_op | source)
XLA Modules:
  0.0 267.1 jit_solution(13330632589642820395)
XLA Ops:
  0.6 6.8 %collective-permute-start = (bf16[192,128]{1,0:T(8,128)(2,1)}, bf16[192,128]{1,0:T(8,128)(2,1)S(1)}, u32[]{:S(2)}, u32[]{:S(2)}) collective-permute-start(bf16[192,128]{1,0:T(8,128)(2,1)} %bitcast.29), channel_id=1, source_target_pairs={{0,8},{1,9},{2,10},{3,11},{4,12},{5,13},{6,14},{7,15},{8,0},{9,1},... | collective-permute-start | bytes 147464 | tf_op jit(solution)/shard_map/ppermute | solution.py:31
  7.4 7.0 %collective-permute-start.1 = (bf16[192,128]{1,0:T(8,128)(2,1)}, bf16[192,128]{1,0:T(8,128)(2,1)S(1)}, u32[]{:S(2)}, u32[]{:S(2)}) collective-permute-start(bf16[192,128]{1,0:T(8,128)(2,1)} %bitcast.30), channel_id=1, source_target_pairs={{0,24},{1,25},{2,26},{3,27},{4,28},{5,29},{6,30},{7,31},{8,16},{9,... | collective-permute-start | bytes 147464 | tf_op jit(solution)/shard_map/ppermute | solution.py:31
  14.5 3.7 %collective-permute-start.2 = (bf16[192,128]{1,0:T(8,128)(2,1)}, bf16[192,128]{1,0:T(8,128)(2,1)S(1)}, u32[]{:S(2)}, u32[]{:S(2)}) collective-permute-start(bf16[192,128]{1,0:T(8,128)(2,1)} %bitcast.31), channel_id=1, source_target_pairs={{0,16},{1,17},{2,18},{3,19},{4,20},{5,21},{6,22},{7,23},{8,24},{9,... | collective-permute-start | bytes 147464 | tf_op jit(solution)/shard_map/ppermute | solution.py:31
  25.9 3.1 %collective-permute-start.3 = (bf16[768,128]{1,0:T(8,128)(2,1)S(1)}, bf16[768,128]{1,0:T(8,128)(2,1)S(1)}, u32[]{:S(2)}, u32[]{:S(2)}) collective-permute-start(bf16[768,128]{1,0:T(8,128)(2,1)S(1)} %pad_maximum_fusion.5), channel_id=1, source_target_pairs={{0,2},{1,3},{2,0},{3,1},{4,6},{5,7},{6,4},{7,5},{8,10},{9,11},{10,... | collective-permute-start | bytes 589832 | tf_op jit(solution)/shard_map/ppermute | solution.py:31
  29.1 4.0 %collective-permute-done.3 = bf16[768,128]{1,0:T(8,128)(2,1)S(1)} collective-permute-done((bf16[768,128]{1,0:T(8,128)(2,1)S(1)}, bf16[768,128]{1,0:T(8,128)(2,1)S(1)}, u32[]{:S(2)}, u32[]{:S(2)}) %collective-permute-start.3) | collective-permute-done | bytes 196640 | tf_op jit(solution)/shard_map/ppermute | solution.py:31
  33.1 4.4 %collective-permute-start.4 = (bf16[1536,128]{1,0:T(8,128)(2,1)S(1)}, bf16[1536,128]{1,0:T(8,128)(2,1)S(1)}, u32[]{:S(2)}, u32[]{:S(2)}) collective-permute-start(bf16[1536,128]{1,0:T(8,128)(2,1)S(1)} %constant_dynamic-update-slice_fusion.refs_0_), channel_id=1, source_target_pairs={{0,6},{1,7},{2,4},{3,5},{4,2},{5,3},{6,0},{7,1},{8,14},{9,15},{10,... | collective-permute-start | bytes 1179656 | tf_op jit(solution)/shard_map/ppermute | solution.py:31
  38.3 3.9 %collective-permute-start.16 = (bf16[384,128]{1,0:T(8,128)(2,1)S(1)}, bf16[384,128]{1,0:T(8,128)(2,1)S(1)}, u32[]{:S(2)}, u32[]{:S(2)}) collective-permute-start(bf16[384,128]{1,0:T(8,128)(2,1)S(1)} %pad_maximum_fusion.10), channel_id=1, source_target_pairs={{0,24},{1,25},{2,26},{3,27},{4,28},{5,29},{6,30},{7,31},{8,16},{9,... | collective-permute-start | bytes 294920 | tf_op jit(solution)/shard_map/ppermute | solution.py:31
  42.3 3.5 %collective-permute-done.16 = bf16[384,128]{1,0:T(8,128)(2,1)S(1)} collective-permute-done((bf16[384,128]{1,0:T(8,128)(2,1)S(1)}, bf16[384,128]{1,0:T(8,128)(2,1)S(1)}, u32[]{:S(2)}, u32[]{:S(2)}) %collective-permute-start.16) | collective-permute-done | bytes 98336 | tf_op jit(solution)/shard_map/ppermute | solution.py:31
  51.0 3.2 %collective-permute-start.29 = (bf16[576,384]{1,0:T(8,128)(2,1)}, bf16[576,384]{1,0:T(8,128)(2,1)}, u32[]{:S(2)}, u32[]{:S(2)}) collective-permute-start(bf16[576,384]{1,0:T(8,128)(2,1)} %pad_maximum_fusion.1), channel_id=1, source_target_pairs={{0,64},{32,96},{64,0},{96,32},{128,192},{160,224},{192,128},{224,1... | collective-permute-start | bytes 1327112 | tf_op jit(solution)/shard_map/ppermute | solution.py:35
  54.2 5.9 %collective-permute-start.5 = (bf16[1536,128]{1,0:T(8,128)(2,1)S(1)}, bf16[1536,128]{1,0:T(8,128)(2,1)}, u32[]{:S(2)}, u32[]{:S(2)}) collective-permute-start(bf16[1536,128]{1,0:T(8,128)(2,1)S(1)} %constant_dynamic-update-slice_fusion.refs_0_), channel_id=1, source_target_pairs={{0,1},{1,0},{2,3},{3,2},{4,5},{5,4},{6,7},{7,6},{8,9},{9,8},{10,11... | collective-permute-start | bytes 1179656 | tf_op jit(solution)/shard_map/ppermute | solution.py:31
  69.1 3.5 %collective-permute-start.7 = (bf16[192,128]{1,0:T(8,128)(2,1)S(1)}, bf16[192,128]{1,0:T(8,128)(2,1)S(1)}, u32[]{:S(2)}, u32[]{:S(2)}) collective-permute-start(bf16[192,128]{1,0:T(8,128)(2,1)S(1)} %tick.2), channel_id=1, source_target_pairs={{0,32},{1,33},{2,34},{3,35},{4,36},{5,37},{6,38},{7,39},{8,40},{9,... | collective-permute-start | bytes 147464 | tf_op jit(solution)/shard_map/ppermute | solution.py:61
  72.6 3.4 %collective-permute-start.8 = (bf16[192,128]{1,0:T(8,128)(2,1)S(1)}, bf16[192,128]{1,0:T(8,128)(2,1)S(1)}, u32[]{:S(2)}, u32[]{:S(2)}) collective-permute-start(bf16[192,128]{1,0:T(8,128)(2,1)S(1)} %tick.2), channel_id=1, source_target_pairs={{0,40},{1,41},{2,42},{3,43},{4,44},{5,45},{6,46},{7,47},{8,32},{9,... | collective-permute-start | bytes 147464 | tf_op jit(solution)/shard_map/ppermute | solution.py:61
  76.0 5.3 %collective-permute-start.9 = (bf16[192,128]{1,0:T(8,128)(2,1)S(1)}, bf16[192,128]{1,0:T(8,128)(2,1)S(1)}, u32[]{:S(2)}, u32[]{:S(2)}) collective-permute-start(bf16[192,128]{1,0:T(8,128)(2,1)S(1)} %tick.2), channel_id=1, source_target_pairs={{0,56},{1,57},{2,58},{3,59},{4,60},{5,61},{6,62},{7,63},{8,48},{9,... | collective-permute-start | bytes 147464 | tf_op jit(solution)/shard_map/ppermute | solution.py:61
  81.3 3.4 %collective-permute-start.10 = (bf16[192,128]{1,0:T(8,128)(2,1)S(1)}, bf16[192,128]{1,0:T(8,128)(2,1)S(1)}, u32[]{:S(2)}, u32[]{:S(2)}) collective-permute-start(bf16[192,128]{1,0:T(8,128)(2,1)S(1)} %tick.2), channel_id=1, source_target_pairs={{0,48},{1,49},{2,50},{3,51},{4,52},{5,53},{6,54},{7,55},{8,56},{9,... | collective-permute-start | bytes 147464 | tf_op jit(solution)/shard_map/ppermute | solution.py:61
  94.4 4.0 %collective-permute-done.11 = bf16[768,128]{1,0:T(8,128)(2,1)S(1)} collective-permute-done((bf16[768,128]{1,0:T(8,128)(2,1)S(1)}, bf16[768,128]{1,0:T(8,128)(2,1)S(1)}, u32[]{:S(2)}, u32[]{:S(2)}) %collective-permute-start.11) | collective-permute-done | bytes 196640 | tf_op jit(solution)/shard_map/ppermute | solution.py:31
  98.5 3.7 %collective-permute-start.12 = (bf16[1536,128]{1,0:T(8,128)(2,1)S(1)}, bf16[1536,128]{1,0:T(8,128)(2,1)S(1)}, u32[]{:S(2)}, u32[]{:S(2)}) collective-permute-start(bf16[1536,128]{1,0:T(8,128)(2,1)S(1)} %constant_dynamic-update-slice_fusion.5.refs_0_), channel_id=1, source_target_pairs={{0,6},{1,7},{2,4},{3,5},{4,2},{5,3},{6,0},{7,1},{8,14},{9,15},{10,... | collective-permute-start | bytes 1179656 | tf_op jit(solution)/shard_map/ppermute | solution.py:31
  102.2 5.8 %collective-permute-start.19 = (bf16[1536,128]{1,0:T(8,128)(2,1)S(1)}, bf16[1536,128]{1,0:T(8,128)(2,1)S(1)}, u32[]{:S(2)}, u32[]{:S(2)}) collective-permute-start(bf16[1536,128]{1,0:T(8,128)(2,1)S(1)} %pad_maximum_fusion.2.refs_4_), channel_id=1, source_target_pairs={{0,1},{1,0},{2,3},{3,2},{4,5},{5,4},{6,7},{7,6},{8,9},{9,8},{10,11... | collective-permute-start | bytes 1179656 | tf_op jit(solution)/shard_map/ppermute | solution.py:31
  118.1 4.5 %collective-permute-start.32 = (bf16[1152,384]{1,0:T(8,128)(2,1)S(1)}, bf16[1152,384]{1,0:T(8,128)(2,1)S(1)}, u32[]{:S(2)}, u32[]{:S(2)}) collective-permute-start(bf16[1152,384]{1,0:T(8,128)(2,1)S(1)} %collective-permute-done.30.refs_9_), channel_id=1, source_target_pairs={{0,128},{32,160},{64,448},{96,480},{128,256},{160,288},{192,64},{2... | collective-permute-start | bytes 2654216 | tf_op jit(solution)/shard_map/ppermute | solution.py:35
  127.3 3.2 %collective-permute-start.22 = (bf16[192,128]{1,0:T(8,128)(2,1)}, bf16[192,128]{1,0:T(8,128)(2,1)S(1)}, u32[]{:S(2)}, u32[]{:S(2)}) collective-permute-start(bf16[192,128]{1,0:T(8,128)(2,1)} %tick.3), channel_id=1, source_target_pairs={{0,24},{1,25},{2,26},{3,27},{4,28},{5,29},{6,30},{7,31},{8,16},{9,... | collective-permute-start | bytes 147464 | tf_op jit(solution)/shard_map/ppermute | solution.py:31
  130.5 6.2 %collective-permute-start.23 = (bf16[192,128]{1,0:T(8,128)(2,1)}, bf16[192,128]{1,0:T(8,128)(2,1)S(1)}, u32[]{:S(2)}, u32[]{:S(2)}) collective-permute-start(bf16[192,128]{1,0:T(8,128)(2,1)} %tick.3), channel_id=1, source_target_pairs={{0,16},{1,17},{2,18},{3,19},{4,20},{5,21},{6,22},{7,23},{8,24},{9,... | collective-permute-start | bytes 147464 | tf_op jit(solution)/shard_map/ppermute | solution.py:31
  142.2 31.5 %collective-permute-start.39 = (bf16[384,128]{1,0:T(8,128)(2,1)S(1)}, bf16[384,128]{1,0:T(8,128)(2,1)S(1)}, u32[]{:S(2)}, u32[]{:S(2)}) collective-permute-start(bf16[384,128]{1,0:T(8,128)(2,1)S(1)} %collective-permute-done.38), channel_id=1, source_target_pairs={{0,8},{1,9},{2,10},{3,11},{4,12},{5,13},{6,14},{7,15},{8,0},{9,1},... | collective-permute-start | bytes 294920 | tf_op jit(solution)/shard_map/ppermute | solution.py:31
  178.7 5.7 %collective-permute-done.40 = bf16[768,128]{1,0:T(8,128)(2,1)S(1)} collective-permute-done((bf16[768,128]{1,0:T(8,128)(2,1)S(1)}, bf16[768,128]{1,0:T(8,128)(2,1)S(1)}, u32[]{:S(2)}, u32[]{:S(2)}) %collective-permute-start.40) | collective-permute-done | bytes 196640 | tf_op jit(solution)/shard_map/ppermute | solution.py:31
  186.4 9.5 %collective-permute-start.25 = (bf16[1536,128]{1,0:T(8,128)(2,1)S(1)}, bf16[1536,128]{1,0:T(8,128)(2,1)S(1)}, u32[]{:S(2)}, u32[]{:S(2)}) collective-permute-start(bf16[1536,128]{1,0:T(8,128)(2,1)S(1)} %constant_dynamic-update-slice_fusion.10.refs_4_), channel_id=1, source_target_pairs={{0,6},{1,7},{2,4},{3,5},{4,2},{5,3},{6,0},{7,1},{8,14},{9,15},{10,... | collective-permute-start | bytes 1179656 | tf_op jit(solution)/shard_map/ppermute | solution.py:31
  196.1 7.8 %collective-permute-start.42 = (bf16[3072,128]{1,0:T(8,128)(2,1)S(1)}, bf16[3072,128]{1,0:T(8,128)(2,1)S(1)}, u32[]{:S(2)}, u32[]{:S(2)}) collective-permute-start(bf16[3072,128]{1,0:T(8,128)(2,1)S(1)} %constant_dynamic-update-slice_fusion.15.refs_4_), channel_id=1, source_target_pairs={{0,6},{1,7},{2,4},{3,5},{4,2},{5,3},{6,0},{7,1},{8,14},{9,15},{10,... | collective-permute-start | bytes 2359304 | tf_op jit(solution)/shard_map/ppermute | solution.py:31
  205.9 6.4 %collective-permute-done.33.refs_12_ = bf16[288,128]{1,0:T(8,128)(2,1)S(1)} collective-permute-done((bf16[288,128]{1,0:T(8,128)(2,1)S(1)}, bf16[288,128]{1,0:T(8,128)(2,1)S(1)}, u32[]{:S(2)}, u32[]{:S(2)}) %collective-permute-start.33) | collective-permute-done | bytes 73760 | tf_op jit(solution)/shard_map/ppermute | solution.py:61
  212.3 5.0 %collective-permute-start.26 = (bf16[1536,128]{1,0:T(8,128)(2,1)S(1)}, bf16[1536,128]{1,0:T(8,128)(2,1)S(1)}, u32[]{:S(2)}, u32[]{:S(2)}) collective-permute-start(bf16[1536,128]{1,0:T(8,128)(2,1)S(1)} %constant_dynamic-update-slice_fusion.10.refs_4_), channel_id=1, source_target_pairs={{0,1},{1,0},{2,3},{3,2},{4,5},{5,4},{6,7},{7,6},{8,9},{9,8},{10,11... | collective-permute-start | bytes 1179656 | tf_op jit(solution)/shard_map/ppermute | solution.py:31
  221.0 3.1 %predict.1 = bf16[576,128]{1,0:T(8,128)(2,1)S(1)} custom-call(s32[4]{0:T(128)S(1)} %pad_add_fusion.where_ref, bf16[1536,128]{1,0:T(8,128)(2,1)S(1)} %constant_dynamic-update-slice_fusion.5.refs_0_, bf16[1536,128]{1,0:T(8,128)(2,1)S(1)} %collective-permute-done.12.refs_1_, bf16[1536,128]{1,0:T(8,128)(2,1)S(1)} %collective-permute-done.13.refs_2_, ...), custom_call_target="tpu_custom_call" | custom-call | tf_op jit(solution)/shard_map/predict/pallas_call | solution.py:196
  233.5 8.5 %collective-permute-done.35.refs_1_ = bf16[1152,128]{1,0:T(8,128)(2,1)S(1)} collective-permute-done((bf16[1152,128]{1,0:T(8,128)(2,1)S(1)}, bf16[1152,128]{1,0:T(8,128)(2,1)S(1)}, u32[]{:S(2)}, u32[]{:S(2)}) %collective-permute-start.35) | collective-permute-done | bytes 294944 | tf_op jit(solution)/shard_map/ppermute | solution.py:35
  243.9 4.0 %collective-permute-start.37 = (bf16[1152,128]{1,0:T(8,128)(2,1)S(1)}, bf16[1152,128]{1,0:T(8,128)(2,1)S(1)}, u32[]{:S(2)}, u32[]{:S(2)}) collective-permute-start(bf16[1152,128]{1,0:T(8,128)(2,1)S(1)} %collective-permute-done.35.refs_1_), channel_id=1, source_target_pairs={{0,128},{32,160},{64,448},{96,480},{128,256},{160,288},{192,64},{2... | collective-permute-start | bytes 884744 | tf_op jit(solution)/shard_map/ppermute | solution.py:35
  250.5 6.5 %collective-permute-done.37.refs_3_ = bf16[1152,128]{1,0:T(8,128)(2,1)S(1)} collective-permute-done((bf16[1152,128]{1,0:T(8,128)(2,1)S(1)}, bf16[1152,128]{1,0:T(8,128)(2,1)S(1)}, u32[]{:S(2)}, u32[]{:S(2)}) %collective-permute-start.37) | collective-permute-done | bytes 294944 | tf_op jit(solution)/shard_map/ppermute | solution.py:35
  259.5 3.5 %collective-permute-start.45 = (bf16[288,384]{1,0:T(8,128)(2,1)S(1)}, bf16[288,384]{1,0:T(8,128)(2,1)S(1)}, u32[]{:S(2)}, u32[]{:S(2)}) collective-permute-start(bf16[288,384]{1,0:T(8,128)(2,1)S(1)} %get-tuple-element.5), channel_id=1, source_target_pairs={{0,32},{32,0},{64,96},{96,64},{128,160},{160,128},{192,224},{224,1... | collective-permute-start | bytes 663560 | tf_op jit(solution)/shard_map/ppermute | solution.py:53
  263.0 3.3 %collective-permute-done.45 = bf16[288,384]{1,0:T(8,128)(2,1)S(1)} collective-permute-done((bf16[288,384]{1,0:T(8,128)(2,1)S(1)}, bf16[288,384]{1,0:T(8,128)(2,1)S(1)}, u32[]{:S(2)}, u32[]{:S(2)}) %collective-permute-start.45) | collective-permute-done | bytes 221216 | tf_op jit(solution)/shard_map/ppermute | solution.py:53
  (115 shorter events, 81.9 us)
Async XLA Ops:
  0.6 23.7 %collective-permute-start = (bf16[192,128]{1,0:T(8,128)(2,1)}, bf16[192,128]{1,0:T(8,128)(2,1)S(1)}, u32[]{:S(2)}, u32[]{:S(2)}) collective-permute-start(bf16[192,128]{1,0:T(8,128)(2,1)} %bitcast.29), channel_id=1, source_target_pairs={{0,8},{1,9},{2,10},{3,11},{4,12},{5,13},{6,14},{7,15},{8,0},{9,1},... | collective-permute-start | bytes 147464 | tf_op jit(solution)/shard_map/ppermute | solution.py:31
  7.4 16.9 %collective-permute-start.1 = (bf16[192,128]{1,0:T(8,128)(2,1)}, bf16[192,128]{1,0:T(8,128)(2,1)S(1)}, u32[]{:S(2)}, u32[]{:S(2)}) collective-permute-start(bf16[192,128]{1,0:T(8,128)(2,1)} %bitcast.30), channel_id=1, source_target_pairs={{0,24},{1,25},{2,26},{3,27},{4,28},{5,29},{6,30},{7,31},{8,16},{9,... | collective-permute-start | bytes 147464 | tf_op jit(solution)/shard_map/ppermute | solution.py:31
  14.5 10.6 %collective-permute-start.2 = (bf16[192,128]{1,0:T(8,128)(2,1)}, bf16[192,128]{1,0:T(8,128)(2,1)S(1)}, u32[]{:S(2)}, u32[]{:S(2)}) collective-permute-start(bf16[192,128]{1,0:T(8,128)(2,1)} %bitcast.31), channel_id=1, source_target_pairs={{0,16},{1,17},{2,18},{3,19},{4,20},{5,21},{6,22},{7,23},{8,24},{9,... | collective-permute-start | bytes 147464 | tf_op jit(solution)/shard_map/ppermute | solution.py:31
  18.2 19.3 %collective-permute-start.15 = (bf16[192,128]{1,0:T(8,128)(2,1)}, bf16[192,128]{1,0:T(8,128)(2,1)S(1)}, u32[]{:S(2)}, u32[]{:S(2)}) collective-permute-start(bf16[192,128]{1,0:T(8,128)(2,1)} %bitcast.38), channel_id=1, source_target_pairs={{0,8},{1,9},{2,10},{3,11},{4,12},{5,13},{6,14},{7,15},{8,0},{9,1},... | collective-permute-start | bytes 147464 | tf_op jit(solution)/shard_map/ppermute | solution.py:31
  20.4 28.8 %collective-permute-start.28 = (bf16[288,384]{1,0:T(8,128)(2,1)}, bf16[288,384]{1,0:T(8,128)(2,1)S(1)}, u32[]{:S(2)}, u32[]{:S(2)}) collective-permute-start(bf16[288,384]{1,0:T(8,128)(2,1)} %bitcast.34), channel_id=1, source_target_pairs={{0,32},{32,0},{64,96},{96,64},{128,160},{160,128},{192,224},{224,1... | collective-permute-start | bytes 663560 | tf_op jit(solution)/shard_map/ppermute | solution.py:53
  33.1 27.0 %collective-permute-start.4 = (bf16[1536,128]{1,0:T(8,128)(2,1)S(1)}, bf16[1536,128]{1,0:T(8,128)(2,1)S(1)}, u32[]{:S(2)}, u32[]{:S(2)}) collective-permute-start(bf16[1536,128]{1,0:T(8,128)(2,1)S(1)} %constant_dynamic-update-slice_fusion.refs_0_), channel_id=1, source_target_pairs={{0,6},{1,7},{2,4},{3,5},{4,2},{5,3},{6,0},{7,1},{8,14},{9,15},{10,... | collective-permute-start | bytes 1179656 | tf_op jit(solution)/shard_map/ppermute | solution.py:31
  47.3 15.4 %collective-permute-start.17 = (bf16[768,128]{1,0:T(8,128)(2,1)}, bf16[768,128]{1,0:T(8,128)(2,1)}, u32[]{:S(2)}, u32[]{:S(2)}) collective-permute-start(bf16[768,128]{1,0:T(8,128)(2,1)} %pad_maximum_fusion.7), channel_id=1, source_target_pairs={{0,2},{1,3},{2,0},{3,1},{4,6},{5,7},{6,4},{7,5},{8,10},{9,11},{10,... | collective-permute-start | bytes 589832 | tf_op jit(solution)/shard_map/ppermute | solution.py:31
  51.0 30.3 %collective-permute-start.29 = (bf16[576,384]{1,0:T(8,128)(2,1)}, bf16[576,384]{1,0:T(8,128)(2,1)}, u32[]{:S(2)}, u32[]{:S(2)}) collective-permute-start(bf16[576,384]{1,0:T(8,128)(2,1)} %pad_maximum_fusion.1), channel_id=1, source_target_pairs={{0,64},{32,96},{64,0},{96,32},{128,192},{160,224},{192,128},{224,1... | collective-permute-start | bytes 1327112 | tf_op jit(solution)/shard_map/ppermute | solution.py:35
  54.2 12.5 %collective-permute-start.5 = (bf16[1536,128]{1,0:T(8,128)(2,1)S(1)}, bf16[1536,128]{1,0:T(8,128)(2,1)}, u32[]{:S(2)}, u32[]{:S(2)}) collective-permute-start(bf16[1536,128]{1,0:T(8,128)(2,1)S(1)} %constant_dynamic-update-slice_fusion.refs_0_), channel_id=1, source_target_pairs={{0,1},{1,0},{2,3},{3,2},{4,5},{5,4},{6,7},{7,6},{8,9},{9,8},{10,11... | collective-permute-start | bytes 1179656 | tf_op jit(solution)/shard_map/ppermute | solution.py:31
  63.9 44.1 %collective-permute-start.18 = (bf16[1536,128]{1,0:T(8,128)(2,1)S(1)}, bf16[1536,128]{1,0:T(8,128)(2,1)S(1)}, u32[]{:S(2)}, u32[]{:S(2)}) collective-permute-start(bf16[1536,128]{1,0:T(8,128)(2,1)S(1)} %pad_maximum_fusion.2.refs_4_), channel_id=1, source_target_pairs={{0,6},{1,7},{2,4},{3,5},{4,2},{5,3},{6,0},{7,1},{8,14},{9,15},{10,... | collective-permute-start | bytes 1179656 | tf_op jit(solution)/shard_map/ppermute | solution.py:31
  69.1 16.8 %collective-permute-start.7 = (bf16[192,128]{1,0:T(8,128)(2,1)S(1)}, bf16[192,128]{1,0:T(8,128)(2,1)S(1)}, u32[]{:S(2)}, u32[]{:S(2)}) collective-permute-start(bf16[192,128]{1,0:T(8,128)(2,1)S(1)} %tick.2), channel_id=1, source_target_pairs={{0,32},{1,33},{2,34},{3,35},{4,36},{5,37},{6,38},{7,39},{8,40},{9,... | collective-permute-start | bytes 147464 | tf_op jit(solution)/shard_map/ppermute | solution.py:61
  72.6 16.2 %collective-permute-start.8 = (bf16[192,128]{1,0:T(8,128)(2,1)S(1)}, bf16[192,128]{1,0:T(8,128)(2,1)S(1)}, u32[]{:S(2)}, u32[]{:S(2)}) collective-permute-start(bf16[192,128]{1,0:T(8,128)(2,1)S(1)} %tick.2), channel_id=1, source_target_pairs={{0,40},{1,41},{2,42},{3,43},{4,44},{5,45},{6,46},{7,47},{8,32},{9,... | collective-permute-start | bytes 147464 | tf_op jit(solution)/shard_map/ppermute | solution.py:61
  76.0 12.9 %collective-permute-start.9 = (bf16[192,128]{1,0:T(8,128)(2,1)S(1)}, bf16[192,128]{1,0:T(8,128)(2,1)S(1)}, u32[]{:S(2)}, u32[]{:S(2)}) collective-permute-start(bf16[192,128]{1,0:T(8,128)(2,1)S(1)} %tick.2), channel_id=1, source_target_pairs={{0,56},{1,57},{2,58},{3,59},{4,60},{5,61},{6,62},{7,63},{8,48},{9,... | collective-permute-start | bytes 147464 | tf_op jit(solution)/shard_map/ppermute | solution.py:61
  81.3 10.4 %collective-permute-start.10 = (bf16[192,128]{1,0:T(8,128)(2,1)S(1)}, bf16[192,128]{1,0:T(8,128)(2,1)S(1)}, u32[]{:S(2)}, u32[]{:S(2)}) collective-permute-start(bf16[192,128]{1,0:T(8,128)(2,1)S(1)} %tick.2), channel_id=1, source_target_pairs={{0,48},{1,49},{2,50},{3,51},{4,52},{5,53},{6,54},{7,55},{8,56},{9,... | collective-permute-start | bytes 147464 | tf_op jit(solution)/shard_map/ppermute | solution.py:61
  85.8 29.2 %collective-permute-start.30 = (bf16[1152,384]{1,0:T(8,128)(2,1)S(1)}, bf16[1152,384]{1,0:T(8,128)(2,1)S(1)}, u32[]{:S(2)}, u32[]{:S(2)}) collective-permute-start(bf16[1152,384]{1,0:T(8,128)(2,1)S(1)} %pad_maximum_fusion.refs_8_), channel_id=1, source_target_pairs={{0,448},{32,480},{64,128},{96,160},{128,64},{160,96},{192,256},{22... | collective-permute-start | bytes 2654216 | tf_op jit(solution)/shard_map/ppermute | solution.py:35
  98.5 13.9 %collective-permute-start.12 = (bf16[1536,128]{1,0:T(8,128)(2,1)S(1)}, bf16[1536,128]{1,0:T(8,128)(2,1)S(1)}, u32[]{:S(2)}, u32[]{:S(2)}) collective-permute-start(bf16[1536,128]{1,0:T(8,128)(2,1)S(1)} %constant_dynamic-update-slice_fusion.5.refs_0_), channel_id=1, source_target_pairs={{0,6},{1,7},{2,4},{3,5},{4,2},{5,3},{6,0},{7,1},{8,14},{9,15},{10,... | collective-permute-start | bytes 1179656 | tf_op jit(solution)/shard_map/ppermute | solution.py:31
  102.2 15.9 %collective-permute-start.19 = (bf16[1536,128]{1,0:T(8,128)(2,1)S(1)}, bf16[1536,128]{1,0:T(8,128)(2,1)S(1)}, u32[]{:S(2)}, u32[]{:S(2)}) collective-permute-start(bf16[1536,128]{1,0:T(8,128)(2,1)S(1)} %pad_maximum_fusion.2.refs_4_), channel_id=1, source_target_pairs={{0,1},{1,0},{2,3},{3,2},{4,5},{5,4},{6,7},{7,6},{8,9},{9,8},{10,11... | collective-permute-start | bytes 1179656 | tf_op jit(solution)/shard_map/ppermute | solution.py:31
  108.0 14.7 %collective-permute-start.20 = (bf16[1536,128]{1,0:T(8,128)(2,1)S(1)}, bf16[1536,128]{1,0:T(8,128)(2,1)S(1)}, u32[]{:S(2)}, u32[]{:S(2)}) collective-permute-start(bf16[1536,128]{1,0:T(8,128)(2,1)S(1)} %collective-permute-done.18.refs_5_), channel_id=1, source_target_pairs={{0,1},{1,0},{2,3},{3,2},{4,5},{5,4},{6,7},{7,6},{8,9},{9,8},{10,11... | collective-permute-start | bytes 1179656 | tf_op jit(solution)/shard_map/ppermute | solution.py:31
  109.9 12.8 %collective-permute-start.13 = (bf16[1536,128]{1,0:T(8,128)(2,1)S(1)}, bf16[1536,128]{1,0:T(8,128)(2,1)S(1)}, u32[]{:S(2)}, u32[]{:S(2)}) collective-permute-start(bf16[1536,128]{1,0:T(8,128)(2,1)S(1)} %constant_dynamic-update-slice_fusion.5.refs_0_), channel_id=1, source_target_pairs={{0,1},{1,0},{2,3},{3,2},{4,5},{5,4},{6,7},{7,6},{8,9},{9,8},{10,11... | collective-permute-start | bytes 1179656 | tf_op jit(solution)/shard_map/ppermute | solution.py:31
  115.0 104.2 %collective-permute-start.31 = (bf16[1152,384]{1,0:T(8,128)(2,1)S(1)}, bf16[1152,384]{1,0:T(8,128)(2,1)S(1)}, u32[]{:S(2)}, u32[]{:S(2)}) collective-permute-start(bf16[1152,384]{1,0:T(8,128)(2,1)S(1)} %collective-permute-done.30.refs_9_), channel_id=1, source_target_pairs={{0,64},{32,96},{64,0},{96,32},{128,192},{160,224},{192,128},{224,1... | collective-permute-start | bytes 2654216 | tf_op jit(solution)/shard_map/ppermute | solution.py:35
  118.1 101.1 %collective-permute-start.32 = (bf16[1152,384]{1,0:T(8,128)(2,1)S(1)}, bf16[1152,384]{1,0:T(8,128)(2,1)S(1)}, u32[]{:S(2)}, u32[]{:S(2)}) collective-permute-start(bf16[1152,384]{1,0:T(8,128)(2,1)S(1)} %collective-permute-done.30.refs_9_), channel_id=1, source_target_pairs={{0,128},{32,160},{64,448},{96,480},{128,256},{160,288},{192,64},{2... | collective-permute-start | bytes 2654216 | tf_op jit(solution)/shard_map/ppermute | solution.py:35
  125.2 13.1 %collective-permute-start.21 = (bf16[192,128]{1,0:T(8,128)(2,1)}, bf16[192,128]{1,0:T(8,128)(2,1)S(1)}, u32[]{:S(2)}, u32[]{:S(2)}) collective-permute-start(bf16[192,128]{1,0:T(8,128)(2,1)} %tick.3), channel_id=1, source_target_pairs={{0,8},{1,9},{2,10},{3,11},{4,12},{5,13},{6,14},{7,15},{8,0},{9,1},... | collective-permute-start | bytes 147464 | tf_op jit(solution)/shard_map/ppermute | solution.py:31
  127.3 11.8 %collective-permute-start.22 = (bf16[192,128]{1,0:T(8,128)(2,1)}, bf16[192,128]{1,0:T(8,128)(2,1)S(1)}, u32[]{:S(2)}, u32[]{:S(2)}) collective-permute-start(bf16[192,128]{1,0:T(8,128)(2,1)} %tick.3), channel_id=1, source_target_pairs={{0,24},{1,25},{2,26},{3,27},{4,28},{5,29},{6,30},{7,31},{8,16},{9,... | collective-permute-start | bytes 147464 | tf_op jit(solution)/shard_map/ppermute | solution.py:31
  140.3 46.1 %collective-permute-start.24 = (bf16[768,128]{1,0:T(8,128)(2,1)S(1)}, bf16[768,128]{1,0:T(8,128)(2,1)S(1)}, u32[]{:S(2)}, u32[]{:S(2)}) collective-permute-start(bf16[768,128]{1,0:T(8,128)(2,1)S(1)} %pad_maximum_fusion.8), channel_id=1, source_target_pairs={{0,2},{1,3},{2,0},{3,1},{4,6},{5,7},{6,4},{7,5},{8,10},{9,11},{10,... | collective-permute-start | bytes 589832 | tf_op jit(solution)/shard_map/ppermute | solution.py:31
  142.2 33.5 %collective-permute-start.39 = (bf16[384,128]{1,0:T(8,128)(2,1)S(1)}, bf16[384,128]{1,0:T(8,128)(2,1)S(1)}, u32[]{:S(2)}, u32[]{:S(2)}) collective-permute-start(bf16[384,128]{1,0:T(8,128)(2,1)S(1)} %collective-permute-done.38), channel_id=1, source_target_pairs={{0,8},{1,9},{2,10},{3,11},{4,12},{5,13},{6,14},{7,15},{8,0},{9,1},... | collective-permute-start | bytes 294920 | tf_op jit(solution)/shard_map/ppermute | solution.py:31
  184.4 11.6 %collective-permute-start.41 = (bf16[1536,128]{1,0:T(8,128)(2,1)S(1)}, bf16[1536,128]{1,0:T(8,128)(2,1)S(1)}, u32[]{:S(2)}, u32[]{:S(2)}) collective-permute-start(bf16[1536,128]{1,0:T(8,128)(2,1)S(1)} %pad_maximum_fusion.3), channel_id=1, source_target_pairs={{0,2},{1,3},{2,0},{3,1},{4,6},{5,7},{6,4},{7,5},{8,10},{9,11},{10,... | collective-permute-start | bytes 1179656 | tf_op jit(solution)/shard_map/ppermute | solution.py:31
  186.4 30.9 %collective-permute-start.25 = (bf16[1536,128]{1,0:T(8,128)(2,1)S(1)}, bf16[1536,128]{1,0:T(8,128)(2,1)S(1)}, u32[]{:S(2)}, u32[]{:S(2)}) collective-permute-start(bf16[1536,128]{1,0:T(8,128)(2,1)S(1)} %constant_dynamic-update-slice_fusion.10.refs_4_), channel_id=1, source_target_pairs={{0,6},{1,7},{2,4},{3,5},{4,2},{5,3},{6,0},{7,1},{8,14},{9,15},{10,... | collective-permute-start | bytes 1179656 | tf_op jit(solution)/shard_map/ppermute | solution.py:31
  196.1 32.0 %collective-permute-start.42 = (bf16[3072,128]{1,0:T(8,128)(2,1)S(1)}, bf16[3072,128]{1,0:T(8,128)(2,1)S(1)}, u32[]{:S(2)}, u32[]{:S(2)}) collective-permute-start(bf16[3072,128]{1,0:T(8,128)(2,1)S(1)} %constant_dynamic-update-slice_fusion.15.refs_4_), channel_id=1, source_target_pairs={{0,6},{1,7},{2,4},{3,5},{4,2},{5,3},{6,0},{7,1},{8,14},{9,15},{10,... | collective-permute-start | bytes 2359304 | tf_op jit(solution)/shard_map/ppermute | solution.py:31
  226.0 21.9 %collective-permute-start.43 = (bf16[3072,128]{1,0:T(8,128)(2,1)S(1)}, bf16[3072,128]{1,0:T(8,128)(2,1)S(1)}, u32[]{:S(2)}, u32[]{:S(2)}) collective-permute-start(bf16[3072,128]{1,0:T(8,128)(2,1)S(1)} %constant_dynamic-update-slice_fusion.15.refs_4_), channel_id=1, source_target_pairs={{0,1},{1,0},{2,3},{3,2},{4,5},{5,4},{6,7},{7,6},{8,9},{9,8},{10,11... | collective-permute-start | bytes 2359304 | tf_op jit(solution)/shard_map/ppermute | solution.py:31
  228.1 28.9 %collective-permute-start.44 = (bf16[3072,128]{1,0:T(8,128)(2,1)S(1)}, bf16[3072,128]{1,0:T(8,128)(2,1)S(1)}, u32[]{:S(2)}, u32[]{:S(2)}) collective-permute-start(bf16[3072,128]{1,0:T(8,128)(2,1)S(1)} %collective-permute-done.42.refs_5_), channel_id=1, source_target_pairs={{0,1},{1,0},{2,3},{3,2},{4,5},{5,4},{6,7},{7,6},{8,9},{9,8},{10,11... | collective-permute-start | bytes 2359304 | tf_op jit(solution)/shard_map/ppermute | solution.py:31
  231.3 10.7 %collective-permute-start.35 = (bf16[1152,128]{1,0:T(8,128)(2,1)S(1)}, bf16[1152,128]{1,0:T(8,128)(2,1)S(1)}, u32[]{:S(2)}, u32[]{:S(2)}) collective-permute-start(bf16[1152,128]{1,0:T(8,128)(2,1)S(1)} %pad_maximum_fusion.4.refs_0_), channel_id=1, source_target_pairs={{0,448},{32,480},{64,128},{96,160},{128,64},{160,96},{192,256},{22... | collective-permute-start | bytes 884744 | tf_op jit(solution)/shard_map/ppermute | solution.py:35
  243.9 13.1 %collective-permute-start.37 = (bf16[1152,128]{1,0:T(8,128)(2,1)S(1)}, bf16[1152,128]{1,0:T(8,128)(2,1)S(1)}, u32[]{:S(2)}, u32[]{:S(2)}) collective-permute-start(bf16[1152,128]{1,0:T(8,128)(2,1)S(1)} %collective-permute-done.35.refs_1_), channel_id=1, source_target_pairs={{0,128},{32,160},{64,448},{96,480},{128,256},{160,288},{192,64},{2... | collective-permute-start | bytes 884744 | tf_op jit(solution)/shard_map/ppermute | solution.py:35
  (22 other events, 333.4 us)

commit v3 on v2

--- a/solution.py
+++ b/solution.py
@@ -49,6 +49,19 @@
     return over_tensor(value, lambda z, x, c: (z, x, c ^ 1))
 
 
+def in_first_segment(value, move):
+    pairs = [(t_index(*p), t_index(*move(*p))) for p in all_t()]
+    return lax.ppermute(value, ("segment", "tensor"), pairs)
+
+
+def first_segment_gather(value):
+    two = stack(value, in_first_segment(value, lambda z, x, c: (z ^ 1, x, c)))
+    four = stack(two, in_first_segment(two, lambda z, x, c: (z ^ 3, x, c)))
+    near = stack(four, in_first_segment(four, lambda z, x, c: (z, x ^ 1, c)))
+    far = in_first_segment(near, lambda z, x, c: (z, x ^ 3, c))
+    return near, far, *[in_first_segment(v, lambda z, x, c: (z, x, c ^ 1)) for v in (near, far)]
+
+
 def zl_swap(value):
     return lax.ppermute(value, "segment", [(i, i ^ 1) for i in range(16)])
 
@@ -80,27 +93,8 @@
     return stack(value, *[z_swap(value, mask) for mask in MASKS[1:]])
 
 
-def z_pairs(value):
-    two = stack(value, z_swap(value, 1))
-    return stack(two, z_swap(two, 3))
-
-
-def x_and_core(value):
-    near = stack(value, x_swap(value, 1))
-    far = x_swap(near, 3)
-    return near, far, core_swap(near), core_swap(far)
-
-
 def other_neighbour(y):
     return y - 1 if y % 2 == 0 else y + 1
-
-
-def y_gather(value):
-    pair = stack(value, over_y(value, lambda y: y ^ 1))
-    second = over_y(pair, other_neighbour)
-    third = over_y(second, lambda y: y ^ 1)
-    fourth = over_y(second, lambda y: y + 2 if y % 2 == 0 else y - 2)
-    return pair, second, third, fourth
 
 
 def y_labels(y):
@@ -243,6 +237,10 @@
     )(where, *diffs, *parts)
 
 
+def together(*values):
+    return lax.optimization_barrier(values)
+
+
 def on_device(entering, fresh_rows, norm_gain, segment_weight, projection, teacher_rows):
     t, segment = lax.axis_index("tensor"), lax.axis_index("segment")
     where = jnp.stack([t & 1, segment, t >> 3, (t >> 1) & 3]).astype(jnp.int32)
@@ -251,23 +249,55 @@
     entering_t, fresh_t = entering[0].T, fresh_rows[0].T
 
     mine_block = projection.T
-    blocks = y_gather(stack(mine_block, zl_swap(mine_block)))
-    taught = (to_next_segment(teacher[0], 0), teacher[1])
-
-    out0 = tick(where, x_and_core(z_direct(entering_t)), weights, entering_t)
+    unit = stack(mine_block, zl_swap(mine_block))
+
+    both_z = z_direct(entering_t)
+    both_z, unit, teacher0 = together(both_z, unit, teacher[0])
+    unit_a = over_y(unit, lambda y: y ^ 1)
+    near = stack(both_z, x_swap(both_z, 1))
+    taught0 = to_next_segment(teacher0, 0)
+    near, unit_a, fresh_t = together(near, unit_a, fresh_t)
+    pair = stack(unit, unit_a)
+    far = x_swap(near, 3)
+    second = over_y(pair, other_neighbour)
+    parts = near, far, core_swap(near), core_swap(far)
+    out0 = tick(where, parts, weights, entering_t)
+    out0, taught0 = together(out0, taught0)
 
     moved = [to_next_segment(out0, mask) for mask in MASKS]
-    earlier = x_and_core(stack(*moved))
-    fresh = x_and_core(z_pairs(fresh_t))
+    earlier_z = stack(*moved)
+    earlier_z, second = together(earlier_z, second)
+    near = stack(earlier_z, x_swap(earlier_z, 1))
+    third = over_y(second, lambda y: y ^ 1)
+    fourth = over_y(second, lambda y: y + 2 if y % 2 == 0 else y - 2)
+    blocks = pair, second, third, fourth
+    far = x_swap(near, 3)
+    earlier = near, far, core_swap(near), core_swap(far)
+    fresh = first_segment_gather(fresh_t)
     mine = jnp.where(segment == 0, fresh_t, moved[0])
     out1 = tick(where, earlier + fresh, weights, mine)
 
     turned = transposition(stack(moved[0], out1))
-    later = x_and_core(z_direct(out1))
-    difference = predict(where, earlier + later, blocks, taught)
-
-    rows = x_and_core(z_pairs(turned))
-    keep, send = gradient(where, y_gather(difference), rows)
+    later_z = z_direct(out1)
+    near = stack(later_z, x_swap(later_z, 1))
+    near, turned = together(near, turned)
+    far = x_swap(near, 3)
+    two = stack(turned, z_swap(turned, 1))
+    far, two = together(far, two)
+    later = near, far, core_swap(near), core_swap(far)
+    rows_z = stack(two, z_swap(two, 3))
+    difference = predict(where, earlier + later, blocks, (taught0, teacher[1]))
+
+    rows_z, _ = together(rows_z, difference)
+    pair = stack(difference, over_y(difference, lambda y: y ^ 1))
+    near = stack(rows_z, x_swap(rows_z, 1))
+    near, _ = together(near, pair)
+    second = over_y(pair, other_neighbour)
+    far = x_swap(near, 3)
+    third = over_y(second, lambda y: y ^ 1)
+    fourth = over_y(second, lambda y: y + 2 if y % 2 == 0 else y - 2)
+    rows = near, far, core_swap(near), core_swap(together(far, second)[0])
+    keep, send = gradient(where, (pair, second, third, fourth), rows)
     total = keep + zl_swap(send).astype(jnp.float32)
     return (out1.T[None], total.T)
 

time: 272 us -> 270 us (level)
  waiting for transfers between devices: 53.1 us -> 71.7 us
  starting transfers between devices: 190 us -> 175 us
  other arithmetic: 10.1 us -> 5.77 us
    ppermute x30 -> x24, starting transfers between devices: 141 us -> 114 us  [over_tensor(): lax.ppermute(value, 'tensor', [(t_index(*p), t_index(*move(*p))) for p in...]
    ppermute x0 -> x6, starting transfers between devices: none -> 24.6 us  [in_first_segment(): return lax.ppermute(value, ('segment', 'tensor'), pairs)]
    ppermute x5, starting transfers between devices: 17.5 us -> 11 us  [to_next_segment(): return lax.ppermute(value, ('segment', 'tensor'), pairs)]
    ppermute x30 -> x24, waiting for transfers between devices: 22.1 us -> 27.7 us  [over_tensor(): lax.ppermute(value, 'tensor', [(t_index(*p), t_index(*move(*p))) for p in...]
    concatenate x12, other arithmetic: 8.69 us -> 3.6 us  [stack(): return jnp.concatenate(values, axis=0)]
    ppermute x8, starting transfers between devices: 23.9 us -> 18.8 us  [over_y(): lax.ppermute(value, 'segment', [(y * 2 + zl, move(y) % NY * 2 + zl) for y...]
    ppermute x2, waiting for transfers between devices: 3.31 us -> 8.05 us  [zl_swap(): return lax.ppermute(value, 'segment', [(i, i ^ 1) for i in range(16)])]
    ppermute x8, waiting for transfers between devices: 18.4 us -> 22.9 us  [over_y(): lax.ppermute(value, 'segment', [(y * 2 + zl, move(y) % NY * 2 + zl) for y...]
  transfers between devices with their start and end apart: 46 -> 46, of which waited for: 15 -> 19; matrix products, arithmetic and copies ran while one was open for 4% -> 3% of each run, Pallas kernels for 3% -> 2%
where the time goes in v3:
time: 270 us; the launch traced here: 268 us
  starting transfers between devices  175 us (65%)
  waiting for transfers between devices  71.7 us (27%)
  Pallas kernels  9.81 us (4%)
  other arithmetic  5.77 us (2%)
  local copies, waits for them, and re-layouts  4.06 us (2%)
    ppermute x24, starting transfers between devices, over_tensor(): lax.ppermute(value, 'tensor', [(t_index(*p), t_index(*move(*p))) for p in...  114 us
    ppermute x24, waiting for transfers between devices, over_tensor(): lax.ppermute(value, 'tensor', [(t_index(*p), t_index(*move(*p))) for p in...  27.7 us
    ppermute x6, starting transfers between devices, in_first_segment(): return lax.ppermute(value, ('segment', 'tensor'), pairs)  24.6 us
    ppermute x8, waiting for transfers between devices, over_y(): lax.ppermute(value, 'segment', [(y * 2 + zl, move(y) % NY * 2 + zl) for y...  22.9 us
    ppermute x8, starting transfers between devices, over_y(): lax.ppermute(value, 'segment', [(y * 2 + zl, move(y) % NY * 2 + zl) for y...  18.8 us
    ppermute x5, waiting for transfers between devices, to_next_segment(): return lax.ppermute(value, ('segment', 'tensor'), pairs)  12.9 us
    ppermute x5, starting transfers between devices, to_next_segment(): return lax.ppermute(value, ('segment', 'tensor'), pairs)  11 us
    ppermute x2, waiting for transfers between devices, zl_swap(): return lax.ppermute(value, 'segment', [(i, i ^ 1) for i in range(16)])  8.05 us
  transfers between devices with their start and end apart: 46, of which 19 were waited for; matrix products, arithmetic and copies ran while one was open for 3% of the time, Pallas kernels for 2%

profile of v3, /device:TPU:1, one launch (start us, length us, event | category | flops | bytes accessed | tf_op | source)
XLA Modules:
  0.0 267.7 jit_solution(12640239433295578308)
XLA Ops:
  0.6 11.6 %collective-permute-start.2 = (bf16[192,128]{1,0:T(8,128)(2,1)}, bf16[192,128]{1,0:T(8,128)(2,1)S(1)}, u32[]{:S(2)}, u32[]{:S(2)}) collective-permute-start(bf16[192,128]{1,0:T(8,128)(2,1)} %bitcast.27), channel_id=1, source_target_pairs={{0,16},{1,17},{2,18},{3,19},{4,20},{5,21},{6,22},{7,23},{8,24},{9,... | collective-permute-start | bytes 147464 | tf_op jit(solution)/shard_map/ppermute | solution.py:31
  14.2 4.0 %collective-permute-start = (bf16[192,128]{1,0:T(8,128)(2,1)}, bf16[192,128]{1,0:T(8,128)(2,1)S(1)}, u32[]{:S(2)}, u32[]{:S(2)}) collective-permute-start(bf16[192,128]{1,0:T(8,128)(2,1)} %bitcast.29), channel_id=1, source_target_pairs={{0,8},{1,9},{2,10},{3,11},{4,12},{5,13},{6,14},{7,15},{8,0},{9,1},... | collective-permute-start | bytes 147464 | tf_op jit(solution)/shard_map/ppermute | solution.py:31
  26.5 3.7 %collective-permute-start.5 = (bf16[576,384]{1,0:T(8,128)(2,1)S(1)}, bf16[576,384]{1,0:T(8,128)(2,1)}, u32[]{:S(2)}, u32[]{:S(2)}) collective-permute-start(bf16[576,384]{1,0:T(8,128)(2,1)S(1)} %pad_maximum_fusion.1), channel_id=1, source_target_pairs={{0,64},{32,96},{64,0},{96,32},{128,192},{160,224},{192,128},{224,1... | collective-permute-start | bytes 1327112 | tf_op jit(solution)/shard_map/ppermute | solution.py:35
  33.3 3.7 %collective-permute-done.4 = bf16[768,128]{1,0:T(8,128)(2,1)S(1)} collective-permute-done((bf16[768,128]{1,0:T(8,128)(2,1)S(1)}, bf16[768,128]{1,0:T(8,128)(2,1)S(1)}, u32[]{:S(2)}, u32[]{:S(2)}) %collective-permute-start.4) | collective-permute-done | bytes 196640 | tf_op jit(solution)/shard_map/ppermute | solution.py:31
  38.2 4.7 %collective-permute-start.6 = (bf16[1536,128]{1,0:T(8,128)(2,1)S(1)}, bf16[1536,128]{1,0:T(8,128)(2,1)S(1)}, u32[]{:S(2)}, u32[]{:S(2)}) collective-permute-start(bf16[1536,128]{1,0:T(8,128)(2,1)S(1)} %pad_maximum_fusion.2.refs_0_), channel_id=1, source_target_pairs={{0,6},{1,7},{2,4},{3,5},{4,2},{5,3},{6,0},{7,1},{8,14},{9,15},{10,... | collective-permute-start | bytes 1179656 | tf_op jit(solution)/shard_map/ppermute | solution.py:31
  44.2 5.3 %collective-permute-start.7 = (bf16[1536,128]{1,0:T(8,128)(2,1)S(1)}, bf16[1536,128]{1,0:T(8,128)(2,1)S(1)}, u32[]{:S(2)}, u32[]{:S(2)}) collective-permute-start(bf16[1536,128]{1,0:T(8,128)(2,1)S(1)} %pad_maximum_fusion.2.refs_0_), channel_id=1, source_target_pairs={{0,1},{1,0},{2,3},{3,2},{4,5},{5,4},{6,7},{7,6},{8,9},{9,8},{10,11... | collective-permute-start | bytes 1179656 | tf_op jit(solution)/shard_map/ppermute | solution.py:31
  49.5 5.4 %collective-permute-start.8 = (bf16[1536,128]{1,0:T(8,128)(2,1)S(1)}, bf16[1536,128]{1,0:T(8,128)(2,1)S(1)}, u32[]{:S(2)}, u32[]{:S(2)}) collective-permute-start(bf16[1536,128]{1,0:T(8,128)(2,1)S(1)} %collective-permute-done.6.refs_1_), channel_id=1, source_target_pairs={{0,1},{1,0},{2,3},{3,2},{4,5},{5,4},{6,7},{7,6},{8,9},{9,8},{10,11... | collective-permute-start | bytes 1179656 | tf_op jit(solution)/shard_map/ppermute | solution.py:31
  55.9 3.3 %collective-permute-start.9 = (bf16[288,128]{1,0:T(8,128)(2,1)S(1)}, bf16[288,128]{1,0:T(8,128)(2,1)S(1)}, u32[]{:S(2)}, u32[]{:S(2)}) collective-permute-start(bf16[288,128]{1,0:T(8,128)(2,1)S(1)} %get-tuple-element.24), channel_id=1, source_target_pairs={{0,32},{1,33},{2,34},{3,35},{4,36},{5,37},{6,38},{7,39},{8,40},{9,... | collective-permute-start | bytes 221192 | tf_op jit(solution)/shard_map/ppermute | solution.py:74
  59.2 3.8 %collective-permute-start.19 = (bf16[192,128]{1,0:T(8,128)(2,1)S(1)}, bf16[192,128]{1,0:T(8,128)(2,1)S(1)}, u32[]{:S(2)}, u32[]{:S(2)}) collective-permute-start(bf16[192,128]{1,0:T(8,128)(2,1)S(1)} %bitcast.33), channel_id=1, source_target_pairs={{0,8},{1,9},{2,10},{3,11},{4,12},{5,13},{6,14},{7,15},{8,0},{9,1},... | collective-permute-start | bytes 147464 | tf_op jit(solution)/shard_map/ppermute | solution.py:54
  66.1 4.9 %collective-permute-start.20 = (bf16[384,128]{1,0:T(8,128)(2,1)S(1)}, bf16[384,128]{1,0:T(8,128)(2,1)S(1)}, u32[]{:S(2)}, u32[]{:S(2)}) collective-permute-start(bf16[384,128]{1,0:T(8,128)(2,1)S(1)} %pad_maximum_fusion.10), channel_id=1, source_target_pairs={{0,24},{1,25},{2,26},{3,27},{4,28},{5,29},{6,30},{7,31},{8,16},{9,... | collective-permute-start | bytes 294920 | tf_op jit(solution)/shard_map/ppermute | solution.py:54
  80.6 6.2 %collective-permute-done.10 = bf16[192,128]{1,0:T(8,128)(2,1)S(1)} collective-permute-done((bf16[192,128]{1,0:T(8,128)(2,1)S(1)}, bf16[192,128]{1,0:T(8,128)(2,1)S(1)}, u32[]{:S(2)}, u32[]{:S(2)}) %collective-permute-start.10) | collective-permute-done | bytes 49184 | tf_op jit(solution)/shard_map/ppermute | solution.py:74
  91.7 3.8 %collective-permute-done.11 = bf16[192,128]{1,0:T(8,128)(2,1)S(1)} collective-permute-done((bf16[192,128]{1,0:T(8,128)(2,1)S(1)}, bf16[192,128]{1,0:T(8,128)(2,1)S(1)}, u32[]{:S(2)}, u32[]{:S(2)}) %collective-permute-start.11) | collective-permute-done | bytes 49184 | tf_op jit(solution)/shard_map/ppermute | solution.py:74
  97.5 4.4 %collective-permute-start.22 = (bf16[1536,128]{1,0:T(8,128)(2,1)S(1)}, bf16[1536,128]{1,0:T(8,128)(2,1)S(1)}, u32[]{:S(2)}, u32[]{:S(2)}) collective-permute-start(bf16[1536,128]{1,0:T(8,128)(2,1)S(1)} %constant_dynamic-update-slice_fusion.4.refs_4_), channel_id=1, source_target_pairs={{0,6},{1,7},{2,4},{3,5},{4,2},{5,3},{6,0},{7,1},{8,14},{9,15},{10,... | collective-permute-start | bytes 1179656 | tf_op jit(solution)/shard_map/ppermute | solution.py:54
  102.0 4.4 %collective-permute-start.16 = (bf16[1536,128]{1,0:T(8,128)(2,1)S(1)}, bf16[1536,128]{1,0:T(8,128)(2,1)S(1)}, u32[]{:S(2)}, u32[]{:S(2)}) collective-permute-start(bf16[1536,128]{1,0:T(8,128)(2,1)S(1)} %constant_dynamic-update-slice_fusion.2.refs_0_), channel_id=1, source_target_pairs={{0,6},{1,7},{2,4},{3,5},{4,2},{5,3},{6,0},{7,1},{8,14},{9,15},{10,... | collective-permute-start | bytes 1179656 | tf_op jit(solution)/shard_map/ppermute | solution.py:31
  106.4 6.6 %collective-permute-start.23 = (bf16[1536,128]{1,0:T(8,128)(2,1)S(1)}, bf16[1536,128]{1,0:T(8,128)(2,1)S(1)}, u32[]{:S(2)}, u32[]{:S(2)}) collective-permute-start(bf16[1536,128]{1,0:T(8,128)(2,1)S(1)} %constant_dynamic-update-slice_fusion.4.refs_4_), channel_id=1, source_target_pairs={{0,1},{1,0},{2,3},{3,2},{4,5},{5,4},{6,7},{7,6},{8,9},{9,8},{10,11... | collective-permute-start | bytes 1179656 | tf_op jit(solution)/shard_map/ppermute | solution.py:54
  117.9 4.5 %collective-permute-start.18 = (bf16[1536,128]{1,0:T(8,128)(2,1)S(1)}, bf16[1536,128]{1,0:T(8,128)(2,1)S(1)}, u32[]{:S(2)}, u32[]{:S(2)}) collective-permute-start(bf16[1536,128]{1,0:T(8,128)(2,1)S(1)} %collective-permute-done.16.refs_1_), channel_id=1, source_target_pairs={{0,1},{1,0},{2,3},{3,2},{4,5},{5,4},{6,7},{7,6},{8,9},{9,8},{10,11... | collective-permute-start | bytes 1179656 | tf_op jit(solution)/shard_map/ppermute | solution.py:31
  128.8 6.5 %collective-permute-start.27 = (bf16[192,128]{1,0:T(8,128)(2,1)}, bf16[192,128]{1,0:T(8,128)(2,1)S(1)}, u32[]{:S(2)}, u32[]{:S(2)}) collective-permute-start(bf16[192,128]{1,0:T(8,128)(2,1)} %tick.3), channel_id=1, source_target_pairs={{0,16},{1,17},{2,18},{3,19},{4,20},{5,21},{6,22},{7,23},{8,24},{9,... | collective-permute-start | bytes 147464 | tf_op jit(solution)/shard_map/ppermute | solution.py:31
  146.9 4.5 %collective-permute-done.28 = bf16[768,128]{1,0:T(8,128)(2,1)S(1)} collective-permute-done((bf16[768,128]{1,0:T(8,128)(2,1)S(1)}, bf16[768,128]{1,0:T(8,128)(2,1)S(1)}, u32[]{:S(2)}, u32[]{:S(2)}) %collective-permute-start.28) | collective-permute-done | bytes 196640 | tf_op jit(solution)/shard_map/ppermute | solution.py:31
  151.5 21.7 %collective-permute-start.30 = (bf16[1536,128]{1,0:T(8,128)(2,1)S(1)}, bf16[1536,128]{1,0:T(8,128)(2,1)S(1)}, u32[]{:S(2)}, u32[]{:S(2)}) collective-permute-start(bf16[1536,128]{1,0:T(8,128)(2,1)S(1)} %constant_dynamic-update-slice_fusion.8.refs_4_), channel_id=1, source_target_pairs={{0,6},{1,7},{2,4},{3,5},{4,2},{5,3},{6,0},{7,1},{8,14},{9,15},{10,... | collective-permute-start | bytes 1179656 | tf_op jit(solution)/shard_map/ppermute | solution.py:31
  175.1 4.6 %collective-permute-done.31 = bf16[384,128]{1,0:T(8,128)(2,1)S(1)} collective-permute-done((bf16[384,128]{1,0:T(8,128)(2,1)S(1)}, bf16[384,128]{1,0:T(8,128)(2,1)S(1)}, u32[]{:S(2)}, u32[]{:S(2)}) %collective-permute-start.31) | collective-permute-done | bytes 98336 | tf_op jit(solution)/shard_map/ppermute | solution.py:31
  181.9 9.1 %collective-permute-start.40 = (bf16[768,128]{1,0:T(8,128)(2,1)S(1)}, bf16[768,128]{1,0:T(8,128)(2,1)S(1)}, u32[]{:S(2)}, u32[]{:S(2)}) collective-permute-start(bf16[768,128]{1,0:T(8,128)(2,1)S(1)} %pad_maximum_fusion.9), channel_id=1, source_target_pairs={{0,24},{1,25},{2,26},{3,27},{4,28},{5,29},{6,30},{7,31},{8,16},{9,... | collective-permute-start | bytes 589832 | tf_op jit(solution)/shard_map/ppermute | solution.py:31
  191.0 4.0 %collective-permute-start.32 = (bf16[1536,128]{1,0:T(8,128)(2,1)S(1)}, bf16[1536,128]{1,0:T(8,128)(2,1)S(1)}, u32[]{:S(2)}, u32[]{:S(2)}) collective-permute-start(bf16[1536,128]{1,0:T(8,128)(2,1)S(1)} %constant_dynamic-update-slice_fusion.8.refs_4_), channel_id=1, source_target_pairs={{0,1},{1,0},{2,3},{3,2},{4,5},{5,4},{6,7},{7,6},{8,9},{9,8},{10,11... | collective-permute-start | bytes 1179656 | tf_op jit(solution)/shard_map/ppermute | solution.py:31
  205.9 5.0 %collective-permute-done.36 = bf16[576,128]{1,0:T(8,128)(2,1)S(1)} collective-permute-done((bf16[576,128]{1,0:T(8,128)(2,1)S(1)}, bf16[576,128]{1,0:T(8,128)(2,1)S(1)}, u32[]{:S(2)}, u32[]{:S(2)}) %collective-permute-start.36) | collective-permute-done | bytes 147488 | tf_op jit(solution)/shard_map/ppermute | solution.py:35
  210.8 3.4 %collective-permute-done.41 = bf16[1536,128]{1,0:T(8,128)(2,1)S(1)} collective-permute-done((bf16[1536,128]{1,0:T(8,128)(2,1)S(1)}, bf16[1536,128]{1,0:T(8,128)(2,1)S(1)}, u32[]{:S(2)}, u32[]{:S(2)}) %collective-permute-start.41) | collective-permute-done | bytes 393248 | tf_op jit(solution)/shard_map/ppermute | solution.py:31
  214.3 4.1 %collective-permute-start.42 = (bf16[3072,128]{1,0:T(8,128)(2,1)S(1)}, bf16[3072,128]{1,0:T(8,128)(2,1)S(1)}, u32[]{:S(2)}, u32[]{:S(2)}) collective-permute-start(bf16[3072,128]{1,0:T(8,128)(2,1)S(1)} %pad_maximum_fusion.refs_4_), channel_id=1, source_target_pairs={{0,6},{1,7},{2,4},{3,5},{4,2},{5,3},{6,0},{7,1},{8,14},{9,15},{10,... | collective-permute-start | bytes 2359304 | tf_op jit(solution)/shard_map/ppermute | solution.py:31
  223.5 5.3 %collective-permute-done.37.refs_1_ = bf16[1152,128]{1,0:T(8,128)(2,1)S(1)} collective-permute-done((bf16[1152,128]{1,0:T(8,128)(2,1)S(1)}, bf16[1152,128]{1,0:T(8,128)(2,1)S(1)}, u32[]{:S(2)}, u32[]{:S(2)}) %collective-permute-start.37) | collective-permute-done | bytes 294944 | tf_op jit(solution)/shard_map/ppermute | solution.py:35
  228.8 6.7 %collective-permute-done.42.refs_5_ = bf16[3072,128]{1,0:T(8,128)(2,1)S(1)} collective-permute-done((bf16[3072,128]{1,0:T(8,128)(2,1)S(1)}, bf16[3072,128]{1,0:T(8,128)(2,1)S(1)}, u32[]{:S(2)}, u32[]{:S(2)}) %collective-permute-start.42) | collective-permute-done | bytes 786464 | tf_op jit(solution)/shard_map/ppermute | solution.py:31
  235.5 3.8 %collective-permute-start.44 = (bf16[3072,128]{1,0:T(8,128)(2,1)S(1)}, bf16[3072,128]{1,0:T(8,128)(2,1)S(1)}, u32[]{:S(2)}, u32[]{:S(2)}) collective-permute-start(bf16[3072,128]{1,0:T(8,128)(2,1)S(1)} %collective-permute-done.42.refs_5_), channel_id=1, source_target_pairs={{0,1},{1,0},{2,3},{3,2},{4,5},{5,4},{6,7},{7,6},{8,9},{9,8},{10,11... | collective-permute-start | bytes 2359304 | tf_op jit(solution)/shard_map/ppermute | solution.py:31
  241.2 3.6 %collective-permute-start.38 = (bf16[1152,128]{1,0:T(8,128)(2,1)S(1)}, bf16[1152,128]{1,0:T(8,128)(2,1)S(1)}, u32[]{:S(2)}, u32[]{:S(2)}) collective-permute-start(bf16[1152,128]{1,0:T(8,128)(2,1)S(1)} %collective-permute-done.37.refs_1_), channel_id=1, source_target_pairs={{0,64},{32,96},{64,0},{96,32},{128,192},{160,224},{192,128},{224,1... | collective-permute-start | bytes 884744 | tf_op jit(solution)/shard_map/ppermute | solution.py:35
  244.8 7.1 %collective-permute-done.39.refs_3_ = bf16[1152,128]{1,0:T(8,128)(2,1)S(1)} collective-permute-done((bf16[1152,128]{1,0:T(8,128)(2,1)S(1)}, bf16[1152,128]{1,0:T(8,128)(2,1)S(1)}, u32[]{:S(2)}, u32[]{:S(2)}) %collective-permute-start.39) | collective-permute-done | bytes 294944 | tf_op jit(solution)/shard_map/ppermute | solution.py:35
  251.9 4.4 %collective-permute-done.38.refs_2_ = bf16[1152,128]{1,0:T(8,128)(2,1)S(1)} collective-permute-done((bf16[1152,128]{1,0:T(8,128)(2,1)S(1)}, bf16[1152,128]{1,0:T(8,128)(2,1)S(1)}, u32[]{:S(2)}, u32[]{:S(2)}) %collective-permute-start.38) | collective-permute-done | bytes 294944 | tf_op jit(solution)/shard_map/ppermute | solution.py:35
  261.2 5.6 %collective-permute-done.45 = bf16[288,384]{1,0:T(8,128)(2,1)S(1)} collective-permute-done((bf16[288,384]{1,0:T(8,128)(2,1)S(1)}, bf16[288,384]{1,0:T(8,128)(2,1)S(1)}, u32[]{:S(2)}, u32[]{:S(2)}) %collective-permute-start.45) | collective-permute-done | bytes 221216 | tf_op jit(solution)/shard_map/ppermute | solution.py:66
  (103 shorter events, 86.8 us)
Async XLA Ops:
  0.6 21.6 %collective-permute-start.2 = (bf16[192,128]{1,0:T(8,128)(2,1)}, bf16[192,128]{1,0:T(8,128)(2,1)S(1)}, u32[]{:S(2)}, u32[]{:S(2)}) collective-permute-start(bf16[192,128]{1,0:T(8,128)(2,1)} %bitcast.27), channel_id=1, source_target_pairs={{0,16},{1,17},{2,18},{3,19},{4,20},{5,21},{6,22},{7,23},{8,24},{9,... | collective-permute-start | bytes 147464 | tf_op jit(solution)/shard_map/ppermute | solution.py:31
  12.2 10.0 %collective-permute-start.1 = (bf16[192,128]{1,0:T(8,128)(2,1)}, bf16[192,128]{1,0:T(8,128)(2,1)S(1)}, u32[]{:S(2)}, u32[]{:S(2)}) collective-permute-start(bf16[192,128]{1,0:T(8,128)(2,1)} %bitcast.28), channel_id=1, source_target_pairs={{0,24},{1,25},{2,26},{3,27},{4,28},{5,29},{6,30},{7,31},{8,16},{9,... | collective-permute-start | bytes 147464 | tf_op jit(solution)/shard_map/ppermute | solution.py:31
  26.5 11.7 %collective-permute-start.5 = (bf16[576,384]{1,0:T(8,128)(2,1)S(1)}, bf16[576,384]{1,0:T(8,128)(2,1)}, u32[]{:S(2)}, u32[]{:S(2)}) collective-permute-start(bf16[576,384]{1,0:T(8,128)(2,1)S(1)} %pad_maximum_fusion.1), channel_id=1, source_target_pairs={{0,64},{32,96},{64,0},{96,32},{128,192},{160,224},{192,128},{224,1... | collective-permute-start | bytes 1327112 | tf_op jit(solution)/shard_map/ppermute | solution.py:35
  38.2 11.3 %collective-permute-start.6 = (bf16[1536,128]{1,0:T(8,128)(2,1)S(1)}, bf16[1536,128]{1,0:T(8,128)(2,1)S(1)}, u32[]{:S(2)}, u32[]{:S(2)}) collective-permute-start(bf16[1536,128]{1,0:T(8,128)(2,1)S(1)} %pad_maximum_fusion.2.refs_0_), channel_id=1, source_target_pairs={{0,6},{1,7},{2,4},{3,5},{4,2},{5,3},{6,0},{7,1},{8,14},{9,15},{10,... | collective-permute-start | bytes 1179656 | tf_op jit(solution)/shard_map/ppermute | solution.py:31
  44.2 26.9 %collective-permute-start.7 = (bf16[1536,128]{1,0:T(8,128)(2,1)S(1)}, bf16[1536,128]{1,0:T(8,128)(2,1)S(1)}, u32[]{:S(2)}, u32[]{:S(2)}) collective-permute-start(bf16[1536,128]{1,0:T(8,128)(2,1)S(1)} %pad_maximum_fusion.2.refs_0_), channel_id=1, source_target_pairs={{0,1},{1,0},{2,3},{3,2},{4,5},{5,4},{6,7},{7,6},{8,9},{9,8},{10,11... | collective-permute-start | bytes 1179656 | tf_op jit(solution)/shard_map/ppermute | solution.py:31
  49.5 21.6 %collective-permute-start.8 = (bf16[1536,128]{1,0:T(8,128)(2,1)S(1)}, bf16[1536,128]{1,0:T(8,128)(2,1)S(1)}, u32[]{:S(2)}, u32[]{:S(2)}) collective-permute-start(bf16[1536,128]{1,0:T(8,128)(2,1)S(1)} %collective-permute-done.6.refs_1_), channel_id=1, source_target_pairs={{0,1},{1,0},{2,3},{3,2},{4,5},{5,4},{6,7},{7,6},{8,9},{9,8},{10,11... | collective-permute-start | bytes 1179656 | tf_op jit(solution)/shard_map/ppermute | solution.py:31
  55.9 16.9 %collective-permute-start.9 = (bf16[288,128]{1,0:T(8,128)(2,1)S(1)}, bf16[288,128]{1,0:T(8,128)(2,1)S(1)}, u32[]{:S(2)}, u32[]{:S(2)}) collective-permute-start(bf16[288,128]{1,0:T(8,128)(2,1)S(1)} %get-tuple-element.24), channel_id=1, source_target_pairs={{0,32},{1,33},{2,34},{3,35},{4,36},{5,37},{6,38},{7,39},{8,40},{9,... | collective-permute-start | bytes 221192 | tf_op jit(solution)/shard_map/ppermute | solution.py:74
  64.1 31.5 %collective-permute-start.14 = (bf16[1152,384]{1,0:T(8,128)(2,1)S(1)}, bf16[1152,384]{1,0:T(8,128)(2,1)S(1)}, u32[]{:S(2)}, u32[]{:S(2)}) collective-permute-start(bf16[1152,384]{1,0:T(8,128)(2,1)S(1)} %constant_dynamic-update-slice_fusion.refs_8_), channel_id=1, source_target_pairs={{0,448},{32,480},{64,128},{96,160},{128,64},{160,96},{192,256},{22... | collective-permute-start | bytes 2654216 | tf_op jit(solution)/shard_map/ppermute | solution.py:35
  66.1 8.7 %collective-permute-start.20 = (bf16[384,128]{1,0:T(8,128)(2,1)S(1)}, bf16[384,128]{1,0:T(8,128)(2,1)S(1)}, u32[]{:S(2)}, u32[]{:S(2)}) collective-permute-start(bf16[384,128]{1,0:T(8,128)(2,1)S(1)} %pad_maximum_fusion.10), channel_id=1, source_target_pairs={{0,24},{1,25},{2,26},{3,27},{4,28},{5,29},{6,30},{7,31},{8,16},{9,... | collective-permute-start | bytes 294920 | tf_op jit(solution)/shard_map/ppermute | solution.py:54
  72.8 13.9 %collective-permute-start.10 = (bf16[192,128]{1,0:T(8,128)(2,1)S(1)}, bf16[192,128]{1,0:T(8,128)(2,1)S(1)}, u32[]{:S(2)}, u32[]{:S(2)}) collective-permute-start(bf16[192,128]{1,0:T(8,128)(2,1)S(1)} %tick.2), channel_id=1, source_target_pairs={{0,32},{1,33},{2,34},{3,35},{4,36},{5,37},{6,38},{7,39},{8,40},{9,... | collective-permute-start | bytes 147464 | tf_op jit(solution)/shard_map/ppermute | solution.py:74
  74.8 22.7 %collective-permute-start.21 = (bf16[768,128]{1,0:T(8,128)(2,1)S(1)}, bf16[768,128]{1,0:T(8,128)(2,1)S(1)}, u32[]{:S(2)}, u32[]{:S(2)}) collective-permute-start(bf16[768,128]{1,0:T(8,128)(2,1)S(1)} %pad_maximum_fusion.7), channel_id=1, source_target_pairs={{0,2},{1,3},{2,0},{3,1},{4,6},{5,7},{6,4},{7,5},{8,10},{9,11},{10,... | collective-permute-start | bytes 589832 | tf_op jit(solution)/shard_map/ppermute | solution.py:54
  76.7 15.0 %collective-permute-start.13 = (bf16[192,128]{1,0:T(8,128)(2,1)S(1)}, bf16[192,128]{1,0:T(8,128)(2,1)S(1)}, u32[]{:S(2)}, u32[]{:S(2)}) collective-permute-start(bf16[192,128]{1,0:T(8,128)(2,1)S(1)} %tick.2), channel_id=1, source_target_pairs={{0,48},{1,49},{2,50},{3,51},{4,52},{5,53},{6,54},{7,55},{8,56},{9,... | collective-permute-start | bytes 147464 | tf_op jit(solution)/shard_map/ppermute | solution.py:74
  78.7 13.1 %collective-permute-start.12 = (bf16[192,128]{1,0:T(8,128)(2,1)S(1)}, bf16[192,128]{1,0:T(8,128)(2,1)S(1)}, u32[]{:S(2)}, u32[]{:S(2)}) collective-permute-start(bf16[192,128]{1,0:T(8,128)(2,1)S(1)} %tick.2), channel_id=1, source_target_pairs={{0,56},{1,57},{2,58},{3,59},{4,60},{5,61},{6,62},{7,63},{8,48},{9,... | collective-permute-start | bytes 147464 | tf_op jit(solution)/shard_map/ppermute | solution.py:74
  86.8 8.7 %collective-permute-start.11 = (bf16[192,128]{1,0:T(8,128)(2,1)S(1)}, bf16[192,128]{1,0:T(8,128)(2,1)S(1)}, u32[]{:S(2)}, u32[]{:S(2)}) collective-permute-start(bf16[192,128]{1,0:T(8,128)(2,1)S(1)} %tick.2), channel_id=1, source_target_pairs={{0,40},{1,41},{2,42},{3,43},{4,44},{5,45},{6,46},{7,47},{8,32},{9,... | collective-permute-start | bytes 147464 | tf_op jit(solution)/shard_map/ppermute | solution.py:74
  97.5 17.4 %collective-permute-start.22 = (bf16[1536,128]{1,0:T(8,128)(2,1)S(1)}, bf16[1536,128]{1,0:T(8,128)(2,1)S(1)}, u32[]{:S(2)}, u32[]{:S(2)}) collective-permute-start(bf16[1536,128]{1,0:T(8,128)(2,1)S(1)} %constant_dynamic-update-slice_fusion.4.refs_4_), channel_id=1, source_target_pairs={{0,6},{1,7},{2,4},{3,5},{4,2},{5,3},{6,0},{7,1},{8,14},{9,15},{10,... | collective-permute-start | bytes 1179656 | tf_op jit(solution)/shard_map/ppermute | solution.py:54
  102.0 15.9 %collective-permute-start.16 = (bf16[1536,128]{1,0:T(8,128)(2,1)S(1)}, bf16[1536,128]{1,0:T(8,128)(2,1)S(1)}, u32[]{:S(2)}, u32[]{:S(2)}) collective-permute-start(bf16[1536,128]{1,0:T(8,128)(2,1)S(1)} %constant_dynamic-update-slice_fusion.2.refs_0_), channel_id=1, source_target_pairs={{0,6},{1,7},{2,4},{3,5},{4,2},{5,3},{6,0},{7,1},{8,14},{9,15},{10,... | collective-permute-start | bytes 1179656 | tf_op jit(solution)/shard_map/ppermute | solution.py:31
  106.4 18.0 %collective-permute-start.23 = (bf16[1536,128]{1,0:T(8,128)(2,1)S(1)}, bf16[1536,128]{1,0:T(8,128)(2,1)S(1)}, u32[]{:S(2)}, u32[]{:S(2)}) collective-permute-start(bf16[1536,128]{1,0:T(8,128)(2,1)S(1)} %constant_dynamic-update-slice_fusion.4.refs_4_), channel_id=1, source_target_pairs={{0,1},{1,0},{2,3},{3,2},{4,5},{5,4},{6,7},{7,6},{8,9},{9,8},{10,11... | collective-permute-start | bytes 1179656 | tf_op jit(solution)/shard_map/ppermute | solution.py:54
  113.0 13.4 %collective-permute-start.17 = (bf16[1536,128]{1,0:T(8,128)(2,1)S(1)}, bf16[1536,128]{1,0:T(8,128)(2,1)S(1)}, u32[]{:S(2)}, u32[]{:S(2)}) collective-permute-start(bf16[1536,128]{1,0:T(8,128)(2,1)S(1)} %constant_dynamic-update-slice_fusion.2.refs_0_), channel_id=1, source_target_pairs={{0,1},{1,0},{2,3},{3,2},{4,5},{5,4},{6,7},{7,6},{8,9},{9,8},{10,11... | collective-permute-start | bytes 1179656 | tf_op jit(solution)/shard_map/ppermute | solution.py:31
  114.9 11.4 %collective-permute-start.24 = (bf16[1536,128]{1,0:T(8,128)(2,1)S(1)}, bf16[1536,128]{1,0:T(8,128)(2,1)S(1)}, u32[]{:S(2)}, u32[]{:S(2)}) collective-permute-start(bf16[1536,128]{1,0:T(8,128)(2,1)S(1)} %collective-permute-done.22.refs_5_), channel_id=1, source_target_pairs={{0,1},{1,0},{2,3},{3,2},{4,5},{5,4},{6,7},{7,6},{8,9},{9,8},{10,11... | collective-permute-start | bytes 1179656 | tf_op jit(solution)/shard_map/ppermute | solution.py:54
  122.5 74.5 %collective-permute-start.35 = (bf16[1152,384]{1,0:T(8,128)(2,1)S(1)}, bf16[1152,384]{1,0:T(8,128)(2,1)S(1)}, u32[]{:S(2)}, u32[]{:S(2)}) collective-permute-start(bf16[1152,384]{1,0:T(8,128)(2,1)S(1)} %collective-permute-done.14.refs_9_), channel_id=1, source_target_pairs={{0,128},{32,160},{64,448},{96,480},{128,256},{160,288},{192,64},{2... | collective-permute-start | bytes 2654216 | tf_op jit(solution)/shard_map/ppermute | solution.py:35
  124.4 72.6 %collective-permute-start.34 = (bf16[1152,384]{1,0:T(8,128)(2,1)S(1)}, bf16[1152,384]{1,0:T(8,128)(2,1)S(1)}, u32[]{:S(2)}, u32[]{:S(2)}) collective-permute-start(bf16[1152,384]{1,0:T(8,128)(2,1)S(1)} %collective-permute-done.14.refs_9_), channel_id=1, source_target_pairs={{0,64},{32,96},{64,0},{96,32},{128,192},{160,224},{192,128},{224,1... | collective-permute-start | bytes 2654216 | tf_op jit(solution)/shard_map/ppermute | solution.py:35
  128.8 13.0 %collective-permute-start.27 = (bf16[192,128]{1,0:T(8,128)(2,1)}, bf16[192,128]{1,0:T(8,128)(2,1)S(1)}, u32[]{:S(2)}, u32[]{:S(2)}) collective-permute-start(bf16[192,128]{1,0:T(8,128)(2,1)} %tick.3), channel_id=1, source_target_pairs={{0,16},{1,17},{2,18},{3,19},{4,20},{5,21},{6,22},{7,23},{8,24},{9,... | collective-permute-start | bytes 147464 | tf_op jit(solution)/shard_map/ppermute | solution.py:31
  141.9 9.6 %collective-permute-start.29 = (bf16[384,128]{1,0:T(8,128)(2,1)S(1)}, bf16[384,128]{1,0:T(8,128)(2,1)S(1)}, u32[]{:S(2)}, u32[]{:S(2)}) collective-permute-start(bf16[384,128]{1,0:T(8,128)(2,1)S(1)} %pad_maximum_fusion.11), channel_id=1, source_target_pairs={{0,0},{1,1},{2,2},{3,3},{4,64},{5,65},{6,66},{7,67},{8,128},{9,129... | collective-permute-start | bytes 294920 | tf_op jit(solution)/shard_map/ppermute | solution.py:85
  151.5 30.5 %collective-permute-start.30 = (bf16[1536,128]{1,0:T(8,128)(2,1)S(1)}, bf16[1536,128]{1,0:T(8,128)(2,1)S(1)}, u32[]{:S(2)}, u32[]{:S(2)}) collective-permute-start(bf16[1536,128]{1,0:T(8,128)(2,1)S(1)} %constant_dynamic-update-slice_fusion.8.refs_4_), channel_id=1, source_target_pairs={{0,6},{1,7},{2,4},{3,5},{4,2},{5,3},{6,0},{7,1},{8,14},{9,15},{10,... | collective-permute-start | bytes 1179656 | tf_op jit(solution)/shard_map/ppermute | solution.py:31
  181.9 15.0 %collective-permute-start.40 = (bf16[768,128]{1,0:T(8,128)(2,1)S(1)}, bf16[768,128]{1,0:T(8,128)(2,1)S(1)}, u32[]{:S(2)}, u32[]{:S(2)}) collective-permute-start(bf16[768,128]{1,0:T(8,128)(2,1)S(1)} %pad_maximum_fusion.9), channel_id=1, source_target_pairs={{0,24},{1,25},{2,26},{3,27},{4,28},{5,29},{6,30},{7,31},{8,16},{9,... | collective-permute-start | bytes 589832 | tf_op jit(solution)/shard_map/ppermute | solution.py:31
  201.8 12.5 %collective-permute-start.41 = (bf16[1536,128]{1,0:T(8,128)(2,1)S(1)}, bf16[1536,128]{1,0:T(8,128)(2,1)S(1)}, u32[]{:S(2)}, u32[]{:S(2)}) collective-permute-start(bf16[1536,128]{1,0:T(8,128)(2,1)S(1)} %pad_maximum_fusion.3), channel_id=1, source_target_pairs={{0,2},{1,3},{2,0},{3,1},{4,6},{5,7},{6,4},{7,5},{8,10},{9,11},{10,... | collective-permute-start | bytes 1179656 | tf_op jit(solution)/shard_map/ppermute | solution.py:31
  214.3 21.2 %collective-permute-start.42 = (bf16[3072,128]{1,0:T(8,128)(2,1)S(1)}, bf16[3072,128]{1,0:T(8,128)(2,1)S(1)}, u32[]{:S(2)}, u32[]{:S(2)}) collective-permute-start(bf16[3072,128]{1,0:T(8,128)(2,1)S(1)} %pad_maximum_fusion.refs_4_), channel_id=1, source_target_pairs={{0,6},{1,7},{2,4},{3,5},{4,2},{5,3},{6,0},{7,1},{8,14},{9,15},{10,... | collective-permute-start | bytes 2359304 | tf_op jit(solution)/shard_map/ppermute | solution.py:31
  218.4 10.4 %collective-permute-start.37 = (bf16[1152,128]{1,0:T(8,128)(2,1)S(1)}, bf16[1152,128]{1,0:T(8,128)(2,1)S(1)}, u32[]{:S(2)}, u32[]{:S(2)}) collective-permute-start(bf16[1152,128]{1,0:T(8,128)(2,1)S(1)} %pad_maximum_fusion.4.refs_0_), channel_id=1, source_target_pairs={{0,448},{32,480},{64,128},{96,160},{128,64},{160,96},{192,256},{22... | collective-permute-start | bytes 884744 | tf_op jit(solution)/shard_map/ppermute | solution.py:35
  220.4 36.0 %collective-permute-start.43 = (bf16[3072,128]{1,0:T(8,128)(2,1)S(1)}, bf16[3072,128]{1,0:T(8,128)(2,1)S(1)}, u32[]{:S(2)}, u32[]{:S(2)}) collective-permute-start(bf16[3072,128]{1,0:T(8,128)(2,1)S(1)} %pad_maximum_fusion.refs_4_), channel_id=1, source_target_pairs={{0,1},{1,0},{2,3},{3,2},{4,5},{5,4},{6,7},{7,6},{8,9},{9,8},{10,11... | collective-permute-start | bytes 2359304 | tf_op jit(solution)/shard_map/ppermute | solution.py:31
  235.5 20.8 %collective-permute-start.44 = (bf16[3072,128]{1,0:T(8,128)(2,1)S(1)}, bf16[3072,128]{1,0:T(8,128)(2,1)S(1)}, u32[]{:S(2)}, u32[]{:S(2)}) collective-permute-start(bf16[3072,128]{1,0:T(8,128)(2,1)S(1)} %collective-permute-done.42.refs_5_), channel_id=1, source_target_pairs={{0,1},{1,0},{2,3},{3,2},{4,5},{5,4},{6,7},{7,6},{8,9},{9,8},{10,11... | collective-permute-start | bytes 2359304 | tf_op jit(solution)/shard_map/ppermute | solution.py:31
  239.3 12.6 %collective-permute-start.39 = (bf16[1152,128]{1,0:T(8,128)(2,1)S(1)}, bf16[1152,128]{1,0:T(8,128)(2,1)S(1)}, u32[]{:S(2)}, u32[]{:S(2)}) collective-permute-start(bf16[1152,128]{1,0:T(8,128)(2,1)S(1)} %collective-permute-done.37.refs_1_), channel_id=1, source_target_pairs={{0,128},{32,160},{64,448},{96,480},{128,256},{160,288},{192,64},{2... | collective-permute-start | bytes 884744 | tf_op jit(solution)/shard_map/ppermute | solution.py:35
  241.2 15.1 %collective-permute-start.38 = (bf16[1152,128]{1,0:T(8,128)(2,1)S(1)}, bf16[1152,128]{1,0:T(8,128)(2,1)S(1)}, u32[]{:S(2)}, u32[]{:S(2)}) collective-permute-start(bf16[1152,128]{1,0:T(8,128)(2,1)S(1)} %collective-permute-done.37.refs_1_), channel_id=1, source_target_pairs={{0,64},{32,96},{64,0},{96,32},{128,192},{160,224},{192,128},{224,1... | collective-permute-start | bytes 884744 | tf_op jit(solution)/shard_map/ppermute | solution.py:35
  (19 other events, 200.8 us)

commit v4 on v2

v4 whole, which is shorter than its diff:
```python
import jax
import jax.numpy as jnp
from jax import lax
from jax.experimental import pallas as pl
from jax.experimental.pallas import tpu as pltpu
from jax.sharding import PartitionSpec as P

EPSILON = 1e-05
TICKS = 2
NZ, NX, NC, NY = 4, 4, 2, 8
ROWS = 128
PIECE = 192
WIDTH = 6144
COLS = 288
BLOCK = 384
MASKS = (0, 1, 3, 2)
VMEM_LIMIT = 24 * 1024 * 1024
SMEM_SPEC = pl.BlockSpec(memory_space=pltpu.SMEM)
VMEM_SPEC = pl.BlockSpec(memory_space=pltpu.VMEM)


def t_index(z, x, c):
    return (z % NZ) * 8 + (x % NX) * 2 + c % NC


def all_t():
    return [(z, x, c) for z in range(NZ) for x in range(NX) for c in range(NC)]


X_GROUPS = [[t_index(z, x, c) for x in range(NX)] for z in range(NZ) for c in range(NC)]


def over_tensor(value, move):
    return lax.ppermute(value, "tensor", [(t_index(*p), t_index(*move(*p))) for p in all_t()])


def over_y(value, move):
    return lax.ppermute(
        value, "segment", [(y * 2 + zl, (move(y) % NY) * 2 + zl) for y in range(NY) for zl in range(2)]
    )


def z_swap(value, mask):
    return over_tensor(value, lambda z, x, c: (z ^ mask, x, c))


def core_swap(value):
    return over_tensor(value, lambda z, x, c: (z, x, c ^ 1))


def zl_swap(value):
    return lax.ppermute(value, "segment", [(i, i ^ 1) for i in range(16)])


def in_first_segment(value, move):
    pairs = [(t_index(*p), t_index(*move(*p))) for p in all_t()]
    return lax.ppermute(value, ("segment", "tensor"), pairs)


def first_segment_x_and_core(value):
    near = stack(value, in_first_segment(value, lambda z, x, c: (z, x ^ 1, c)))
    far = in_first_segment(near, lambda z, x, c: (z, x ^ 3, c))
    return near, far, *[in_first_segment(v, lambda z, x, c: (z, x, c ^ 1)) for v in (near, far)]


def to_next_segment(value, mask):
    pairs = []
    for s in range(16):
        for z, x, c in all_t():
            pairs.append((s * 32 + t_index(z, x, c), ((s + 1) % 16) * 32 + t_index(z ^ mask, x, c)))
    return lax.ppermute(value, ("segment", "tensor"), pairs)


def transposition(value):
    pairs = []
    for yy in range(NY):
        for zl in range(2):
            for z, x, c in all_t():
                y = z * 2 + (x >> 1)
                there = t_index(yy >> 1, (yy & 1) * 2 + (x & 1), c)
                pairs.append(((yy * 2 + zl) * 32 + t_index(z, x, c), (y * 2 + zl) * 32 + there))
    return lax.ppermute(value, ("segment", "tensor"), pairs)


def stack(*values):
    return jnp.concatenate(values, axis=0)


def together(*values):
    return lax.optimization_barrier(values)


def z_direct(value):
    return stack(value, *[z_swap(value, mask) for mask in MASKS[1:]])


def x_and_core(value):
    own = lax.all_gather(value, "tensor", axis=0, tiled=True, axis_index_groups=X_GROUPS)
    return own, core_swap(own)


def other_neighbour(y):
    return y - 1 if y % 2 == 0 else y + 1


def y_labels(y):
    def other(v):
        return lax.rem(v + jnp.where(lax.rem(v, 2) == 0, NY - 1, 1), NY)

    away = lax.rem(y + jnp.where(lax.rem(y, 2) == 0, NY - 2, 2), NY)
    return y, other(y), other(y ^ 1), other(away)


def scaled_weights(weights, gain):
    return (weights.astype(jnp.float32) * gain).astype(jnp.bfloat16)


def pieces(where_ref, parts):
    core, z_mine, x_mine = where_ref[0], where_ref[2], where_ref[3]
    if len(parts) == 2:
        for ref, c in zip(parts, (core, core ^ 1), strict=True):
            for i in range(NX):
                for j in range(NZ):
                    yield ref, i * NZ + j, z_mine ^ MASKS[j], i, c
    else:
        for ref, far, c in zip(parts, (0, 1, 0, 1), (core, core, core ^ 1, core ^ 1), strict=True):
            for i in range(2):
                for j in range(NZ):
                    yield ref, i * NZ + j, z_mine ^ MASKS[j], x_mine ^ MASKS[2 * far + i], c


def feature_start(z, x, c):
    return pl.multiple_of((z * 8 + x * 2 + c) * PIECE, PIECE)


def tick_kernel(where_ref, own_ref, other_ref, weight_ref, mine_ref, out_ref, full):
    square = jnp.zeros((8, ROWS), jnp.float32)
    for ref, k, z, x, c in pieces(where_ref, (own_ref, other_ref)):
        piece = ref[k * PIECE : (k + 1) * PIECE, :]
        full[pl.ds(feature_start(z, x, c), PIECE), :] = piece
        wide = piece.astype(jnp.float32)
        square += jnp.sum((wide * wide).reshape(PIECE // 8, 8, ROWS), axis=0)
    mean_square = jnp.sum(square, axis=0, keepdims=True) * (1.0 / WIDTH)
    scale = lax.rsqrt(mean_square + EPSILON)
    hidden = jnp.dot(weight_ref[...], full[...], preferred_element_type=jnp.float32) * scale
    silu = hidden / (1.0 + jnp.exp(-hidden))
    out_ref[...] = (mine_ref[...].astype(jnp.float32) + silu).astype(jnp.bfloat16)


def tick(where, parts, weights, mine):
    return pl.pallas_call(
        tick_kernel,
        out_shape=jax.ShapeDtypeStruct((PIECE, ROWS), jnp.bfloat16),
        in_specs=[SMEM_SPEC] + [VMEM_SPEC] * 4,
        out_specs=VMEM_SPEC,
        scratch_shapes=[pltpu.VMEM((WIDTH, ROWS), jnp.bfloat16)],
        compiler_params=pltpu.CompilerParams(vmem_limit_bytes=VMEM_LIMIT),
        name="tick",
    )(where, *parts, weights, mine)


def predict_kernel(where_ref, *refs):
    earlier, wrapped, later = refs[:2], refs[2:6], refs[6:8]
    block_ref, taught0_ref, taught1_ref, out_ref, full = refs[8:]

    def fill(parts, tau):
        for ref, k, z, x, c in pieces(where_ref, parts):
            at = pl.ds(feature_start(z, x, c), PIECE)
            full[at, tau * ROWS : (tau + 1) * ROWS] = ref[k * PIECE : (k + 1) * PIECE, :]

    first = where_ref[1] == 0

    @pl.when(first)
    def _():
        fill(wrapped, 0)

    @pl.when(jnp.logical_not(first))
    def _():
        fill(earlier, 0)

    fill(later, 1)
    total = jnp.zeros((COLS, TICKS * ROWS), jnp.float32)
    for s in range(16):
        total += jnp.dot(
            block_ref[s * COLS : (s + 1) * COLS, :],
            full[s * BLOCK : (s + 1) * BLOCK, :],
            preferred_element_type=jnp.float32,
        )
    for tau, taught in enumerate((taught0_ref[0], taught1_ref[1])):
        difference = total[:, tau * ROWS : (tau + 1) * ROWS] - taught.astype(jnp.float32)
        out_ref[tau * COLS : (tau + 1) * COLS, :] = difference.astype(jnp.bfloat16)


def predict(where, rows, blocks, taught):
    return pl.pallas_call(
        predict_kernel,
        out_shape=jax.ShapeDtypeStruct((TICKS * COLS, ROWS), jnp.bfloat16),
        in_specs=[SMEM_SPEC] + [VMEM_SPEC] * 11,
        out_specs=VMEM_SPEC,
        scratch_shapes=[pltpu.VMEM((WIDTH, TICKS * ROWS), jnp.bfloat16)],
        compiler_params=pltpu.CompilerParams(vmem_limit_bytes=VMEM_LIMIT),
        name="predict",
    )(where, *rows, blocks, *taught)


def gradient_kernel(where_ref, *refs):
    diffs, (rows_ref, keep_ref, send_ref, rows) = refs[:4], refs[4:]
    segment = where_ref[1]
    for z, x, c in all_t():
        start = ((x & 1) * 2 + c) * PIECE
        for tau in range(TICKS):
            source = (t_index(z, x, c) * TICKS + tau) * PIECE
            columns = slice(tau * ROWS, (tau + 1) * ROWS)
            rows[z * 2 + (x >> 1), start : start + PIECE, columns] = rows_ref[source : source + PIECE, :]
    half = segment & 1
    for part, out_ref in ((half ^ 1, send_ref), (half, keep_ref)):
        total = jnp.zeros((COLS, BLOCK), jnp.float32)
        for ref, y in zip(diffs, y_labels(segment >> 1), strict=True):
            for i in range(2):
                both = [ref[(i * TICKS + tau) * COLS : (i * TICKS + tau + 1) * COLS, :] for tau in range(TICKS)]
                total += lax.dot_general(
                    jnp.concatenate(both, axis=1),
                    rows[y ^ i, pl.ds(pl.multiple_of(part * BLOCK, BLOCK), BLOCK), :],
                    (((1,), (1,)), ((), ())),
                    preferred_element_type=jnp.float32,
                )
        out_ref[...] = (total * (1.0 / (TICKS * ROWS))).astype(out_ref.dtype)


def gradient(where, diffs, rows):
    return pl.pallas_call(
        gradient_kernel,
        out_shape=(
            jax.ShapeDtypeStruct((COLS, BLOCK), jnp.float32),
            jax.ShapeDtypeStruct((COLS, BLOCK), jnp.bfloat16),
        ),
        in_specs=[SMEM_SPEC] + [VMEM_SPEC] * 5,
        out_specs=(VMEM_SPEC, VMEM_SPEC),
        scratch_shapes=[pltpu.VMEM((NY, 2 * BLOCK, TICKS * ROWS), jnp.bfloat16)],
        compiler_params=pltpu.CompilerParams(vmem_limit_bytes=VMEM_LIMIT),
        name="gradient",
    )(where, *diffs, rows)


def on_device(entering, fresh_rows, norm_gain, segment_weight, projection, teacher_rows):
    t, segment = lax.axis_index("tensor"), lax.axis_index("segment")
    where = jnp.stack([t & 1, segment, t >> 3, (t >> 1) & 3]).astype(jnp.int32)
    weights = scaled_weights(segment_weight[0], norm_gain)
    teacher = teacher_rows[0].swapaxes(1, 2)
    entering_t, fresh_t = entering[0].T, fresh_rows[0].T

    blocks = lax.all_gather(projection.T, "segment", axis=0, tiled=True)
    taught0 = to_next_segment(teacher, 0)

    start = stack(entering_t, fresh_t)
    got = [start] + [z_swap(start, mask) for mask in MASKS[1:]]
    fresh_z = stack(*[v[PIECE:] for v in got])
    out0 = tick(where, x_and_core(stack(*[v[:PIECE] for v in got])), weights, entering_t)

    out0, taught0 = together(out0, taught0)
    moved = [to_next_segment(out0, mask) for mask in MASKS]
    moved_z = stack(*moved)
    first = segment == 0
    earlier = x_and_core(jnp.where(first, fresh_z, moved_z))
    wrapped = first_segment_x_and_core(together(moved_z, earlier[0])[0])
    out1 = tick(where, earlier, weights, jnp.where(first, fresh_t, moved[0]))

    turned = transposition(stack(moved[0], out1))
    later_z = z_direct(out1)
    turned, _ = together(turned, later_z)
    rows = lax.all_gather(turned, "tensor", axis=0, tiled=True)
    later = x_and_core(later_z)
    difference = predict(where, earlier + wrapped + later, blocks, (taught0, teacher))

    pair = stack(difference, over_y(difference, lambda y: y ^ 1))
    second = over_y(pair, other_neighbour)
    third = over_y(second, lambda y: y ^ 1)
    fourth = over_y(second, lambda y: y + 2 if y % 2 == 0 else y - 2)
    keep, send = gradient(where, (pair, second, third, fourth), rows)
    total = keep + zl_swap(send).astype(jnp.float32)
    return (out1.T[None], total.T)


def solution(mesh):
    return jax.shard_map(
        on_device,
        mesh=mesh,
        in_specs=(
            P("segment", None, "tensor"),
            P(None, None, "tensor"),
            P("segment", None),
            P("segment", "tensor", None),
            P("segment", "tensor"),
            P("segment", None, None, "tensor"),
        ),
        out_specs=(P("segment", None, "tensor"), P("segment", "tensor")),
        check_vma=False,
    )
```

time: 272 us -> 238 us (0.88)
  the two profiles are of different devices: /device:TPU:1 before, /device:TPU:258 now
where the time goes in v4:
time: 238 us; the launch traced here: 237 us
  starting transfers between devices  89.8 us (38%)
  waiting for transfers between devices  53.3 us (22%)
  blocking collectives  49.1 us (21%)
  between operations  14.5 us (6%)
  local copies, waits for them, and re-layouts  13 us (5%)
  Pallas kernels  9.73 us (4%)
  other arithmetic  7.23 us (3%)
    all_gather x3, blocking collectives, x_and_core(): lax.all_gather(value, 'tensor', axis=0, tiled=True, axis_index_groups=X_G...  49.1 us
    ppermute x9, starting transfers between devices, over_tensor(): lax.ppermute(value, 'tensor', [(t_index(*p), t_index(*move(*p))) for p in...  31.7 us
    ppermute x4, waiting for transfers between devices, over_y(): lax.ppermute(value, 'segment', [(y * 2 + zl, move(y) % NY * 2 + zl) for y...  27.1 us
    ppermute x5, starting transfers between devices, to_next_segment(): return lax.ppermute(value, ('segment', 'tensor'), pairs)  21.9 us
    ppermute x4, starting transfers between devices, in_first_segment(): return lax.ppermute(value, ('segment', 'tensor'), pairs)  13.6 us
    ppermute x1, starting transfers between devices, transposition(): return lax.ppermute(value, ('segment', 'tensor'), pairs)  12.9 us
    unnamed x35, local copies, waits for them, and re-layouts  11.7 us
    ppermute x4, starting transfers between devices, over_y(): lax.ppermute(value, 'segment', [(y * 2 + zl, move(y) % NY * 2 + zl) for y...  7.67 us
  transfers between devices with their start and end apart: 26, of which 12 were waited for; matrix products, arithmetic and copies ran while one was open for 3% of the time, Pallas kernels for 3%

profile of v4, /device:TPU:258, one launch (start us, length us, event | category | flops | bytes accessed | tf_op | source)
XLA Modules:
  0.0 236.5 jit_solution(17872374474138057330)
XLA Ops:
  10.7 7.9 %collective-permute-start.1 = (bf16[384,128]{1,0:T(8,128)(2,1)S(1)}, bf16[384,128]{1,0:T(8,128)(2,1)S(1)}, u32[]{:S(2)}, u32[]{:S(2)}) collective-permute-start(bf16[384,128]{1,0:T(8,128)(2,1)S(1)} %pad_maximum_fusion.3), channel_id=1, source_target_pairs={{0,24},{1,25},{2,26},{3,27},{4,28},{5,29},{6,30},{7,31},{8,16},{9,... | collective-permute-start | bytes 294920 | tf_op jit(solution)/shard_map/ppermute | solution.py:34
  18.6 2.5 %collective-permute-start = (bf16[384,128]{1,0:T(8,128)(2,1)S(1)}, bf16[384,128]{1,0:T(8,128)(2,1)S(1)}, u32[]{:S(2)}, u32[]{:S(2)}) collective-permute-start(bf16[384,128]{1,0:T(8,128)(2,1)S(1)} %pad_maximum_fusion.3), channel_id=1, source_target_pairs={{0,8},{1,9},{2,10},{3,11},{4,12},{5,13},{6,14},{7,15},{8,0},{9,1},... | collective-permute-start | bytes 294920 | tf_op jit(solution)/shard_map/ppermute | solution.py:34
  21.0 3.4 %collective-permute-start.4 = (bf16[2,288,128]{2,1,0:T(8,128)(2,1)}, bf16[2,288,128]{2,1,0:T(8,128)(2,1)S(1)}, u32[]{:S(2)}, u32[]{:S(2)}) collective-permute-start(bf16[2,288,128]{2,1,0:T(8,128)(2,1)} %bitcast.27), channel_id=1, source_target_pairs={{0,32},{1,33},{2,34},{3,35},{4,36},{5,37},{6,38},{7,39},{8,40},{9,... | collective-permute-start | bytes 442376 | tf_op jit(solution)/shard_map/ppermute | solution.py:71
  25.1 3.4 %collective-permute-done = bf16[384,128]{1,0:T(8,128)(2,1)S(1)} collective-permute-done((bf16[384,128]{1,0:T(8,128)(2,1)S(1)}, bf16[384,128]{1,0:T(8,128)(2,1)S(1)}, u32[]{:S(2)}, u32[]{:S(2)}) %collective-permute-start) | collective-permute-done | bytes 98336 | tf_op jit(solution)/shard_map/ppermute | solution.py:34
  29.9 14.2 %all_gather.15.own_ref = bf16[3072,128]{1,0:T(8,128)(2,1)S(1)} all-gather(bf16[768,128]{1,0:T(8,128)(2,1)S(1)} %pad_maximum_fusion.1), channel_id=1, replica_groups={{0,2,4,6},{1,3,5,7},{8,10,12,14},{9,11,13,15},{16,18,20,22},{17,19,21,2..., dimensions={0}, use_global_device_ids=true | all-gather | bytes 983040 | tf_op jit(solution)/shard_map/all_gather | solution.py:98
  46.0 2.1 fusion.weight_ref
  48.4 2.4 %tick.2 = bf16[192,128]{1,0:T(8,128)(2,1)S(1)} custom-call(s32[4]{0:T(128)S(1)} %pad_add_fusion.where_ref, bf16[3072,128]{1,0:T(8,128)(2,1)S(1)} %all_gather.15.own_ref, bf16[3072,128]{1,0:T(8,128)(2,1)} %collective-permute-done.3.other_ref, bf16[192,6144]{1,0:T(8,128)(2,1)S(1)} %fusion.weight_ref, bf16[192,128]{1,0:T(8,128)(2,1)S(1)} %bitcast.26), custom_call_target="tpu_custom_call" | custom-call | tf_op jit(solution)/shard_map/tick/pallas_call | solution.py:151
  50.8 1.9 collective-permute-start.5
  52.7 4.2 %collective-permute-start.6 = (bf16[192,128]{1,0:T(8,128)(2,1)S(1)}, bf16[192,128]{1,0:T(8,128)(2,1)S(1)}, u32[]{:S(2)}, u32[]{:S(2)}) collective-permute-start(bf16[192,128]{1,0:T(8,128)(2,1)S(1)} %tick.2), channel_id=1, source_target_pairs={{0,40},{1,41},{2,42},{3,43},{4,44},{5,45},{6,46},{7,47},{8,32},{9,... | collective-permute-start | bytes 147464 | tf_op jit(solution)/shard_map/ppermute | solution.py:71
  56.9 3.7 %collective-permute-start.7 = (bf16[192,128]{1,0:T(8,128)(2,1)S(1)}, bf16[192,128]{1,0:T(8,128)(2,1)S(1)}, u32[]{:S(2)}, u32[]{:S(2)}) collective-permute-start(bf16[192,128]{1,0:T(8,128)(2,1)S(1)} %tick.2), channel_id=1, source_target_pairs={{0,56},{1,57},{2,58},{3,59},{4,60},{5,61},{6,62},{7,63},{8,48},{9,... | collective-permute-start | bytes 147464 | tf_op jit(solution)/shard_map/ppermute | solution.py:71
  60.7 8.6 %collective-permute-start.8 = (bf16[192,128]{1,0:T(8,128)(2,1)S(1)}, bf16[192,128]{1,0:T(8,128)(2,1)S(1)}, u32[]{:S(2)}, u32[]{:S(2)}) collective-permute-start(bf16[192,128]{1,0:T(8,128)(2,1)S(1)} %tick.2), channel_id=1, source_target_pairs={{0,48},{1,49},{2,50},{3,51},{4,52},{5,53},{6,54},{7,55},{8,56},{9,... | collective-permute-start | bytes 147464 | tf_op jit(solution)/shard_map/ppermute | solution.py:71
  69.4 3.2 %collective-permute-done.8 = bf16[192,128]{1,0:T(8,128)(2,1)S(1)} collective-permute-done((bf16[192,128]{1,0:T(8,128)(2,1)S(1)}, bf16[192,128]{1,0:T(8,128)(2,1)S(1)}, u32[]{:S(2)}, u32[]{:S(2)}) %collective-permute-start.8) | collective-permute-done | bytes 49184 | tf_op jit(solution)/shard_map/ppermute | solution.py:71
  74.3 13.8 %all_gather.16.own_ref.refs_0_ = bf16[3072,128]{1,0:T(8,128)(2,1)S(1)} all-gather(bf16[768,128]{1,0:T(8,128)(2,1)S(1)} %maximum_select_fusion), channel_id=1, replica_groups={{0,2,4,6},{1,3,5,7},{8,10,12,14},{9,11,13,15},{16,18,20,22},{17,19,21,2..., dimensions={0}, use_global_device_ids=true | all-gather | bytes 983040 | tf_op jit(solution)/shard_map/all_gather | solution.py:98
  90.0 2.3 collective-permute-done.9.other_ref.refs_1_
  92.2 2.4 %tick.3 = bf16[192,128]{1,0:T(8,128)(2,1)} custom-call(s32[4]{0:T(128)S(1)} %pad_add_fusion.where_ref, bf16[3072,128]{1,0:T(8,128)(2,1)S(1)} %all_gather.16.own_ref.refs_0_, bf16[3072,128]{1,0:T(8,128)(2,1)S(1)} %collective-permute-done.9.other_ref.refs_1_, bf16[192,6144]{1,0:T(8,128)(2,1)S(1)} %fusion.weight_ref, ...), custom_call_target="tpu_custom_call" | custom-call | tf_op jit(solution)/shard_map/tick/pallas_call | solution.py:151
  94.7 9.4 %collective-permute-start.16 = (bf16[192,128]{1,0:T(8,128)(2,1)}, bf16[192,128]{1,0:T(8,128)(2,1)S(1)}, u32[]{:S(2)}, u32[]{:S(2)}) collective-permute-start(bf16[192,128]{1,0:T(8,128)(2,1)} %tick.3), channel_id=1, source_target_pairs={{0,16},{1,17},{2,18},{3,19},{4,20},{5,21},{6,22},{7,23},{8,24},{9,... | collective-permute-start | bytes 147464 | tf_op jit(solution)/shard_map/ppermute | solution.py:34
  106.0 2.5 %collective-permute-start.14 = (bf16[192,128]{1,0:T(8,128)(2,1)}, bf16[192,128]{1,0:T(8,128)(2,1)S(1)}, u32[]{:S(2)}, u32[]{:S(2)}) collective-permute-start(bf16[192,128]{1,0:T(8,128)(2,1)} %tick.3), channel_id=1, source_target_pairs={{0,8},{1,9},{2,10},{3,11},{4,12},{5,13},{6,14},{7,15},{8,0},{9,1},... | collective-permute-start | bytes 147464 | tf_op jit(solution)/shard_map/ppermute | solution.py:34
  109.3 12.9 %collective-permute-start.22 = (bf16[384,128]{1,0:T(8,128)(2,1)S(1)}, bf16[384,128]{1,0:T(8,128)(2,1)S(1)}, u32[]{:S(2)}, u32[]{:S(2)}) collective-permute-start(bf16[384,128]{1,0:T(8,128)(2,1)S(1)} %pad_maximum_fusion.4), channel_id=1, source_target_pairs={{0,0},{1,1},{2,2},{3,3},{4,64},{5,65},{6,66},{7,67},{8,128},{9,129... | collective-permute-start | bytes 294920 | tf_op jit(solution)/shard_map/ppermute | solution.py:82
  123.0 5.0 %collective-permute-done.22 = bf16[384,128]{1,0:T(8,128)(2,1)S(1)} collective-permute-done((bf16[384,128]{1,0:T(8,128)(2,1)S(1)}, bf16[384,128]{1,0:T(8,128)(2,1)S(1)}, u32[]{:S(2)}, u32[]{:S(2)}) %collective-permute-start.22) | collective-permute-done | bytes 98336 | tf_op jit(solution)/shard_map/ppermute | solution.py:82
  128.7 3.0 %collective-permute-start.10 = (bf16[768,128]{1,0:T(8,128)(2,1)S(1)}, bf16[768,128]{1,0:T(8,128)(2,1)S(1)}, u32[]{:S(2)}, u32[]{:S(2)}) collective-permute-start(bf16[768,128]{1,0:T(8,128)(2,1)S(1)} %copy-done.13), channel_id=1, source_target_pairs={{0,2},{1,3},{2,0},{3,1},{4,6},{5,7},{6,4},{7,5},{8,10},{9,11},{10,... | collective-permute-start | bytes 589832 | tf_op jit(solution)/shard_map/ppermute | solution.py:57
  131.7 4.6 %collective-permute-done.10 = bf16[768,128]{1,0:T(8,128)(2,1)S(1)} collective-permute-done((bf16[768,128]{1,0:T(8,128)(2,1)S(1)}, bf16[768,128]{1,0:T(8,128)(2,1)S(1)}, u32[]{:S(2)}, u32[]{:S(2)}) %collective-permute-start.10) | collective-permute-done | bytes 196640 | tf_op jit(solution)/shard_map/ppermute | solution.py:57
  136.3 6.3 %collective-permute-start.11 = (bf16[1536,128]{1,0:T(8,128)(2,1)S(1)}, bf16[1536,128]{1,0:T(8,128)(2,1)S(1)}, u32[]{:S(2)}, u32[]{:S(2)}) collective-permute-start(bf16[1536,128]{1,0:T(8,128)(2,1)S(1)} %constant_dynamic-update-slice_fusion.4.refs_2_), channel_id=1, source_target_pairs={{0,6},{1,7},{2,4},{3,5},{4,2},{5,3},{6,0},{7,1},{8,14},{9,15},{10,... | collective-permute-start | bytes 1179656 | tf_op jit(solution)/shard_map/ppermute | solution.py:57
  142.6 21.1 %all_gather.17.refs_6_ = bf16[3072,128]{1,0:T(8,128)(2,1)S(1)} all-gather(bf16[768,128]{1,0:T(8,128)(2,1)S(1)} %pad_maximum_fusion.2), channel_id=1, replica_groups={{0,2,4,6},{1,3,5,7},{8,10,12,14},{9,11,13,15},{16,18,20,22},{17,19,21,2..., dimensions={0}, use_global_device_ids=true | all-gather | bytes 983040 | tf_op jit(solution)/shard_map/all_gather | solution.py:98
  165.6 2.4 %collective-permute-start.12 = (bf16[1536,128]{1,0:T(8,128)(2,1)S(1)}, bf16[1536,128]{1,0:T(8,128)(2,1)S(1)}, u32[]{:S(2)}, u32[]{:S(2)}) collective-permute-start(bf16[1536,128]{1,0:T(8,128)(2,1)S(1)} %constant_dynamic-update-slice_fusion.4.refs_2_), channel_id=1, source_target_pairs={{0,1},{1,0},{2,3},{3,2},{4,5},{5,4},{6,7},{7,6},{8,9},{9,8},{10,11... | collective-permute-start | bytes 1179656 | tf_op jit(solution)/shard_map/ppermute | solution.py:57
  172.4 2.0 copy-done
  179.4 2.5 %predict.1 = bf16[576,128]{1,0:T(8,128)(2,1)S(1)} custom-call(s32[4]{0:T(128)S(1)} %pad_add_fusion.where_ref, bf16[3072,128]{1,0:T(8,128)(2,1)S(1)} %all_gather.16.own_ref.refs_0_, bf16[3072,128]{1,0:T(8,128)(2,1)S(1)} %copy-done.3, bf16[1536,128]{1,0:T(8,128)(2,1)S(1)} %constant_dynamic-update-slice_fusion.4.refs_2_, ...), custom_call_target="tpu_custom_call" | custom-call | tf_op jit(solution)/shard_map/predict/pallas_call | solution.py:195
  183.8 5.8 %collective-permute-done.18 = bf16[576,128]{1,0:T(8,128)(2,1)S(1)} collective-permute-done((bf16[576,128]{1,0:T(8,128)(2,1)S(1)}, bf16[576,128]{1,0:T(8,128)(2,1)S(1)}, u32[]{:S(2)}, u32[]{:S(2)}) %collective-permute-start.18) | collective-permute-done | bytes 147488 | tf_op jit(solution)/shard_map/ppermute | solution.py:38
  191.6 9.5 %collective-permute-done.19.refs_1_ = bf16[1152,128]{1,0:T(8,128)(2,1)S(1)} collective-permute-done((bf16[1152,128]{1,0:T(8,128)(2,1)S(1)}, bf16[1152,128]{1,0:T(8,128)(2,1)S(1)}, u32[]{:S(2)}, u32[]{:S(2)}) %collective-permute-start.19) | collective-permute-done | bytes 294944 | tf_op jit(solution)/shard_map/ppermute | solution.py:38
  204.9 8.0 %collective-permute-done.20.refs_2_ = bf16[1152,128]{1,0:T(8,128)(2,1)S(1)} collective-permute-done((bf16[1152,128]{1,0:T(8,128)(2,1)S(1)}, bf16[1152,128]{1,0:T(8,128)(2,1)S(1)}, u32[]{:S(2)}, u32[]{:S(2)}) %collective-permute-start.20) | collective-permute-done | bytes 294944 | tf_op jit(solution)/shard_map/ppermute | solution.py:38
  212.9 3.8 %collective-permute-done.21.refs_3_ = bf16[1152,128]{1,0:T(8,128)(2,1)S(1)} collective-permute-done((bf16[1152,128]{1,0:T(8,128)(2,1)S(1)}, bf16[1152,128]{1,0:T(8,128)(2,1)S(1)}, u32[]{:S(2)}, u32[]{:S(2)}) %collective-permute-start.21) | collective-permute-done | bytes 294944 | tf_op jit(solution)/shard_map/ppermute | solution.py:38
  218.6 2.4 %gradient.1 = (f32[288,384]{1,0:T(8,128)S(1)}, bf16[288,384]{1,0:T(8,128)(2,1)S(1)}) custom-call(s32[4]{0:T(128)S(1)} %pad_add_fusion.where_ref, bf16[1152,128]{1,0:T(8,128)(2,1)S(1)} %pad_maximum_fusion.refs_0_, bf16[1152,128]{1,0:T(8,128)(2,1)S(1)} %collective-permute-done.19.refs_1_, bf16[1152,128]{1,0:T(8,128)(2,1)S(1)} %collective-permute-done.20.refs_2_, ...), custom_call_target="tpu_custom_call" | custom-call | tf_op jit(solution)/shard_map/gradient/pallas_call | solution.py:231
  223.0 5.9 %collective-permute-done.23 = bf16[288,384]{1,0:T(8,128)(2,1)S(1)} collective-permute-done((bf16[288,384]{1,0:T(8,128)(2,1)S(1)}, bf16[288,384]{1,0:T(8,128)(2,1)S(1)}, u32[]{:S(2)}, u32[]{:S(2)}) %collective-permute-start.23) | collective-permute-done | bytes 221216 | tf_op jit(solution)/shard_map/ppermute | solution.py:52
  (79 shorter events, 39.0 us)
Async XLA Ops:
  7.2 165.2 %all-gather.3.cloned.1.call-start = ((), (), s32[]{:S(2)}) async-start(), calls=%async_computation | async-start | bytes 3760128 | tf_op jit(solution)/shard_map/all_gather | solution.py:252
  7.9 208.8 %all-gather.5.cloned.1.call-start = ((), (), s32[]{:S(2)}) async-start(), calls=%async_computation.1 | async-start | bytes 3244032 | tf_op jit(solution)/shard_map/all_gather | solution.py:271
  8.8 15.6 %collective-permute-start.2 = (bf16[384,128]{1,0:T(8,128)(2,1)S(1)}, bf16[384,128]{1,0:T(8,128)(2,1)S(1)}, u32[]{:S(2)}, u32[]{:S(2)}) collective-permute-start(bf16[384,128]{1,0:T(8,128)(2,1)S(1)} %pad_maximum_fusion.3), channel_id=1, source_target_pairs={{0,16},{1,17},{2,18},{3,19},{4,20},{5,21},{6,22},{7,23},{8,24},{9,... | collective-permute-start | bytes 294920 | tf_op jit(solution)/shard_map/ppermute | solution.py:34
  10.7 13.7 %collective-permute-start.1 = (bf16[384,128]{1,0:T(8,128)(2,1)S(1)}, bf16[384,128]{1,0:T(8,128)(2,1)S(1)}, u32[]{:S(2)}, u32[]{:S(2)}) collective-permute-start(bf16[384,128]{1,0:T(8,128)(2,1)S(1)} %pad_maximum_fusion.3), channel_id=1, source_target_pairs={{0,24},{1,25},{2,26},{3,27},{4,28},{5,29},{6,30},{7,31},{8,16},{9,... | collective-permute-start | bytes 294920 | tf_op jit(solution)/shard_map/ppermute | solution.py:34
  18.6 9.9 %collective-permute-start = (bf16[384,128]{1,0:T(8,128)(2,1)S(1)}, bf16[384,128]{1,0:T(8,128)(2,1)S(1)}, u32[]{:S(2)}, u32[]{:S(2)}) collective-permute-start(bf16[384,128]{1,0:T(8,128)(2,1)S(1)} %pad_maximum_fusion.3), channel_id=1, source_target_pairs={{0,8},{1,9},{2,10},{3,11},{4,12},{5,13},{6,14},{7,15},{8,0},{9,1},... | collective-permute-start | bytes 294920 | tf_op jit(solution)/shard_map/ppermute | solution.py:34
  21.0 29.7 %collective-permute-start.4 = (bf16[2,288,128]{2,1,0:T(8,128)(2,1)}, bf16[2,288,128]{2,1,0:T(8,128)(2,1)S(1)}, u32[]{:S(2)}, u32[]{:S(2)}) collective-permute-start(bf16[2,288,128]{2,1,0:T(8,128)(2,1)} %bitcast.27), channel_id=1, source_target_pairs={{0,32},{1,33},{2,34},{3,35},{4,36},{5,37},{6,38},{7,39},{8,40},{9,... | collective-permute-start | bytes 442376 | tf_op jit(solution)/shard_map/ppermute | solution.py:71
  25.1 23.3 %copy-start.4 = (bf16[1,128,192]{1,2,0:T(8,128)(2,1)S(1)}, bf16[1,128,192]{1,2,0:T(8,128)(2,1)}, u32[]{:S(2)}) copy-start(bf16[1,128,192]{1,2,0:T(8,128)(2,1)} %param.6) | copy-start | bytes 147460
  44.1 4.3 %collective-permute-start.3 = (bf16[3072,128]{1,0:T(8,128)(2,1)S(1)}, bf16[3072,128]{1,0:T(8,128)(2,1)}, u32[]{:S(2)}, u32[]{:S(2)}) collective-permute-start(bf16[3072,128]{1,0:T(8,128)(2,1)S(1)} %all_gather.15.own_ref), channel_id=1, source_target_pairs={{0,1},{1,0},{2,3},{3,2},{4,5},{5,4},{6,7},{7,6},{8,9},{9,8},{10,11... | collective-permute-start | bytes 2359304 | tf_op jit(solution)/shard_map/ppermute | solution.py:34
  48.1 21.2 %copy-start.14 = (bf16[1,128,192]{1,2,0:T(8,128)(2,1)S(1)}, bf16[1,128,192]{1,2,0:T(8,128)(2,1)}, u32[]{:S(2)}) copy-start(bf16[1,128,192]{1,2,0:T(8,128)(2,1)} %param.7) | copy-start | bytes 147460
  50.8 58.5 %copy-start.10 = (bf16[2,288,128]{2,1,0:T(8,128)(2,1)}, bf16[2,288,128]{2,1,0:T(8,128)(2,1)S(1)}, u32[]{:S(2)}) copy-start(bf16[2,288,128]{2,1,0:T(8,128)(2,1)S(1)} %collective-permute-done.4.refs_9_) | copy-start | bytes 442372
  50.8 18.6 %collective-permute-start.5 = (bf16[192,128]{1,0:T(8,128)(2,1)S(1)}, bf16[192,128]{1,0:T(8,128)(2,1)S(1)}, u32[]{:S(2)}, u32[]{:S(2)}) collective-permute-start(bf16[192,128]{1,0:T(8,128)(2,1)S(1)} %tick.2), channel_id=1, source_target_pairs={{0,32},{1,33},{2,34},{3,35},{4,36},{5,37},{6,38},{7,39},{8,40},{9,... | collective-permute-start | bytes 147464 | tf_op jit(solution)/shard_map/ppermute | solution.py:71
  52.7 16.7 %collective-permute-start.6 = (bf16[192,128]{1,0:T(8,128)(2,1)S(1)}, bf16[192,128]{1,0:T(8,128)(2,1)S(1)}, u32[]{:S(2)}, u32[]{:S(2)}) collective-permute-start(bf16[192,128]{1,0:T(8,128)(2,1)S(1)} %tick.2), channel_id=1, source_target_pairs={{0,40},{1,41},{2,42},{3,43},{4,44},{5,45},{6,46},{7,47},{8,32},{9,... | collective-permute-start | bytes 147464 | tf_op jit(solution)/shard_map/ppermute | solution.py:71
  56.9 12.5 %collective-permute-start.7 = (bf16[192,128]{1,0:T(8,128)(2,1)S(1)}, bf16[192,128]{1,0:T(8,128)(2,1)S(1)}, u32[]{:S(2)}, u32[]{:S(2)}) collective-permute-start(bf16[192,128]{1,0:T(8,128)(2,1)S(1)} %tick.2), channel_id=1, source_target_pairs={{0,56},{1,57},{2,58},{3,59},{4,60},{5,61},{6,62},{7,63},{8,48},{9,... | collective-permute-start | bytes 147464 | tf_op jit(solution)/shard_map/ppermute | solution.py:71
  60.7 12.0 %collective-permute-start.8 = (bf16[192,128]{1,0:T(8,128)(2,1)S(1)}, bf16[192,128]{1,0:T(8,128)(2,1)S(1)}, u32[]{:S(2)}, u32[]{:S(2)}) collective-permute-start(bf16[192,128]{1,0:T(8,128)(2,1)S(1)} %tick.2), channel_id=1, source_target_pairs={{0,48},{1,49},{2,50},{3,51},{4,52},{5,53},{6,54},{7,55},{8,56},{9,... | collective-permute-start | bytes 147464 | tf_op jit(solution)/shard_map/ppermute | solution.py:71
  74.3 54.4 %copy-start.13 = (bf16[768,128]{1,0:T(8,128)(2,1)S(1)}, bf16[768,128]{1,0:T(8,128)(2,1)}, u32[]{:S(2)}) copy-start(bf16[768,128]{1,0:T(8,128)(2,1)} %copy-done.12) | copy-start | bytes 589828
  88.1 4.2 %collective-permute-start.9 = (bf16[3072,128]{1,0:T(8,128)(2,1)S(1)}, bf16[3072,128]{1,0:T(8,128)(2,1)S(1)}, u32[]{:S(2)}, u32[]{:S(2)}) collective-permute-start(bf16[3072,128]{1,0:T(8,128)(2,1)S(1)} %all_gather.16.own_ref.refs_0_), channel_id=1, source_target_pairs={{0,1},{1,0},{2,3},{3,2},{4,5},{5,4},{6,7},{7,6},{8,9},{9,8},{10,11... | collective-permute-start | bytes 2359304 | tf_op jit(solution)/shard_map/ppermute | solution.py:34
  92.2 2.4 %copy-start.2 = (bf16[3072,128]{1,0:T(8,128)(2,1)}, bf16[3072,128]{1,0:T(8,128)(2,1)S(1)}, u32[]{:S(2)}) copy-start(bf16[3072,128]{1,0:T(8,128)(2,1)S(1)} %collective-permute-done.9.other_ref.refs_1_) | copy-start | bytes 2359300
  94.7 27.5 %collective-permute-start.16 = (bf16[192,128]{1,0:T(8,128)(2,1)}, bf16[192,128]{1,0:T(8,128)(2,1)S(1)}, u32[]{:S(2)}, u32[]{:S(2)}) collective-permute-start(bf16[192,128]{1,0:T(8,128)(2,1)} %tick.3), channel_id=1, source_target_pairs={{0,16},{1,17},{2,18},{3,19},{4,20},{5,21},{6,22},{7,23},{8,24},{9,... | collective-permute-start | bytes 147464 | tf_op jit(solution)/shard_map/ppermute | solution.py:34
  104.1 18.1 %collective-permute-start.15 = (bf16[192,128]{1,0:T(8,128)(2,1)}, bf16[192,128]{1,0:T(8,128)(2,1)S(1)}, u32[]{:S(2)}, u32[]{:S(2)}) collective-permute-start(bf16[192,128]{1,0:T(8,128)(2,1)} %tick.3), channel_id=1, source_target_pairs={{0,24},{1,25},{2,26},{3,27},{4,28},{5,29},{6,30},{7,31},{8,16},{9,... | collective-permute-start | bytes 147464 | tf_op jit(solution)/shard_map/ppermute | solution.py:34
  106.0 16.2 %collective-permute-start.14 = (bf16[192,128]{1,0:T(8,128)(2,1)}, bf16[192,128]{1,0:T(8,128)(2,1)S(1)}, u32[]{:S(2)}, u32[]{:S(2)}) collective-permute-start(bf16[192,128]{1,0:T(8,128)(2,1)} %tick.3), channel_id=1, source_target_pairs={{0,8},{1,9},{2,10},{3,11},{4,12},{5,13},{6,14},{7,15},{8,0},{9,1},... | collective-permute-start | bytes 147464 | tf_op jit(solution)/shard_map/ppermute | solution.py:34
  109.3 18.7 %collective-permute-start.22 = (bf16[384,128]{1,0:T(8,128)(2,1)S(1)}, bf16[384,128]{1,0:T(8,128)(2,1)S(1)}, u32[]{:S(2)}, u32[]{:S(2)}) collective-permute-start(bf16[384,128]{1,0:T(8,128)(2,1)S(1)} %pad_maximum_fusion.4), channel_id=1, source_target_pairs={{0,0},{1,1},{2,2},{3,3},{4,64},{5,65},{6,66},{7,67},{8,128},{9,129... | collective-permute-start | bytes 294920 | tf_op jit(solution)/shard_map/ppermute | solution.py:82
  128.7 7.6 %collective-permute-start.10 = (bf16[768,128]{1,0:T(8,128)(2,1)S(1)}, bf16[768,128]{1,0:T(8,128)(2,1)S(1)}, u32[]{:S(2)}, u32[]{:S(2)}) collective-permute-start(bf16[768,128]{1,0:T(8,128)(2,1)S(1)} %copy-done.13), channel_id=1, source_target_pairs={{0,2},{1,3},{2,0},{3,1},{4,6},{5,7},{6,4},{7,5},{8,10},{9,11},{10,... | collective-permute-start | bytes 589832 | tf_op jit(solution)/shard_map/ppermute | solution.py:57
  136.3 31.7 %collective-permute-start.11 = (bf16[1536,128]{1,0:T(8,128)(2,1)S(1)}, bf16[1536,128]{1,0:T(8,128)(2,1)S(1)}, u32[]{:S(2)}, u32[]{:S(2)}) collective-permute-start(bf16[1536,128]{1,0:T(8,128)(2,1)S(1)} %constant_dynamic-update-slice_fusion.4.refs_2_), channel_id=1, source_target_pairs={{0,6},{1,7},{2,4},{3,5},{4,2},{5,3},{6,0},{7,1},{8,14},{9,15},{10,... | collective-permute-start | bytes 1179656 | tf_op jit(solution)/shard_map/ppermute | solution.py:57
  163.7 8.7 %collective-permute-start.17 = (bf16[3072,128]{1,0:T(8,128)(2,1)S(1)}, bf16[3072,128]{1,0:T(8,128)(2,1)S(1)}, u32[]{:S(2)}, u32[]{:S(2)}) collective-permute-start(bf16[3072,128]{1,0:T(8,128)(2,1)S(1)} %all_gather.17.refs_6_), channel_id=1, source_target_pairs={{0,1},{1,0},{2,3},{3,2},{4,5},{5,4},{6,7},{7,6},{8,9},{9,8},{10,11... | collective-permute-start | bytes 2359304 | tf_op jit(solution)/shard_map/ppermute | solution.py:34
  165.6 4.4 %collective-permute-start.12 = (bf16[1536,128]{1,0:T(8,128)(2,1)S(1)}, bf16[1536,128]{1,0:T(8,128)(2,1)S(1)}, u32[]{:S(2)}, u32[]{:S(2)}) collective-permute-start(bf16[1536,128]{1,0:T(8,128)(2,1)S(1)} %constant_dynamic-update-slice_fusion.4.refs_2_), channel_id=1, source_target_pairs={{0,1},{1,0},{2,3},{3,2},{4,5},{5,4},{6,7},{7,6},{8,9},{9,8},{10,11... | collective-permute-start | bytes 1179656 | tf_op jit(solution)/shard_map/ppermute | solution.py:57
  168.0 3.6 %collective-permute-start.13 = (bf16[1536,128]{1,0:T(8,128)(2,1)S(1)}, bf16[1536,128]{1,0:T(8,128)(2,1)S(1)}, u32[]{:S(2)}, u32[]{:S(2)}) collective-permute-start(bf16[1536,128]{1,0:T(8,128)(2,1)S(1)} %collective-permute-done.11.refs_3_), channel_id=1, source_target_pairs={{0,1},{1,0},{2,3},{3,2},{4,5},{5,4},{6,7},{7,6},{8,9},{9,8},{10,11... | collective-permute-start | bytes 1179656 | tf_op jit(solution)/shard_map/ppermute | solution.py:57
  172.4 2.0 copy-start
  181.9 7.8 %collective-permute-start.18 = (bf16[576,128]{1,0:T(8,128)(2,1)S(1)}, bf16[576,128]{1,0:T(8,128)(2,1)S(1)}, u32[]{:S(2)}, u32[]{:S(2)}) collective-permute-start(bf16[576,128]{1,0:T(8,128)(2,1)S(1)} %predict.1), channel_id=1, source_target_pairs={{0,64},{32,96},{64,0},{96,32},{128,192},{160,224},{192,128},{224,1... | collective-permute-start | bytes 442376 | tf_op jit(solution)/shard_map/ppermute | solution.py:38
  189.7 11.4 %collective-permute-start.19 = (bf16[1152,128]{1,0:T(8,128)(2,1)S(1)}, bf16[1152,128]{1,0:T(8,128)(2,1)S(1)}, u32[]{:S(2)}, u32[]{:S(2)}) collective-permute-start(bf16[1152,128]{1,0:T(8,128)(2,1)S(1)} %pad_maximum_fusion.refs_0_), channel_id=1, source_target_pairs={{0,448},{32,480},{64,128},{96,160},{128,64},{160,96},{192,256},{22... | collective-permute-start | bytes 884744 | tf_op jit(solution)/shard_map/ppermute | solution.py:38
  201.1 11.8 %collective-permute-start.20 = (bf16[1152,128]{1,0:T(8,128)(2,1)S(1)}, bf16[1152,128]{1,0:T(8,128)(2,1)S(1)}, u32[]{:S(2)}, u32[]{:S(2)}) collective-permute-start(bf16[1152,128]{1,0:T(8,128)(2,1)S(1)} %collective-permute-done.19.refs_1_), channel_id=1, source_target_pairs={{0,64},{32,96},{64,0},{96,32},{128,192},{160,224},{192,128},{224,1... | collective-permute-start | bytes 884744 | tf_op jit(solution)/shard_map/ppermute | solution.py:38
  203.0 13.7 %collective-permute-start.21 = (bf16[1152,128]{1,0:T(8,128)(2,1)S(1)}, bf16[1152,128]{1,0:T(8,128)(2,1)S(1)}, u32[]{:S(2)}, u32[]{:S(2)}) collective-permute-start(bf16[1152,128]{1,0:T(8,128)(2,1)S(1)} %collective-permute-done.19.refs_1_), channel_id=1, source_target_pairs={{0,128},{32,160},{64,448},{96,480},{128,256},{160,288},{192,64},{2... | collective-permute-start | bytes 884744 | tf_op jit(solution)/shard_map/ppermute | solution.py:38
  221.1 7.8 %collective-permute-start.23 = (bf16[288,384]{1,0:T(8,128)(2,1)S(1)}, bf16[288,384]{1,0:T(8,128)(2,1)S(1)}, u32[]{:S(2)}, u32[]{:S(2)}) collective-permute-start(bf16[288,384]{1,0:T(8,128)(2,1)S(1)} %get-tuple-element.13), channel_id=1, source_target_pairs={{0,32},{32,0},{64,96},{96,64},{128,160},{160,128},{192,224},{224,1... | collective-permute-start | bytes 663560 | tf_op jit(solution)/shard_map/ppermute | solution.py:52
  (10 other events, 9.7 us)
Sparse Core Ops, SparseCore 0:
  10.1 106.0 all-gather.2
  128.8 62.4 all-gather.4

commit v5 on v4

v5 whole, which is shorter than its diff:
```python
import jax
import jax.numpy as jnp
from jax import lax
from jax.experimental import pallas as pl
from jax.experimental.pallas import tpu as pltpu
from jax.sharding import PartitionSpec as P

EPSILON = 1e-05
TICKS = 2
NZ, NX, NC, NY = 4, 4, 2, 8
ROWS = 128
PIECE = 192
WIDTH = 6144
COLS = 288
BLOCK = 384
COLUMN = 768
RIDE = 960
VMEM_LIMIT = 32 * 1024 * 1024
SMEM_SPEC = pl.BlockSpec(memory_space=pltpu.SMEM)
VMEM_SPEC = pl.BlockSpec(memory_space=pltpu.VMEM)


def t_index(z, x, c):
    return (z % NZ) * 8 + (x % NX) * 2 + c % NC


def all_t():
    return [(z, x, c) for z in range(NZ) for x in range(NX) for c in range(NC)]


Z_GROUPS = [[t_index(z, x, c) for z in range(NZ)] for x in range(NX) for c in range(NC)]
Y_GROUPS = [[y * 2 + zl for y in range(NY)] for zl in range(2)]
X_GROUPS = [[t_index(z, x, c) for x in range(NX)] for z in range(NZ) for c in range(NC)]


def over_tensor(value, move):
    return lax.ppermute(value, "tensor", [(t_index(*p), t_index(*move(*p))) for p in all_t()])


def over_y(value, move):
    return lax.ppermute(
        value, "segment", [(y * 2 + zl, (move(y) % NY) * 2 + zl) for y in range(NY) for zl in range(2)]
    )


def core_swap(value):
    return over_tensor(value, lambda z, x, c: (z, x, c ^ 1))


def zl_swap(value):
    return lax.ppermute(value, "segment", [(i, i ^ 1) for i in range(16)])


def transposition(value):
    pairs = []
    for yy in range(NY):
        for zl in range(2):
            for z, x, c in all_t():
                y = z * 2 + (x >> 1)
                there = t_index(yy >> 1, (yy & 1) * 2 + (x & 1), c)
                pairs.append(((yy * 2 + zl) * 32 + t_index(z, x, c), (y * 2 + zl) * 32 + there))
    return lax.ppermute(value, ("segment", "tensor"), pairs)


def stack(*values):
    return jnp.concatenate(values, axis=0)


def together(*values):
    return lax.optimization_barrier(values)


def gather(value, axis, groups):
    return lax.all_gather(value, axis, axis=0, tiled=True, axis_index_groups=groups)


def z_gather(value):
    return gather(value, "tensor", Z_GROUPS)


def x_gather(value):
    return gather(value, "tensor", X_GROUPS)


def whole(shape):
    return pl.BlockSpec(shape, lambda i: (0,) * len(shape))


def other_neighbour(y):
    return y - 1 if y % 2 == 0 else y + 1


def y_labels(y):
    def other(v):
        return lax.rem(v + jnp.where(lax.rem(v, 2) == 0, NY - 1, 1), NY)

    away = lax.rem(y + jnp.where(lax.rem(y, 2) == 0, NY - 2, 2), NY)
    return y, other(y), other(y ^ 1), other(away)


def scaled_weights(weights, gain):
    return (weights.astype(jnp.float32) * gain).astype(jnp.bfloat16)


def feature_start(z, x, c):
    return pl.multiple_of((z * 8 + x * 2 + c) * PIECE, PIECE)


def hidden_rows(where_ref, own_ref, other_ref, weight_ref, mine_ref, full):
    core = where_ref[0]
    stride = own_ref.shape[0] // NX
    square = jnp.zeros((8, ROWS), jnp.float32)
    for ref, c in ((own_ref, core), (other_ref, core ^ 1)):
        for x in range(NX):
            for z in range(NZ):
                source = x * stride + z * PIECE
                piece = ref[source : source + PIECE, :]
                full[pl.ds(feature_start(z, x, c), PIECE), :] = piece
                wide = piece.astype(jnp.float32)
                square += jnp.sum((wide * wide).reshape(PIECE // 8, 8, ROWS), axis=0)
    mean_square = jnp.sum(square, axis=0, keepdims=True) * (1.0 / WIDTH)
    scale = lax.rsqrt(mean_square + EPSILON)
    hidden = jnp.dot(weight_ref[...], full[...], preferred_element_type=jnp.float32) * scale
    silu = hidden / (1.0 + jnp.exp(-hidden))
    return (mine_ref[...].astype(jnp.float32) + silu).astype(jnp.bfloat16)


def first_tick_kernel(where_ref, own_ref, other_ref, weight_ref, mine_ref, out_ref, full):
    out_ref[...] = hidden_rows(where_ref, own_ref, other_ref, weight_ref, mine_ref, full)


def second_tick_kernel(
    where_ref, own_ref, other_ref, weight_ref, mine_ref, before_ref, out_ref, both_ref, next_ref, full
):
    out = hidden_rows(where_ref, own_ref, other_ref, weight_ref, mine_ref, full)
    out_ref[...] = out
    both_ref[:PIECE, :] = before_ref[...]
    both_ref[PIECE:, :] = out
    next_ref[:PIECE, :] = out
    for x in range(NX):
        source = x * RIDE + COLUMN
        next_ref[(x + 1) * PIECE : (x + 2) * PIECE, :] = own_ref[source : source + PIECE, :]


def tick(kernel, out_rows, *operands):
    return pl.pallas_call(
        kernel,
        out_shape=[jax.ShapeDtypeStruct((rows, ROWS), jnp.bfloat16) for rows in out_rows],
        in_specs=[SMEM_SPEC] + [VMEM_SPEC] * (len(operands) - 1),
        out_specs=[VMEM_SPEC] * len(out_rows),
        scratch_shapes=[pltpu.VMEM((WIDTH, ROWS), jnp.bfloat16)],
        compiler_params=pltpu.CompilerParams(vmem_limit_bytes=VMEM_LIMIT),
        name="tick",
    )(*operands)


def predict_kernel(
    where_ref, first_own_ref, first_other_ref, own_ref, other_ref, block_ref, teacher_ref, out_ref, full
):
    core, segment = where_ref[0], where_ref[1]
    for ref, c in ((first_own_ref, core), (first_other_ref, core ^ 1)):
        for z in range(NZ):
            for x in range(NX):
                source = z * RIDE + (x + 1) * PIECE
                full[pl.ds(feature_start(z, x, c), PIECE), :ROWS] = ref[source : source + PIECE, :]
    for ref, c in ((own_ref, core), (other_ref, core ^ 1)):
        for x in range(NX):
            for z in range(NZ):
                source = (x * NZ + z) * PIECE
                full[pl.ds(feature_start(z, x, c), PIECE), ROWS:] = ref[source : source + PIECE, :]
    total = jnp.zeros((COLS, TICKS * ROWS), jnp.float32)
    for y in range(NY):
        for j in range(2):
            owner = y * 2 + ((segment & 1) ^ j)
            total += jnp.dot(
                block_ref[(y * 2 + j) * COLS : (y * 2 + j + 1) * COLS, :],
                full[pl.ds(pl.multiple_of(owner * BLOCK, BLOCK), BLOCK), :],
                preferred_element_type=jnp.float32,
            )
    for tau in range(TICKS):
        difference = total[:, tau * ROWS : (tau + 1) * ROWS] - teacher_ref[tau].astype(jnp.float32)
        out_ref[tau * COLS : (tau + 1) * COLS, :] = difference.astype(jnp.bfloat16)


def predict(where, *operands):
    return pl.pallas_call(
        predict_kernel,
        grid=(1,),
        out_shape=jax.ShapeDtypeStruct((TICKS * COLS, ROWS), jnp.bfloat16),
        in_specs=[SMEM_SPEC] + [whole(v.shape) for v in operands],
        out_specs=whole((TICKS * COLS, ROWS)),
        scratch_shapes=[pltpu.VMEM((WIDTH, TICKS * ROWS), jnp.bfloat16)],
        compiler_params=pltpu.CompilerParams(vmem_limit_bytes=VMEM_LIMIT),
        name="predict",
    )(where, *operands)


def gradient_kernel(where_ref, *refs):
    diffs, (rows_ref, keep_ref, send_ref, rows) = refs[:4], refs[4:]
    segment = where_ref[1]
    for z, x, c in all_t():
        start = ((x & 1) * 2 + c) * PIECE
        for tau in range(TICKS):
            source = (t_index(z, x, c) * TICKS + tau) * PIECE
            columns = slice(tau * ROWS, (tau + 1) * ROWS)
            rows[z * 2 + (x >> 1), start : start + PIECE, columns] = rows_ref[source : source + PIECE, :]
    half = segment & 1
    for part, out_ref in ((half ^ 1, send_ref), (half, keep_ref)):
        total = jnp.zeros((COLS, BLOCK), jnp.float32)
        for ref, y in zip(diffs, y_labels(segment >> 1), strict=True):
            for i in range(2):
                both = [ref[(i * TICKS + tau) * COLS : (i * TICKS + tau + 1) * COLS, :] for tau in range(TICKS)]
                total += lax.dot_general(
                    jnp.concatenate(both, axis=1),
                    rows[y ^ i, pl.ds(pl.multiple_of(part * BLOCK, BLOCK), BLOCK), :],
                    (((1,), (1,)), ((), ())),
                    preferred_element_type=jnp.float32,
                )
        out_ref[...] = (total * (1.0 / (TICKS * ROWS))).astype(out_ref.dtype)


def gradient(where, diffs, rows):
    return pl.pallas_call(
        gradient_kernel,
        out_shape=(
            jax.ShapeDtypeStruct((COLS, BLOCK), jnp.float32),
            jax.ShapeDtypeStruct((COLS, BLOCK), jnp.bfloat16),
        ),
        grid=(1,),
        in_specs=[SMEM_SPEC] + [whole(v.shape) for v in (*diffs, rows)],
        out_specs=(whole((COLS, BLOCK)), whole((COLS, BLOCK))),
        scratch_shapes=[pltpu.VMEM((NY, 2 * BLOCK, TICKS * ROWS), jnp.bfloat16)],
        compiler_params=pltpu.CompilerParams(vmem_limit_bytes=VMEM_LIMIT),
        name="gradient",
    )(where, *diffs, rows)


def on_device(entering, fresh_rows, norm_gain, segment_weight, projection, teacher_rows):
    t, segment = lax.axis_index("tensor"), lax.axis_index("segment")
    where = jnp.stack([t & 1, segment]).astype(jnp.int32)
    weights = scaled_weights(segment_weight[0], norm_gain)
    teacher = teacher_rows[0].swapaxes(1, 2)
    entering_t, fresh_t = entering[0].T, fresh_rows[0].T

    mine_block = projection.T
    first = z_gather(entering_t)
    other_block, first = together(zl_swap(mine_block), first)
    blocks = gather(stack(mine_block, other_block), "segment", Y_GROUPS)
    own = x_gather(first)
    (out0,) = tick(first_tick_kernel, (PIECE,), where, own, core_swap(own), weights, entering_t)

    shifted = lax.ppermute(out0, "segment", [(i, i + 1) for i in range(15)])
    mine = jnp.where(segment == 0, fresh_t, shifted)
    own = x_gather(stack(z_gather(mine), out0))
    out1, both, following = tick(
        second_tick_kernel, (PIECE, 2 * PIECE, RIDE), where, own, core_swap(own), weights, mine, out0
    )

    turned = transposition(both)
    first_own = z_gather(following)
    turned, blocks, first_own = together(turned, blocks, first_own)
    rows = lax.all_gather(turned, "tensor", axis=0, tiled=True)
    own = x_gather(first_own.reshape(NZ, RIDE, ROWS)[:, :PIECE].reshape(COLUMN, ROWS))
    difference = predict(where, first_own, core_swap(first_own), own, core_swap(own), blocks, teacher)

    pair = stack(difference, over_y(difference, lambda y: y ^ 1))
    second = over_y(pair, other_neighbour)
    third = over_y(second, lambda y: y ^ 1)
    fourth = over_y(second, lambda y: y + 2 if y % 2 == 0 else y - 2)
    keep, send = gradient(where, (pair, second, third, fourth), rows)
    total = keep + zl_swap(send).astype(jnp.float32)
    return (out1.T[None], total.T)


def solution(mesh):
    return jax.shard_map(
        on_device,
        mesh=mesh,
        in_specs=(
            P("segment", None, "tensor"),
            P(None, None, "tensor"),
            P("segment", None),
            P("segment", "tensor", None),
            P("segment", "tensor"),
            P("segment", None, None, "tensor"),
        ),
        out_specs=(P("segment", None, "tensor"), P("segment", "tensor")),
        check_vma=False,
    )
```

time: 238 us -> 219 us (0.920)
  the two profiles are of different devices: /device:TPU:258 before, /device:TPU:1 now
where the time goes in v5:
time: 219 us; the launch traced here: 217 us
  blocking collectives  104 us (47%)
  starting transfers between devices  47.4 us (22%)
  waiting for transfers between devices  32.7 us (15%)
  between operations  14.2 us (6%)
  Pallas kernels  9.68 us (4%)
  other arithmetic  4.86 us (2%)
  local copies, waits for them, and re-layouts  4.53 us (2%)
    all_gather x6, blocking collectives, gather(): lax.all_gather(value, axis, axis=0, tiled=True, axis_index_groups=groups)  104 us
    ppermute x4, starting transfers between devices, over_tensor(): lax.ppermute(value, 'tensor', [(t_index(*p), t_index(*move(*p))) for p in...  25.4 us
    ppermute x4, waiting for transfers between devices, over_y(): lax.ppermute(value, 'segment', [(y * 2 + zl, move(y) % NY * 2 + zl) for y...  22.7 us
    ppermute x4, starting transfers between devices, over_y(): lax.ppermute(value, 'segment', [(y * 2 + zl, move(y) % NY * 2 + zl) for y...  13.2 us
    ppermute x2, starting transfers between devices, zl_swap(): return lax.ppermute(value, 'segment', [(i, i ^ 1) for i in range(16)])  6.75 us
    pallas_call x2, Pallas kernels, tick(): pl.pallas_call(kernel, out_shape=[jax.ShapeDtypeStruct((rows, ROWS), jnp....  4.77 us
    ppermute x2, waiting for transfers between devices, zl_swap(): return lax.ppermute(value, 'segment', [(i, i ^ 1) for i in range(16)])  4.75 us
    unnamed x12, local copies, waits for them, and re-layouts  4.52 us
  transfers between devices with their start and end apart: 14, of which 8 were waited for; matrix products, arithmetic and copies ran while one was open for 1% of the time, Pallas kernels for 3%

profile of v5, /device:TPU:1, one launch (start us, length us, event | category | flops | bytes accessed | tf_op | source)
XLA Modules:
  0.0 217.5 jit_solution(4401952377076809582)
XLA Ops:
  7.2 4.8 %collective-permute-start = (bf16[288,384]{1,0:T(8,128)(2,1)}, bf16[288,384]{1,0:T(8,128)(2,1)S(1)}, u32[]{:S(2)}, u32[]{:S(2)}) collective-permute-start(bf16[288,384]{1,0:T(8,128)(2,1)} %bitcast.29), channel_id=1, source_target_pairs={{0,32},{32,0},{64,96},{96,64},{128,160},{160,128},{192,224},{224,1... | collective-permute-start | bytes 663560 | tf_op jit(solution)/shard_map/ppermute | solution.py:51
  12.0 19.2 %all_gather.24 = bf16[768,128]{1,0:T(8,128)(2,1)S(1)} all-gather(bf16[192,128]{1,0:T(8,128)(2,1)} %bitcast.25), channel_id=1, replica_groups={{0,8,16,24},{1,9,17,25},{2,10,18,26},{3,11,19,27},{4,12,20,28},{5,13,21..., dimensions={0}, use_global_device_ids=true | all-gather | bytes 245760 | tf_op jit(solution)/shard_map/all_gather | solution.py:74
  31.3 1.7 pad_maximum_fusion
  33.1 11.1 %all_gather.25.own_ref = bf16[3072,128]{1,0:T(8,128)(2,1)S(1)} all-gather(bf16[768,128]{1,0:T(8,128)(2,1)S(1)} %all_gather.24), channel_id=1, replica_groups={{0,2,4,6},{1,3,5,7},{8,10,12,14},{9,11,13,15},{16,18,20,22},{17,19,21,2..., dimensions={0}, use_global_device_ids=true | all-gather | bytes 983040 | tf_op jit(solution)/shard_map/all_gather | solution.py:74
  44.2 8.7 %collective-permute-start.1 = (bf16[3072,128]{1,0:T(8,128)(2,1)S(1)}, bf16[3072,128]{1,0:T(8,128)(2,1)}, u32[]{:S(2)}, u32[]{:S(2)}) collective-permute-start(bf16[3072,128]{1,0:T(8,128)(2,1)S(1)} %all_gather.25.own_ref), channel_id=1, source_target_pairs={{0,1},{1,0},{2,3},{3,2},{4,5},{5,4},{6,7},{7,6},{8,9},{9,8},{10,11... | collective-permute-start | bytes 2359304 | tf_op jit(solution)/shard_map/ppermute | solution.py:37
  53.0 2.2 %fusion.weight_ref = bf16[192,6144]{1,0:T(8,128)(2,1)S(1)} fusion(bf16[1,192,6144]{2,1,0:T(8,128)(2,1)} %param.9, f32[6144]{0:T(1024)} %bitcast.31), kind=kLoop, calls=%fused_computation.1 | loop fusion | flops 3538944 | bytes 4743168 | tf_op jit(solution)/shard_map/convert_element_type | solution.py:102
  55.3 2.4 %tick.2.before_ref = bf16[192,128]{1,0:T(8,128)(2,1)S(1)} custom-call(s32[2]{0:T(128)S(1)} %pad_add_fusion.where_ref, bf16[3072,128]{1,0:T(8,128)(2,1)S(1)} %all_gather.25.own_ref, bf16[3072,128]{1,0:T(8,128)(2,1)} %collective-permute-done.1.other_ref, bf16[192,6144]{1,0:T(8,128)(2,1)S(1)} %fusion.weight_ref, bf16[192,128]{1,0:T(8,128)(2,1)S(1)} %bitcast.26), custom_call_target="tpu_custom_call" | custom-call | tf_op jit(solution)/shard_map/tick/pallas_call | solution.py:146
  57.6 1.3 collective-permute-start.2
  60.1 11.9 %all_gather.26 = bf16[768,128]{1,0:T(8,128)(2,1)S(1)} all-gather(bf16[192,128]{1,0:T(8,128)(2,1)S(1)} %bitcast_select_fusion.mine_ref), channel_id=1, replica_groups={{0,8,16,24},{1,9,17,25},{2,10,18,26},{3,11,19,27},{4,12,20,28},{5,13,21..., dimensions={0}, use_global_device_ids=true | all-gather | bytes 245760 | tf_op jit(solution)/shard_map/all_gather | solution.py:74
  72.0 12.4 %all_gather.27.own_ref = bf16[3840,128]{1,0:T(8,128)(2,1)S(1)} all-gather(bf16[960,128]{1,0:T(8,128)(2,1)S(1)} %pad_maximum_fusion.2), channel_id=1, replica_groups={{0,2,4,6},{1,3,5,7},{8,10,12,14},{9,11,13,15},{16,18,20,22},{17,19,21,2..., dimensions={0}, use_global_device_ids=true | all-gather | bytes 1228800 | tf_op jit(solution)/shard_map/all_gather | solution.py:74
  84.4 7.9 %collective-permute-start.3 = (bf16[3840,128]{1,0:T(8,128)(2,1)S(1)}, bf16[3840,128]{1,0:T(8,128)(2,1)S(1)}, u32[]{:S(2)}, u32[]{:S(2)}) collective-permute-start(bf16[3840,128]{1,0:T(8,128)(2,1)S(1)} %all_gather.27.own_ref), channel_id=1, source_target_pairs={{0,1},{1,0},{2,3},{3,2},{4,5},{5,4},{6,7},{7,6},{8,9},{9,8},{10,11... | collective-permute-start | bytes 2949128 | tf_op jit(solution)/shard_map/ppermute | solution.py:37
  92.3 2.2 collective-permute-done.3.other_ref
  94.5 2.4 %tick.3 = (bf16[192,128]{1,0:T(8,128)(2,1)}, bf16[384,128]{1,0:T(8,128)(2,1)S(1)}, bf16[960,128]{1,0:T(8,128)(2,1)S(1)}) custom-call(s32[2]{0:T(128)S(1)} %pad_add_fusion.where_ref, bf16[3840,128]{1,0:T(8,128)(2,1)S(1)} %all_gather.27.own_ref, bf16[3840,128]{1,0:T(8,128)(2,1)S(1)} %collective-permute-done.3.other_ref, bf16[192,6144]{1,0:T(8,128)(2,1)S(1)} %fusion.weight_ref, ...), custom_call_target="tpu_custom_call" | custom-call | tf_op jit(solution)/shard_map/tick/pallas_call | solution.py:146
  97.5 38.0 %all_gather.29.first_own_ref = bf16[3840,128]{1,0:T(8,128)(2,1)S(1)} all-gather(bf16[960,128]{1,0:T(8,128)(2,1)S(1)} %get-tuple-element.16), channel_id=1, replica_groups={{0,8,16,24},{1,9,17,25},{2,10,18,26},{3,11,19,27},{4,12,20,28},{5,13,21..., dimensions={0}, use_global_device_ids=true | all-gather | bytes 1228800 | tf_op jit(solution)/shard_map/all_gather | solution.py:74
  136.2 3.4 %collective-permute-start.5 = (bf16[3840,128]{1,0:T(8,128)(2,1)S(1)}, bf16[3840,128]{1,0:T(8,128)(2,1)S(1)}, u32[]{:S(2)}, u32[]{:S(2)}) collective-permute-start(bf16[3840,128]{1,0:T(8,128)(2,1)S(1)} %all_gather.29.first_own_ref), channel_id=1, source_target_pairs={{0,1},{1,0},{2,3},{3,2},{4,5},{5,4},{6,7},{7,6},{8,9},{9,8},{10,11... | collective-permute-start | bytes 2949128 | tf_op jit(solution)/shard_map/ppermute | solution.py:37
  139.6 11.5 %all_gather.30.own_ref = bf16[3072,128]{1,0:T(8,128)(2,1)S(1)} all-gather(bf16[768,128]{1,0:T(8,128)(2,1)S(1)} %bitcast.28), channel_id=1, replica_groups={{0,2,4,6},{1,3,5,7},{8,10,12,14},{9,11,13,15},{16,18,20,22},{17,19,21,2..., dimensions={0}, use_global_device_ids=true | all-gather | bytes 983040 | tf_op jit(solution)/shard_map/all_gather | solution.py:74
  151.1 5.4 %collective-permute-start.6 = (bf16[3072,128]{1,0:T(8,128)(2,1)S(1)}, bf16[3072,128]{1,0:T(8,128)(2,1)S(1)}, u32[]{:S(2)}, u32[]{:S(2)}) collective-permute-start(bf16[3072,128]{1,0:T(8,128)(2,1)S(1)} %all_gather.30.own_ref), channel_id=1, source_target_pairs={{0,1},{1,0},{2,3},{3,2},{4,5},{5,4},{6,7},{7,6},{8,9},{9,8},{10,11... | collective-permute-start | bytes 2359304 | tf_op jit(solution)/shard_map/ppermute | solution.py:37
  156.5 1.9 collective-permute-done.6.other_ref
  158.4 2.0 copy-done
  160.4 2.5 %predict.1 = bf16[576,128]{1,0:T(8,128)(2,1)S(1)} custom-call(s32[2]{0:T(128)S(1)} %pad_add_fusion.where_ref, bf16[3840,128]{1,0:T(8,128)(2,1)S(1)} %all_gather.29.first_own_ref, bf16[3840,128]{1,0:T(8,128)(2,1)S(1)} %collective-permute-done.5.first_other_ref, bf16[3072,128]{1,0:T(8,128)(2,1)S(1)} %all_gather.30.own_ref, ...), custom_call_target="tpu_custom_call" | custom-call | tf_op jit(solution)/shard_map/predict/pallas_call | solution.py:186
  162.9 1.9 collective-permute-start.7
  164.8 5.0 %collective-permute-done.7 = bf16[576,128]{1,0:T(8,128)(2,1)S(1)} collective-permute-done((bf16[576,128]{1,0:T(8,128)(2,1)S(1)}, bf16[576,128]{1,0:T(8,128)(2,1)S(1)}, u32[]{:S(2)}, u32[]{:S(2)}) %collective-permute-start.7) | collective-permute-done | bytes 147488 | tf_op jit(solution)/shard_map/ppermute | solution.py:41
  169.9 5.2 %collective-permute-start.8 = (bf16[1152,128]{1,0:T(8,128)(2,1)S(1)}, bf16[1152,128]{1,0:T(8,128)(2,1)S(1)}, u32[]{:S(2)}, u32[]{:S(2)}) collective-permute-start(bf16[1152,128]{1,0:T(8,128)(2,1)S(1)} %pad_maximum_fusion.1.refs_0_), channel_id=1, source_target_pairs={{0,448},{32,480},{64,128},{96,160},{128,64},{160,96},{192,256},{22... | collective-permute-start | bytes 884744 | tf_op jit(solution)/shard_map/ppermute | solution.py:41
  175.1 6.6 %collective-permute-done.8.refs_1_ = bf16[1152,128]{1,0:T(8,128)(2,1)S(1)} collective-permute-done((bf16[1152,128]{1,0:T(8,128)(2,1)S(1)}, bf16[1152,128]{1,0:T(8,128)(2,1)S(1)}, u32[]{:S(2)}, u32[]{:S(2)}) %collective-permute-start.8) | collective-permute-done | bytes 294944 | tf_op jit(solution)/shard_map/ppermute | solution.py:41
  181.7 1.9 collective-permute-start.9
  183.6 4.2 %collective-permute-start.10 = (bf16[1152,128]{1,0:T(8,128)(2,1)S(1)}, bf16[1152,128]{1,0:T(8,128)(2,1)S(1)}, u32[]{:S(2)}, u32[]{:S(2)}) collective-permute-start(bf16[1152,128]{1,0:T(8,128)(2,1)S(1)} %collective-permute-done.8.refs_1_), channel_id=1, source_target_pairs={{0,128},{32,160},{64,448},{96,480},{128,256},{160,288},{192,64},{2... | collective-permute-start | bytes 884744 | tf_op jit(solution)/shard_map/ppermute | solution.py:41
  187.8 3.1 %collective-permute-done.9.refs_2_ = bf16[1152,128]{1,0:T(8,128)(2,1)S(1)} collective-permute-done((bf16[1152,128]{1,0:T(8,128)(2,1)S(1)}, bf16[1152,128]{1,0:T(8,128)(2,1)S(1)}, u32[]{:S(2)}, u32[]{:S(2)}) %collective-permute-start.9) | collective-permute-done | bytes 294944 | tf_op jit(solution)/shard_map/ppermute | solution.py:41
  190.8 8.0 %collective-permute-done.10.refs_3_ = bf16[1152,128]{1,0:T(8,128)(2,1)S(1)} collective-permute-done((bf16[1152,128]{1,0:T(8,128)(2,1)S(1)}, bf16[1152,128]{1,0:T(8,128)(2,1)S(1)}, u32[]{:S(2)}, u32[]{:S(2)}) %collective-permute-start.10) | collective-permute-done | bytes 294944 | tf_op jit(solution)/shard_map/ppermute | solution.py:41
  198.8 1.9 copy-done.1
  200.7 2.4 %gradient.1 = (f32[288,384]{1,0:T(8,128)S(1)}, bf16[288,384]{1,0:T(8,128)(2,1)S(1)}) custom-call(s32[2]{0:T(128)S(1)} %pad_add_fusion.where_ref, bf16[1152,128]{1,0:T(8,128)(2,1)S(1)} %pad_maximum_fusion.1.refs_0_, bf16[1152,128]{1,0:T(8,128)(2,1)S(1)} %collective-permute-done.8.refs_1_, bf16[1152,128]{1,0:T(8,128)(2,1)S(1)} %collective-permute-done.9.refs_2_, ...), custom_call_target="tpu_custom_call" | custom-call | tf_op jit(solution)/shard_map/gradient/pallas_call | solution.py:223
  203.2 1.9 collective-permute-start.11
  205.1 4.7 %collective-permute-done.11 = bf16[288,384]{1,0:T(8,128)(2,1)S(1)} collective-permute-done((bf16[288,384]{1,0:T(8,128)(2,1)S(1)}, bf16[288,384]{1,0:T(8,128)(2,1)S(1)}, u32[]{:S(2)}, u32[]{:S(2)}) %collective-permute-start.11) | collective-permute-done | bytes 221216 | tf_op jit(solution)/shard_map/ppermute | solution.py:51
  (28 shorter events, 3.5 us)
Async XLA Ops:
  7.2 128.4 %all-gather.3.cloned.1.call-start = ((), (), s32[]{:S(2)}) async-start(), calls=%async_computation | async-start | bytes 3981312 | tf_op jit(solution)/shard_map/all_gather | solution.py:74
  7.2 24.1 %collective-permute-start = (bf16[288,384]{1,0:T(8,128)(2,1)}, bf16[288,384]{1,0:T(8,128)(2,1)S(1)}, u32[]{:S(2)}, u32[]{:S(2)}) collective-permute-start(bf16[288,384]{1,0:T(8,128)(2,1)} %bitcast.29), channel_id=1, source_target_pairs={{0,32},{32,0},{64,96},{96,64},{128,160},{160,128},{192,224},{224,1... | collective-permute-start | bytes 663560 | tf_op jit(solution)/shard_map/ppermute | solution.py:51
  33.0 22.2 %copy-start.2 = (bf16[1,128,192]{1,2,0:T(8,128)(2,1)S(1)}, bf16[1,128,192]{1,2,0:T(8,128)(2,1)}, u32[]{:S(2)}) copy-start(bf16[1,128,192]{1,2,0:T(8,128)(2,1)} %param.6) | copy-start | bytes 147460
  33.1 165.8 %all-gather.5.cloned.1.call-start = ((), (), s32[]{:S(2)}) async-start(), calls=%async_computation.1 | async-start | bytes 3244032 | tf_op jit(solution)/shard_map/all_gather | solution.py:262
  44.2 11.0 %collective-permute-start.1 = (bf16[3072,128]{1,0:T(8,128)(2,1)S(1)}, bf16[3072,128]{1,0:T(8,128)(2,1)}, u32[]{:S(2)}, u32[]{:S(2)}) collective-permute-start(bf16[3072,128]{1,0:T(8,128)(2,1)S(1)} %all_gather.25.own_ref), channel_id=1, source_target_pairs={{0,1},{1,0},{2,3},{3,2},{4,5},{5,4},{6,7},{7,6},{8,9},{9,8},{10,11... | collective-permute-start | bytes 2359304 | tf_op jit(solution)/shard_map/ppermute | solution.py:37
  55.2 4.9 %copy-start.5 = (bf16[1,128,192]{1,2,0:T(8,128)(2,1)S(1)}, bf16[1,128,192]{1,2,0:T(8,128)(2,1)}, u32[]{:S(2)}) copy-start(bf16[1,128,192]{1,2,0:T(8,128)(2,1)} %param.7) | copy-start | bytes 147460
  57.6 2.5 %collective-permute-start.2 = (bf16[192,128]{1,0:T(8,128)(2,1)S(1)}, bf16[192,128]{1,0:T(8,128)(2,1)S(1)}, u32[]{:S(2)}, u32[]{:S(2)}) collective-permute-start(bf16[192,128]{1,0:T(8,128)(2,1)S(1)} %tick.2.before_ref), channel_id=1, source_target_pairs={{0,32},{32,64},{64,96},{96,128},{128,160},{160,192},{192,224},{224... | collective-permute-start | bytes 147464 | tf_op jit(solution)/shard_map/ppermute | solution.py:252
  84.4 74.1 %copy-start.3 = (bf16[1,2,128,288]{2,3,1,0:T(8,128)(2,1)S(1)}, bf16[1,2,128,288]{2,3,1,0:T(8,128)(2,1)}, u32[]{:S(2)}) copy-start(bf16[1,2,128,288]{2,3,1,0:T(8,128)(2,1)} %param.11) | copy-start | bytes 442372
  84.4 10.1 %collective-permute-start.3 = (bf16[3840,128]{1,0:T(8,128)(2,1)S(1)}, bf16[3840,128]{1,0:T(8,128)(2,1)S(1)}, u32[]{:S(2)}, u32[]{:S(2)}) collective-permute-start(bf16[3840,128]{1,0:T(8,128)(2,1)S(1)} %all_gather.27.own_ref), channel_id=1, source_target_pairs={{0,1},{1,0},{2,3},{3,2},{4,5},{5,4},{6,7},{7,6},{8,9},{9,8},{10,11... | collective-permute-start | bytes 2949128 | tf_op jit(solution)/shard_map/ppermute | solution.py:37
  96.9 38.7 %collective-permute-start.4 = (bf16[384,128]{1,0:T(8,128)(2,1)S(1)}, bf16[384,128]{1,0:T(8,128)(2,1)S(1)}, u32[]{:S(2)}, u32[]{:S(2)}) collective-permute-start(bf16[384,128]{1,0:T(8,128)(2,1)S(1)} %get-tuple-element.14), channel_id=1, source_target_pairs={{0,0},{1,1},{2,2},{3,3},{4,64},{5,65},{6,66},{7,67},{8,128},{9,129... | collective-permute-start | bytes 294920 | tf_op jit(solution)/shard_map/ppermute | solution.py:62
  135.5 0.6 copy-start.4
  136.2 22.2 %collective-permute-start.5 = (bf16[3840,128]{1,0:T(8,128)(2,1)S(1)}, bf16[3840,128]{1,0:T(8,128)(2,1)S(1)}, u32[]{:S(2)}, u32[]{:S(2)}) collective-permute-start(bf16[3840,128]{1,0:T(8,128)(2,1)S(1)} %all_gather.29.first_own_ref), channel_id=1, source_target_pairs={{0,1},{1,0},{2,3},{3,2},{4,5},{5,4},{6,7},{7,6},{8,9},{9,8},{10,11... | collective-permute-start | bytes 2949128 | tf_op jit(solution)/shard_map/ppermute | solution.py:37
  151.1 7.3 %collective-permute-start.6 = (bf16[3072,128]{1,0:T(8,128)(2,1)S(1)}, bf16[3072,128]{1,0:T(8,128)(2,1)S(1)}, u32[]{:S(2)}, u32[]{:S(2)}) collective-permute-start(bf16[3072,128]{1,0:T(8,128)(2,1)S(1)} %all_gather.30.own_ref), channel_id=1, source_target_pairs={{0,1},{1,0},{2,3},{3,2},{4,5},{5,4},{6,7},{7,6},{8,9},{9,8},{10,11... | collective-permute-start | bytes 2359304 | tf_op jit(solution)/shard_map/ppermute | solution.py:37
  158.4 2.0 copy-start
  162.9 7.0 %collective-permute-start.7 = (bf16[576,128]{1,0:T(8,128)(2,1)S(1)}, bf16[576,128]{1,0:T(8,128)(2,1)S(1)}, u32[]{:S(2)}, u32[]{:S(2)}) collective-permute-start(bf16[576,128]{1,0:T(8,128)(2,1)S(1)} %predict.1), channel_id=1, source_target_pairs={{0,64},{32,96},{64,0},{96,32},{128,192},{160,224},{192,128},{224,1... | collective-permute-start | bytes 442376 | tf_op jit(solution)/shard_map/ppermute | solution.py:41
  169.9 11.8 %collective-permute-start.8 = (bf16[1152,128]{1,0:T(8,128)(2,1)S(1)}, bf16[1152,128]{1,0:T(8,128)(2,1)S(1)}, u32[]{:S(2)}, u32[]{:S(2)}) collective-permute-start(bf16[1152,128]{1,0:T(8,128)(2,1)S(1)} %pad_maximum_fusion.1.refs_0_), channel_id=1, source_target_pairs={{0,448},{32,480},{64,128},{96,160},{128,64},{160,96},{192,256},{22... | collective-permute-start | bytes 884744 | tf_op jit(solution)/shard_map/ppermute | solution.py:41
  181.7 9.2 %collective-permute-start.9 = (bf16[1152,128]{1,0:T(8,128)(2,1)S(1)}, bf16[1152,128]{1,0:T(8,128)(2,1)S(1)}, u32[]{:S(2)}, u32[]{:S(2)}) collective-permute-start(bf16[1152,128]{1,0:T(8,128)(2,1)S(1)} %collective-permute-done.8.refs_1_), channel_id=1, source_target_pairs={{0,64},{32,96},{64,0},{96,32},{128,192},{160,224},{192,128},{224,1... | collective-permute-start | bytes 884744 | tf_op jit(solution)/shard_map/ppermute | solution.py:41
  183.6 15.2 %collective-permute-start.10 = (bf16[1152,128]{1,0:T(8,128)(2,1)S(1)}, bf16[1152,128]{1,0:T(8,128)(2,1)S(1)}, u32[]{:S(2)}, u32[]{:S(2)}) collective-permute-start(bf16[1152,128]{1,0:T(8,128)(2,1)S(1)} %collective-permute-done.8.refs_1_), channel_id=1, source_target_pairs={{0,128},{32,160},{64,448},{96,480},{128,256},{160,288},{192,64},{2... | collective-permute-start | bytes 884744 | tf_op jit(solution)/shard_map/ppermute | solution.py:41
  198.8 1.9 copy-start.1
  203.2 6.7 %collective-permute-start.11 = (bf16[288,384]{1,0:T(8,128)(2,1)S(1)}, bf16[288,384]{1,0:T(8,128)(2,1)S(1)}, u32[]{:S(2)}, u32[]{:S(2)}) collective-permute-start(bf16[288,384]{1,0:T(8,128)(2,1)S(1)} %get-tuple-element.21), channel_id=1, source_target_pairs={{0,32},{32,0},{64,96},{96,64},{128,160},{160,128},{192,224},{224,1... | collective-permute-start | bytes 663560 | tf_op jit(solution)/shard_map/ppermute | solution.py:51
Sparse Core Ops, SparseCore 0:
  33.2 52.1 all-gather.2
  136.3 60.9 all-gather.4

commit v6 on v5

--- a/solution.py
+++ b/solution.py
@@ -29,6 +29,7 @@
 
 
 Z_GROUPS = [[t_index(z, x, c) for z in range(NZ)] for x in range(NX) for c in range(NC)]
+SECOND_Y_GROUPS = [[(2 * i + p) * 2 + zl for i in range(NY // 2)] for p in range(2) for zl in range(2)]
 Y_GROUPS = [[y * 2 + zl for y in range(NY)] for zl in range(2)]
 X_GROUPS = [[t_index(z, x, c) for x in range(NX)] for z in range(NZ) for c in range(NC)]
 
@@ -84,18 +85,6 @@
 
 def whole(shape):
     return pl.BlockSpec(shape, lambda i: (0,) * len(shape))
-
-
-def other_neighbour(y):
-    return y - 1 if y % 2 == 0 else y + 1
-
-
-def y_labels(y):
-    def other(v):
-        return lax.rem(v + jnp.where(lax.rem(v, 2) == 0, NY - 1, 1), NY)
-
-    away = lax.rem(y + jnp.where(lax.rem(y, 2) == 0, NY - 2, 2), NY)
-    return y, other(y), other(y ^ 1), other(away)
 
 
 def scaled_weights(weights, gain):
@@ -130,12 +119,10 @@
 
 
 def second_tick_kernel(
-    where_ref, own_ref, other_ref, weight_ref, mine_ref, before_ref, out_ref, both_ref, next_ref, full
+    where_ref, own_ref, other_ref, weight_ref, mine_ref, out_ref, next_ref, full
 ):
     out = hidden_rows(where_ref, own_ref, other_ref, weight_ref, mine_ref, full)
     out_ref[...] = out
-    both_ref[:PIECE, :] = before_ref[...]
-    both_ref[PIECE:, :] = out
     next_ref[:PIECE, :] = out
     for x in range(NX):
         source = x * RIDE + COLUMN
@@ -195,8 +182,7 @@
     )(where, *operands)
 
 
-def gradient_kernel(where_ref, *refs):
-    diffs, (rows_ref, keep_ref, send_ref, rows) = refs[:4], refs[4:]
+def gradient_kernel(where_ref, near_ref, far_ref, rows_ref, keep_ref, send_ref, rows):
     segment = where_ref[1]
     for z, x, c in all_t():
         start = ((x & 1) * 2 + c) * PIECE
@@ -204,22 +190,22 @@
             source = (t_index(z, x, c) * TICKS + tau) * PIECE
             columns = slice(tau * ROWS, (tau + 1) * ROWS)
             rows[z * 2 + (x >> 1), start : start + PIECE, columns] = rows_ref[source : source + PIECE, :]
-    half = segment & 1
+    half, parity = segment & 1, (segment >> 1) & 1
     for part, out_ref in ((half ^ 1, send_ref), (half, keep_ref)):
         total = jnp.zeros((COLS, BLOCK), jnp.float32)
-        for ref, y in zip(diffs, y_labels(segment >> 1), strict=True):
-            for i in range(2):
+        for ref, p in ((near_ref, parity), (far_ref, parity ^ 1)):
+            for i in range(NY // 2):
                 both = [ref[(i * TICKS + tau) * COLS : (i * TICKS + tau + 1) * COLS, :] for tau in range(TICKS)]
                 total += lax.dot_general(
                     jnp.concatenate(both, axis=1),
-                    rows[y ^ i, pl.ds(pl.multiple_of(part * BLOCK, BLOCK), BLOCK), :],
+                    rows[2 * i + p, pl.ds(pl.multiple_of(part * BLOCK, BLOCK), BLOCK), :],
                     (((1,), (1,)), ((), ())),
                     preferred_element_type=jnp.float32,
                 )
         out_ref[...] = (total * (1.0 / (TICKS * ROWS))).astype(out_ref.dtype)
 
 
-def gradient(where, diffs, rows):
+def gradient(where, *operands):
     return pl.pallas_call(
         gradient_kernel,
         out_shape=(
@@ -227,12 +213,12 @@
             jax.ShapeDtypeStruct((COLS, BLOCK), jnp.bfloat16),
         ),
         grid=(1,),
-        in_specs=[SMEM_SPEC] + [whole(v.shape) for v in (*diffs, rows)],
+        in_specs=[SMEM_SPEC] + [whole(v.shape) for v in operands],
         out_specs=(whole((COLS, BLOCK)), whole((COLS, BLOCK))),
         scratch_shapes=[pltpu.VMEM((NY, 2 * BLOCK, TICKS * ROWS), jnp.bfloat16)],
         compiler_params=pltpu.CompilerParams(vmem_limit_bytes=VMEM_LIMIT),
         name="gradient",
-    )(where, *diffs, rows)
+    )(where, *operands)
 
 
 def on_device(entering, fresh_rows, norm_gain, segment_weight, projection, teacher_rows):
@@ -251,23 +237,19 @@
 
     shifted = lax.ppermute(out0, "segment", [(i, i + 1) for i in range(15)])
     mine = jnp.where(segment == 0, fresh_t, shifted)
-    own = x_gather(stack(z_gather(mine), out0))
-    out1, both, following = tick(
-        second_tick_kernel, (PIECE, 2 * PIECE, RIDE), where, own, core_swap(own), weights, mine, out0
-    )
-
-    turned = transposition(both)
+    column = z_gather(mine)
+    turned0 = transposition(together(out0, column)[0])
+    own = x_gather(stack(column, out0))
+    out1, following = tick(second_tick_kernel, (PIECE, RIDE), where, own, core_swap(own), weights, mine)
+
     first_own = z_gather(following)
-    turned, blocks, first_own = together(turned, blocks, first_own)
+    turned, blocks, first_own = together(stack(turned0, transposition(out1)), blocks, first_own)
     rows = lax.all_gather(turned, "tensor", axis=0, tiled=True)
     own = x_gather(first_own.reshape(NZ, RIDE, ROWS)[:, :PIECE].reshape(COLUMN, ROWS))
     difference = predict(where, first_own, core_swap(first_own), own, core_swap(own), blocks, teacher)
 
-    pair = stack(difference, over_y(difference, lambda y: y ^ 1))
-    second = over_y(pair, other_neighbour)
-    third = over_y(second, lambda y: y ^ 1)
-    fourth = over_y(second, lambda y: y + 2 if y % 2 == 0 else y - 2)
-    keep, send = gradient(where, (pair, second, third, fourth), rows)
+    near = gather(difference, "segment", SECOND_Y_GROUPS)
+    keep, send = gradient(where, near, over_y(near, lambda y: y ^ 1), rows)
     total = keep + zl_swap(send).astype(jnp.float32)
     return (out1.T[None], total.T)
 

time: 219 us -> 219 us (level)
  blocking collectives: 104 us -> 119 us
  starting transfers between devices: 47.4 us -> 39.2 us
  waiting for transfers between devices: 32.7 us -> 27.4 us
    all_gather x6 -> x7, blocking collectives: 104 us -> 119 us  [gather(): lax.all_gather(value, axis, axis=0, tiled=True, axis_index_groups=groups)]
    ppermute x4 -> x1, starting transfers between devices: 13.2 us -> 1.91 us  [over_y(): lax.ppermute(value, 'segment', [(y * 2 + zl, move(y) % NY * 2 + zl) for y...]
    ppermute x4 -> x1, waiting for transfers between devices: 22.7 us -> 12.5 us  [over_y(): lax.ppermute(value, 'segment', [(y * 2 + zl, move(y) % NY * 2 + zl) for y...]
    all_gather x1, waiting for transfers between devices: 0.01 us -> 3.56 us  [on_device(): rows = lax.all_gather(turned, 'tensor', axis=0, tiled=True)]
    unnamed x12 -> x10, local copies, waits for them, and re-layouts: 4.52 us -> 3.9 us
  transfers between devices with their start and end apart: 14 -> 12, of which waited for: 8 -> 6; matrix products, arithmetic and copies ran while one was open for 1% -> 1% of each run, Pallas kernels for 3% -> 3%
where the time goes in v6:
time: 219 us
  blocking collectives  119 us (54%)
  starting transfers between devices  39.2 us (18%)
  waiting for transfers between devices  27.4 us (13%)
  between operations  14.2 us (6%)
  Pallas kernels  9.68 us (4%)
  other arithmetic  5.48 us (3%)
  local copies, waits for them, and re-layouts  3.92 us (2%)
    all_gather x7, blocking collectives, gather(): lax.all_gather(value, axis, axis=0, tiled=True, axis_index_groups=groups)  119 us
    ppermute x4, starting transfers between devices, over_tensor(): lax.ppermute(value, 'tensor', [(t_index(*p), t_index(*move(*p))) for p in...  27 us
    ppermute x1, waiting for transfers between devices, over_y(): lax.ppermute(value, 'segment', [(y * 2 + zl, move(y) % NY * 2 + zl) for y...  12.5 us
    ppermute x2, starting transfers between devices, zl_swap(): return lax.ppermute(value, 'segment', [(i, i ^ 1) for i in range(16)])  6.75 us
    ppermute x2, waiting for transfers between devices, zl_swap(): return lax.ppermute(value, 'segment', [(i, i ^ 1) for i in range(16)])  6.75 us
    pallas_call x2, Pallas kernels, tick(): pl.pallas_call(kernel, out_shape=[jax.ShapeDtypeStruct((rows, ROWS), jnp....  4.77 us
  transfers between devices with their start and end apart: 12, of which 6 were waited for; matrix products, arithmetic and copies ran while one was open for 1% of the time, Pallas kernels for 3%

profile of v6, /device:TPU:1, one launch (start us, length us, event | category | flops | bytes accessed | tf_op | source)
XLA Modules:
  0.0 218.8 jit_solution(2241064251793382324)
XLA Ops:
  7.2 4.8 %collective-permute-start = (bf16[288,384]{1,0:T(8,128)(2,1)}, bf16[288,384]{1,0:T(8,128)(2,1)S(1)}, u32[]{:S(2)}, u32[]{:S(2)}) collective-permute-start(bf16[288,384]{1,0:T(8,128)(2,1)} %bitcast.29), channel_id=1, source_target_pairs={{0,32},{32,0},{64,96},{96,64},{128,160},{160,128},{192,224},{224,1... | collective-permute-start | bytes 663560 | tf_op jit(solution)/shard_map/ppermute | solution.py:52
  12.0 19.2 %all_gather.27 = bf16[768,128]{1,0:T(8,128)(2,1)S(1)} all-gather(bf16[192,128]{1,0:T(8,128)(2,1)} %bitcast.25), channel_id=1, replica_groups={{0,8,16,24},{1,9,17,25},{2,10,18,26},{3,11,19,27},{4,12,20,28},{5,13,21..., dimensions={0}, use_global_device_ids=true | all-gather | bytes 245760 | tf_op jit(solution)/shard_map/all_gather | solution.py:75
  31.3 1.7 pad_maximum_fusion
  33.1 11.1 %all_gather.28.own_ref = bf16[3072,128]{1,0:T(8,128)(2,1)S(1)} all-gather(bf16[768,128]{1,0:T(8,128)(2,1)S(1)} %all_gather.27), channel_id=1, replica_groups={{0,2,4,6},{1,3,5,7},{8,10,12,14},{9,11,13,15},{16,18,20,22},{17,19,21,2..., dimensions={0}, use_global_device_ids=true | all-gather | bytes 983040 | tf_op jit(solution)/shard_map/all_gather | solution.py:75
  44.2 8.7 %collective-permute-start.1 = (bf16[3072,128]{1,0:T(8,128)(2,1)S(1)}, bf16[3072,128]{1,0:T(8,128)(2,1)}, u32[]{:S(2)}, u32[]{:S(2)}) collective-permute-start(bf16[3072,128]{1,0:T(8,128)(2,1)S(1)} %all_gather.28.own_ref), channel_id=1, source_target_pairs={{0,1},{1,0},{2,3},{3,2},{4,5},{5,4},{6,7},{7,6},{8,9},{9,8},{10,11... | collective-permute-start | bytes 2359304 | tf_op jit(solution)/shard_map/ppermute | solution.py:38
  53.0 2.2 fusion.weight_ref
  55.3 2.4 %tick.2 = bf16[192,128]{1,0:T(8,128)(2,1)S(1)} custom-call(s32[2]{0:T(128)S(1)} %pad_add_fusion.where_ref, bf16[3072,128]{1,0:T(8,128)(2,1)S(1)} %all_gather.28.own_ref, bf16[3072,128]{1,0:T(8,128)(2,1)} %collective-permute-done.1.other_ref, bf16[192,6144]{1,0:T(8,128)(2,1)S(1)} %fusion.weight_ref, bf16[192,128]{1,0:T(8,128)(2,1)S(1)} %bitcast.26), custom_call_target="tpu_custom_call" | custom-call | tf_op jit(solution)/shard_map/tick/pallas_call | solution.py:133
  57.6 1.3 collective-permute-start.2
  58.9 1.2 collective-permute-done.2
  60.1 11.9 %all_gather.29 = bf16[768,128]{1,0:T(8,128)(2,1)S(1)} all-gather(bf16[192,128]{1,0:T(8,128)(2,1)S(1)} %bitcast_select_fusion.mine_ref), channel_id=1, replica_groups={{0,8,16,24},{1,9,17,25},{2,10,18,26},{3,11,19,27},{4,12,20,28},{5,13,21..., dimensions={0}, use_global_device_ids=true | all-gather | bytes 245760 | tf_op jit(solution)/shard_map/all_gather | solution.py:75
  72.0 12.4 %all_gather.30.own_ref = bf16[3840,128]{1,0:T(8,128)(2,1)S(1)} all-gather(bf16[960,128]{1,0:T(8,128)(2,1)S(1)} %pad_maximum_fusion.1), channel_id=1, replica_groups={{0,2,4,6},{1,3,5,7},{8,10,12,14},{9,11,13,15},{16,18,20,22},{17,19,21,2..., dimensions={0}, use_global_device_ids=true | all-gather | bytes 1228800 | tf_op jit(solution)/shard_map/all_gather | solution.py:75
  84.4 7.9 %collective-permute-start.3 = (bf16[3840,128]{1,0:T(8,128)(2,1)S(1)}, bf16[3840,128]{1,0:T(8,128)(2,1)S(1)}, u32[]{:S(2)}, u32[]{:S(2)}) collective-permute-start(bf16[3840,128]{1,0:T(8,128)(2,1)S(1)} %all_gather.30.own_ref), channel_id=1, source_target_pairs={{0,1},{1,0},{2,3},{3,2},{4,5},{5,4},{6,7},{7,6},{8,9},{9,8},{10,11... | collective-permute-start | bytes 2949128 | tf_op jit(solution)/shard_map/ppermute | solution.py:38
  92.3 0.7 collective-permute-start.4
  93.0 1.5 collective-permute-done.3.other_ref
  94.5 2.4 %tick.3 = (bf16[192,128]{1,0:T(8,128)(2,1)}, bf16[960,128]{1,0:T(8,128)(2,1)S(1)}) custom-call(s32[2]{0:T(128)S(1)} %pad_add_fusion.where_ref, bf16[3840,128]{1,0:T(8,128)(2,1)S(1)} %all_gather.30.own_ref, bf16[3840,128]{1,0:T(8,128)(2,1)S(1)} %collective-permute-done.3.other_ref, bf16[192,6144]{1,0:T(8,128)(2,1)S(1)} %fusion.weight_ref, ...), custom_call_target="tpu_custom_call" | custom-call | tf_op jit(solution)/shard_map/tick/pallas_call | solution.py:133
  96.9 1.4 collective-permute-start.5
  98.3 35.5 %all_gather.32.first_own_ref = bf16[3840,128]{1,0:T(8,128)(2,1)S(1)} all-gather(bf16[960,128]{1,0:T(8,128)(2,1)S(1)} %get-tuple-element.16), channel_id=1, replica_groups={{0,8,16,24},{1,9,17,25},{2,10,18,26},{3,11,19,27},{4,12,20,28},{5,13,21..., dimensions={0}, use_global_device_ids=true | all-gather | bytes 1228800 | tf_op jit(solution)/shard_map/all_gather | solution.py:75
  134.5 5.4 %collective-permute-start.6 = (bf16[3840,128]{1,0:T(8,128)(2,1)S(1)}, bf16[3840,128]{1,0:T(8,128)(2,1)S(1)}, u32[]{:S(2)}, u32[]{:S(2)}) collective-permute-start(bf16[3840,128]{1,0:T(8,128)(2,1)S(1)} %all_gather.32.first_own_ref), channel_id=1, source_target_pairs={{0,1},{1,0},{2,3},{3,2},{4,5},{5,4},{6,7},{7,6},{8,9},{9,8},{10,11... | collective-permute-start | bytes 2949128 | tf_op jit(solution)/shard_map/ppermute | solution.py:38
  140.0 11.5 %all_gather.33.own_ref = bf16[3072,128]{1,0:T(8,128)(2,1)S(1)} all-gather(bf16[768,128]{1,0:T(8,128)(2,1)S(1)} %bitcast.28), channel_id=1, replica_groups={{0,2,4,6},{1,3,5,7},{8,10,12,14},{9,11,13,15},{16,18,20,22},{17,19,21,2..., dimensions={0}, use_global_device_ids=true | all-gather | bytes 983040 | tf_op jit(solution)/shard_map/all_gather | solution.py:75
  151.5 4.9 %collective-permute-start.7 = (bf16[3072,128]{1,0:T(8,128)(2,1)S(1)}, bf16[3072,128]{1,0:T(8,128)(2,1)S(1)}, u32[]{:S(2)}, u32[]{:S(2)}) collective-permute-start(bf16[3072,128]{1,0:T(8,128)(2,1)S(1)} %all_gather.33.own_ref), channel_id=1, source_target_pairs={{0,1},{1,0},{2,3},{3,2},{4,5},{5,4},{6,7},{7,6},{8,9},{9,8},{10,11... | collective-permute-start | bytes 2359304 | tf_op jit(solution)/shard_map/ppermute | solution.py:38
  156.4 1.9 collective-permute-done.7.other_ref
  158.3 2.0 copy-done
  160.3 2.5 %predict.1 = bf16[576,128]{1,0:T(8,128)(2,1)S(1)} custom-call(s32[2]{0:T(128)S(1)} %pad_add_fusion.where_ref, bf16[3840,128]{1,0:T(8,128)(2,1)S(1)} %all_gather.32.first_own_ref, bf16[3840,128]{1,0:T(8,128)(2,1)S(1)} %collective-permute-done.6.first_other_ref, bf16[3072,128]{1,0:T(8,128)(2,1)S(1)} %all_gather.33.own_ref, ...), custom_call_target="tpu_custom_call" | custom-call | tf_op jit(solution)/shard_map/predict/pallas_call | solution.py:173
  162.8 17.3 %all_gather.34.near_ref = bf16[2304,128]{1,0:T(8,128)(2,1)S(1)} all-gather(bf16[576,128]{1,0:T(8,128)(2,1)S(1)} %predict.1), channel_id=1, replica_groups={{0,128,256,384},{32,160,288,416},{64,192,320,448},{96,224,352,480},{1,1..., dimensions={0}, use_global_device_ids=true | all-gather | bytes 737280 | tf_op jit(solution)/shard_map/all_gather | solution.py:75
  180.1 1.9 collective-permute-start.8
  182.0 12.5 %collective-permute-done.8.far_ref = bf16[2304,128]{1,0:T(8,128)(2,1)S(1)} collective-permute-done((bf16[2304,128]{1,0:T(8,128)(2,1)S(1)}, bf16[2304,128]{1,0:T(8,128)(2,1)S(1)}, u32[]{:S(2)}, u32[]{:S(2)}) %collective-permute-start.8) | collective-permute-done | bytes 589856 | tf_op jit(solution)/shard_map/ppermute | solution.py:42
  194.6 3.6 %all-gather.5.cloned.1.call-done.rows_ref = bf16[12288,128]{1,0:T(8,128)(2,1)} async-done(((bf16[384,128]{1,0:T(8,128)(2,1)}), bf16[12288,128]{1,0:T(8,128)(2,1)}) %all-gather.5.cloned.1.call-update) | async-done | bytes 3145744 | tf_op jit(solution)/shard_map/all_gather | solution.py:247
  198.2 1.9 copy-done.1
  200.0 2.5 %gradient.1 = (f32[288,384]{1,0:T(8,128)S(1)}, bf16[288,384]{1,0:T(8,128)(2,1)S(1)}) custom-call(s32[2]{0:T(128)S(1)} %pad_add_fusion.where_ref, bf16[2304,128]{1,0:T(8,128)(2,1)S(1)} %all_gather.34.near_ref, bf16[2304,128]{1,0:T(8,128)(2,1)S(1)} %collective-permute-done.8.far_ref, bf16[12288,128]{1,0:T(8,128)(2,1)S(1)} %copy-done.1), custom_call_target="tpu_custom_call" | custom-call | tf_op jit(solution)/shard_map/gradient/pallas_call | solution.py:209
  202.5 1.9 collective-permute-start.9
  204.4 6.7 %collective-permute-done.9 = bf16[288,384]{1,0:T(8,128)(2,1)S(1)} collective-permute-done((bf16[288,384]{1,0:T(8,128)(2,1)S(1)}, bf16[288,384]{1,0:T(8,128)(2,1)S(1)}, u32[]{:S(2)}, u32[]{:S(2)}) %collective-permute-start.9) | collective-permute-done | bytes 221216 | tf_op jit(solution)/shard_map/ppermute | solution.py:52
  211.2 0.8 add_bitcast_fusion
  (23 shorter events, 0.9 us)
Async XLA Ops:
  7.2 127.3 %all-gather.3.cloned.1.call-start = ((), (), s32[]{:S(2)}) async-start(), calls=%async_computation | async-start | bytes 3981312 | tf_op jit(solution)/shard_map/all_gather | solution.py:75
  7.2 24.1 %collective-permute-start = (bf16[288,384]{1,0:T(8,128)(2,1)}, bf16[288,384]{1,0:T(8,128)(2,1)S(1)}, u32[]{:S(2)}, u32[]{:S(2)}) collective-permute-start(bf16[288,384]{1,0:T(8,128)(2,1)} %bitcast.29), channel_id=1, source_target_pairs={{0,32},{32,0},{64,96},{96,64},{128,160},{160,128},{192,224},{224,1... | collective-permute-start | bytes 663560 | tf_op jit(solution)/shard_map/ppermute | solution.py:52
  33.0 22.2 %copy-start.2 = (bf16[1,128,192]{1,2,0:T(8,128)(2,1)S(1)}, bf16[1,128,192]{1,2,0:T(8,128)(2,1)}, u32[]{:S(2)}) copy-start(bf16[1,128,192]{1,2,0:T(8,128)(2,1)} %param.6) | copy-start | bytes 147460
  33.1 165.1 %all-gather.5.cloned.1.call-start = ((), (), s32[]{:S(2)}) async-start(), calls=%async_computation.1 | async-start | bytes 3244032 | tf_op jit(solution)/shard_map/all_gather | solution.py:247
  44.2 11.0 %collective-permute-start.1 = (bf16[3072,128]{1,0:T(8,128)(2,1)S(1)}, bf16[3072,128]{1,0:T(8,128)(2,1)}, u32[]{:S(2)}, u32[]{:S(2)}) collective-permute-start(bf16[3072,128]{1,0:T(8,128)(2,1)S(1)} %all_gather.28.own_ref), channel_id=1, source_target_pairs={{0,1},{1,0},{2,3},{3,2},{4,5},{5,4},{6,7},{7,6},{8,9},{9,8},{10,11... | collective-permute-start | bytes 2359304 | tf_op jit(solution)/shard_map/ppermute | solution.py:38
  55.2 4.9 %copy-start.4 = (bf16[1,128,192]{1,2,0:T(8,128)(2,1)S(1)}, bf16[1,128,192]{1,2,0:T(8,128)(2,1)}, u32[]{:S(2)}) copy-start(bf16[1,128,192]{1,2,0:T(8,128)(2,1)} %param.7) | copy-start | bytes 147460
  57.6 2.5 %collective-permute-start.2 = (bf16[192,128]{1,0:T(8,128)(2,1)S(1)}, bf16[192,128]{1,0:T(8,128)(2,1)S(1)}, u32[]{:S(2)}, u32[]{:S(2)}) collective-permute-start(bf16[192,128]{1,0:T(8,128)(2,1)S(1)} %tick.2), channel_id=1, source_target_pairs={{0,32},{32,64},{64,96},{96,128},{128,160},{160,192},{192,224},{224... | collective-permute-start | bytes 147464 | tf_op jit(solution)/shard_map/ppermute | solution.py:238
  84.4 74.0 %copy-start.3 = (bf16[1,2,128,288]{2,3,1,0:T(8,128)(2,1)S(1)}, bf16[1,2,128,288]{2,3,1,0:T(8,128)(2,1)}, u32[]{:S(2)}) copy-start(bf16[1,2,128,288]{2,3,1,0:T(8,128)(2,1)} %param.11) | copy-start | bytes 442372
  84.4 10.1 %collective-permute-start.3 = (bf16[3840,128]{1,0:T(8,128)(2,1)S(1)}, bf16[3840,128]{1,0:T(8,128)(2,1)S(1)}, u32[]{:S(2)}, u32[]{:S(2)}) collective-permute-start(bf16[3840,128]{1,0:T(8,128)(2,1)S(1)} %all_gather.30.own_ref), channel_id=1, source_target_pairs={{0,1},{1,0},{2,3},{3,2},{4,5},{5,4},{6,7},{7,6},{8,9},{9,8},{10,11... | collective-permute-start | bytes 2949128 | tf_op jit(solution)/shard_map/ppermute | solution.py:38
  92.3 41.5 %collective-permute-start.4 = (bf16[192,128]{1,0:T(8,128)(2,1)S(1)}, bf16[192,128]{1,0:T(8,128)(2,1)S(1)}, u32[]{:S(2)}, u32[]{:S(2)}) collective-permute-start(bf16[192,128]{1,0:T(8,128)(2,1)S(1)} %tick.2), channel_id=1, source_target_pairs={{0,0},{1,1},{2,2},{3,3},{4,64},{5,65},{6,66},{7,67},{8,128},{9,129... | collective-permute-start | bytes 147464 | tf_op jit(solution)/shard_map/ppermute | solution.py:63
  96.9 37.0 %collective-permute-start.5 = (bf16[192,128]{1,0:T(8,128)(2,1)}, bf16[192,128]{1,0:T(8,128)(2,1)S(1)}, u32[]{:S(2)}, u32[]{:S(2)}) collective-permute-start(bf16[192,128]{1,0:T(8,128)(2,1)} %get-tuple-element.13), channel_id=1, source_target_pairs={{0,0},{1,1},{2,2},{3,3},{4,64},{5,65},{6,66},{7,67},{8,128},{9,129... | collective-permute-start | bytes 147464 | tf_op jit(solution)/shard_map/ppermute | solution.py:63
  134.5 23.8 %collective-permute-start.6 = (bf16[3840,128]{1,0:T(8,128)(2,1)S(1)}, bf16[3840,128]{1,0:T(8,128)(2,1)S(1)}, u32[]{:S(2)}, u32[]{:S(2)}) collective-permute-start(bf16[3840,128]{1,0:T(8,128)(2,1)S(1)} %all_gather.32.first_own_ref), channel_id=1, source_target_pairs={{0,1},{1,0},{2,3},{3,2},{4,5},{5,4},{6,7},{7,6},{8,9},{9,8},{10,11... | collective-permute-start | bytes 2949128 | tf_op jit(solution)/shard_map/ppermute | solution.py:38
  151.5 6.8 %collective-permute-start.7 = (bf16[3072,128]{1,0:T(8,128)(2,1)S(1)}, bf16[3072,128]{1,0:T(8,128)(2,1)S(1)}, u32[]{:S(2)}, u32[]{:S(2)}) collective-permute-start(bf16[3072,128]{1,0:T(8,128)(2,1)S(1)} %all_gather.33.own_ref), channel_id=1, source_target_pairs={{0,1},{1,0},{2,3},{3,2},{4,5},{5,4},{6,7},{7,6},{8,9},{9,8},{10,11... | collective-permute-start | bytes 2359304 | tf_op jit(solution)/shard_map/ppermute | solution.py:38
  158.3 2.0 copy-start
  180.1 14.5 %collective-permute-start.8 = (bf16[2304,128]{1,0:T(8,128)(2,1)S(1)}, bf16[2304,128]{1,0:T(8,128)(2,1)S(1)}, u32[]{:S(2)}, u32[]{:S(2)}) collective-permute-start(bf16[2304,128]{1,0:T(8,128)(2,1)S(1)} %all_gather.34.near_ref), channel_id=1, source_target_pairs={{0,64},{32,96},{64,0},{96,32},{128,192},{160,224},{192,128},{224,1... | collective-permute-start | bytes 1769480 | tf_op jit(solution)/shard_map/ppermute | solution.py:42
  198.2 1.9 copy-start.1
  202.5 8.7 %collective-permute-start.9 = (bf16[288,384]{1,0:T(8,128)(2,1)S(1)}, bf16[288,384]{1,0:T(8,128)(2,1)S(1)}, u32[]{:S(2)}, u32[]{:S(2)}) collective-permute-start(bf16[288,384]{1,0:T(8,128)(2,1)S(1)} %get-tuple-element.21), channel_id=1, source_target_pairs={{0,32},{32,0},{64,96},{96,64},{128,160},{160,128},{192,224},{224,1... | collective-permute-start | bytes 663560 | tf_op jit(solution)/shard_map/ppermute | solution.py:52
Sparse Core Ops, SparseCore 0:
  33.2 52.1 all-gather.2
  134.7 63.4 all-gather.4

commit v7 on v6

--- a/solution.py
+++ b/solution.py
@@ -29,6 +29,7 @@
 
 
 Z_GROUPS = [[t_index(z, x, c) for z in range(NZ)] for x in range(NX) for c in range(NC)]
+ZC_GROUPS = [[t_index(z, x, c) for z in range(NZ) for c in range(NC)] for x in range(NX)]
 SECOND_Y_GROUPS = [[(2 * i + p) * 2 + zl for i in range(NY // 2)] for p in range(2) for zl in range(2)]
 Y_GROUPS = [[y * 2 + zl for y in range(NY)] for zl in range(2)]
 X_GROUPS = [[t_index(z, x, c) for x in range(NX)] for z in range(NZ) for c in range(NC)]
@@ -142,7 +143,7 @@
 
 
 def predict_kernel(
-    where_ref, first_own_ref, first_other_ref, own_ref, other_ref, block_ref, teacher_ref, out_ref, full
+    where_ref, first_own_ref, first_other_ref, own_ref, other_ref, teacher_ref, block_ref, out_ref, full
 ):
     core, segment = where_ref[0], where_ref[1]
     for ref, c in ((first_own_ref, core), (first_other_ref, core ^ 1)):
@@ -153,7 +154,7 @@
     for ref, c in ((own_ref, core), (other_ref, core ^ 1)):
         for x in range(NX):
             for z in range(NZ):
-                source = (x * NZ + z) * PIECE
+                source = x * RIDE + z * PIECE
                 full[pl.ds(feature_start(z, x, c), PIECE), ROWS:] = ref[source : source + PIECE, :]
     total = jnp.zeros((COLS, TICKS * ROWS), jnp.float32)
     for y in range(NY):
@@ -182,26 +183,28 @@
     )(where, *operands)
 
 
-def gradient_kernel(where_ref, near_ref, far_ref, rows_ref, keep_ref, send_ref, rows):
+def gradient_kernel(
+    where_ref, near_ref, low_ref, high_ref, rows0_ref, rows1_ref, keep_ref, send_ref, rows
+):
     segment = where_ref[1]
     for z, x, c in all_t():
-        start = ((x & 1) * 2 + c) * PIECE
-        for tau in range(TICKS):
-            source = (t_index(z, x, c) * TICKS + tau) * PIECE
-            columns = slice(tau * ROWS, (tau + 1) * ROWS)
-            rows[z * 2 + (x >> 1), start : start + PIECE, columns] = rows_ref[source : source + PIECE, :]
+        y, start = z * 2 + (x >> 1), ((x & 1) * 2 + c) * PIECE
+        source0, source1 = t_index(z, x, c) * PIECE, ((z * NC + c) * NX + x) * PIECE
+        rows[y, start : start + PIECE, :ROWS] = rows0_ref[source0 : source0 + PIECE, :]
+        rows[y, start : start + PIECE, ROWS:] = rows1_ref[source1 : source1 + PIECE, :]
     half, parity = segment & 1, (segment >> 1) & 1
+    held = [(near_ref, i, i, parity) for i in range(NY // 2)]
+    held += [(low_ref, i, i, parity ^ 1) for i in range(2)] + [(high_ref, i, i + 2, parity ^ 1) for i in range(2)]
     for part, out_ref in ((half ^ 1, send_ref), (half, keep_ref)):
         total = jnp.zeros((COLS, BLOCK), jnp.float32)
-        for ref, p in ((near_ref, parity), (far_ref, parity ^ 1)):
-            for i in range(NY // 2):
-                both = [ref[(i * TICKS + tau) * COLS : (i * TICKS + tau + 1) * COLS, :] for tau in range(TICKS)]
-                total += lax.dot_general(
-                    jnp.concatenate(both, axis=1),
-                    rows[2 * i + p, pl.ds(pl.multiple_of(part * BLOCK, BLOCK), BLOCK), :],
-                    (((1,), (1,)), ((), ())),
-                    preferred_element_type=jnp.float32,
-                )
+        for ref, k, i, p in held:
+            both = [ref[(k * TICKS + tau) * COLS : (k * TICKS + tau + 1) * COLS, :] for tau in range(TICKS)]
+            total += lax.dot_general(
+                jnp.concatenate(both, axis=1),
+                rows[2 * i + p, pl.ds(pl.multiple_of(part * BLOCK, BLOCK), BLOCK), :],
+                (((1,), (1,)), ((), ())),
+                preferred_element_type=jnp.float32,
+            )
         out_ref[...] = (total * (1.0 / (TICKS * ROWS))).astype(out_ref.dtype)
 
 
@@ -238,18 +241,25 @@
     shifted = lax.ppermute(out0, "segment", [(i, i + 1) for i in range(15)])
     mine = jnp.where(segment == 0, fresh_t, shifted)
     column = z_gather(mine)
-    turned0 = transposition(together(out0, column)[0])
     own = x_gather(stack(column, out0))
+    turned0, own = together(transposition(out0), own)
+    rows0 = lax.all_gather(turned0, "tensor", axis=0, tiled=True)
     out1, following = tick(second_tick_kernel, (PIECE, RIDE), where, own, core_swap(own), weights, mine)
 
     first_own = z_gather(following)
-    turned, blocks, first_own = together(stack(turned0, transposition(out1)), blocks, first_own)
-    rows = lax.all_gather(turned, "tensor", axis=0, tiled=True)
-    own = x_gather(first_own.reshape(NZ, RIDE, ROWS)[:, :PIECE].reshape(COLUMN, ROWS))
-    difference = predict(where, first_own, core_swap(first_own), own, core_swap(own), blocks, teacher)
+    turned1, blocks, first_own = together(transposition(out1), blocks, first_own)
+    column = first_own.reshape(NZ, RIDE, ROWS)[:, :PIECE].reshape(COLUMN, ROWS)
+    own, first_other = together(x_gather(stack(column, turned1)), core_swap(first_own))
+    other = core_swap(own)
+    columns1, _ = together(own.reshape(NX, RIDE, ROWS)[:, COLUMN:].reshape(COLUMN, ROWS), other)
+    rows1 = gather(columns1, "tensor", ZC_GROUPS)
+    difference = predict(where, first_own, first_other, own, other, teacher, blocks)
 
     near = gather(difference, "segment", SECOND_Y_GROUPS)
-    keep, send = gradient(where, near, over_y(near, lambda y: y ^ 1), rows)
+    middle = TICKS * TICKS * COLS
+    low = over_y(near[:middle], lambda y: y ^ 1)
+    high = over_y(near[middle:], lambda y: y - 1 if y % 2 == 0 else y + 1)
+    keep, send = gradient(where, near, low, high, rows0, rows1)
     total = keep + zl_swap(send).astype(jnp.float32)
     return (out1.T[None], total.T)
 

time: 219 us -> 222 us (1.014)
  waiting for transfers between devices: 27.4 us -> 15.6 us
  blocking collectives: 119 us -> 125 us
  starting transfers between devices: 39.2 us -> 43.4 us
  local copies, waits for them, and re-layouts: 3.92 us -> 7.73 us
    all_gather x7, blocking collectives: 119 us -> 125 us  [gather(): lax.all_gather(value, axis, axis=0, tiled=True, axis_index_groups=groups)]
    ppermute x1 -> x2, starting transfers between devices: 1.91 us -> 7.65 us  [over_y(): lax.ppermute(value, 'segment', [(y * 2 + zl, move(y) % NY * 2 + zl) for y...]
    ppermute x1 -> x2, waiting for transfers between devices: 12.5 us -> 7.28 us  [over_y(): lax.ppermute(value, 'segment', [(y * 2 + zl, move(y) % NY * 2 + zl) for y...]
    ppermute x4, starting transfers between devices: 27 us -> 22.8 us  [over_tensor(): lax.ppermute(value, 'tensor', [(t_index(*p), t_index(*move(*p))) for p in...]
    all_gather x1, waiting for transfers between devices: 3.56 us -> 0.02 us  [on_device(): rows0 = lax.all_gather(turned0, 'tensor', axis=0, tiled=True)]
    unnamed x10 -> x20, local copies, waits for them, and re-layouts: 3.9 us -> 6.99 us
    ppermute x2, waiting for transfers between devices: 6.75 us -> 4.09 us  [zl_swap(): return lax.ppermute(value, 'segment', [(i, i ^ 1) for i in range(16)])]
    ppermute x2, starting transfers between devices: 6.75 us -> 9.23 us  [zl_swap(): return lax.ppermute(value, 'segment', [(i, i ^ 1) for i in range(16)])]
  transfers between devices with their start and end apart: 12 -> 14, of which waited for: 6 -> 6; matrix products, arithmetic and copies ran while one was open for 1% -> 1% of each run, Pallas kernels for 3% -> 4%
where the time goes in v7:
time: 222 us; the launch traced here: 221 us
  blocking collectives  125 us (56%)
  starting transfers between devices  43.4 us (20%)
  waiting for transfers between devices  15.6 us (7%)
  between operations  14 us (6%)
  Pallas kernels  10.3 us (5%)
  local copies, waits for them, and re-layouts  7.73 us (3%)
  other arithmetic  4.85 us (2%)
    all_gather x7, blocking collectives, gather(): lax.all_gather(value, axis, axis=0, tiled=True, axis_index_groups=groups)  125 us
    ppermute x4, starting transfers between devices, over_tensor(): lax.ppermute(value, 'tensor', [(t_index(*p), t_index(*move(*p))) for p in...  22.8 us
    ppermute x2, starting transfers between devices, zl_swap(): return lax.ppermute(value, 'segment', [(i, i ^ 1) for i in range(16)])  9.23 us
    ppermute x2, starting transfers between devices, over_y(): lax.ppermute(value, 'segment', [(y * 2 + zl, move(y) % NY * 2 + zl) for y...  7.65 us
    ppermute x2, waiting for transfers between devices, over_y(): lax.ppermute(value, 'segment', [(y * 2 + zl, move(y) % NY * 2 + zl) for y...  7.28 us
    unnamed x20, local copies, waits for them, and re-layouts  6.99 us
    pallas_call x2, Pallas kernels, tick(): pl.pallas_call(kernel, out_shape=[jax.ShapeDtypeStruct((rows, ROWS), jnp....  5.42 us
  transfers between devices with their start and end apart: 14, of which 6 were waited for; matrix products, arithmetic and copies ran while one was open for 1% of the time, Pallas kernels for 4%

profile of v7, /device:TPU:1, one launch (start us, length us, event | category | flops | bytes accessed | tf_op | source)
XLA Modules:
  0.0 221.0 jit_solution(7759845618063552354)
XLA Ops:
  7.2 4.8 %collective-permute-start = (bf16[288,384]{1,0:T(8,128)(2,1)}, bf16[288,384]{1,0:T(8,128)(2,1)S(1)}, u32[]{:S(2)}, u32[]{:S(2)}) collective-permute-start(bf16[288,384]{1,0:T(8,128)(2,1)} %bitcast.33), channel_id=1, source_target_pairs={{0,32},{32,0},{64,96},{96,64},{128,160},{160,128},{192,224},{224,1... | collective-permute-start | bytes 663560 | tf_op jit(solution)/shard_map/ppermute | solution.py:53
  12.1 19.2 %all_gather.30 = bf16[768,128]{1,0:T(8,128)(2,1)S(1)} all-gather(bf16[192,128]{1,0:T(8,128)(2,1)} %bitcast.28), channel_id=1, replica_groups={{0,8,16,24},{1,9,17,25},{2,10,18,26},{3,11,19,27},{4,12,20,28},{5,13,21..., dimensions={0}, use_global_device_ids=true | all-gather | bytes 245760 | tf_op jit(solution)/shard_map/all_gather | solution.py:76
  31.3 1.7 pad_maximum_fusion
  33.1 11.1 %all_gather.31.own_ref = bf16[3072,128]{1,0:T(8,128)(2,1)S(1)} all-gather(bf16[768,128]{1,0:T(8,128)(2,1)S(1)} %all_gather.30), channel_id=1, replica_groups={{0,2,4,6},{1,3,5,7},{8,10,12,14},{9,11,13,15},{16,18,20,22},{17,19,21,2..., dimensions={0}, use_global_device_ids=true | all-gather | bytes 983040 | tf_op jit(solution)/shard_map/all_gather | solution.py:76
  44.2 8.7 %collective-permute-start.1 = (bf16[3072,128]{1,0:T(8,128)(2,1)S(1)}, bf16[3072,128]{1,0:T(8,128)(2,1)}, u32[]{:S(2)}, u32[]{:S(2)}) collective-permute-start(bf16[3072,128]{1,0:T(8,128)(2,1)S(1)} %all_gather.31.own_ref), channel_id=1, source_target_pairs={{0,1},{1,0},{2,3},{3,2},{4,5},{5,4},{6,7},{7,6},{8,9},{9,8},{10,11... | collective-permute-start | bytes 2359304 | tf_op jit(solution)/shard_map/ppermute | solution.py:39
  53.0 2.2 fusion.weight_ref
  55.3 2.4 %tick.2 = bf16[192,128]{1,0:T(8,128)(2,1)S(1)} custom-call(s32[2]{0:T(128)S(1)} %pad_add_fusion.where_ref, bf16[3072,128]{1,0:T(8,128)(2,1)S(1)} %all_gather.31.own_ref, bf16[3072,128]{1,0:T(8,128)(2,1)} %collective-permute-done.1.other_ref, bf16[192,6144]{1,0:T(8,128)(2,1)S(1)} %fusion.weight_ref, bf16[192,128]{1,0:T(8,128)(2,1)S(1)} %bitcast.29), custom_call_target="tpu_custom_call" | custom-call | tf_op jit(solution)/shard_map/tick/pallas_call | solution.py:134
  57.6 1.3 collective-permute-start.3
  60.1 22.2 %all_gather.32 = bf16[768,128]{1,0:T(8,128)(2,1)S(1)} all-gather(bf16[192,128]{1,0:T(8,128)(2,1)S(1)} %bitcast_select_fusion.mine_ref), channel_id=1, replica_groups={{0,8,16,24},{1,9,17,25},{2,10,18,26},{3,11,19,27},{4,12,20,28},{5,13,21..., dimensions={0}, use_global_device_ids=true | all-gather | bytes 245760 | tf_op jit(solution)/shard_map/all_gather | solution.py:76
  82.3 12.6 %all_gather.33.own_ref = bf16[3840,128]{1,0:T(8,128)(2,1)S(1)} all-gather(bf16[960,128]{1,0:T(8,128)(2,1)S(1)} %pad_maximum_fusion.1), channel_id=1, replica_groups={{0,2,4,6},{1,3,5,7},{8,10,12,14},{9,11,13,15},{16,18,20,22},{17,19,21,2..., dimensions={0}, use_global_device_ids=true | all-gather | bytes 1228800 | tf_op jit(solution)/shard_map/all_gather | solution.py:76
  94.9 5.9 %collective-permute-start.4 = (bf16[3840,128]{1,0:T(8,128)(2,1)S(1)}, bf16[3840,128]{1,0:T(8,128)(2,1)}, u32[]{:S(2)}, u32[]{:S(2)}) collective-permute-start(bf16[3840,128]{1,0:T(8,128)(2,1)S(1)} %all_gather.33.own_ref), channel_id=1, source_target_pairs={{0,1},{1,0},{2,3},{3,2},{4,5},{5,4},{6,7},{7,6},{8,9},{9,8},{10,11... | collective-permute-start | bytes 2949128 | tf_op jit(solution)/shard_map/ppermute | solution.py:39
  100.9 2.2 %collective-permute-done.4.other_ref = bf16[3840,128]{1,0:T(8,128)(2,1)} collective-permute-done((bf16[3840,128]{1,0:T(8,128)(2,1)S(1)}, bf16[3840,128]{1,0:T(8,128)(2,1)}, u32[]{:S(2)}, u32[]{:S(2)}) %collective-permute-start.4) | collective-permute-done | bytes 983072 | tf_op jit(solution)/shard_map/ppermute | solution.py:39
  103.2 3.1 %tick.3 = (bf16[192,128]{1,0:T(8,128)(2,1)}, bf16[960,128]{1,0:T(8,128)(2,1)S(1)}) custom-call(s32[2]{0:T(128)S(1)} %pad_add_fusion.where_ref, bf16[3840,128]{1,0:T(8,128)(2,1)S(1)} %all_gather.33.own_ref, bf16[3840,128]{1,0:T(8,128)(2,1)} %collective-permute-done.4.other_ref, bf16[192,6144]{1,0:T(8,128)(2,1)S(1)} %fusion.weight_ref, ...), custom_call_target="tpu_custom_call" | custom-call | tf_op jit(solution)/shard_map/tick/pallas_call | solution.py:134
  106.2 1.6 collective-permute-start.5
  107.8 27.8 %all_gather.35.first_own_ref = bf16[3840,128]{1,0:T(8,128)(2,1)S(1)} all-gather(bf16[960,128]{1,0:T(8,128)(2,1)S(1)} %get-tuple-element.20), channel_id=1, replica_groups={{0,8,16,24},{1,9,17,25},{2,10,18,26},{3,11,19,27},{4,12,20,28},{5,13,21..., dimensions={0}, use_global_device_ids=true | all-gather | bytes 1228800 | tf_op jit(solution)/shard_map/all_gather | solution.py:76
  135.6 5.0 %collective-permute-start.6 = (bf16[3840,128]{1,0:T(8,128)(2,1)S(1)}, bf16[3840,128]{1,0:T(8,128)(2,1)S(1)}, u32[]{:S(2)}, u32[]{:S(2)}) collective-permute-start(bf16[3840,128]{1,0:T(8,128)(2,1)S(1)} %all_gather.35.first_own_ref), channel_id=1, source_target_pairs={{0,1},{1,0},{2,3},{3,2},{4,5},{5,4},{6,7},{7,6},{8,9},{9,8},{10,11... | collective-permute-start | bytes 2949128 | tf_op jit(solution)/shard_map/ppermute | solution.py:39
  140.7 15.1 %all_gather.36.own_ref = bf16[3840,128]{1,0:T(8,128)(2,1)S(1)} all-gather(bf16[960,128]{1,0:T(8,128)(2,1)S(1)} %pad_maximum_fusion.2), channel_id=1, replica_groups={{0,2,4,6},{1,3,5,7},{8,10,12,14},{9,11,13,15},{16,18,20,22},{17,19,21,2..., dimensions={0}, use_global_device_ids=true | all-gather | bytes 1228800 | tf_op jit(solution)/shard_map/all_gather | solution.py:76
  155.8 3.2 %collective-permute-start.7 = (bf16[3840,128]{1,0:T(8,128)(2,1)S(1)}, bf16[3840,128]{1,0:T(8,128)(2,1)S(1)}, u32[]{:S(2)}, u32[]{:S(2)}) collective-permute-start(bf16[3840,128]{1,0:T(8,128)(2,1)S(1)} %all_gather.36.own_ref), channel_id=1, source_target_pairs={{0,1},{1,0},{2,3},{3,2},{4,5},{5,4},{6,7},{7,6},{8,9},{9,8},{10,11... | collective-permute-start | bytes 2949128 | tf_op jit(solution)/shard_map/ppermute | solution.py:39
  159.6 1.5 collective-permute-done.7.other_ref
  162.1 2.0 copy-done
  164.1 1.2 copy-done.4
  165.3 2.5 %predict.1 = bf16[576,128]{1,0:T(8,128)(2,1)S(1)} custom-call(s32[2]{0:T(128)S(1)} %pad_add_fusion.where_ref, bf16[3840,128]{1,0:T(8,128)(2,1)S(1)} %all_gather.35.first_own_ref, bf16[3840,128]{1,0:T(8,128)(2,1)S(1)} %collective-permute-done.6.first_other_ref, bf16[3840,128]{1,0:T(8,128)(2,1)S(1)} %all_gather.36.own_ref, bf16[3840,128]{1,0:T(8,128)(2,1)S(1)} %copy-done.4, ...), custom_call_target="tpu_custom_call" | custom-call | tf_op jit(solution)/shard_map/predict/pallas_call | solution.py:174
  167.8 17.1 %all_gather.37.near_ref = bf16[2304,128]{1,0:T(8,128)(2,1)S(1)} all-gather(bf16[576,128]{1,0:T(8,128)(2,1)S(1)} %predict.1), channel_id=1, replica_groups={{0,128,256,384},{32,160,288,416},{64,192,320,448},{96,224,352,480},{1,1..., dimensions={0}, use_global_device_ids=true | all-gather | bytes 737280 | tf_op jit(solution)/shard_map/all_gather | solution.py:76
  184.9 4.5 %collective-permute-start.8 = (bf16[1152,128]{1,0:T(8,128)(2,1)S(1)}, bf16[1152,128]{1,0:T(8,128)(2,1)S(1)}, u32[]{:S(2)}, u32[]{:S(2)}) collective-permute-start(bf16[1152,128]{1,0:T(8,128)(2,1)S(1)} %get-tuple-element.31), channel_id=1, source_target_pairs={{0,64},{32,96},{64,0},{96,32},{128,192},{160,224},{192,128},{224,1... | collective-permute-start | bytes 884744 | tf_op jit(solution)/shard_map/ppermute | solution.py:43
  189.5 3.1 %collective-permute-start.9 = (bf16[1152,128]{1,0:T(8,128)(2,1)S(1)}, bf16[1152,128]{1,0:T(8,128)(2,1)S(1)}, u32[]{:S(2)}, u32[]{:S(2)}) collective-permute-start(bf16[1152,128]{1,0:T(8,128)(2,1)S(1)} %get-tuple-element.30), channel_id=1, source_target_pairs={{0,448},{32,480},{64,128},{96,160},{128,64},{160,96},{192,256},{22... | collective-permute-start | bytes 884744 | tf_op jit(solution)/shard_map/ppermute | solution.py:43
  192.6 2.6 %collective-permute-done.8.low_ref = bf16[1152,128]{1,0:T(8,128)(2,1)S(1)} collective-permute-done((bf16[1152,128]{1,0:T(8,128)(2,1)S(1)}, bf16[1152,128]{1,0:T(8,128)(2,1)S(1)}, u32[]{:S(2)}, u32[]{:S(2)}) %collective-permute-start.8) | collective-permute-done | bytes 294944 | tf_op jit(solution)/shard_map/ppermute | solution.py:43
  195.2 4.7 %collective-permute-done.9.high_ref = bf16[1152,128]{1,0:T(8,128)(2,1)S(1)} collective-permute-done((bf16[1152,128]{1,0:T(8,128)(2,1)S(1)}, bf16[1152,128]{1,0:T(8,128)(2,1)S(1)}, u32[]{:S(2)}, u32[]{:S(2)}) %collective-permute-start.9) | collective-permute-done | bytes 294944 | tf_op jit(solution)/shard_map/ppermute | solution.py:43
  199.9 1.4 copy-done.1
  201.3 1.4 copy-done.2
  202.7 2.5 %gradient.1 = (f32[288,384]{1,0:T(8,128)S(1)}, bf16[288,384]{1,0:T(8,128)(2,1)S(1)}) custom-call(s32[2]{0:T(128)S(1)} %pad_add_fusion.where_ref, bf16[2304,128]{1,0:T(8,128)(2,1)S(1)} %all_gather.37.near_ref, bf16[1152,128]{1,0:T(8,128)(2,1)S(1)} %collective-permute-done.8.low_ref, bf16[1152,128]{1,0:T(8,128)(2,1)S(1)} %collective-permute-done.9.high_ref, ...), custom_call_target="tpu_custom_call" | custom-call | tf_op jit(solution)/shard_map/gradient/pallas_call | solution.py:212
  205.2 4.4 %collective-permute-start.10 = (bf16[288,384]{1,0:T(8,128)(2,1)S(1)}, bf16[288,384]{1,0:T(8,128)(2,1)S(1)}, u32[]{:S(2)}, u32[]{:S(2)}) collective-permute-start(bf16[288,384]{1,0:T(8,128)(2,1)S(1)} %get-tuple-element.29), channel_id=1, source_target_pairs={{0,32},{32,0},{64,96},{96,64},{128,160},{160,128},{192,224},{224,1... | collective-permute-start | bytes 663560 | tf_op jit(solution)/shard_map/ppermute | solution.py:53
  209.6 4.1 %collective-permute-done.10 = bf16[288,384]{1,0:T(8,128)(2,1)S(1)} collective-permute-done((bf16[288,384]{1,0:T(8,128)(2,1)S(1)}, bf16[288,384]{1,0:T(8,128)(2,1)S(1)}, u32[]{:S(2)}, u32[]{:S(2)}) %collective-permute-start.10) | collective-permute-done | bytes 221216 | tf_op jit(solution)/shard_map/ppermute | solution.py:53
  (40 shorter events, 4.0 us)
Async XLA Ops:
  7.2 45.8 %copy-start.9 = (f32[1,6144]{1,0:T(1,128)S(1)}, f32[1,6144]{1,0:T(1,128)}, u32[]{:S(2)}) copy-start(f32[1,6144]{1,0:T(1,128)} %param.8) | copy-start | bytes 73732
  7.2 128.4 %all-gather.4.cloned.1.call-start = ((), (), s32[]{:S(2)}) async-start(), calls=%async_computation | async-start | bytes 3981312 | tf_op jit(solution)/shard_map/all_gather | solution.py:76
  7.2 24.1 %collective-permute-start = (bf16[288,384]{1,0:T(8,128)(2,1)}, bf16[288,384]{1,0:T(8,128)(2,1)S(1)}, u32[]{:S(2)}, u32[]{:S(2)}) collective-permute-start(bf16[288,384]{1,0:T(8,128)(2,1)} %bitcast.33), channel_id=1, source_target_pairs={{0,32},{32,0},{64,96},{96,64},{128,160},{160,128},{192,224},{224,1... | collective-permute-start | bytes 663560 | tf_op jit(solution)/shard_map/ppermute | solution.py:53
  33.1 159.5 %all-gather.6.cloned.1.call-start = ((), (), s32[]{:S(2)}) async-start(), calls=%async_computation.1 | async-start | bytes 1622016 | tf_op jit(solution)/shard_map/all_gather | solution.py:246
  44.2 11.0 %collective-permute-start.1 = (bf16[3072,128]{1,0:T(8,128)(2,1)S(1)}, bf16[3072,128]{1,0:T(8,128)(2,1)}, u32[]{:S(2)}, u32[]{:S(2)}) collective-permute-start(bf16[3072,128]{1,0:T(8,128)(2,1)S(1)} %all_gather.31.own_ref), channel_id=1, source_target_pairs={{0,1},{1,0},{2,3},{3,2},{4,5},{5,4},{6,7},{7,6},{8,9},{9,8},{10,11... | collective-permute-start | bytes 2359304 | tf_op jit(solution)/shard_map/ppermute | solution.py:39
  53.0 2.3 %copy-start.5 = (bf16[1,128,192]{1,2,0:T(8,128)(2,1)S(1)}, bf16[1,128,192]{1,2,0:T(8,128)(2,1)}, u32[]{:S(2)}) copy-start(bf16[1,128,192]{1,2,0:T(8,128)(2,1)} %param.6) | copy-start | bytes 147460
  55.2 4.9 %copy-start.8 = (bf16[1,128,192]{1,2,0:T(8,128)(2,1)S(1)}, bf16[1,128,192]{1,2,0:T(8,128)(2,1)}, u32[]{:S(2)}) copy-start(bf16[1,128,192]{1,2,0:T(8,128)(2,1)} %param.7) | copy-start | bytes 147460
  57.6 2.5 %collective-permute-start.3 = (bf16[192,128]{1,0:T(8,128)(2,1)S(1)}, bf16[192,128]{1,0:T(8,128)(2,1)S(1)}, u32[]{:S(2)}, u32[]{:S(2)}) collective-permute-start(bf16[192,128]{1,0:T(8,128)(2,1)S(1)} %tick.2), channel_id=1, source_target_pairs={{0,32},{32,64},{64,96},{96,128},{128,160},{160,192},{192,224},{224... | collective-permute-start | bytes 147464 | tf_op jit(solution)/shard_map/ppermute | solution.py:241
  59.0 36.0 %collective-permute-start.2 = (bf16[192,128]{1,0:T(8,128)(2,1)S(1)}, bf16[192,128]{1,0:T(8,128)(2,1)S(1)}, u32[]{:S(2)}, u32[]{:S(2)}) collective-permute-start(bf16[192,128]{1,0:T(8,128)(2,1)S(1)} %tick.2), channel_id=1, source_target_pairs={{0,0},{1,1},{2,2},{3,3},{4,64},{5,65},{6,66},{7,67},{8,128},{9,129... | collective-permute-start | bytes 147464 | tf_op jit(solution)/shard_map/ppermute | solution.py:64
  94.9 5.9 %copy-start.7 = (bf16[192,128]{1,0:T(8,128)(2,1)}, bf16[192,128]{1,0:T(8,128)(2,1)S(1)}, u32[]{:S(2)}) copy-start(bf16[192,128]{1,0:T(8,128)(2,1)S(1)} %collective-permute-done.2) | copy-start | bytes 147460
  94.9 8.2 %collective-permute-start.4 = (bf16[3840,128]{1,0:T(8,128)(2,1)S(1)}, bf16[3840,128]{1,0:T(8,128)(2,1)}, u32[]{:S(2)}, u32[]{:S(2)}) collective-permute-start(bf16[3840,128]{1,0:T(8,128)(2,1)S(1)} %all_gather.33.own_ref), channel_id=1, source_target_pairs={{0,1},{1,0},{2,3},{3,2},{4,5},{5,4},{6,7},{7,6},{8,9},{9,8},{10,11... | collective-permute-start | bytes 2949128 | tf_op jit(solution)/shard_map/ppermute | solution.py:39
  100.9 99.0 %all-gather.8.cloned.1.call-start = ((), (), s32[]{:S(2)}) async-start(), calls=%async_computation.2 | async-start | bytes 1769472 | tf_op jit(solution)/shard_map/all_gather | solution.py:76
  106.2 55.9 %copy-start.6 = (bf16[1,2,128,288]{2,3,1,0:T(8,128)(2,1)S(1)}, bf16[1,2,128,288]{2,3,1,0:T(8,128)(2,1)}, u32[]{:S(2)}) copy-start(bf16[1,2,128,288]{2,3,1,0:T(8,128)(2,1)} %param.11) | copy-start | bytes 442372
  106.2 29.4 %collective-permute-start.5 = (bf16[192,128]{1,0:T(8,128)(2,1)}, bf16[192,128]{1,0:T(8,128)(2,1)S(1)}, u32[]{:S(2)}, u32[]{:S(2)}) collective-permute-start(bf16[192,128]{1,0:T(8,128)(2,1)} %get-tuple-element.18), channel_id=1, source_target_pairs={{0,0},{1,1},{2,2},{3,3},{4,64},{5,65},{6,66},{7,67},{8,128},{9,129... | collective-permute-start | bytes 147464 | tf_op jit(solution)/shard_map/ppermute | solution.py:64
  135.6 20.2 %collective-permute-start.6 = (bf16[3840,128]{1,0:T(8,128)(2,1)S(1)}, bf16[3840,128]{1,0:T(8,128)(2,1)S(1)}, u32[]{:S(2)}, u32[]{:S(2)}) collective-permute-start(bf16[3840,128]{1,0:T(8,128)(2,1)S(1)} %all_gather.35.first_own_ref), channel_id=1, source_target_pairs={{0,1},{1,0},{2,3},{3,2},{4,5},{5,4},{6,7},{7,6},{8,9},{9,8},{10,11... | collective-permute-start | bytes 2949128 | tf_op jit(solution)/shard_map/ppermute | solution.py:39
  155.8 5.3 %collective-permute-start.7 = (bf16[3840,128]{1,0:T(8,128)(2,1)S(1)}, bf16[3840,128]{1,0:T(8,128)(2,1)S(1)}, u32[]{:S(2)}, u32[]{:S(2)}) collective-permute-start(bf16[3840,128]{1,0:T(8,128)(2,1)S(1)} %all_gather.36.own_ref), channel_id=1, source_target_pairs={{0,1},{1,0},{2,3},{3,2},{4,5},{5,4},{6,7},{7,6},{8,9},{9,8},{10,11... | collective-permute-start | bytes 2949128 | tf_op jit(solution)/shard_map/ppermute | solution.py:39
  161.1 1.0 copy-start.3
  162.1 2.0 copy-start
  164.1 1.2 copy-start.4
  184.9 10.3 %collective-permute-start.8 = (bf16[1152,128]{1,0:T(8,128)(2,1)S(1)}, bf16[1152,128]{1,0:T(8,128)(2,1)S(1)}, u32[]{:S(2)}, u32[]{:S(2)}) collective-permute-start(bf16[1152,128]{1,0:T(8,128)(2,1)S(1)} %get-tuple-element.31), channel_id=1, source_target_pairs={{0,64},{32,96},{64,0},{96,32},{128,192},{160,224},{192,128},{224,1... | collective-permute-start | bytes 884744 | tf_op jit(solution)/shard_map/ppermute | solution.py:43
  189.5 10.4 %collective-permute-start.9 = (bf16[1152,128]{1,0:T(8,128)(2,1)S(1)}, bf16[1152,128]{1,0:T(8,128)(2,1)S(1)}, u32[]{:S(2)}, u32[]{:S(2)}) collective-permute-start(bf16[1152,128]{1,0:T(8,128)(2,1)S(1)} %get-tuple-element.30), channel_id=1, source_target_pairs={{0,448},{32,480},{64,128},{96,160},{128,64},{160,96},{192,256},{22... | collective-permute-start | bytes 884744 | tf_op jit(solution)/shard_map/ppermute | solution.py:43
  199.9 1.4 copy-start.1
  201.3 1.4 copy-start.2
  205.2 8.5 %collective-permute-start.10 = (bf16[288,384]{1,0:T(8,128)(2,1)S(1)}, bf16[288,384]{1,0:T(8,128)(2,1)S(1)}, u32[]{:S(2)}, u32[]{:S(2)}) collective-permute-start(bf16[288,384]{1,0:T(8,128)(2,1)S(1)} %get-tuple-element.29), channel_id=1, source_target_pairs={{0,32},{32,0},{64,96},{96,64},{128,160},{160,128},{192,224},{224,1... | collective-permute-start | bytes 663560 | tf_op jit(solution)/shard_map/ppermute | solution.py:53
Sparse Core Ops, SparseCore 0:
  33.2 56.3 all-gather.3
  101.0 60.7 all-gather.5
  164.6 32.7 all-gather.7

commit v8 on v6

--- a/solution.py
+++ b/solution.py
@@ -29,6 +29,7 @@
 
 
 Z_GROUPS = [[t_index(z, x, c) for z in range(NZ)] for x in range(NX) for c in range(NC)]
+ZC_GROUPS = [[t_index(z, x, c) for z in range(NZ) for c in range(NC)] for x in range(NX)]
 SECOND_Y_GROUPS = [[(2 * i + p) * 2 + zl for i in range(NY // 2)] for p in range(2) for zl in range(2)]
 Y_GROUPS = [[y * 2 + zl for y in range(NY)] for zl in range(2)]
 X_GROUPS = [[t_index(z, x, c) for x in range(NX)] for z in range(NZ) for c in range(NC)]
@@ -119,14 +120,12 @@
 
 
 def second_tick_kernel(
-    where_ref, own_ref, other_ref, weight_ref, mine_ref, out_ref, next_ref, full
+    where_ref, own_ref, other_ref, weight_ref, mine_ref, before_ref, out_ref, both_ref, full
 ):
     out = hidden_rows(where_ref, own_ref, other_ref, weight_ref, mine_ref, full)
     out_ref[...] = out
-    next_ref[:PIECE, :] = out
-    for x in range(NX):
-        source = x * RIDE + COLUMN
-        next_ref[(x + 1) * PIECE : (x + 2) * PIECE, :] = own_ref[source : source + PIECE, :]
+    both_ref[:PIECE, :] = before_ref[...]
+    both_ref[PIECE:, :] = out
 
 
 def tick(kernel, out_rows, *operands):
@@ -141,15 +140,11 @@
     )(*operands)
 
 
-def predict_kernel(
-    where_ref, first_own_ref, first_other_ref, own_ref, other_ref, block_ref, teacher_ref, out_ref, full
-):
+def predict_kernel(where_ref, first_ref, own_ref, other_ref, block_ref, teacher_ref, out_ref, full):
     core, segment = where_ref[0], where_ref[1]
-    for ref, c in ((first_own_ref, core), (first_other_ref, core ^ 1)):
-        for z in range(NZ):
-            for x in range(NX):
-                source = z * RIDE + (x + 1) * PIECE
-                full[pl.ds(feature_start(z, x, c), PIECE), :ROWS] = ref[source : source + PIECE, :]
+    for z, x, c in all_t():
+        source, at = ((z * NC + c) * NX + x) * PIECE, t_index(z, x, c) * PIECE
+        full[at : at + PIECE, :ROWS] = first_ref[source : source + PIECE, :]
     for ref, c in ((own_ref, core), (other_ref, core ^ 1)):
         for x in range(NX):
             for z in range(NZ):
@@ -237,16 +232,18 @@
 
     shifted = lax.ppermute(out0, "segment", [(i, i + 1) for i in range(15)])
     mine = jnp.where(segment == 0, fresh_t, shifted)
-    column = z_gather(mine)
-    turned0 = transposition(together(out0, column)[0])
-    own = x_gather(stack(column, out0))
-    out1, following = tick(second_tick_kernel, (PIECE, RIDE), where, own, core_swap(own), weights, mine)
-
-    first_own = z_gather(following)
-    turned, blocks, first_own = together(stack(turned0, transposition(out1)), blocks, first_own)
+    own = x_gather(stack(z_gather(mine), out0))
+    column = own.reshape(NX, RIDE, ROWS)[:, COLUMN:].reshape(COLUMN, ROWS)
+    first_rows = gather(column, "tensor", ZC_GROUPS)
+    out1, both = tick(
+        second_tick_kernel, (PIECE, 2 * PIECE), where, own, core_swap(own), weights, mine, out0
+    )
+
+    second = z_gather(out1)
+    turned, blocks, second = together(transposition(both), blocks, second)
     rows = lax.all_gather(turned, "tensor", axis=0, tiled=True)
-    own = x_gather(first_own.reshape(NZ, RIDE, ROWS)[:, :PIECE].reshape(COLUMN, ROWS))
-    difference = predict(where, first_own, core_swap(first_own), own, core_swap(own), blocks, teacher)
+    own = x_gather(second)
+    difference = predict(where, first_rows, own, core_swap(own), blocks, teacher)
 
     near = gather(difference, "segment", SECOND_Y_GROUPS)
     keep, send = gradient(where, near, over_y(near, lambda y: y ^ 1), rows)

time: 219 us -> 224 us (1.023)
  waiting for transfers between devices: 27.4 us -> 34.7 us
  starting transfers between devices: 39.2 us -> 33.5 us
  local copies, waits for them, and re-layouts: 3.92 us -> 7.54 us
    all_gather x1, waiting for transfers between devices: 3.56 us -> 9.04 us  [on_device(): rows = lax.all_gather(turned, 'tensor', axis=0, tiled=True)]
    ppermute x4 -> x3, starting transfers between devices: 27 us -> 22.7 us  [over_tensor(): lax.ppermute(value, 'tensor', [(t_index(*p), t_index(*move(*p))) for p in...]
    unnamed x10 -> x14, local copies, waits for them, and re-layouts: 3.9 us -> 6.86 us
  transfers between devices with their start and end apart: 12 -> 11, of which waited for: 6 -> 6; matrix products, arithmetic and copies ran while one was open for 1% -> 1% of each run, Pallas kernels for 3% -> 3%
where the time goes in v8:
time: 224 us
  blocking collectives  120 us (54%)
  waiting for transfers between devices  34.7 us (15%)
  starting transfers between devices  33.5 us (15%)
  between operations  13.9 us (6%)
  Pallas kernels  9.66 us (4%)
  local copies, waits for them, and re-layouts  7.54 us (3%)
  other arithmetic  4.84 us (2%)
    all_gather x7, blocking collectives, gather(): lax.all_gather(value, axis, axis=0, tiled=True, axis_index_groups=groups)  120 us
    ppermute x3, starting transfers between devices, over_tensor(): lax.ppermute(value, 'tensor', [(t_index(*p), t_index(*move(*p))) for p in...  22.7 us
    ppermute x1, waiting for transfers between devices, over_y(): lax.ppermute(value, 'segment', [(y * 2 + zl, move(y) % NY * 2 + zl) for y...  13.6 us
    all_gather x1, waiting for transfers between devices, on_device(): rows = lax.all_gather(turned, 'tensor', axis=0, tiled=True)  9.04 us
    unnamed x14, local copies, waits for them, and re-layouts  6.86 us
    ppermute x2, starting transfers between devices, zl_swap(): return lax.ppermute(value, 'segment', [(i, i ^ 1) for i in range(16)])  6.75 us
    ppermute x2, waiting for transfers between devices, zl_swap(): return lax.ppermute(value, 'segment', [(i, i ^ 1) for i in range(16)])  6.75 us
    pallas_call x2, Pallas kernels, tick(): pl.pallas_call(kernel, out_shape=[jax.ShapeDtypeStruct((rows, ROWS), jnp....  4.75 us
  transfers between devices with their start and end apart: 11, of which 6 were waited for; matrix products, arithmetic and copies ran while one was open for 1% of the time, Pallas kernels for 3%

profile of v8, /device:TPU:1, one launch (start us, length us, event | category | flops | bytes accessed | tf_op | source)
XLA Modules:
  0.0 223.7 jit_solution(4985809876377941308)
XLA Ops:
  7.2 4.8 %collective-permute-start = (bf16[288,384]{1,0:T(8,128)(2,1)}, bf16[288,384]{1,0:T(8,128)(2,1)S(1)}, u32[]{:S(2)}, u32[]{:S(2)}) collective-permute-start(bf16[288,384]{1,0:T(8,128)(2,1)} %bitcast.29), channel_id=1, source_target_pairs={{0,32},{32,0},{64,96},{96,64},{128,160},{160,128},{192,224},{224,1... | collective-permute-start | bytes 663560 | tf_op jit(solution)/shard_map/ppermute | solution.py:53
  12.0 19.2 %all_gather.30 = bf16[768,128]{1,0:T(8,128)(2,1)S(1)} all-gather(bf16[192,128]{1,0:T(8,128)(2,1)} %bitcast.25), channel_id=1, replica_groups={{0,8,16,24},{1,9,17,25},{2,10,18,26},{3,11,19,27},{4,12,20,28},{5,13,21..., dimensions={0}, use_global_device_ids=true | all-gather | bytes 245760 | tf_op jit(solution)/shard_map/all_gather | solution.py:76
  31.3 1.7 pad_maximum_fusion
  33.1 11.1 %all_gather.31.own_ref = bf16[3072,128]{1,0:T(8,128)(2,1)S(1)} all-gather(bf16[768,128]{1,0:T(8,128)(2,1)S(1)} %all_gather.30), channel_id=1, replica_groups={{0,2,4,6},{1,3,5,7},{8,10,12,14},{9,11,13,15},{16,18,20,22},{17,19,21,2..., dimensions={0}, use_global_device_ids=true | all-gather | bytes 983040 | tf_op jit(solution)/shard_map/all_gather | solution.py:76
  44.2 8.7 %collective-permute-start.1 = (bf16[3072,128]{1,0:T(8,128)(2,1)S(1)}, bf16[3072,128]{1,0:T(8,128)(2,1)}, u32[]{:S(2)}, u32[]{:S(2)}) collective-permute-start(bf16[3072,128]{1,0:T(8,128)(2,1)S(1)} %all_gather.31.own_ref), channel_id=1, source_target_pairs={{0,1},{1,0},{2,3},{3,2},{4,5},{5,4},{6,7},{7,6},{8,9},{9,8},{10,11... | collective-permute-start | bytes 2359304 | tf_op jit(solution)/shard_map/ppermute | solution.py:39
  53.0 2.2 fusion.weight_ref
  55.3 2.4 %tick.2.before_ref = bf16[192,128]{1,0:T(8,128)(2,1)S(1)} custom-call(s32[2]{0:T(128)S(1)} %pad_add_fusion.where_ref, bf16[3072,128]{1,0:T(8,128)(2,1)S(1)} %all_gather.31.own_ref, bf16[3072,128]{1,0:T(8,128)(2,1)} %collective-permute-done.1.other_ref, bf16[192,6144]{1,0:T(8,128)(2,1)S(1)} %fusion.weight_ref, bf16[192,128]{1,0:T(8,128)(2,1)S(1)} %bitcast.26), custom_call_target="tpu_custom_call" | custom-call | tf_op jit(solution)/shard_map/tick/pallas_call | solution.py:132
  57.6 1.3 collective-permute-start.2
  58.9 1.2 collective-permute-done.2
  60.1 11.9 %all_gather.32 = bf16[768,128]{1,0:T(8,128)(2,1)S(1)} all-gather(bf16[192,128]{1,0:T(8,128)(2,1)S(1)} %bitcast_select_fusion.mine_ref), channel_id=1, replica_groups={{0,8,16,24},{1,9,17,25},{2,10,18,26},{3,11,19,27},{4,12,20,28},{5,13,21..., dimensions={0}, use_global_device_ids=true | all-gather | bytes 245760 | tf_op jit(solution)/shard_map/all_gather | solution.py:76
  72.0 12.4 %all_gather.33.own_ref = bf16[3840,128]{1,0:T(8,128)(2,1)S(1)} all-gather(bf16[960,128]{1,0:T(8,128)(2,1)S(1)} %pad_maximum_fusion.1), channel_id=1, replica_groups={{0,2,4,6},{1,3,5,7},{8,10,12,14},{9,11,13,15},{16,18,20,22},{17,19,21,2..., dimensions={0}, use_global_device_ids=true | all-gather | bytes 1228800 | tf_op jit(solution)/shard_map/all_gather | solution.py:76
  84.4 0.7 slice.4
  85.1 7.8 %collective-permute-start.3 = (bf16[3840,128]{1,0:T(8,128)(2,1)S(1)}, bf16[3840,128]{1,0:T(8,128)(2,1)S(1)}, u32[]{:S(2)}, u32[]{:S(2)}) collective-permute-start(bf16[3840,128]{1,0:T(8,128)(2,1)S(1)} %all_gather.33.own_ref), channel_id=1, source_target_pairs={{0,1},{1,0},{2,3},{3,2},{4,5},{5,4},{6,7},{7,6},{8,9},{9,8},{10,11... | collective-permute-start | bytes 2949128 | tf_op jit(solution)/shard_map/ppermute | solution.py:39
  92.9 2.2 collective-permute-done.3.other_ref
  95.1 2.4 %tick.3 = (bf16[192,128]{1,0:T(8,128)(2,1)}, bf16[384,128]{1,0:T(8,128)(2,1)S(1)}) custom-call(s32[2]{0:T(128)S(1)} %pad_add_fusion.where_ref, bf16[3840,128]{1,0:T(8,128)(2,1)S(1)} %all_gather.33.own_ref, bf16[3840,128]{1,0:T(8,128)(2,1)S(1)} %collective-permute-done.3.other_ref, bf16[192,6144]{1,0:T(8,128)(2,1)S(1)} %fusion.weight_ref, ...), custom_call_target="tpu_custom_call" | custom-call | tf_op jit(solution)/shard_map/tick/pallas_call | solution.py:132
  98.2 34.9 %all_gather.36 = bf16[768,128]{1,0:T(8,128)(2,1)S(1)} all-gather(bf16[192,128]{1,0:T(8,128)(2,1)} %get-tuple-element.12), channel_id=1, replica_groups={{0,8,16,24},{1,9,17,25},{2,10,18,26},{3,11,19,27},{4,12,20,28},{5,13,21..., dimensions={0}, use_global_device_ids=true | all-gather | bytes 245760 | tf_op jit(solution)/shard_map/all_gather | solution.py:76
  133.8 10.8 %all_gather.37.own_ref = bf16[3072,128]{1,0:T(8,128)(2,1)S(1)} all-gather(bf16[768,128]{1,0:T(8,128)(2,1)S(1)} %all_gather.36), channel_id=1, replica_groups={{0,2,4,6},{1,3,5,7},{8,10,12,14},{9,11,13,15},{16,18,20,22},{17,19,21,2..., dimensions={0}, use_global_device_ids=true | all-gather | bytes 983040 | tf_op jit(solution)/shard_map/all_gather | solution.py:76
  144.6 6.2 %collective-permute-start.5 = (bf16[3072,128]{1,0:T(8,128)(2,1)S(1)}, bf16[3072,128]{1,0:T(8,128)(2,1)S(1)}, u32[]{:S(2)}, u32[]{:S(2)}) collective-permute-start(bf16[3072,128]{1,0:T(8,128)(2,1)S(1)} %all_gather.37.own_ref), channel_id=1, source_target_pairs={{0,1},{1,0},{2,3},{3,2},{4,5},{5,4},{6,7},{7,6},{8,9},{9,8},{10,11... | collective-permute-start | bytes 2359304 | tf_op jit(solution)/shard_map/ppermute | solution.py:39
  150.8 1.9 collective-permute-done.5.other_ref
  152.7 2.0 copy-done
  154.7 1.4 copy-done.2
  156.1 0.9 copy-done.4
  157.0 2.5 %predict.1 = bf16[576,128]{1,0:T(8,128)(2,1)S(1)} custom-call(s32[2]{0:T(128)S(1)} %pad_add_fusion.where_ref, bf16[6144,128]{1,0:T(8,128)(2,1)S(1)} %copy-done.2, bf16[3072,128]{1,0:T(8,128)(2,1)S(1)} %all_gather.37.own_ref, bf16[3072,128]{1,0:T(8,128)(2,1)S(1)} %collective-permute-done.5.other_ref, bf16[4608,384]{1,0:T(8,128)(2,1)S(1)} %copy-done, ...), custom_call_target="tpu_custom_call" | custom-call | tf_op jit(solution)/shard_map/predict/pallas_call | solution.py:168
  159.5 19.3 %all_gather.38.near_ref = bf16[2304,128]{1,0:T(8,128)(2,1)S(1)} all-gather(bf16[576,128]{1,0:T(8,128)(2,1)S(1)} %predict.1), channel_id=1, replica_groups={{0,128,256,384},{32,160,288,416},{64,192,320,448},{96,224,352,480},{1,1..., dimensions={0}, use_global_device_ids=true | all-gather | bytes 737280 | tf_op jit(solution)/shard_map/all_gather | solution.py:76
  178.8 1.9 collective-permute-start.6
  180.7 13.6 %collective-permute-done.6.far_ref = bf16[2304,128]{1,0:T(8,128)(2,1)S(1)} collective-permute-done((bf16[2304,128]{1,0:T(8,128)(2,1)S(1)}, bf16[2304,128]{1,0:T(8,128)(2,1)S(1)}, u32[]{:S(2)}, u32[]{:S(2)}) %collective-permute-start.6) | collective-permute-done | bytes 589856 | tf_op jit(solution)/shard_map/ppermute | solution.py:43
  194.3 9.0 %all-gather.8.cloned.1.call-done.rows_ref = bf16[12288,128]{1,0:T(8,128)(2,1)} async-done(((bf16[384,128]{1,0:T(8,128)(2,1)}), bf16[12288,128]{1,0:T(8,128)(2,1)}) %all-gather.8.cloned.1.call-update) | async-done | bytes 3145744 | tf_op jit(solution)/shard_map/all_gather | solution.py:244
  203.4 1.9 copy-done.1
  205.3 2.4 %gradient.1 = (f32[288,384]{1,0:T(8,128)S(1)}, bf16[288,384]{1,0:T(8,128)(2,1)S(1)}) custom-call(s32[2]{0:T(128)S(1)} %pad_add_fusion.where_ref, bf16[2304,128]{1,0:T(8,128)(2,1)S(1)} %all_gather.38.near_ref, bf16[2304,128]{1,0:T(8,128)(2,1)S(1)} %collective-permute-done.6.far_ref, bf16[12288,128]{1,0:T(8,128)(2,1)S(1)} %copy-done.1), custom_call_target="tpu_custom_call" | custom-call | tf_op jit(solution)/shard_map/gradient/pallas_call | solution.py:204
  207.7 1.9 collective-permute-start.7
  209.7 6.7 %collective-permute-done.7 = bf16[288,384]{1,0:T(8,128)(2,1)S(1)} collective-permute-done((bf16[288,384]{1,0:T(8,128)(2,1)S(1)}, bf16[288,384]{1,0:T(8,128)(2,1)S(1)}, u32[]{:S(2)}, u32[]{:S(2)}) %collective-permute-start.7) | collective-permute-done | bytes 221216 | tf_op jit(solution)/shard_map/ppermute | solution.py:53
  216.4 0.8 add_bitcast_fusion
  (25 shorter events, 1.6 us)
Async XLA Ops:
  7.2 126.0 %all-gather.6.cloned.1.call-start = ((), (), s32[]{:S(2)}) async-start(), calls=%async_computation.1 | async-start | bytes 3981312 | tf_op jit(solution)/shard_map/all_gather | solution.py:76
  7.2 24.1 %collective-permute-start = (bf16[288,384]{1,0:T(8,128)(2,1)}, bf16[288,384]{1,0:T(8,128)(2,1)S(1)}, u32[]{:S(2)}, u32[]{:S(2)}) collective-permute-start(bf16[288,384]{1,0:T(8,128)(2,1)} %bitcast.29), channel_id=1, source_target_pairs={{0,32},{32,0},{64,96},{96,64},{128,160},{160,128},{192,224},{224,1... | collective-permute-start | bytes 663560 | tf_op jit(solution)/shard_map/ppermute | solution.py:53
  33.0 22.2 %copy-start.3 = (bf16[1,128,192]{1,2,0:T(8,128)(2,1)S(1)}, bf16[1,128,192]{1,2,0:T(8,128)(2,1)}, u32[]{:S(2)}) copy-start(bf16[1,128,192]{1,2,0:T(8,128)(2,1)} %param.6) | copy-start | bytes 147460
  33.1 117.8 %all-gather.4.cloned.1.call-start = ((), (), s32[]{:S(2)}) async-start(), calls=%async_computation | async-start | bytes 1769472 | tf_op jit(solution)/shard_map/all_gather | solution.py:76
  44.2 11.0 %collective-permute-start.1 = (bf16[3072,128]{1,0:T(8,128)(2,1)S(1)}, bf16[3072,128]{1,0:T(8,128)(2,1)}, u32[]{:S(2)}, u32[]{:S(2)}) collective-permute-start(bf16[3072,128]{1,0:T(8,128)(2,1)S(1)} %all_gather.31.own_ref), channel_id=1, source_target_pairs={{0,1},{1,0},{2,3},{3,2},{4,5},{5,4},{6,7},{7,6},{8,9},{9,8},{10,11... | collective-permute-start | bytes 2359304 | tf_op jit(solution)/shard_map/ppermute | solution.py:39
  55.2 4.9 %copy-start.6 = (bf16[1,128,192]{1,2,0:T(8,128)(2,1)S(1)}, bf16[1,128,192]{1,2,0:T(8,128)(2,1)}, u32[]{:S(2)}) copy-start(bf16[1,128,192]{1,2,0:T(8,128)(2,1)} %param.7) | copy-start | bytes 147460
  57.6 2.5 %collective-permute-start.2 = (bf16[192,128]{1,0:T(8,128)(2,1)S(1)}, bf16[192,128]{1,0:T(8,128)(2,1)S(1)}, u32[]{:S(2)}, u32[]{:S(2)}) collective-permute-start(bf16[192,128]{1,0:T(8,128)(2,1)S(1)} %tick.2.before_ref), channel_id=1, source_target_pairs={{0,32},{32,64},{64,96},{96,128},{128,160},{160,192},{192,224},{224... | collective-permute-start | bytes 147464 | tf_op jit(solution)/shard_map/ppermute | solution.py:233
  85.1 118.3 %all-gather.8.cloned.1.call-start = ((), (), s32[]{:S(2)}) async-start(), calls=%async_computation.2 | async-start | bytes 3244032 | tf_op jit(solution)/shard_map/all_gather | solution.py:244
  85.1 10.0 %collective-permute-start.3 = (bf16[3840,128]{1,0:T(8,128)(2,1)S(1)}, bf16[3840,128]{1,0:T(8,128)(2,1)S(1)}, u32[]{:S(2)}, u32[]{:S(2)}) collective-permute-start(bf16[3840,128]{1,0:T(8,128)(2,1)S(1)} %all_gather.33.own_ref), channel_id=1, source_target_pairs={{0,1},{1,0},{2,3},{3,2},{4,5},{5,4},{6,7},{7,6},{8,9},{9,8},{10,11... | collective-permute-start | bytes 2949128 | tf_op jit(solution)/shard_map/ppermute | solution.py:39
  97.5 35.6 %collective-permute-start.4 = (bf16[384,128]{1,0:T(8,128)(2,1)S(1)}, bf16[384,128]{1,0:T(8,128)(2,1)S(1)}, u32[]{:S(2)}, u32[]{:S(2)}) collective-permute-start(bf16[384,128]{1,0:T(8,128)(2,1)S(1)} %get-tuple-element.13), channel_id=1, source_target_pairs={{0,0},{1,1},{2,2},{3,3},{4,64},{5,65},{6,66},{7,67},{8,128},{9,129... | collective-permute-start | bytes 294920 | tf_op jit(solution)/shard_map/ppermute | solution.py:64
  133.1 0.6 copy-start.5
  144.6 8.1 %collective-permute-start.5 = (bf16[3072,128]{1,0:T(8,128)(2,1)S(1)}, bf16[3072,128]{1,0:T(8,128)(2,1)S(1)}, u32[]{:S(2)}, u32[]{:S(2)}) collective-permute-start(bf16[3072,128]{1,0:T(8,128)(2,1)S(1)} %all_gather.37.own_ref), channel_id=1, source_target_pairs={{0,1},{1,0},{2,3},{3,2},{4,5},{5,4},{6,7},{7,6},{8,9},{9,8},{10,11... | collective-permute-start | bytes 2359304 | tf_op jit(solution)/shard_map/ppermute | solution.py:39
  152.7 2.0 copy-start
  154.7 1.4 copy-start.2
  156.1 0.9 copy-start.4
  178.8 15.5 %collective-permute-start.6 = (bf16[2304,128]{1,0:T(8,128)(2,1)S(1)}, bf16[2304,128]{1,0:T(8,128)(2,1)S(1)}, u32[]{:S(2)}, u32[]{:S(2)}) collective-permute-start(bf16[2304,128]{1,0:T(8,128)(2,1)S(1)} %all_gather.38.near_ref), channel_id=1, source_target_pairs={{0,64},{32,96},{64,0},{96,32},{128,192},{160,224},{192,128},{224,1... | collective-permute-start | bytes 1769480 | tf_op jit(solution)/shard_map/ppermute | solution.py:43
  203.4 1.9 copy-start.1
  207.7 8.7 %collective-permute-start.7 = (bf16[288,384]{1,0:T(8,128)(2,1)S(1)}, bf16[288,384]{1,0:T(8,128)(2,1)S(1)}, u32[]{:S(2)}, u32[]{:S(2)}) collective-permute-start(bf16[288,384]{1,0:T(8,128)(2,1)S(1)} %get-tuple-element.19), channel_id=1, source_target_pairs={{0,32},{32,0},{64,96},{96,64},{128,160},{160,128},{192,224},{224,1... | collective-permute-start | bytes 663560 | tf_op jit(solution)/shard_map/ppermute | solution.py:53
Sparse Core Ops, SparseCore 0:
  33.2 52.1 all-gather.5
  87.5 52.9 all-gather.3
  143.6 59.7 all-gather.7

commit v9 on v8

--- a/solution.py
+++ b/solution.py
@@ -13,8 +13,6 @@
 WIDTH = 6144
 COLS = 288
 BLOCK = 384
-COLUMN = 768
-RIDE = 960
 VMEM_LIMIT = 32 * 1024 * 1024
 SMEM_SPEC = pl.BlockSpec(memory_space=pltpu.SMEM)
 VMEM_SPEC = pl.BlockSpec(memory_space=pltpu.VMEM)
@@ -29,7 +27,6 @@
 
 
 Z_GROUPS = [[t_index(z, x, c) for z in range(NZ)] for x in range(NX) for c in range(NC)]
-ZC_GROUPS = [[t_index(z, x, c) for z in range(NZ) for c in range(NC)] for x in range(NX)]
 SECOND_Y_GROUPS = [[(2 * i + p) * 2 + zl for i in range(NY // 2)] for p in range(2) for zl in range(2)]
 Y_GROUPS = [[y * 2 + zl for y in range(NY)] for zl in range(2)]
 X_GROUPS = [[t_index(z, x, c) for x in range(NX)] for z in range(NZ) for c in range(NC)]
@@ -51,6 +48,10 @@
 
 def zl_swap(value):
     return lax.ppermute(value, "segment", [(i, i ^ 1) for i in range(16)])
+
+
+def to_next_segment(value):
+    return lax.ppermute(value, "segment", [(s, (s + 1) % 16) for s in range(16)])
 
 
 def transposition(value):
@@ -96,18 +97,20 @@
     return pl.multiple_of((z * 8 + x * 2 + c) * PIECE, PIECE)
 
 
-def hidden_rows(where_ref, own_ref, other_ref, weight_ref, mine_ref, full):
+def fill(where_ref, own_ref, other_ref, full, columns):
     core = where_ref[0]
-    stride = own_ref.shape[0] // NX
-    square = jnp.zeros((8, ROWS), jnp.float32)
     for ref, c in ((own_ref, core), (other_ref, core ^ 1)):
         for x in range(NX):
             for z in range(NZ):
-                source = x * stride + z * PIECE
-                piece = ref[source : source + PIECE, :]
-                full[pl.ds(feature_start(z, x, c), PIECE), :] = piece
-                wide = piece.astype(jnp.float32)
-                square += jnp.sum((wide * wide).reshape(PIECE // 8, 8, ROWS), axis=0)
+                source = (x * NZ + z) * PIECE
+                full[pl.ds(feature_start(z, x, c), PIECE), columns] = ref[source : source + PIECE, :]
+
+
+def output_rows(weight_ref, mine_ref, full):
+    square = jnp.zeros((8, ROWS), jnp.float32)
+    for k in range(WIDTH // PIECE):
+        wide = full[k * PIECE : (k + 1) * PIECE, :].astype(jnp.float32)
+        square += jnp.sum((wide * wide).reshape(PIECE // 8, 8, ROWS), axis=0)
     mean_square = jnp.sum(square, axis=0, keepdims=True) * (1.0 / WIDTH)
     scale = lax.rsqrt(mean_square + EPSILON)
     hidden = jnp.dot(weight_ref[...], full[...], preferred_element_type=jnp.float32) * scale
@@ -116,15 +119,26 @@
 
 
 def first_tick_kernel(where_ref, own_ref, other_ref, weight_ref, mine_ref, out_ref, full):
-    out_ref[...] = hidden_rows(where_ref, own_ref, other_ref, weight_ref, mine_ref, full)
+    fill(where_ref, own_ref, other_ref, full, slice(0, ROWS))
+    out_ref[...] = output_rows(weight_ref, mine_ref, full)
 
 
 def second_tick_kernel(
-    where_ref, own_ref, other_ref, weight_ref, mine_ref, before_ref, out_ref, both_ref, full
+    where_ref, own_ref, other_ref, fresh_ref, weight_ref, mine_ref, moved_ref, out_ref, both_ref, full
 ):
-    out = hidden_rows(where_ref, own_ref, other_ref, weight_ref, mine_ref, full)
+    first = where_ref[1] == 0
+
+    @pl.when(first)
+    def _():
+        full[...] = fresh_ref[...]
+
+    @pl.when(jnp.logical_not(first))
+    def _():
+        fill(where_ref, own_ref, other_ref, full, slice(0, ROWS))
+
+    out = output_rows(weight_ref, mine_ref, full)
     out_ref[...] = out
-    both_ref[:PIECE, :] = before_ref[...]
+    both_ref[:PIECE, :] = moved_ref[...]
     both_ref[PIECE:, :] = out
 
 
@@ -140,16 +154,12 @@
     )(*operands)
 
 
-def predict_kernel(where_ref, first_ref, own_ref, other_ref, block_ref, teacher_ref, out_ref, full):
-    core, segment = where_ref[0], where_ref[1]
-    for z, x, c in all_t():
-        source, at = ((z * NC + c) * NX + x) * PIECE, t_index(z, x, c) * PIECE
-        full[at : at + PIECE, :ROWS] = first_ref[source : source + PIECE, :]
-    for ref, c in ((own_ref, core), (other_ref, core ^ 1)):
-        for x in range(NX):
-            for z in range(NZ):
-                source = (x * NZ + z) * PIECE
-                full[pl.ds(feature_start(z, x, c), PIECE), ROWS:] = ref[source : source + PIECE, :]
+def predict_kernel(
+    where_ref, own0_ref, other0_ref, own1_ref, other1_ref, block_ref, taught0_ref, taught1_ref, out_ref, full
+):
+    segment = where_ref[1]
+    fill(where_ref, own0_ref, other0_ref, full, slice(0, ROWS))
+    fill(where_ref, own1_ref, other1_ref, full, slice(ROWS, 2 * ROWS))
     total = jnp.zeros((COLS, TICKS * ROWS), jnp.float32)
     for y in range(NY):
         for j in range(2):
@@ -159,8 +169,8 @@
                 full[pl.ds(pl.multiple_of(owner * BLOCK, BLOCK), BLOCK), :],
                 preferred_element_type=jnp.float32,
             )
-    for tau in range(TICKS):
-        difference = total[:, tau * ROWS : (tau + 1) * ROWS] - teacher_ref[tau].astype(jnp.float32)
+    for tau, taught in enumerate((taught0_ref[0], taught1_ref[1])):
+        difference = total[:, tau * ROWS : (tau + 1) * ROWS] - taught.astype(jnp.float32)
         out_ref[tau * COLS : (tau + 1) * COLS, :] = difference.astype(jnp.bfloat16)
 
 
@@ -224,26 +234,28 @@
     entering_t, fresh_t = entering[0].T, fresh_rows[0].T
 
     mine_block = projection.T
+    fresh_all = lax.all_gather(fresh_t, "tensor", axis=0, tiled=True)
     first = z_gather(entering_t)
     other_block, first = together(zl_swap(mine_block), first)
     blocks = gather(stack(mine_block, other_block), "segment", Y_GROUPS)
     own = x_gather(first)
+    taught0 = to_next_segment(together(teacher, own)[0])
     (out0,) = tick(first_tick_kernel, (PIECE,), where, own, core_swap(own), weights, entering_t)
 
-    shifted = lax.ppermute(out0, "segment", [(i, i + 1) for i in range(15)])
-    mine = jnp.where(segment == 0, fresh_t, shifted)
-    own = x_gather(stack(z_gather(mine), out0))
-    column = own.reshape(NX, RIDE, ROWS)[:, COLUMN:].reshape(COLUMN, ROWS)
-    first_rows = gather(column, "tensor", ZC_GROUPS)
+    moved = to_next_segment(out0)
+    moved, taught0 = together(moved, taught0)
+    mine = jnp.where(segment == 0, fresh_t, moved)
+    own0 = x_gather(z_gather(moved))
+    other0 = core_swap(own0)
     out1, both = tick(
-        second_tick_kernel, (PIECE, 2 * PIECE), where, own, core_swap(own), weights, mine, out0
+        second_tick_kernel, (PIECE, 2 * PIECE), where, own0, other0, fresh_all, weights, mine, moved
     )
 
     second = z_gather(out1)
-    turned, blocks, second = together(transposition(both), blocks, second)
+    turned, second = together(transposition(both), second)
     rows = lax.all_gather(turned, "tensor", axis=0, tiled=True)
-    own = x_gather(second)
-    difference = predict(where, first_rows, own, core_swap(own), blocks, teacher)
+    own1 = x_gather(second)
+    difference = predict(where, own0, other0, own1, core_swap(own1), blocks, taught0, teacher)
 
     near = gather(difference, "segment", SECOND_Y_GROUPS)
     keep, send = gradient(where, near, over_y(near, lambda y: y ^ 1), rows)

time: 224 us -> 228 us (1.018)
  blocking collectives: 120 us -> 109 us
  waiting for transfers between devices: 34.7 us -> 42.9 us
  starting transfers between devices: 33.5 us -> 38.6 us
    all_gather x7, blocking collectives: 120 us -> 109 us  [gather(): lax.all_gather(value, axis, axis=0, tiled=True, axis_index_groups=groups)]
    all_gather x1, waiting for transfers between devices: 9.04 us -> 17.5 us  [on_device(): rows = lax.all_gather(turned, 'tensor', axis=0, tiled=True)]
    ppermute x1 -> x2, starting transfers between devices: 1.29 us -> 6.2 us  [to_next_segment(): lax.ppermute(value, 'segment', [(s, (s + 1) % 16) for s in range(16)])]
    unnamed x14 -> x12, local copies, waits for them, and re-layouts: 6.86 us -> 5.95 us
  transfers between devices with their start and end apart: 11 -> 12, of which waited for: 6 -> 7; matrix products, arithmetic and copies ran while one was open for 1% -> 2% of each run, Pallas kernels for 3% -> 4%
where the time goes in v9:
time: 228 us; the launch traced here: 227 us
  blocking collectives  109 us (48%)
  waiting for transfers between devices  42.9 us (19%)
  starting transfers between devices  38.6 us (17%)
  between operations  13.9 us (6%)
  Pallas kernels  10.8 us (5%)
  local copies, waits for them, and re-layouts  5.95 us (3%)
  other arithmetic  5.6 us (2%)
    all_gather x7, blocking collectives, gather(): lax.all_gather(value, axis, axis=0, tiled=True, axis_index_groups=groups)  109 us
    ppermute x3, starting transfers between devices, over_tensor(): lax.ppermute(value, 'tensor', [(t_index(*p), t_index(*move(*p))) for p in...  22.9 us
    all_gather x1, waiting for transfers between devices, on_device(): rows = lax.all_gather(turned, 'tensor', axis=0, tiled=True)  17.5 us
    ppermute x1, waiting for transfers between devices, over_y(): lax.ppermute(value, 'segment', [(y * 2 + zl, move(y) % NY * 2 + zl) for y...  11.7 us
    ppermute x2, waiting for transfers between devices, zl_swap(): return lax.ppermute(value, 'segment', [(i, i ^ 1) for i in range(16)])  6.75 us
    ppermute x2, starting transfers between devices, zl_swap(): return lax.ppermute(value, 'segment', [(i, i ^ 1) for i in range(16)])  6.75 us
    ppermute x2, starting transfers between devices, to_next_segment(): lax.ppermute(value, 'segment', [(s, (s + 1) % 16) for s in range(16)])  6.2 us
    unnamed x12, local copies, waits for them, and re-layouts  5.95 us
  transfers between devices with their start and end apart: 12, of which 7 were waited for; matrix products, arithmetic and copies ran while one was open for 2% of the time, Pallas kernels for 4%

profile of v9, /device:TPU:1, one launch (start us, length us, event | category | flops | bytes accessed | tf_op | source)
XLA Modules:
  0.0 226.9 jit_solution(15069937908077882522)
XLA Ops:
  7.9 4.8 %collective-permute-start = (bf16[288,384]{1,0:T(8,128)(2,1)}, bf16[288,384]{1,0:T(8,128)(2,1)S(1)}, u32[]{:S(2)}, u32[]{:S(2)}) collective-permute-start(bf16[288,384]{1,0:T(8,128)(2,1)} %bitcast.26), channel_id=1, source_target_pairs={{0,32},{32,0},{64,96},{96,64},{128,160},{160,128},{192,224},{224,1... | collective-permute-start | bytes 663560 | tf_op jit(solution)/shard_map/ppermute | solution.py:50
  12.8 19.2 %all_gather.30 = bf16[768,128]{1,0:T(8,128)(2,1)S(1)} all-gather(bf16[192,128]{1,0:T(8,128)(2,1)} %bitcast.22), channel_id=1, replica_groups={{0,8,16,24},{1,9,17,25},{2,10,18,26},{3,11,19,27},{4,12,20,28},{5,13,21..., dimensions={0}, use_global_device_ids=true | all-gather | bytes 245760 | tf_op jit(solution)/shard_map/all_gather | solution.py:77
  32.0 1.7 pad_maximum_fusion
  33.8 11.9 %all_gather.31.own_ref = bf16[3072,128]{1,0:T(8,128)(2,1)S(1)} all-gather(bf16[768,128]{1,0:T(8,128)(2,1)S(1)} %all_gather.30), channel_id=1, replica_groups={{0,2,4,6},{1,3,5,7},{8,10,12,14},{9,11,13,15},{16,18,20,22},{17,19,21,2..., dimensions={0}, use_global_device_ids=true | all-gather | bytes 983040 | tf_op jit(solution)/shard_map/all_gather | solution.py:77
  45.7 8.2 %collective-permute-start.1 = (bf16[3072,128]{1,0:T(8,128)(2,1)S(1)}, bf16[3072,128]{1,0:T(8,128)(2,1)}, u32[]{:S(2)}, u32[]{:S(2)}) collective-permute-start(bf16[3072,128]{1,0:T(8,128)(2,1)S(1)} %all_gather.31.own_ref), channel_id=1, source_target_pairs={{0,1},{1,0},{2,3},{3,2},{4,5},{5,4},{6,7},{7,6},{8,9},{9,8},{10,11... | collective-permute-start | bytes 2359304 | tf_op jit(solution)/shard_map/ppermute | solution.py:36
  54.0 2.1 fusion.weight_ref
  56.2 1.9 collective-permute-start.3
  58.2 2.3 %tick.2 = bf16[192,128]{1,0:T(8,128)(2,1)S(1)} custom-call(s32[2]{0:T(128)S(1)} %pad_add_fusion.where_ref, bf16[3072,128]{1,0:T(8,128)(2,1)S(1)} %all_gather.31.own_ref, bf16[3072,128]{1,0:T(8,128)(2,1)} %collective-permute-done.1.other_ref, bf16[192,6144]{1,0:T(8,128)(2,1)S(1)} %fusion.weight_ref, bf16[192,128]{1,0:T(8,128)(2,1)S(1)} %bitcast.23), custom_call_target="tpu_custom_call" | custom-call | tf_op jit(solution)/shard_map/tick/pallas_call | solution.py:146
  60.5 4.3 %collective-permute-start.2 = (bf16[192,128]{1,0:T(8,128)(2,1)S(1)}, bf16[192,128]{1,0:T(8,128)(2,1)S(1)}, u32[]{:S(2)}, u32[]{:S(2)}) collective-permute-start(bf16[192,128]{1,0:T(8,128)(2,1)S(1)} %tick.2), channel_id=1, source_target_pairs={{0,32},{32,64},{64,96},{96,128},{128,160},{160,192},{192,224},{224... | collective-permute-start | bytes 147464 | tf_op jit(solution)/shard_map/ppermute | solution.py:54
  64.8 0.9 collective-permute-done.3.taught0_ref
  65.7 2.1 collective-permute-done.2.moved_ref
  67.9 11.8 %all_gather.32 = bf16[768,128]{1,0:T(8,128)(2,1)S(1)} all-gather(bf16[192,128]{1,0:T(8,128)(2,1)S(1)} %collective-permute-done.2.moved_ref), channel_id=1, replica_groups={{0,8,16,24},{1,9,17,25},{2,10,18,26},{3,11,19,27},{4,12,20,28},{5,13,21..., dimensions={0}, use_global_device_ids=true | all-gather | bytes 245760 | tf_op jit(solution)/shard_map/all_gather | solution.py:77
  79.7 10.4 %all_gather.33.own_ref.own0_ref = bf16[3072,128]{1,0:T(8,128)(2,1)S(1)} all-gather(bf16[768,128]{1,0:T(8,128)(2,1)S(1)} %all_gather.32), channel_id=1, replica_groups={{0,2,4,6},{1,3,5,7},{8,10,12,14},{9,11,13,15},{16,18,20,22},{17,19,21,2..., dimensions={0}, use_global_device_ids=true | all-gather | bytes 983040 | tf_op jit(solution)/shard_map/all_gather | solution.py:77
  90.1 8.3 %collective-permute-start.4 = (bf16[3072,128]{1,0:T(8,128)(2,1)S(1)}, bf16[3072,128]{1,0:T(8,128)(2,1)}, u32[]{:S(2)}, u32[]{:S(2)}) collective-permute-start(bf16[3072,128]{1,0:T(8,128)(2,1)S(1)} %all_gather.33.own_ref.own0_ref), channel_id=1, source_target_pairs={{0,1},{1,0},{2,3},{3,2},{4,5},{5,4},{6,7},{7,6},{8,9},{9,8},{10,11... | collective-permute-start | bytes 2359304 | tf_op jit(solution)/shard_map/ppermute | solution.py:36
  98.5 0.8 broadcast_select_fusion.mine_ref
  99.3 1.2 collective-permute-done.4.other_ref.other0_ref
  100.5 1.4 copy-done.2
  101.9 3.0 %tick.3 = (bf16[192,128]{1,0:T(8,128)(2,1)}, bf16[384,128]{1,0:T(8,128)(2,1)S(1)}) custom-call(s32[2]{0:T(128)S(1)} %pad_add_fusion.where_ref, bf16[3072,128]{1,0:T(8,128)(2,1)S(1)} %all_gather.33.own_ref.own0_ref, bf16[3072,128]{1,0:T(8,128)(2,1)} %collective-permute-done.4.other_ref.other0_ref, bf16[6144,128]{1,0:T(8,128)(2,1)S(1)} %copy-done.2, ...), custom_call_target="tpu_custom_call" | custom-call | tf_op jit(solution)/shard_map/tick/pallas_call | solution.py:146
  105.5 26.5 %all_gather.35 = bf16[768,128]{1,0:T(8,128)(2,1)S(1)} all-gather(bf16[192,128]{1,0:T(8,128)(2,1)} %get-tuple-element.16), channel_id=1, replica_groups={{0,8,16,24},{1,9,17,25},{2,10,18,26},{3,11,19,27},{4,12,20,28},{5,13,21..., dimensions={0}, use_global_device_ids=true | all-gather | bytes 245760 | tf_op jit(solution)/shard_map/all_gather | solution.py:77
  132.7 11.8 %all_gather.36.own1_ref = bf16[3072,128]{1,0:T(8,128)(2,1)S(1)} all-gather(bf16[768,128]{1,0:T(8,128)(2,1)S(1)} %all_gather.35), channel_id=1, replica_groups={{0,2,4,6},{1,3,5,7},{8,10,12,14},{9,11,13,15},{16,18,20,22},{17,19,21,2..., dimensions={0}, use_global_device_ids=true | all-gather | bytes 983040 | tf_op jit(solution)/shard_map/all_gather | solution.py:77
  144.4 6.4 %collective-permute-start.6 = (bf16[3072,128]{1,0:T(8,128)(2,1)S(1)}, bf16[3072,128]{1,0:T(8,128)(2,1)S(1)}, u32[]{:S(2)}, u32[]{:S(2)}) collective-permute-start(bf16[3072,128]{1,0:T(8,128)(2,1)S(1)} %all_gather.36.own1_ref), channel_id=1, source_target_pairs={{0,1},{1,0},{2,3},{3,2},{4,5},{5,4},{6,7},{7,6},{8,9},{9,8},{10,11... | collective-permute-start | bytes 2359304 | tf_op jit(solution)/shard_map/ppermute | solution.py:36
  150.8 1.9 collective-permute-done.6.other1_ref
  152.7 2.0 copy-done
  154.7 3.1 %predict.1 = bf16[576,128]{1,0:T(8,128)(2,1)S(1)} custom-call(s32[2]{0:T(128)S(1)} %pad_add_fusion.where_ref, bf16[3072,128]{1,0:T(8,128)(2,1)S(1)} %all_gather.33.own_ref.own0_ref, bf16[3072,128]{1,0:T(8,128)(2,1)} %collective-permute-done.4.other_ref.other0_ref, bf16[3072,128]{1,0:T(8,128)(2,1)S(1)} %all_gather.36.own1_ref, ...), custom_call_target="tpu_custom_call" | custom-call | tf_op jit(solution)/shard_map/predict/pallas_call | solution.py:178
  157.8 17.5 %all_gather.38.near_ref = bf16[2304,128]{1,0:T(8,128)(2,1)S(1)} all-gather(bf16[576,128]{1,0:T(8,128)(2,1)S(1)} %predict.1), channel_id=1, replica_groups={{0,128,256,384},{32,160,288,416},{64,192,320,448},{96,224,352,480},{1,1..., dimensions={0}, use_global_device_ids=true | all-gather | bytes 737280 | tf_op jit(solution)/shard_map/all_gather | solution.py:77
  175.3 1.9 collective-permute-start.7
  177.2 11.7 %collective-permute-done.7.far_ref = bf16[2304,128]{1,0:T(8,128)(2,1)S(1)} collective-permute-done((bf16[2304,128]{1,0:T(8,128)(2,1)S(1)}, bf16[2304,128]{1,0:T(8,128)(2,1)S(1)}, u32[]{:S(2)}, u32[]{:S(2)}) %collective-permute-start.7) | collective-permute-done | bytes 589856 | tf_op jit(solution)/shard_map/ppermute | solution.py:40
  189.0 17.5 %all-gather.8.cloned.1.call-done.rows_ref = bf16[12288,128]{1,0:T(8,128)(2,1)} async-done(((bf16[384,128]{1,0:T(8,128)(2,1)}), bf16[12288,128]{1,0:T(8,128)(2,1)}) %all-gather.8.cloned.1.call-update) | async-done | bytes 3145744 | tf_op jit(solution)/shard_map/all_gather | solution.py:256
  206.5 1.9 copy-done.1
  208.4 2.5 %gradient.1 = (f32[288,384]{1,0:T(8,128)S(1)}, bf16[288,384]{1,0:T(8,128)(2,1)S(1)}) custom-call(s32[2]{0:T(128)S(1)} %pad_add_fusion.where_ref, bf16[2304,128]{1,0:T(8,128)(2,1)S(1)} %all_gather.38.near_ref, bf16[2304,128]{1,0:T(8,128)(2,1)S(1)} %collective-permute-done.7.far_ref, bf16[12288,128]{1,0:T(8,128)(2,1)S(1)} %copy-done.1), custom_call_target="tpu_custom_call" | custom-call | tf_op jit(solution)/shard_map/gradient/pallas_call | solution.py:214
  210.9 1.9 collective-permute-start.8
  212.8 6.8 %collective-permute-done.8 = bf16[288,384]{1,0:T(8,128)(2,1)S(1)} collective-permute-done((bf16[288,384]{1,0:T(8,128)(2,1)S(1)}, bf16[288,384]{1,0:T(8,128)(2,1)S(1)}, u32[]{:S(2)}, u32[]{:S(2)}) %collective-permute-start.8) | collective-permute-done | bytes 221216 | tf_op jit(solution)/shard_map/ppermute | solution.py:50
  (23 shorter events, 3.0 us)
Async XLA Ops:
  7.2 93.3 %all-gather.4.cloned.1.call-start = ((), (), s32[]{:S(2)}) async-start(), calls=%async_computation | async-start | bytes 1622016 | tf_op jit(solution)/shard_map/all_gather | solution.py:237
  7.9 144.8 %all-gather.6.cloned.1.call-start = ((), (), s32[]{:S(2)}) async-start(), calls=%async_computation.1 | async-start | bytes 3981312 | tf_op jit(solution)/shard_map/all_gather | solution.py:77
  7.9 24.1 %collective-permute-start = (bf16[288,384]{1,0:T(8,128)(2,1)}, bf16[288,384]{1,0:T(8,128)(2,1)S(1)}, u32[]{:S(2)}, u32[]{:S(2)}) collective-permute-start(bf16[288,384]{1,0:T(8,128)(2,1)} %bitcast.26), channel_id=1, source_target_pairs={{0,32},{32,0},{64,96},{96,64},{128,160},{160,128},{192,224},{224,1... | collective-permute-start | bytes 663560 | tf_op jit(solution)/shard_map/ppermute | solution.py:50
  33.8 22.4 %copy-start.4 = (bf16[1,2,128,288]{2,3,1,0:T(8,128)(2,1)S(1)}, bf16[1,2,128,288]{2,3,1,0:T(8,128)(2,1)}, u32[]{:S(2)}) copy-start(bf16[1,2,128,288]{2,3,1,0:T(8,128)(2,1)} %param.11) | copy-start | bytes 442372
  33.8 24.4 %copy-start.3 = (bf16[1,128,192]{1,2,0:T(8,128)(2,1)S(1)}, bf16[1,128,192]{1,2,0:T(8,128)(2,1)}, u32[]{:S(2)}) copy-start(bf16[1,128,192]{1,2,0:T(8,128)(2,1)} %param.6) | copy-start | bytes 147460
  33.8 172.7 %all-gather.8.cloned.1.call-start = ((), (), s32[]{:S(2)}) async-start(), calls=%async_computation.2 | async-start | bytes 3244032 | tf_op jit(solution)/shard_map/all_gather | solution.py:256
  45.7 12.4 %collective-permute-start.1 = (bf16[3072,128]{1,0:T(8,128)(2,1)S(1)}, bf16[3072,128]{1,0:T(8,128)(2,1)}, u32[]{:S(2)}, u32[]{:S(2)}) collective-permute-start(bf16[3072,128]{1,0:T(8,128)(2,1)S(1)} %all_gather.31.own_ref), channel_id=1, source_target_pairs={{0,1},{1,0},{2,3},{3,2},{4,5},{5,4},{6,7},{7,6},{8,9},{9,8},{10,11... | collective-permute-start | bytes 2359304 | tf_op jit(solution)/shard_map/ppermute | solution.py:36
  56.2 9.6 %collective-permute-start.3 = (bf16[2,288,128]{2,1,0:T(8,128)(2,1)S(1)}, bf16[2,288,128]{2,1,0:T(8,128)(2,1)S(1)}, u32[]{:S(2)}, u32[]{:S(2)}) collective-permute-start(bf16[2,288,128]{2,1,0:T(8,128)(2,1)S(1)} %bitcast.24), channel_id=1, source_target_pairs={{0,32},{32,64},{64,96},{96,128},{128,160},{160,192},{192,224},{224... | collective-permute-start | bytes 442376 | tf_op jit(solution)/shard_map/ppermute | solution.py:54
  60.5 7.4 %collective-permute-start.2 = (bf16[192,128]{1,0:T(8,128)(2,1)S(1)}, bf16[192,128]{1,0:T(8,128)(2,1)S(1)}, u32[]{:S(2)}, u32[]{:S(2)}) collective-permute-start(bf16[192,128]{1,0:T(8,128)(2,1)S(1)} %tick.2), channel_id=1, source_target_pairs={{0,32},{32,64},{64,96},{96,128},{128,160},{160,192},{192,224},{224... | collective-permute-start | bytes 147464 | tf_op jit(solution)/shard_map/ppermute | solution.py:54
  90.1 10.4 %collective-permute-start.4 = (bf16[3072,128]{1,0:T(8,128)(2,1)S(1)}, bf16[3072,128]{1,0:T(8,128)(2,1)}, u32[]{:S(2)}, u32[]{:S(2)}) collective-permute-start(bf16[3072,128]{1,0:T(8,128)(2,1)S(1)} %all_gather.33.own_ref.own0_ref), channel_id=1, source_target_pairs={{0,1},{1,0},{2,3},{3,2},{4,5},{5,4},{6,7},{7,6},{8,9},{9,8},{10,11... | collective-permute-start | bytes 2359304 | tf_op jit(solution)/shard_map/ppermute | solution.py:36
  100.5 1.4 copy-start.2
  104.8 27.2 %collective-permute-start.5 = (bf16[384,128]{1,0:T(8,128)(2,1)S(1)}, bf16[384,128]{1,0:T(8,128)(2,1)S(1)}, u32[]{:S(2)}, u32[]{:S(2)}) collective-permute-start(bf16[384,128]{1,0:T(8,128)(2,1)S(1)} %get-tuple-element.17), channel_id=1, source_target_pairs={{0,0},{1,1},{2,2},{3,3},{4,64},{5,65},{6,66},{7,67},{8,128},{9,129... | collective-permute-start | bytes 294920 | tf_op jit(solution)/shard_map/ppermute | solution.py:65
  132.0 0.6 copy-start.5
  144.4 8.3 %collective-permute-start.6 = (bf16[3072,128]{1,0:T(8,128)(2,1)S(1)}, bf16[3072,128]{1,0:T(8,128)(2,1)S(1)}, u32[]{:S(2)}, u32[]{:S(2)}) collective-permute-start(bf16[3072,128]{1,0:T(8,128)(2,1)S(1)} %all_gather.36.own1_ref), channel_id=1, source_target_pairs={{0,1},{1,0},{2,3},{3,2},{4,5},{5,4},{6,7},{7,6},{8,9},{9,8},{10,11... | collective-permute-start | bytes 2359304 | tf_op jit(solution)/shard_map/ppermute | solution.py:36
  152.7 2.0 copy-start
  175.3 13.7 %collective-permute-start.7 = (bf16[2304,128]{1,0:T(8,128)(2,1)S(1)}, bf16[2304,128]{1,0:T(8,128)(2,1)S(1)}, u32[]{:S(2)}, u32[]{:S(2)}) collective-permute-start(bf16[2304,128]{1,0:T(8,128)(2,1)S(1)} %all_gather.38.near_ref), channel_id=1, source_target_pairs={{0,64},{32,96},{64,0},{96,32},{128,192},{160,224},{192,128},{224,1... | collective-permute-start | bytes 1769480 | tf_op jit(solution)/shard_map/ppermute | solution.py:40
  206.5 1.9 copy-start.1
  210.9 8.7 %collective-permute-start.8 = (bf16[288,384]{1,0:T(8,128)(2,1)S(1)}, bf16[288,384]{1,0:T(8,128)(2,1)S(1)}, u32[]{:S(2)}, u32[]{:S(2)}) collective-permute-start(bf16[288,384]{1,0:T(8,128)(2,1)S(1)} %get-tuple-element.23), channel_id=1, source_target_pairs={{0,32},{32,0},{64,96},{96,64},{128,160},{160,128},{192,224},{224,1... | collective-permute-start | bytes 663560 | tf_op jit(solution)/shard_map/ppermute | solution.py:50
Sparse Core Ops, SparseCore 0:
  11.1 64.6 all-gather.3
  78.5 60.9 all-gather.5
  142.7 63.8 all-gather.7

commit v10 on v9

--- a/solution.py
+++ b/solution.py
@@ -27,6 +27,7 @@
 
 
 Z_GROUPS = [[t_index(z, x, c) for z in range(NZ)] for x in range(NX) for c in range(NC)]
+XC_GROUPS = [[t_index(z, x, c) for x in range(NX) for c in range(NC)] for z in range(NZ)]
 SECOND_Y_GROUPS = [[(2 * i + p) * 2 + zl for i in range(NY // 2)] for p in range(2) for zl in range(2)]
 Y_GROUPS = [[y * 2 + zl for y in range(NY)] for zl in range(2)]
 X_GROUPS = [[t_index(z, x, c) for x in range(NX)] for z in range(NZ) for c in range(NC)]
@@ -130,7 +131,9 @@
 
     @pl.when(first)
     def _():
-        full[...] = fresh_ref[...]
+        for z, x, c in all_t():
+            source, at = ((x * NC + c) * NZ + z) * PIECE, t_index(z, x, c) * PIECE
+            full[at : at + PIECE, :] = fresh_ref[source : source + PIECE, :]
 
     @pl.when(jnp.logical_not(first))
     def _():
@@ -234,11 +237,12 @@
     entering_t, fresh_t = entering[0].T, fresh_rows[0].T
 
     mine_block = projection.T
-    fresh_all = lax.all_gather(fresh_t, "tensor", axis=0, tiled=True)
-    first = z_gather(entering_t)
-    other_block, first = together(zl_swap(mine_block), first)
+    start = z_gather(stack(entering_t, fresh_t)).reshape(NZ, 2, PIECE, ROWS)
+    fresh_all = gather(start[:, 1].reshape(NZ * PIECE, ROWS), "tensor", XC_GROUPS)
+    first = start[:, 0].reshape(NZ * PIECE, ROWS)
+    own = x_gather(first)
+    other_block, own = together(zl_swap(mine_block), own)
     blocks = gather(stack(mine_block, other_block), "segment", Y_GROUPS)
-    own = x_gather(first)
     taught0 = to_next_segment(together(teacher, own)[0])
     (out0,) = tick(first_tick_kernel, (PIECE,), where, own, core_swap(own), weights, entering_t)
 

time: 228 us -> 217 us (0.952)
  waiting for transfers between devices: 42.9 us -> 32.2 us
  starting transfers between devices: 38.6 us -> 34.5 us
  blocking collectives: 109 us -> 112 us
    all_gather x1, waiting for transfers between devices: 17.5 us -> 4.79 us  [on_device(): rows = lax.all_gather(turned, 'tensor', axis=0, tiled=True)]
    all_gather x7, blocking collectives: 109 us -> 112 us  [gather(): lax.all_gather(value, axis, axis=0, tiled=True, axis_index_groups=groups)]
    ppermute x1, waiting for transfers between devices: 11.7 us -> 14.3 us  [over_y(): lax.ppermute(value, 'segment', [(y * 2 + zl, move(y) % NY * 2 + zl) for y...]
    ppermute x3, starting transfers between devices: 22.9 us -> 20.5 us  [over_tensor(): lax.ppermute(value, 'tensor', [(t_index(*p), t_index(*move(*p))) for p in...]
    unnamed x12 -> x14, local copies, waits for them, and re-layouts: 5.95 us -> 5.96 us
where the time goes in v10:
time: 217 us; the launch traced here: 216 us
  blocking collectives  112 us (52%)
  starting transfers between devices  34.5 us (16%)
  waiting for transfers between devices  32.2 us (15%)
  between operations  13.9 us (6%)
  Pallas kernels  10.8 us (5%)
  local copies, waits for them, and re-layouts  6.67 us (3%)
  other arithmetic  6.49 us (3%)
    all_gather x7, blocking collectives, gather(): lax.all_gather(value, axis, axis=0, tiled=True, axis_index_groups=groups)  112 us
    ppermute x3, starting transfers between devices, over_tensor(): lax.ppermute(value, 'tensor', [(t_index(*p), t_index(*move(*p))) for p in...  20.5 us
    ppermute x1, waiting for transfers between devices, over_y(): lax.ppermute(value, 'segment', [(y * 2 + zl, move(y) % NY * 2 + zl) for y...  14.3 us
    ppermute x2, waiting for transfers between devices, zl_swap(): return lax.ppermute(value, 'segment', [(i, i ^ 1) for i in range(16)])  6.75 us
    ppermute x2, starting transfers between devices, to_next_segment(): lax.ppermute(value, 'segment', [(s, (s + 1) % 16) for s in range(16)])  6.28 us
    unnamed x14, local copies, waits for them, and re-layouts  5.96 us
    pallas_call x2, Pallas kernels, tick(): pl.pallas_call(kernel, out_shape=[jax.ShapeDtypeStruct((rows, ROWS), jnp....  5.29 us
    ppermute x2, starting transfers between devices, zl_swap(): return lax.ppermute(value, 'segment', [(i, i ^ 1) for i in range(16)])  5.08 us
  transfers between devices with their start and end apart: 12, of which 7 were waited for; matrix products, arithmetic and copies ran while one was open for 2% of the time, Pallas kernels for 4%

profile of v10, /device:TPU:1, one launch (start us, length us, event | category | flops | bytes accessed | tf_op | source)
XLA Modules:
  0.0 216.5 jit_solution(12615049527215045295)
XLA Ops:
  7.2 0.8 pad_maximum_fusion.1
  8.1 19.9 %all_gather.30 = bf16[1536,128]{1,0:T(8,128)(2,1)S(1)} all-gather(bf16[384,128]{1,0:T(8,128)(2,1)S(1)} %pad_maximum_fusion.1), channel_id=1, replica_groups={{0,8,16,24},{1,9,17,25},{2,10,18,26},{3,11,19,27},{4,12,20,28},{5,13,21..., dimensions={0}, use_global_device_ids=true | all-gather | bytes 491520 | tf_op jit(solution)/shard_map/all_gather | solution.py:78
  28.7 3.2 %collective-permute-start = (bf16[288,384]{1,0:T(8,128)(2,1)}, bf16[288,384]{1,0:T(8,128)(2,1)S(1)}, u32[]{:S(2)}, u32[]{:S(2)}) collective-permute-start(bf16[288,384]{1,0:T(8,128)(2,1)} %bitcast.32), channel_id=1, source_target_pairs={{0,32},{32,0},{64,96},{96,64},{128,160},{160,128},{192,224},{224,1... | collective-permute-start | bytes 663560 | tf_op jit(solution)/shard_map/ppermute | solution.py:51
  31.9 11.3 %all_gather.31.own_ref = bf16[3072,128]{1,0:T(8,128)(2,1)S(1)} all-gather(bf16[768,128]{1,0:T(8,128)(2,1)S(1)} %bitcast.31), channel_id=1, replica_groups={{0,2,4,6},{1,3,5,7},{8,10,12,14},{9,11,13,15},{16,18,20,22},{17,19,21,2..., dimensions={0}, use_global_device_ids=true | all-gather | bytes 983040 | tf_op jit(solution)/shard_map/all_gather | solution.py:78
  43.2 1.8 pad_maximum_fusion
  45.1 7.9 %collective-permute-start.1 = (bf16[3072,128]{1,0:T(8,128)(2,1)S(1)}, bf16[3072,128]{1,0:T(8,128)(2,1)}, u32[]{:S(2)}, u32[]{:S(2)}) collective-permute-start(bf16[3072,128]{1,0:T(8,128)(2,1)S(1)} %all_gather.31.own_ref), channel_id=1, source_target_pairs={{0,1},{1,0},{2,3},{3,2},{4,5},{5,4},{6,7},{7,6},{8,9},{9,8},{10,11... | collective-permute-start | bytes 2359304 | tf_op jit(solution)/shard_map/ppermute | solution.py:37
  53.0 2.2 %fusion.weight_ref = bf16[192,6144]{1,0:T(8,128)(2,1)S(1)} fusion(bf16[1,192,6144]{2,1,0:T(8,128)(2,1)} %param.9, f32[6144]{0:T(1024)S(1)} %bitcast.36), kind=kLoop, calls=%fused_computation.1 | loop fusion | flops 3538944 | bytes 4743168 | tf_op jit(solution)/shard_map/convert_element_type | solution.py:94
  55.2 2.5 %collective-permute-start.3 = (bf16[2,288,128]{2,1,0:T(8,128)(2,1)S(1)}, bf16[2,288,128]{2,1,0:T(8,128)(2,1)S(1)}, u32[]{:S(2)}, u32[]{:S(2)}) collective-permute-start(bf16[2,288,128]{2,1,0:T(8,128)(2,1)S(1)} %bitcast.27), channel_id=1, source_target_pairs={{0,32},{32,64},{64,96},{96,128},{128,160},{160,192},{192,224},{224... | collective-permute-start | bytes 442376 | tf_op jit(solution)/shard_map/ppermute | solution.py:55
  57.8 2.3 %tick.2 = bf16[192,128]{1,0:T(8,128)(2,1)S(1)} custom-call(s32[2]{0:T(128)S(1)} %pad_add_fusion.where_ref, bf16[3072,128]{1,0:T(8,128)(2,1)S(1)} %all_gather.31.own_ref, bf16[3072,128]{1,0:T(8,128)(2,1)} %collective-permute-done.1.other_ref, bf16[192,6144]{1,0:T(8,128)(2,1)S(1)} %fusion.weight_ref, bf16[192,128]{1,0:T(8,128)(2,1)S(1)} %bitcast.26), custom_call_target="tpu_custom_call" | custom-call | tf_op jit(solution)/shard_map/tick/pallas_call | solution.py:149
  60.1 3.7 %collective-permute-start.2 = (bf16[192,128]{1,0:T(8,128)(2,1)S(1)}, bf16[192,128]{1,0:T(8,128)(2,1)S(1)}, u32[]{:S(2)}, u32[]{:S(2)}) collective-permute-start(bf16[192,128]{1,0:T(8,128)(2,1)S(1)} %tick.2), channel_id=1, source_target_pairs={{0,32},{32,64},{64,96},{96,128},{128,160},{160,192},{192,224},{224... | collective-permute-start | bytes 147464 | tf_op jit(solution)/shard_map/ppermute | solution.py:55
  64.7 2.4 %collective-permute-done.2.moved_ref = bf16[192,128]{1,0:T(8,128)(2,1)S(1)} collective-permute-done((bf16[192,128]{1,0:T(8,128)(2,1)S(1)}, bf16[192,128]{1,0:T(8,128)(2,1)S(1)}, u32[]{:S(2)}, u32[]{:S(2)}) %collective-permute-start.2) | collective-permute-done | bytes 49184 | tf_op jit(solution)/shard_map/ppermute | solution.py:55
  67.1 12.3 %all_gather.32 = bf16[768,128]{1,0:T(8,128)(2,1)S(1)} all-gather(bf16[192,128]{1,0:T(8,128)(2,1)S(1)} %collective-permute-done.2.moved_ref), channel_id=1, replica_groups={{0,8,16,24},{1,9,17,25},{2,10,18,26},{3,11,19,27},{4,12,20,28},{5,13,21..., dimensions={0}, use_global_device_ids=true | all-gather | bytes 245760 | tf_op jit(solution)/shard_map/all_gather | solution.py:78
  79.3 11.7 %all_gather.33.own_ref.own0_ref = bf16[3072,128]{1,0:T(8,128)(2,1)S(1)} all-gather(bf16[768,128]{1,0:T(8,128)(2,1)S(1)} %all_gather.32), channel_id=1, replica_groups={{0,2,4,6},{1,3,5,7},{8,10,12,14},{9,11,13,15},{16,18,20,22},{17,19,21,2..., dimensions={0}, use_global_device_ids=true | all-gather | bytes 983040 | tf_op jit(solution)/shard_map/all_gather | solution.py:78
  91.1 6.8 %collective-permute-start.4 = (bf16[3072,128]{1,0:T(8,128)(2,1)S(1)}, bf16[3072,128]{1,0:T(8,128)(2,1)}, u32[]{:S(2)}, u32[]{:S(2)}) collective-permute-start(bf16[3072,128]{1,0:T(8,128)(2,1)S(1)} %all_gather.33.own_ref.own0_ref), channel_id=1, source_target_pairs={{0,1},{1,0},{2,3},{3,2},{4,5},{5,4},{6,7},{7,6},{8,9},{9,8},{10,11... | collective-permute-start | bytes 2359304 | tf_op jit(solution)/shard_map/ppermute | solution.py:37
  97.8 0.8 broadcast_select_fusion.mine_ref
  98.7 1.2 collective-permute-done.4.other_ref.other0_ref
  99.9 1.4 copy-done.2
  101.3 3.0 %tick.3 = (bf16[192,128]{1,0:T(8,128)(2,1)}, bf16[384,128]{1,0:T(8,128)(2,1)S(1)}) custom-call(s32[2]{0:T(128)S(1)} %pad_add_fusion.where_ref, bf16[3072,128]{1,0:T(8,128)(2,1)S(1)} %all_gather.33.own_ref.own0_ref, bf16[3072,128]{1,0:T(8,128)(2,1)} %collective-permute-done.4.other_ref.other0_ref, bf16[6144,128]{1,0:T(8,128)(2,1)S(1)} %copy-done.2, ...), custom_call_target="tpu_custom_call" | custom-call | tf_op jit(solution)/shard_map/tick/pallas_call | solution.py:149
  104.9 28.9 %all_gather.35 = bf16[768,128]{1,0:T(8,128)(2,1)S(1)} all-gather(bf16[192,128]{1,0:T(8,128)(2,1)} %get-tuple-element.16), channel_id=1, replica_groups={{0,8,16,24},{1,9,17,25},{2,10,18,26},{3,11,19,27},{4,12,20,28},{5,13,21..., dimensions={0}, use_global_device_ids=true | all-gather | bytes 245760 | tf_op jit(solution)/shard_map/all_gather | solution.py:78
  134.4 11.4 %all_gather.36.own1_ref = bf16[3072,128]{1,0:T(8,128)(2,1)S(1)} all-gather(bf16[768,128]{1,0:T(8,128)(2,1)S(1)} %all_gather.35), channel_id=1, replica_groups={{0,2,4,6},{1,3,5,7},{8,10,12,14},{9,11,13,15},{16,18,20,22},{17,19,21,2..., dimensions={0}, use_global_device_ids=true | all-gather | bytes 983040 | tf_op jit(solution)/shard_map/all_gather | solution.py:78
  145.8 5.8 %collective-permute-start.6 = (bf16[3072,128]{1,0:T(8,128)(2,1)S(1)}, bf16[3072,128]{1,0:T(8,128)(2,1)S(1)}, u32[]{:S(2)}, u32[]{:S(2)}) collective-permute-start(bf16[3072,128]{1,0:T(8,128)(2,1)S(1)} %all_gather.36.own1_ref), channel_id=1, source_target_pairs={{0,1},{1,0},{2,3},{3,2},{4,5},{5,4},{6,7},{7,6},{8,9},{9,8},{10,11... | collective-permute-start | bytes 2359304 | tf_op jit(solution)/shard_map/ppermute | solution.py:37
  151.6 1.9 collective-permute-done.6.other1_ref
  153.5 2.0 copy-done
  155.5 3.1 %predict.1 = bf16[576,128]{1,0:T(8,128)(2,1)S(1)} custom-call(s32[2]{0:T(128)S(1)} %pad_add_fusion.where_ref, bf16[3072,128]{1,0:T(8,128)(2,1)S(1)} %all_gather.33.own_ref.own0_ref, bf16[3072,128]{1,0:T(8,128)(2,1)} %collective-permute-done.4.other_ref.other0_ref, bf16[3072,128]{1,0:T(8,128)(2,1)S(1)} %all_gather.36.own1_ref, ...), custom_call_target="tpu_custom_call" | custom-call | tf_op jit(solution)/shard_map/predict/pallas_call | solution.py:181
  158.6 16.5 %all_gather.38.near_ref = bf16[2304,128]{1,0:T(8,128)(2,1)S(1)} all-gather(bf16[576,128]{1,0:T(8,128)(2,1)S(1)} %predict.1), channel_id=1, replica_groups={{0,128,256,384},{32,160,288,416},{64,192,320,448},{96,224,352,480},{1,1..., dimensions={0}, use_global_device_ids=true | all-gather | bytes 737280 | tf_op jit(solution)/shard_map/all_gather | solution.py:78
  175.1 1.9 collective-permute-start.7
  177.0 14.3 %collective-permute-done.7.far_ref = bf16[2304,128]{1,0:T(8,128)(2,1)S(1)} collective-permute-done((bf16[2304,128]{1,0:T(8,128)(2,1)S(1)}, bf16[2304,128]{1,0:T(8,128)(2,1)S(1)}, u32[]{:S(2)}, u32[]{:S(2)}) %collective-permute-start.7) | collective-permute-done | bytes 589856 | tf_op jit(solution)/shard_map/ppermute | solution.py:41
  191.3 4.8 %all-gather.8.cloned.1.call-done.rows_ref = bf16[12288,128]{1,0:T(8,128)(2,1)} async-done(((bf16[384,128]{1,0:T(8,128)(2,1)}), bf16[12288,128]{1,0:T(8,128)(2,1)}) %all-gather.8.cloned.1.call-update) | async-done | bytes 3145744 | tf_op jit(solution)/shard_map/all_gather | solution.py:260
  196.1 1.9 copy-done.1
  198.0 2.5 %gradient.1 = (f32[288,384]{1,0:T(8,128)S(1)}, bf16[288,384]{1,0:T(8,128)(2,1)S(1)}) custom-call(s32[2]{0:T(128)S(1)} %pad_add_fusion.where_ref, bf16[2304,128]{1,0:T(8,128)(2,1)S(1)} %all_gather.38.near_ref, bf16[2304,128]{1,0:T(8,128)(2,1)S(1)} %collective-permute-done.7.far_ref, bf16[12288,128]{1,0:T(8,128)(2,1)S(1)} %copy-done.1), custom_call_target="tpu_custom_call" | custom-call | tf_op jit(solution)/shard_map/gradient/pallas_call | solution.py:217
  200.4 1.9 collective-permute-start.8
  202.4 6.7 %collective-permute-done.8 = bf16[288,384]{1,0:T(8,128)(2,1)S(1)} collective-permute-done((bf16[288,384]{1,0:T(8,128)(2,1)S(1)}, bf16[288,384]{1,0:T(8,128)(2,1)S(1)}, u32[]{:S(2)}, u32[]{:S(2)}) %collective-permute-start.8) | collective-permute-done | bytes 221216 | tf_op jit(solution)/shard_map/ppermute | solution.py:51
  (27 shorter events, 3.9 us)
Async XLA Ops:
  7.2 45.8 %copy-start.6 = (f32[1,6144]{1,0:T(1,128)S(1)}, f32[1,6144]{1,0:T(1,128)}, u32[]{:S(2)}) copy-start(f32[1,6144]{1,0:T(1,128)} %param.8) | copy-start | bytes 73732
  7.2 92.7 %all-gather.4.cloned.1.call-start = ((), (), s32[]{:S(2)}) async-start(), calls=%async_computation | async-start | bytes 1769472 | tf_op jit(solution)/shard_map/all_gather | solution.py:78
  28.7 124.9 %all-gather.6.cloned.1.call-start = ((), (), s32[]{:S(2)}) async-start(), calls=%async_computation.1 | async-start | bytes 3981312 | tf_op jit(solution)/shard_map/all_gather | solution.py:78
  28.7 14.5 %collective-permute-start = (bf16[288,384]{1,0:T(8,128)(2,1)}, bf16[288,384]{1,0:T(8,128)(2,1)S(1)}, u32[]{:S(2)}, u32[]{:S(2)}) collective-permute-start(bf16[288,384]{1,0:T(8,128)(2,1)} %bitcast.32), channel_id=1, source_target_pairs={{0,32},{32,0},{64,96},{96,64},{128,160},{160,128},{192,224},{224,1... | collective-permute-start | bytes 663560 | tf_op jit(solution)/shard_map/ppermute | solution.py:51
  43.2 11.9 %copy-start.4 = (bf16[1,2,128,288]{2,3,1,0:T(8,128)(2,1)S(1)}, bf16[1,2,128,288]{2,3,1,0:T(8,128)(2,1)}, u32[]{:S(2)}) copy-start(bf16[1,2,128,288]{2,3,1,0:T(8,128)(2,1)} %param.11) | copy-start | bytes 442372
  43.2 14.6 %copy-start.3 = (bf16[1,128,192]{1,2,0:T(8,128)(2,1)S(1)}, bf16[1,128,192]{1,2,0:T(8,128)(2,1)}, u32[]{:S(2)}) copy-start(bf16[1,128,192]{1,2,0:T(8,128)(2,1)} %param.6) | copy-start | bytes 147460
  45.0 151.1 %all-gather.8.cloned.1.call-start = ((), (), s32[]{:S(2)}) async-start(), calls=%async_computation.2 | async-start | bytes 3244032 | tf_op jit(solution)/shard_map/all_gather | solution.py:260
  45.1 12.7 %collective-permute-start.1 = (bf16[3072,128]{1,0:T(8,128)(2,1)S(1)}, bf16[3072,128]{1,0:T(8,128)(2,1)}, u32[]{:S(2)}, u32[]{:S(2)}) collective-permute-start(bf16[3072,128]{1,0:T(8,128)(2,1)S(1)} %all_gather.31.own_ref), channel_id=1, source_target_pairs={{0,1},{1,0},{2,3},{3,2},{4,5},{5,4},{6,7},{7,6},{8,9},{9,8},{10,11... | collective-permute-start | bytes 2359304 | tf_op jit(solution)/shard_map/ppermute | solution.py:37
  55.2 9.5 %collective-permute-start.3 = (bf16[2,288,128]{2,1,0:T(8,128)(2,1)S(1)}, bf16[2,288,128]{2,1,0:T(8,128)(2,1)S(1)}, u32[]{:S(2)}, u32[]{:S(2)}) collective-permute-start(bf16[2,288,128]{2,1,0:T(8,128)(2,1)S(1)} %bitcast.27), channel_id=1, source_target_pairs={{0,32},{32,64},{64,96},{96,128},{128,160},{160,192},{192,224},{224... | collective-permute-start | bytes 442376 | tf_op jit(solution)/shard_map/ppermute | solution.py:55
  60.1 6.9 %collective-permute-start.2 = (bf16[192,128]{1,0:T(8,128)(2,1)S(1)}, bf16[192,128]{1,0:T(8,128)(2,1)S(1)}, u32[]{:S(2)}, u32[]{:S(2)}) collective-permute-start(bf16[192,128]{1,0:T(8,128)(2,1)S(1)} %tick.2), channel_id=1, source_target_pairs={{0,32},{32,64},{64,96},{96,128},{128,160},{160,192},{192,224},{224... | collective-permute-start | bytes 147464 | tf_op jit(solution)/shard_map/ppermute | solution.py:55
  91.1 8.8 %collective-permute-start.4 = (bf16[3072,128]{1,0:T(8,128)(2,1)S(1)}, bf16[3072,128]{1,0:T(8,128)(2,1)}, u32[]{:S(2)}, u32[]{:S(2)}) collective-permute-start(bf16[3072,128]{1,0:T(8,128)(2,1)S(1)} %all_gather.33.own_ref.own0_ref), channel_id=1, source_target_pairs={{0,1},{1,0},{2,3},{3,2},{4,5},{5,4},{6,7},{7,6},{8,9},{9,8},{10,11... | collective-permute-start | bytes 2359304 | tf_op jit(solution)/shard_map/ppermute | solution.py:37
  99.9 1.4 copy-start.2
  104.2 29.5 %collective-permute-start.5 = (bf16[384,128]{1,0:T(8,128)(2,1)S(1)}, bf16[384,128]{1,0:T(8,128)(2,1)S(1)}, u32[]{:S(2)}, u32[]{:S(2)}) collective-permute-start(bf16[384,128]{1,0:T(8,128)(2,1)S(1)} %get-tuple-element.17), channel_id=1, source_target_pairs={{0,0},{1,1},{2,2},{3,3},{4,64},{5,65},{6,66},{7,67},{8,128},{9,129... | collective-permute-start | bytes 294920 | tf_op jit(solution)/shard_map/ppermute | solution.py:66
  133.8 0.6 copy-start.5
  145.8 7.7 %collective-permute-start.6 = (bf16[3072,128]{1,0:T(8,128)(2,1)S(1)}, bf16[3072,128]{1,0:T(8,128)(2,1)S(1)}, u32[]{:S(2)}, u32[]{:S(2)}) collective-permute-start(bf16[3072,128]{1,0:T(8,128)(2,1)S(1)} %all_gather.36.own1_ref), channel_id=1, source_target_pairs={{0,1},{1,0},{2,3},{3,2},{4,5},{5,4},{6,7},{7,6},{8,9},{9,8},{10,11... | collective-permute-start | bytes 2359304 | tf_op jit(solution)/shard_map/ppermute | solution.py:37
  153.5 2.0 copy-start
  175.1 16.2 %collective-permute-start.7 = (bf16[2304,128]{1,0:T(8,128)(2,1)S(1)}, bf16[2304,128]{1,0:T(8,128)(2,1)S(1)}, u32[]{:S(2)}, u32[]{:S(2)}) collective-permute-start(bf16[2304,128]{1,0:T(8,128)(2,1)S(1)} %all_gather.38.near_ref), channel_id=1, source_target_pairs={{0,64},{32,96},{64,0},{96,32},{128,192},{160,224},{192,128},{224,1... | collective-permute-start | bytes 1769480 | tf_op jit(solution)/shard_map/ppermute | solution.py:41
  196.1 1.9 copy-start.1
  200.4 8.7 %collective-permute-start.8 = (bf16[288,384]{1,0:T(8,128)(2,1)S(1)}, bf16[288,384]{1,0:T(8,128)(2,1)S(1)}, u32[]{:S(2)}, u32[]{:S(2)}) collective-permute-start(bf16[288,384]{1,0:T(8,128)(2,1)S(1)} %get-tuple-element.23), channel_id=1, source_target_pairs={{0,32},{32,0},{64,96},{96,64},{128,160},{160,128},{192,224},{224,1... | collective-permute-start | bytes 663560 | tf_op jit(solution)/shard_map/ppermute | solution.py:51
Sparse Core Ops, SparseCore 0:
  28.8 32.2 all-gather.3
  63.7 54.1 all-gather.5
  134.5 61.5 all-gather.7

commit v11 on v10

--- a/solution.py
+++ b/solution.py
@@ -255,8 +255,8 @@
         second_tick_kernel, (PIECE, 2 * PIECE), where, own0, other0, fresh_all, weights, mine, moved
     )
 
+    turned, out1 = together(transposition(both), out1)
     second = z_gather(out1)
-    turned, second = together(transposition(both), second)
     rows = lax.all_gather(turned, "tensor", axis=0, tiled=True)
     own1 = x_gather(second)
     difference = predict(where, own0, other0, own1, core_swap(own1), blocks, taught0, teacher)

time: 217 us -> 223 us (1.028); the launches traced: 216 us -> 220 us
  waiting for transfers between devices: 32.2 us -> 21.6 us
  starting transfers between devices: 34.5 us -> 42.4 us
  blocking collectives: 112 us -> 118 us
    all_gather x7, blocking collectives: 112 us -> 118 us  [gather(): lax.all_gather(value, axis, axis=0, tiled=True, axis_index_groups=groups)]
    ppermute x2, starting transfers between devices: 5.08 us -> 9.91 us  [zl_swap(): return lax.ppermute(value, 'segment', [(i, i ^ 1) for i in range(16)])]
    all_gather x1, waiting for transfers between devices: 4.79 us -> 0.01 us  [on_device(): rows = lax.all_gather(turned, 'tensor', axis=0, tiled=True)]
    ppermute x2, waiting for transfers between devices: 6.75 us -> 3.31 us  [zl_swap(): return lax.ppermute(value, 'segment', [(i, i ^ 1) for i in range(16)])]
    ppermute x3, starting transfers between devices: 20.5 us -> 23.5 us  [over_tensor(): lax.ppermute(value, 'tensor', [(t_index(*p), t_index(*move(*p))) for p in...]
    ppermute x1, waiting for transfers between devices: 14.3 us -> 12 us  [over_y(): lax.ppermute(value, 'segment', [(y * 2 + zl, move(y) % NY * 2 + zl) for y...]
  transfers between devices with their start and end apart: 12 -> 12, of which waited for: 7 -> 6; matrix products, arithmetic and copies ran while one was open for 2% -> 2% of each run, Pallas kernels for 4% -> 4%
where the time goes in v11:
time: 223 us; the launch traced here: 220 us
  blocking collectives  118 us (53%)
  starting transfers between devices  42.4 us (19%)
  waiting for transfers between devices  21.6 us (10%)
  between operations  13.9 us (6%)
  Pallas kernels  10.8 us (5%)
  local copies, waits for them, and re-layouts  6.65 us (3%)
  other arithmetic  6.49 us (3%)
    all_gather x7, blocking collectives, gather(): lax.all_gather(value, axis, axis=0, tiled=True, axis_index_groups=groups)  118 us
    ppermute x3, starting transfers between devices, over_tensor(): lax.ppermute(value, 'tensor', [(t_index(*p), t_index(*move(*p))) for p in...  23.5 us
    ppermute x1, waiting for transfers between devices, over_y(): lax.ppermute(value, 'segment', [(y * 2 + zl, move(y) % NY * 2 + zl) for y...  12 us
    ppermute x2, starting transfers between devices, zl_swap(): return lax.ppermute(value, 'segment', [(i, i ^ 1) for i in range(16)])  9.91 us
    ppermute x2, starting transfers between devices, to_next_segment(): lax.ppermute(value, 'segment', [(s, (s + 1) % 16) for s in range(16)])  6.28 us
    unnamed x14, local copies, waits for them, and re-layouts  5.94 us
    pallas_call x2, Pallas kernels, tick(): pl.pallas_call(kernel, out_shape=[jax.ShapeDtypeStruct((rows, ROWS), jnp....  5.29 us
  transfers between devices with their start and end apart: 12, of which 6 were waited for; matrix products, arithmetic and copies ran while one was open for 2% of the time, Pallas kernels for 4%

profile of v11, /device:TPU:1, one launch (start us, length us, event | category | flops | bytes accessed | tf_op | source)
XLA Modules:
  0.0 219.7 jit_solution(9326459270547554439)
XLA Ops:
  7.2 0.8 pad_maximum_fusion.1
  8.1 19.9 %all_gather.30 = bf16[1536,128]{1,0:T(8,128)(2,1)S(1)} all-gather(bf16[384,128]{1,0:T(8,128)(2,1)S(1)} %pad_maximum_fusion.1), channel_id=1, replica_groups={{0,8,16,24},{1,9,17,25},{2,10,18,26},{3,11,19,27},{4,12,20,28},{5,13,21..., dimensions={0}, use_global_device_ids=true | all-gather | bytes 491520 | tf_op jit(solution)/shard_map/all_gather | solution.py:78
  28.7 3.2 %collective-permute-start = (bf16[288,384]{1,0:T(8,128)(2,1)}, bf16[288,384]{1,0:T(8,128)(2,1)S(1)}, u32[]{:S(2)}, u32[]{:S(2)}) collective-permute-start(bf16[288,384]{1,0:T(8,128)(2,1)} %bitcast.32), channel_id=1, source_target_pairs={{0,32},{32,0},{64,96},{96,64},{128,160},{160,128},{192,224},{224,1... | collective-permute-start | bytes 663560 | tf_op jit(solution)/shard_map/ppermute | solution.py:51
  31.9 11.3 %all_gather.31.own_ref = bf16[3072,128]{1,0:T(8,128)(2,1)S(1)} all-gather(bf16[768,128]{1,0:T(8,128)(2,1)S(1)} %bitcast.31), channel_id=1, replica_groups={{0,2,4,6},{1,3,5,7},{8,10,12,14},{9,11,13,15},{16,18,20,22},{17,19,21,2..., dimensions={0}, use_global_device_ids=true | all-gather | bytes 983040 | tf_op jit(solution)/shard_map/all_gather | solution.py:78
  43.2 1.8 pad_maximum_fusion
  45.1 7.9 %collective-permute-start.1 = (bf16[3072,128]{1,0:T(8,128)(2,1)S(1)}, bf16[3072,128]{1,0:T(8,128)(2,1)}, u32[]{:S(2)}, u32[]{:S(2)}) collective-permute-start(bf16[3072,128]{1,0:T(8,128)(2,1)S(1)} %all_gather.31.own_ref), channel_id=1, source_target_pairs={{0,1},{1,0},{2,3},{3,2},{4,5},{5,4},{6,7},{7,6},{8,9},{9,8},{10,11... | collective-permute-start | bytes 2359304 | tf_op jit(solution)/shard_map/ppermute | solution.py:37
  53.0 2.2 fusion.weight_ref
  55.2 2.5 %collective-permute-start.3 = (bf16[2,288,128]{2,1,0:T(8,128)(2,1)S(1)}, bf16[2,288,128]{2,1,0:T(8,128)(2,1)S(1)}, u32[]{:S(2)}, u32[]{:S(2)}) collective-permute-start(bf16[2,288,128]{2,1,0:T(8,128)(2,1)S(1)} %bitcast.27), channel_id=1, source_target_pairs={{0,32},{32,64},{64,96},{96,128},{128,160},{160,192},{192,224},{224... | collective-permute-start | bytes 442376 | tf_op jit(solution)/shard_map/ppermute | solution.py:55
  57.8 2.3 %tick.2 = bf16[192,128]{1,0:T(8,128)(2,1)S(1)} custom-call(s32[2]{0:T(128)S(1)} %pad_add_fusion.where_ref, bf16[3072,128]{1,0:T(8,128)(2,1)S(1)} %all_gather.31.own_ref, bf16[3072,128]{1,0:T(8,128)(2,1)} %collective-permute-done.1.other_ref, bf16[192,6144]{1,0:T(8,128)(2,1)S(1)} %fusion.weight_ref, bf16[192,128]{1,0:T(8,128)(2,1)S(1)} %bitcast.26), custom_call_target="tpu_custom_call" | custom-call | tf_op jit(solution)/shard_map/tick/pallas_call | solution.py:149
  60.1 3.7 %collective-permute-start.2 = (bf16[192,128]{1,0:T(8,128)(2,1)S(1)}, bf16[192,128]{1,0:T(8,128)(2,1)S(1)}, u32[]{:S(2)}, u32[]{:S(2)}) collective-permute-start(bf16[192,128]{1,0:T(8,128)(2,1)S(1)} %tick.2), channel_id=1, source_target_pairs={{0,32},{32,64},{64,96},{96,128},{128,160},{160,192},{192,224},{224... | collective-permute-start | bytes 147464 | tf_op jit(solution)/shard_map/ppermute | solution.py:55
  64.7 2.4 %collective-permute-done.2.moved_ref = bf16[192,128]{1,0:T(8,128)(2,1)S(1)} collective-permute-done((bf16[192,128]{1,0:T(8,128)(2,1)S(1)}, bf16[192,128]{1,0:T(8,128)(2,1)S(1)}, u32[]{:S(2)}, u32[]{:S(2)}) %collective-permute-start.2) | collective-permute-done | bytes 49184 | tf_op jit(solution)/shard_map/ppermute | solution.py:55
  67.1 12.3 %all_gather.32 = bf16[768,128]{1,0:T(8,128)(2,1)S(1)} all-gather(bf16[192,128]{1,0:T(8,128)(2,1)S(1)} %collective-permute-done.2.moved_ref), channel_id=1, replica_groups={{0,8,16,24},{1,9,17,25},{2,10,18,26},{3,11,19,27},{4,12,20,28},{5,13,21..., dimensions={0}, use_global_device_ids=true | all-gather | bytes 245760 | tf_op jit(solution)/shard_map/all_gather | solution.py:78
  79.3 11.7 %all_gather.33.own_ref.own0_ref = bf16[3072,128]{1,0:T(8,128)(2,1)S(1)} all-gather(bf16[768,128]{1,0:T(8,128)(2,1)S(1)} %all_gather.32), channel_id=1, replica_groups={{0,2,4,6},{1,3,5,7},{8,10,12,14},{9,11,13,15},{16,18,20,22},{17,19,21,2..., dimensions={0}, use_global_device_ids=true | all-gather | bytes 983040 | tf_op jit(solution)/shard_map/all_gather | solution.py:78
  91.1 6.8 %collective-permute-start.4 = (bf16[3072,128]{1,0:T(8,128)(2,1)S(1)}, bf16[3072,128]{1,0:T(8,128)(2,1)}, u32[]{:S(2)}, u32[]{:S(2)}) collective-permute-start(bf16[3072,128]{1,0:T(8,128)(2,1)S(1)} %all_gather.33.own_ref.own0_ref), channel_id=1, source_target_pairs={{0,1},{1,0},{2,3},{3,2},{4,5},{5,4},{6,7},{7,6},{8,9},{9,8},{10,11... | collective-permute-start | bytes 2359304 | tf_op jit(solution)/shard_map/ppermute | solution.py:37
  97.8 0.8 broadcast_select_fusion.mine_ref
  98.7 1.2 collective-permute-done.4.other_ref.other0_ref
  99.9 1.4 copy-done.2
  101.3 3.0 %tick.3 = (bf16[192,128]{1,0:T(8,128)(2,1)}, bf16[384,128]{1,0:T(8,128)(2,1)S(1)}) custom-call(s32[2]{0:T(128)S(1)} %pad_add_fusion.where_ref, bf16[3072,128]{1,0:T(8,128)(2,1)S(1)} %all_gather.33.own_ref.own0_ref, bf16[3072,128]{1,0:T(8,128)(2,1)} %collective-permute-done.4.other_ref.other0_ref, bf16[6144,128]{1,0:T(8,128)(2,1)S(1)} %copy-done.2, ...), custom_call_target="tpu_custom_call" | custom-call | tf_op jit(solution)/shard_map/tick/pallas_call | solution.py:149
  105.6 32.9 %all_gather.35 = bf16[768,128]{1,0:T(8,128)(2,1)S(1)} all-gather(bf16[192,128]{1,0:T(8,128)(2,1)} %get-tuple-element.18), channel_id=1, replica_groups={{0,8,16,24},{1,9,17,25},{2,10,18,26},{3,11,19,27},{4,12,20,28},{5,13,21..., dimensions={0}, use_global_device_ids=true | all-gather | bytes 245760 | tf_op jit(solution)/shard_map/all_gather | solution.py:78
  138.5 11.5 %all_gather.36.own1_ref = bf16[3072,128]{1,0:T(8,128)(2,1)S(1)} all-gather(bf16[768,128]{1,0:T(8,128)(2,1)S(1)} %all_gather.35), channel_id=1, replica_groups={{0,2,4,6},{1,3,5,7},{8,10,12,14},{9,11,13,15},{16,18,20,22},{17,19,21,2..., dimensions={0}, use_global_device_ids=true | all-gather | bytes 983040 | tf_op jit(solution)/shard_map/all_gather | solution.py:78
  150.0 8.9 %collective-permute-start.6 = (bf16[3072,128]{1,0:T(8,128)(2,1)S(1)}, bf16[3072,128]{1,0:T(8,128)(2,1)S(1)}, u32[]{:S(2)}, u32[]{:S(2)}) collective-permute-start(bf16[3072,128]{1,0:T(8,128)(2,1)S(1)} %all_gather.36.own1_ref), channel_id=1, source_target_pairs={{0,1},{1,0},{2,3},{3,2},{4,5},{5,4},{6,7},{7,6},{8,9},{9,8},{10,11... | collective-permute-start | bytes 2359304 | tf_op jit(solution)/shard_map/ppermute | solution.py:37
  158.9 1.9 collective-permute-done.6.other1_ref
  160.8 2.0 copy-done
  162.8 3.1 %predict.1 = bf16[576,128]{1,0:T(8,128)(2,1)S(1)} custom-call(s32[2]{0:T(128)S(1)} %pad_add_fusion.where_ref, bf16[3072,128]{1,0:T(8,128)(2,1)S(1)} %all_gather.33.own_ref.own0_ref, bf16[3072,128]{1,0:T(8,128)(2,1)} %collective-permute-done.4.other_ref.other0_ref, bf16[3072,128]{1,0:T(8,128)(2,1)S(1)} %all_gather.36.own1_ref, ...), custom_call_target="tpu_custom_call" | custom-call | tf_op jit(solution)/shard_map/predict/pallas_call | solution.py:181
  165.9 18.2 %all_gather.38.near_ref = bf16[2304,128]{1,0:T(8,128)(2,1)S(1)} all-gather(bf16[576,128]{1,0:T(8,128)(2,1)S(1)} %predict.1), channel_id=1, replica_groups={{0,128,256,384},{32,160,288,416},{64,192,320,448},{96,224,352,480},{1,1..., dimensions={0}, use_global_device_ids=true | all-gather | bytes 737280 | tf_op jit(solution)/shard_map/all_gather | solution.py:78
  184.1 1.9 collective-permute-start.7
  186.0 12.0 %collective-permute-done.7.far_ref = bf16[2304,128]{1,0:T(8,128)(2,1)S(1)} collective-permute-done((bf16[2304,128]{1,0:T(8,128)(2,1)S(1)}, bf16[2304,128]{1,0:T(8,128)(2,1)S(1)}, u32[]{:S(2)}, u32[]{:S(2)}) %collective-permute-start.7) | collective-permute-done | bytes 589856 | tf_op jit(solution)/shard_map/ppermute | solution.py:41
  198.0 1.9 copy-done.1
  199.9 2.5 %gradient.1 = (f32[288,384]{1,0:T(8,128)S(1)}, bf16[288,384]{1,0:T(8,128)(2,1)S(1)}) custom-call(s32[2]{0:T(128)S(1)} %pad_add_fusion.where_ref, bf16[2304,128]{1,0:T(8,128)(2,1)S(1)} %all_gather.38.near_ref, bf16[2304,128]{1,0:T(8,128)(2,1)S(1)} %collective-permute-done.7.far_ref, bf16[12288,128]{1,0:T(8,128)(2,1)S(1)} %copy-done.1), custom_call_target="tpu_custom_call" | custom-call | tf_op jit(solution)/shard_map/gradient/pallas_call | solution.py:217
  202.3 6.7 %collective-permute-start.8 = (bf16[288,384]{1,0:T(8,128)(2,1)S(1)}, bf16[288,384]{1,0:T(8,128)(2,1)S(1)}, u32[]{:S(2)}, u32[]{:S(2)}) collective-permute-start(bf16[288,384]{1,0:T(8,128)(2,1)S(1)} %get-tuple-element.23), channel_id=1, source_target_pairs={{0,32},{32,0},{64,96},{96,64},{128,160},{160,128},{192,224},{224,1... | collective-permute-start | bytes 663560 | tf_op jit(solution)/shard_map/ppermute | solution.py:51
  209.1 3.3 %collective-permute-done.8 = bf16[288,384]{1,0:T(8,128)(2,1)S(1)} collective-permute-done((bf16[288,384]{1,0:T(8,128)(2,1)S(1)}, bf16[288,384]{1,0:T(8,128)(2,1)S(1)}, u32[]{:S(2)}, u32[]{:S(2)}) %collective-permute-start.8) | collective-permute-done | bytes 221216 | tf_op jit(solution)/shard_map/ppermute | solution.py:51
  212.4 0.8 add_bitcast_fusion
  (27 shorter events, 3.0 us)
Async XLA Ops:
  7.2 45.8 %copy-start.6 = (f32[1,6144]{1,0:T(1,128)S(1)}, f32[1,6144]{1,0:T(1,128)}, u32[]{:S(2)}) copy-start(f32[1,6144]{1,0:T(1,128)} %param.8) | copy-start | bytes 73732
  7.2 92.7 %all-gather.4.cloned.1.call-start = ((), (), s32[]{:S(2)}) async-start(), calls=%async_computation | async-start | bytes 1769472 | tf_op jit(solution)/shard_map/all_gather | solution.py:78
  28.7 132.2 %all-gather.6.cloned.1.call-start = ((), (), s32[]{:S(2)}) async-start(), calls=%async_computation.1 | async-start | bytes 3981312 | tf_op jit(solution)/shard_map/all_gather | solution.py:78
  28.7 14.5 %collective-permute-start = (bf16[288,384]{1,0:T(8,128)(2,1)}, bf16[288,384]{1,0:T(8,128)(2,1)S(1)}, u32[]{:S(2)}, u32[]{:S(2)}) collective-permute-start(bf16[288,384]{1,0:T(8,128)(2,1)} %bitcast.32), channel_id=1, source_target_pairs={{0,32},{32,0},{64,96},{96,64},{128,160},{160,128},{192,224},{224,1... | collective-permute-start | bytes 663560 | tf_op jit(solution)/shard_map/ppermute | solution.py:51
  43.2 11.9 %copy-start.4 = (bf16[1,2,128,288]{2,3,1,0:T(8,128)(2,1)S(1)}, bf16[1,2,128,288]{2,3,1,0:T(8,128)(2,1)}, u32[]{:S(2)}) copy-start(bf16[1,2,128,288]{2,3,1,0:T(8,128)(2,1)} %param.11) | copy-start | bytes 442372
  43.2 14.6 %copy-start.3 = (bf16[1,128,192]{1,2,0:T(8,128)(2,1)S(1)}, bf16[1,128,192]{1,2,0:T(8,128)(2,1)}, u32[]{:S(2)}) copy-start(bf16[1,128,192]{1,2,0:T(8,128)(2,1)} %param.6) | copy-start | bytes 147460
  45.0 153.0 %all-gather.8.cloned.1.call-start = ((), (), s32[]{:S(2)}) async-start(), calls=%async_computation.2 | async-start | bytes 3244032 | tf_op jit(solution)/shard_map/all_gather | solution.py:260
  45.1 12.7 %collective-permute-start.1 = (bf16[3072,128]{1,0:T(8,128)(2,1)S(1)}, bf16[3072,128]{1,0:T(8,128)(2,1)}, u32[]{:S(2)}, u32[]{:S(2)}) collective-permute-start(bf16[3072,128]{1,0:T(8,128)(2,1)S(1)} %all_gather.31.own_ref), channel_id=1, source_target_pairs={{0,1},{1,0},{2,3},{3,2},{4,5},{5,4},{6,7},{7,6},{8,9},{9,8},{10,11... | collective-permute-start | bytes 2359304 | tf_op jit(solution)/shard_map/ppermute | solution.py:37
  55.2 9.5 %collective-permute-start.3 = (bf16[2,288,128]{2,1,0:T(8,128)(2,1)S(1)}, bf16[2,288,128]{2,1,0:T(8,128)(2,1)S(1)}, u32[]{:S(2)}, u32[]{:S(2)}) collective-permute-start(bf16[2,288,128]{2,1,0:T(8,128)(2,1)S(1)} %bitcast.27), channel_id=1, source_target_pairs={{0,32},{32,64},{64,96},{96,128},{128,160},{160,192},{192,224},{224... | collective-permute-start | bytes 442376 | tf_op jit(solution)/shard_map/ppermute | solution.py:55
  60.1 6.9 %collective-permute-start.2 = (bf16[192,128]{1,0:T(8,128)(2,1)S(1)}, bf16[192,128]{1,0:T(8,128)(2,1)S(1)}, u32[]{:S(2)}, u32[]{:S(2)}) collective-permute-start(bf16[192,128]{1,0:T(8,128)(2,1)S(1)} %tick.2), channel_id=1, source_target_pairs={{0,32},{32,64},{64,96},{96,128},{128,160},{160,192},{192,224},{224... | collective-permute-start | bytes 147464 | tf_op jit(solution)/shard_map/ppermute | solution.py:55
  91.1 8.8 %collective-permute-start.4 = (bf16[3072,128]{1,0:T(8,128)(2,1)S(1)}, bf16[3072,128]{1,0:T(8,128)(2,1)}, u32[]{:S(2)}, u32[]{:S(2)}) collective-permute-start(bf16[3072,128]{1,0:T(8,128)(2,1)S(1)} %all_gather.33.own_ref.own0_ref), channel_id=1, source_target_pairs={{0,1},{1,0},{2,3},{3,2},{4,5},{5,4},{6,7},{7,6},{8,9},{9,8},{10,11... | collective-permute-start | bytes 2359304 | tf_op jit(solution)/shard_map/ppermute | solution.py:37
  99.9 1.4 copy-start.2
  104.2 0.7 collective-permute-start.5
  104.9 0.6 copy-start.5
  150.0 10.8 %collective-permute-start.6 = (bf16[3072,128]{1,0:T(8,128)(2,1)S(1)}, bf16[3072,128]{1,0:T(8,128)(2,1)S(1)}, u32[]{:S(2)}, u32[]{:S(2)}) collective-permute-start(bf16[3072,128]{1,0:T(8,128)(2,1)S(1)} %all_gather.36.own1_ref), channel_id=1, source_target_pairs={{0,1},{1,0},{2,3},{3,2},{4,5},{5,4},{6,7},{7,6},{8,9},{9,8},{10,11... | collective-permute-start | bytes 2359304 | tf_op jit(solution)/shard_map/ppermute | solution.py:37
  160.8 2.0 copy-start
  184.1 13.9 %collective-permute-start.7 = (bf16[2304,128]{1,0:T(8,128)(2,1)S(1)}, bf16[2304,128]{1,0:T(8,128)(2,1)S(1)}, u32[]{:S(2)}, u32[]{:S(2)}) collective-permute-start(bf16[2304,128]{1,0:T(8,128)(2,1)S(1)} %all_gather.38.near_ref), channel_id=1, source_target_pairs={{0,64},{32,96},{64,0},{96,32},{128,192},{160,224},{192,128},{224,1... | collective-permute-start | bytes 1769480 | tf_op jit(solution)/shard_map/ppermute | solution.py:41
  198.0 1.9 copy-start.1
  202.3 10.1 %collective-permute-start.8 = (bf16[288,384]{1,0:T(8,128)(2,1)S(1)}, bf16[288,384]{1,0:T(8,128)(2,1)S(1)}, u32[]{:S(2)}, u32[]{:S(2)}) collective-permute-start(bf16[288,384]{1,0:T(8,128)(2,1)S(1)} %get-tuple-element.23), channel_id=1, source_target_pairs={{0,32},{32,0},{64,96},{96,64},{128,160},{160,128},{192,224},{224,1... | collective-permute-start | bytes 663560 | tf_op jit(solution)/shard_map/ppermute | solution.py:51
Sparse Core Ops, SparseCore 0:
  28.8 32.2 all-gather.3
  63.7 54.2 all-gather.5
  121.1 68.0 all-gather.7
